TPU v7x, 32 devices: a whole 2x2x4 slice. The times are simulated.
32 devices in a mesh: ctx: 8 (over z, y), seq: 4 (over x, core).
Axes of the slice: x: 2, y: 2, z: 4, core: 2. Of those that a mesh axis runs over, the one named last changes fastest.
Arguments:
- query_matrix: bfloat16 [32768, 2048], P(('seq', 'ctx')), parts along dimension 0, may hold values from -7 to 7
- key_vectors: bfloat16 [32768, 2048], P(('seq', 'ctx')), parts along dimension 0, may hold values from -7.5 to 7.5
- value_vectors: bfloat16 [32768, 4096], P(('seq', 'ctx')), parts along dimension 0, may hold values from -6 to 6
- input_gate: float32 [8, 32768], P(None, ('seq', 'ctx')), parts along dimension 1, may hold values from -4 to 300
- forget_gate: float32 [8, 32768], P(None, ('seq', 'ctx')), parts along dimension 1, may hold values from 0 to 12.7
Outputs:
- hidden_state: bfloat16 [32768, 4096], P(('seq', 'ctx')), parts along dimension 0
- final_memory: float32 [32, 256, 512], P('seq', 'ctx'), parts along dimension 0
- final_normalizer: float32 [32, 256], P('seq', 'ctx'), parts along dimension 0
- final_stabilizer: float32 [32], P('seq'), parts along dimension 0
There are 4 independent parts, one for each index of `seq`. A program takes and returns all parts, laid end to end along the dimension named above; each array names one. Nothing has to cross between parts.
All inputs are finite; a program needn't handle non-finite values.
Results may differ from a plain program's by a relative error of at most 0.0056.
Values sent between devices are 32-bit elements; how exact they have to be, the bound alone decides.
No kernel may reach another device: no remote copies, remote signals or barrier semaphores. Data moves between devices by JAX's collectives and lax.ppermute only.
A program may use at most 192 MiB of HBM per device.

v0:
```python
import math

import jax
import jax.numpy as jnp
from jax import lax
from jax.sharding import PartitionSpec as P

H = 8
DQK = 256
DV = 512


VERY_NEGATIVE = -1e30


def prefix_2(part, axis, combine, identity):
    place = lax.axis_index(axis)
    gathered = jax.tree.map(lambda a: lax.all_gather(a, axis), part)
    state = jax.tree.map(lambda a, e: jnp.zeros_like(a) + jnp.asarray(e, a.dtype), part, identity)

    def one(turn, state):
        return combine(
            state, jax.tree.map(lambda a: lax.dynamic_index_in_dim(a, turn, 0, False), gathered)
        )

    return lax.fori_loop(0, place, one, state)


def summarize(key_vectors, value_vectors, input_gate, cumulated):
    decay_sum = cumulated[:, -1]
    exponent = decay_sum[:, None] - cumulated + input_gate
    stabilizer = jnp.max(exponent, axis=1)
    weight = jnp.exp(exponent - stabilizer[:, None])

    def summarize_one_head(head_index):
        key_rows = lax.dynamic_slice_in_dim(key_vectors, head_index * DQK, DQK, 1).astype(
            jnp.float32
        )
        value_rows = lax.dynamic_slice_in_dim(value_vectors, head_index * DV, DV, 1)
        scaled = key_rows * weight[head_index][:, None]
        matrix_memory = lax.dot_general(
            scaled.astype(jnp.bfloat16),
            value_rows,
            (((0,), (0,)), ((), ())),
            preferred_element_type=jnp.float32,
        )
        return (matrix_memory, jnp.sum(scaled, axis=0))

    matrix_memory, normal = lax.map(summarize_one_head, jnp.arange(H, dtype=jnp.int32))
    return (matrix_memory, normal, stabilizer, decay_sum)


def combine(earlier, later):
    first_memory, first_normal, first_stab, first_decay = earlier
    second_memory, second_normal, second_stab, second_decay = later
    stabilizer = jnp.maximum(first_stab + second_decay, second_stab)
    first_scale = jnp.exp(first_stab + second_decay - stabilizer)
    second_scale = jnp.exp(second_stab - stabilizer)
    matrix_memory = (
        first_memory * first_scale[..., None, None] + second_memory * second_scale[..., None, None]
    )
    normal = first_normal * first_scale[..., None] + second_normal * second_scale[..., None]
    return (matrix_memory, normal, stabilizer, first_decay + second_decay)


def block_output(
    query_matrix,
    key_vectors,
    value_vectors,
    input_gate,
    cumulated,
    prefix_memory,
    prefix_normal,
    prefix_stab,
):
    length = query_matrix.shape[0]
    scaling = 1.0 / math.sqrt(DQK)
    memory_b = prefix_memory.astype(jnp.bfloat16)
    row_index = lax.broadcasted_iota(jnp.int32, (length, length), 0)
    col_index = lax.broadcasted_iota(jnp.int32, (length, length), 1)
    causal = row_index >= col_index

    def block_one_head(head_index, out_buffer):
        head_index = jnp.asarray(head_index).astype(jnp.int32)
        query_rows = lax.dynamic_slice_in_dim(query_matrix, head_index * DQK, DQK, 1)
        key_rows = lax.dynamic_slice_in_dim(key_vectors, head_index * DQK, DQK, 1)
        value_rows = lax.dynamic_slice_in_dim(value_vectors, head_index * DV, DV, 1)
        scores = (
            lax.dot_general(
                query_rows, key_rows, (((1,), (1,)), ((), ())), preferred_element_type=jnp.float32
            )
            * scaling
        )
        cum_head = cumulated[head_index]
        gate_head = input_gate[head_index]
        exponent = jnp.where(
            causal, cum_head[:, None] - cum_head[None, :] + gate_head[None, :], VERY_NEGATIVE
        )
        carried = cum_head + prefix_stab[head_index]
        stabilizer = jnp.maximum(carried, jnp.max(exponent, axis=1))
        weights = jnp.where(causal, jnp.exp(exponent - stabilizer[:, None]) * scores, 0.0)
        factor = jnp.exp(carried - stabilizer)
        carried_term = (
            jnp.dot(query_rows, memory_b[head_index], preferred_element_type=jnp.float32) * scaling
        )
        numerator = factor[:, None] * carried_term + jnp.dot(
            weights.astype(jnp.bfloat16), value_rows, preferred_element_type=jnp.float32
        )
        query_normal = (
            jnp.sum(query_rows.astype(jnp.float32) * prefix_normal[head_index][None, :], axis=1)
            * scaling
        )
        denominator = factor * query_normal + jnp.sum(weights, axis=1)
        result = numerator / jnp.maximum(jnp.abs(denominator), jnp.exp(-stabilizer))[:, None]
        return lax.dynamic_update_slice_in_dim(
            out_buffer, result.astype(jnp.bfloat16), head_index * DV, 1
        )

    return lax.fori_loop(0, H, block_one_head, jnp.zeros((length, H * DV), jnp.bfloat16))


def shards(query_matrix, key_vectors, value_vectors, input_gate, forget_gate):
    log_forget = jax.nn.log_sigmoid(forget_gate)
    cumulated = jnp.cumsum(log_forget, axis=1)
    matrix_memory, normal, stabilizer, decay_sum = summarize(
        key_vectors, value_vectors, input_gate, cumulated
    )
    identity = (
        jnp.zeros_like(matrix_memory),
        jnp.zeros_like(normal),
        jnp.full(stabilizer.shape, VERY_NEGATIVE, jnp.float32),
        jnp.zeros_like(decay_sum),
    )
    prefix = prefix_2((matrix_memory, normal, stabilizer, decay_sum), "ctx", combine, identity)
    hidden_state = block_output(
        query_matrix,
        key_vectors,
        value_vectors,
        input_gate,
        cumulated,
        prefix[0],
        prefix[1],
        prefix[2],
    )
    grand_decay = lax.psum(decay_sum, "ctx")
    post_decay_memory = grand_decay - prefix[3] - decay_sum
    end_stab = stabilizer + post_decay_memory
    final_stabilizer = lax.pmax(end_stab, "ctx")
    rescale = jnp.exp(end_stab - final_stabilizer)
    final_memory, final_normalizer = (
        lax.psum_scatter(
            matrix_memory * rescale[:, None, None], "ctx", scatter_dimension=1, tiled=True
        ),
        lax.psum_scatter(normal * rescale[:, None], "ctx", scatter_dimension=1, tiled=True),
    )
    return (hidden_state, final_memory, final_normalizer, final_stabilizer)


def solution(mesh):
    in_specs = (
        P(("seq", "ctx"), None),
        P(("seq", "ctx"), None),
        P(("seq", "ctx"), None),
        P(None, ("seq", "ctx")),
        P(None, ("seq", "ctx")),
    )
    out_specs = (P(("seq", "ctx"), None), P("seq", "ctx", None), P("seq", "ctx"), P("seq"))
    return jax.shard_map(shards, mesh=mesh, in_specs=in_specs, out_specs=out_specs, check_vma=False)
```

profile of v0, /device:TPU:0, one launch (start us, length us, event | category | flops | bytes accessed | tf_op | source)
XLA Modules:
  0.0 949.5 jit_solution(7290483065592333095)
XLA Ops:
  8.0 2.3 reduce-window.6
  10.9 1.0 fusion.35
  11.8 0.8 subtract_exponential_fusion.3
  12.7 2.6 broadcast.64.clone
  15.3 65.1 %while.43 = (s32[]{:T(128)}, f32[8,256,512]{2,1,0:T(8,128)}, f32[8,256]{1,0:T(8,128)S(1)}, s32[8]{0:T(128)S(1)}, bf16[1024,2048]{1,0:T(8,128)(2,1)}, /*index=5*/...) while((s32[]{:T(128)}, f32[8,256,512]{2,1,0:T(8,128)}, ...), condition=%wide.region_5.6_spmd, body=%wide.region_3.5_spmd.sunk | while | flops 270008064 | bytes 2641699 | solution.py:49
  19.1 3.0 fusion.56
  22.1 1.3 fusion.57
  27.3 3.0 fusion.56
  30.2 1.3 fusion.57
  35.4 3.0 fusion.56
  38.4 1.3 fusion.57
  43.5 3.0 fusion.56
  46.5 1.3 fusion.57
  51.7 3.0 fusion.56
  54.7 1.3 fusion.57
  59.8 3.0 fusion.56
  62.8 1.3 fusion.57
  68.0 3.0 fusion.56
  70.9 1.3 fusion.57
  76.1 3.0 fusion.56
  79.1 1.3 fusion.57
  82.8 65.0 %all-reduce.2 = (f32[64]{0:T(128)S(1)}, f32[64]{0:T(128)S(1)}, f32[8]{0:T(128)S(1)}) all-reduce(f32[64]{0:T(128)S(1)} %dynamic-update-slice, f32[64]{0:T(128)S(1)} %dynamic-update-slice.1, f32[8]{0:T(128)S(1)} %slice_reduce_fusion.1), channel_id=2, replica_groups=mesh['ctx'=8,'seq'=4] {'ctx'}, use_global_device_ids=true, to_apply=%add | all-reduce | flops 136 | bytes 1088
  147.9 44.6 %all-gather.3 = f32[64,256]{1,0:T(8,128)S(1)} all-gather(f32[8,256]{1,0:T(8,128)S(1)} %get-tuple-element.286), channel_id=5, replica_groups=mesh['ctx'=8,'seq'=4] {'ctx'}, dimensions={0}, use_global_device_ids=true | all-gather | bytes 73728 | tf_op jit(solution)/shard_map/all_gather | solution.py:18
  192.5 530.3 %all-gather.6.cloned.1.call-done = f32[64,256,512]{2,1,0:T(8,128)} async-done(((f32[8,256,512]{2,1,0:T(8,128)}), f32[64,256,512]{2,1,0:T(8,128)}) %all-gather.6.cloned.1.call-update) | async-done | bytes 33554448 | tf_op jit(solution)/shard_map/all_gather | solution.py:18
  722.7 2.5 broadcast.64
  725.3 67.1 %pmax.7 = f32[8]{0:T(128)S(1)} all-reduce(f32[8]{0:T(128)S(1)} %subtract_add_fusion.1), channel_id=1, replica_groups=mesh['ctx'=8,'seq'=4] {'ctx'}, use_global_device_ids=true, to_apply=%region_14.15 | all-reduce | flops 8 | bytes 64 | tf_op jit(solution)/shard_map/pmax | solution.py:148
  793.4 4.9 broadcast_multiply_fusion
  798.3 2.5 convert_element_type.30
  800.8 4.4 broadcast_in_dim.42
  805.2 108.5 %while.45 = (s32[]{:T(128)}, bf16[1024,4096]{1,0:T(8,128)(2,1)}, bf16[1024,2048]{1,0:T(8,128)(2,1)}, bf16[8,256,512]{2,1,0:T(8,128)(2,1)S(1)}, f32[8,1024]{1,0:T...) while((s32[]{:T(128)}, bf16[1024,4096]{1,0:T(8,128)(2,1)}, ...), condition=%wide.region_12.13_spmd.clone.clone, body=%wide.region_8.12_spmd.clone.clone.sunk | while | flops 1897669632 | bytes 12948253 | solution.py:119
  807.7 3.6 fusion.65
  811.2 3.1 fusion.66
  814.4 1.3 multiply_reduce_fusion.2
  816.3 2.5 fusion.68
  821.2 3.6 fusion.65
  824.7 3.1 fusion.66
  827.9 1.3 multiply_reduce_fusion.2
  829.8 2.5 fusion.68
  834.7 3.6 fusion.65
  838.3 3.1 fusion.66
  841.5 1.3 multiply_reduce_fusion.2
  843.4 2.5 fusion.68
  848.3 3.6 fusion.65
  851.8 3.1 fusion.66
  855.0 1.3 multiply_reduce_fusion.2
  856.9 2.5 fusion.68
  861.8 3.6 fusion.65
  865.4 3.1 fusion.66
  868.6 1.3 multiply_reduce_fusion.2
  870.5 2.5 fusion.68
  875.4 3.6 fusion.65
  879.0 3.2 fusion.66
  882.2 1.3 multiply_reduce_fusion.2
  884.1 2.5 fusion.68
  889.0 3.6 fusion.65
  892.6 3.2 fusion.66
  895.8 1.3 multiply_reduce_fusion.2
  897.7 2.5 fusion.68
  902.6 3.6 fusion.65
  906.2 3.2 fusion.66
  909.4 1.3 multiply_reduce_fusion.2
  911.3 2.5 fusion.68
  913.8 1.4 copy.13
  915.1 27.8 %reduce-scatter.5.cloned.1.call-done = f32[8,32,512]{2,1,0:T(8,128)} async-done(((f32[8,256,512]{2,1,0:T(8,128)}), f32[8,32,512]{2,1,0:T(8,128)}) %reduce-scatter.5.cloned.1.call-update) | async-done | bytes 524304 | tf_op jit(solution)/shard_map/reduce_scatter | solution.py:151
  (107 shorter events, 33.7 us)
Async XLA Ops:
  7.2 715.6 %all-gather.6.cloned.1.call-start = ((), (), s32[]{:S(2)}) async-start(), calls=%async_computation.3 | async-start | bytes 37748736 | tf_op jit(solution)/shard_map/all_gather | solution.py:18
  80.4 0.7 copy-start.1
  80.4 833.3 %reduce-scatter.7.cloned.1.call-start = ((), (), s32[]{:S(2)}) async-start(), calls=%async_computation.4 | async-start | bytes 147456
  792.4 5.9 copy-start
  793.3 149.6 %reduce-scatter.5.cloned.1.call-start = ((), (), s32[]{:S(2)}) async-start(), calls=%async_computation.2 | async-start | bytes 4718592 | tf_op jit(solution)/shard_map/reduce_scatter | solution.py:151
Sparse Core Ops, SparseCore 0:
  80.6 642.1 all-gather.5
  793.4 58.2 reduce-scatter.6
  856.0 86.9 reduce-scatter.4
where the time goes:
time: 953 us; the launch traced here: 949 us
  waiting for transfers between devices  558 us (59%)
  blocking collectives  177 us (19%)
  matrix products  97.5 us (10%)
  other arithmetic  46.1 us (5%)
  local copies, waits for them, and re-layouts  29.9 us (3%)
  loops' own time  26.5 us (3%)
  between operations  14.5 us (2%)
    all_gather x1, waiting for transfers between devices, prefix_2(): gathered = jax.tree.map(lambda a: lax.all_gather(a, axis), part)  530 us
    pmax x1, blocking collectives, shards(): final_stabilizer = lax.pmax(end_stab, 'ctx')  67.1 us
    unnamed x1, blocking collectives  65 us
    all_gather x1, blocking collectives, prefix_2(): gathered = jax.tree.map(lambda a: lax.all_gather(a, axis), part)  44.6 us
    dot_general x8, matrix products, block_one_head(): lax.dot_general(query_rows, key_rows, (((1,), (1,)), ((), ())), preferred...  28.5 us
    reduce_scatter x1, waiting for transfers between devices, shards(): lax.psum_scatter(matrix_memory * rescale[:, None, None], 'ctx', scatter_d...  27.8 us
    another operation x1, loops' own time, summarize(): lax.map(summarize_one_head, jnp.arange(H, dtype=jnp.int32))  26.2 us
    dot_general x8, matrix products, block_one_head(): jnp.dot(weights.astype(jnp.bfloat16), value_rows, preferred_element_type=...  25.3 us
  transfers between devices with their start and end apart: 3, of which 2 were waited for; matrix products, arithmetic and copies ran while one was open for 13% of the time, Pallas kernels for 0%

commit v1 on v0

v1 whole, which is shorter than its diff:
```python
import functools

import jax
import jax.numpy as jnp
from jax import lax
from jax.experimental import pallas as pl
from jax.experimental.pallas import tpu as pltpu
from jax.sharding import PartitionSpec as P

VERY_NEGATIVE = -1e30
LANES = 128
MIB = 1 << 20

ROW_A, ROW_B, ROW_KEEP, ROW_RECV, ROW_SEND_P, ROW_SEND_S, ROW_OWN_P, ROW_OWN_S, ROW_FIN_P, ROW_FIN_L = range(10)
TABLE_ROWS = 16


def params(mib):
    return pltpu.CompilerParams(vmem_limit_bytes=mib * MIB)


def cost(flops, bytes_accessed, transcendentals=0):
    return pl.CostEstimate(
        flops=int(flops), bytes_accessed=int(bytes_accessed), transcendentals=int(transcendentals)
    )


def lane_iota(shape):
    return lax.broadcasted_iota(jnp.int32, shape, len(shape) - 1)


def pick_lane(block, lane):
    return jnp.sum(jnp.where(lane_iota(block.shape) == lane, block, 0.0), axis=1, keepdims=True)


def gates_kernel(input_ref, forget_ref, rows_ref, columns_ref, stats_ref):
    heads, tokens = input_ref.shape
    gate = forget_ref[...]
    cumulated = jnp.minimum(gate, 0.0) - jnp.log1p(jnp.exp(-jnp.abs(gate)))
    lanes = lane_iota((heads, tokens))
    step = 1
    while step < tokens:
        cumulated = cumulated + jnp.where(lanes >= step, pltpu.roll(cumulated, step, 1), 0.0)
        step *= 2
    level = input_ref[...] - cumulated
    running = level
    step = 1
    while step < tokens:
        running = jnp.maximum(
            running, jnp.where(lanes >= step, pltpu.roll(running, step, 1), VERY_NEGATIVE)
        )
        step *= 2
    highest = jnp.max(level, axis=1, keepdims=True)
    decay = cumulated[:, tokens - 1 : tokens]
    weight = jnp.exp(level - highest)
    rows_ref[...] = level
    filler = jnp.zeros((LANES - 3 * heads, tokens), jnp.float32)
    columns_ref[...] = jnp.concatenate([weight, running, cumulated, filler], axis=0).T
    lane = lane_iota((heads, LANES))
    stats_ref[...] = jnp.where(lane == 0, decay + highest, jnp.where(lane == 1, decay, 0.0))


def gates(input_gate, forget_gate):
    heads, tokens = input_gate.shape
    return pl.pallas_call(
        gates_kernel,
        out_shape=(
            jax.ShapeDtypeStruct((heads, tokens), jnp.float32),
            jax.ShapeDtypeStruct((tokens, LANES), jnp.float32),
            jax.ShapeDtypeStruct((heads, LANES), jnp.float32),
        ),
        cost_estimate=cost(1e6, 1e6),
        name="gates",
    )(input_gate, forget_gate)


def summary_of(head, key_ref, value_ref, columns_ref):
    weight = pick_lane(columns_ref[...], head)
    scaled = key_ref[...].astype(jnp.float32) * weight
    memory = lax.dot_general(
        scaled.astype(jnp.bfloat16),
        value_ref[...],
        (((0,), (0,)), ((), ())),
        preferred_element_type=jnp.float32,
    )
    return memory, jnp.sum(scaled, axis=0, keepdims=True)


def summary_kernel(first_ref, key_ref, value_ref, columns_ref, normal_ref, *memory_refs, count):
    turn = pl.program_id(0)
    memory, normal = summary_of(first_ref[0] + turn, key_ref, value_ref, columns_ref)
    normal_ref[0] = normal
    half = memory.shape[1] // 2
    for place in range(count):

        @pl.when(turn == place)
        def _():
            memory_refs[2 * place][...] = memory[:, :half]
            memory_refs[2 * place + 1][...] = memory[:, half:]


def summaries(first, count, keys, values, columns, dqk, dv):
    tokens = keys.shape[0]
    half = dv // 2
    outs = pl.pallas_call(
        functools.partial(summary_kernel, count=count),
        grid_spec=pltpu.PrefetchScalarGridSpec(
            num_scalar_prefetch=1,
            grid=(count,),
            in_specs=[
                pl.BlockSpec((tokens, dqk), lambda i, f: (0, f[0] + i)),
                pl.BlockSpec((tokens, dv), lambda i, f: (0, f[0] + i)),
                pl.BlockSpec((tokens, LANES), lambda i, f: (0, 0)),
            ],
            out_specs=[pl.BlockSpec((1, 1, dqk), lambda i, f: (i, 0, 0))]
            + [pl.BlockSpec((dqk, half), lambda i, f: (0, 0))] * (2 * count),
        ),
        out_shape=[jax.ShapeDtypeStruct((count, 1, dqk), jnp.float32)]
        + [jax.ShapeDtypeStruct((dqk, half), jnp.float32)] * (2 * count),
        compiler_params=params(32),
        cost_estimate=cost(
            2 * count * tokens * dqk * dv, count * (2 * tokens * (dqk + dv) + 4 * dqk * dv)
        ),
        name="summaries",
    )(first, keys, values, columns)
    return outs[0], outs[1:]


def weights_kernel(place_ref, gathered_ref, table_ref, prefix_ref, final_ref, tops_ref, *, blocks, skew):
    heads = gathered_ref.shape[1]
    dqk = gathered_ref.shape[2] - LANES
    lane_heads = heads // 2
    levels = blocks // 2
    place = place_ref[0]
    side = lax.rem(place, 2)
    level = lax.div(place, 2)

    tops, decays, normals = [], [], []
    for block in range(blocks):
        held = gathered_ref[lax.rem(block - place + blocks, blocks)]
        normals.append(held[:, :dqk])
        tops.append(held[:, dqk : dqk + 1])
        decays.append(held[:, dqk + 1 : dqk + 2])

    pick = lambda at, value, otherwise: jnp.where(level == at, value, otherwise)
    top = jnp.full((heads, 1), VERY_NEGATIVE, jnp.float32)
    normal = jnp.zeros((heads, dqk), jnp.float32)
    zero = jnp.zeros((heads, 1), jnp.float32)
    mine_a = mine_b = mine_first = mine_second = zero
    carry_p = carry_s = zero
    prefix_top, prefix_normal = zero, normal
    own_top = top
    scales = []
    for z in range(levels):
        t0, t1, d0, d1 = tops[2 * z], tops[2 * z + 1], decays[2 * z], decays[2 * z + 1]
        pair_top = jnp.maximum(t0 + d1, t1)
        first, second = jnp.exp(t0 + d1 - pair_top), jnp.exp(t1 - pair_top)
        pair_normal = normals[2 * z] * first + normals[2 * z + 1] * second
        middle_top = jnp.maximum(top + d0, t0)
        alpha, beta = jnp.exp(top + d0 - middle_top), jnp.exp(t0 - middle_top)
        middle_normal = normal * alpha + normals[2 * z] * beta
        pair_decay = d0 + d1
        next_top = jnp.maximum(top + pair_decay, pair_top)
        a, b = jnp.exp(top + pair_decay - next_top), jnp.exp(pair_top - next_top)
        mine_a, mine_b = pick(z, a, mine_a), pick(z, b, mine_b)
        mine_first, mine_second = pick(z, first, mine_first), pick(z, second, mine_second)
        carry_p, carry_s = pick(z, alpha, carry_p), pick(z, beta, carry_s)
        prefix_top = pick(z, jnp.where(side == 0, top, middle_top), prefix_top)
        prefix_normal = pick(z, jnp.where(side == 0, normal, middle_normal), prefix_normal)
        normal = normal * a + pair_normal * b
        top = next_top
        scales.append((a, b))
    later = jnp.ones((heads, 1), jnp.float32)
    final_p = final_l = zero
    for z in reversed(range(levels)):
        a, b = scales[z]
        final_l = pick(z, b * later, final_l)
        later = later * a
        final_p = pick(z, later, final_p)

    one = jnp.ones((heads, 1), jnp.float32)
    by_side = lambda zero_value, one_value: jnp.where(side == 0, zero_value, one_value)
    lanes = lane_iota((heads, LANES))
    rows = lax.broadcasted_iota(jnp.int32, (heads, LANES), 0)
    head_of_chunk = lane_heads * side + lax.div(lanes, 2)
    head_of_step = lane_heads * side + lax.div(
        jnp.clip(lanes - skew * level, 0, 2 * lane_heads - 1), 2
    )

    def spread(column, heads_wanted):
        return jnp.sum(jnp.where(rows == heads_wanted, column, 0.0), axis=0, keepdims=True)

    entries = {
        ROW_A: spread(mine_a, head_of_step),
        ROW_B: spread(mine_b, head_of_step),
        ROW_KEEP: spread(by_side(mine_first, mine_second), head_of_chunk),
        ROW_RECV: spread(by_side(mine_second, mine_first), head_of_chunk),
        ROW_SEND_P: spread(by_side(carry_p, one), head_of_chunk),
        ROW_SEND_S: spread(by_side(carry_s, zero), head_of_chunk),
        ROW_OWN_P: spread(by_side(one, carry_p), head_of_chunk),
        ROW_OWN_S: spread(by_side(zero, carry_s), head_of_chunk),
        ROW_FIN_P: spread(final_p, head_of_chunk),
        ROW_FIN_L: spread(final_l, head_of_chunk),
    }
    empty = jnp.zeros((1, LANES), jnp.float32)
    table_ref[...] = jnp.concatenate([entries.get(r, empty) for r in range(TABLE_ROWS)], axis=0)
    prefix_ref[...] = prefix_normal
    final_ref[...] = normal
    tops_ref[...] = jnp.where(lanes == 0, prefix_top, jnp.where(lanes == 1, top, 0.0))


def weights(place, gathered, skew):
    blocks, heads, width = gathered.shape
    dqk = width - LANES
    return pl.pallas_call(
        functools.partial(weights_kernel, blocks=blocks, skew=skew),
        grid_spec=pltpu.PrefetchScalarGridSpec(
            num_scalar_prefetch=1,
            grid=(1,),
            in_specs=[pl.BlockSpec((blocks, heads, width), lambda i, p: (0, 0, 0))],
            out_specs=[
                pl.BlockSpec((TABLE_ROWS, LANES), lambda i, p: (0, 0)),
                pl.BlockSpec((heads, dqk), lambda i, p: (0, 0)),
                pl.BlockSpec((heads, dqk), lambda i, p: (0, 0)),
                pl.BlockSpec((heads, LANES), lambda i, p: (0, 0)),
            ],
        ),
        out_shape=[
            jax.ShapeDtypeStruct((TABLE_ROWS, LANES), jnp.float32),
            jax.ShapeDtypeStruct((heads, dqk), jnp.float32),
            jax.ShapeDtypeStruct((heads, dqk), jnp.float32),
            jax.ShapeDtypeStruct((heads, LANES), jnp.float32),
        ],
        cost_estimate=cost(1e6, 1e6),
        name="weights",
    )(place, gathered)


def attention_kernel(query_ref, key_ref, value_ref, rows_ref, columns_ref, *rest, first):
    out_ref, sums_ref = rest[-2:]
    turn = pl.program_id(0)
    head = first + turn
    tokens = query_ref.shape[0]
    heads = rows_ref.shape[0]
    tile = min(256, tokens)
    level = rows_ref[pl.ds(head, 1), :]
    lanes = lane_iota((tile, LANES))
    rows = lax.broadcasted_iota(jnp.int32, (tile, tile), 0)
    causal = rows >= lax.broadcasted_iota(jnp.int32, (tile, tile), 1)

    @pl.when(turn == 0)
    def _():
        sums_ref[...] = jnp.zeros_like(sums_ref)

    for start in range(0, tokens, tile):
        stop = start + tile
        here = pl.ds(start, tile)
        query = query_ref[here, :]
        running = pick_lane(columns_ref[here, :], heads + head)
        scores = lax.dot_general(
            query, key_ref[:stop, :], (((1,), (1,)), ((), ())), preferred_element_type=jnp.float32
        )
        attn = jnp.exp(level[:, :stop] - running) * scores
        last = jnp.where(causal, attn[:, start:], 0.0)
        attn = jnp.concatenate([attn[:, :start], last], axis=1) if start else last
        total = jnp.sum(attn, axis=1, keepdims=True)
        sums_ref[here, :] = jnp.where(lanes == head, total, sums_ref[here, :])
        out_ref[here, :] = jnp.dot(
            attn.astype(jnp.bfloat16), value_ref[:stop, :], preferred_element_type=jnp.float32
        ).astype(jnp.bfloat16)


def attention(first, count, queries, keys, values, rows, columns, held, dqk, dv):
    tokens = queries.shape[0]
    heads = rows.shape[0]
    in_specs = [
        pl.BlockSpec((tokens, dqk), lambda i: (0, first + i)),
        pl.BlockSpec((tokens, dqk), lambda i: (0, first + i)),
        pl.BlockSpec((tokens, dv), lambda i: (0, first + i)),
        pl.BlockSpec((heads, tokens), lambda i: (0, 0)),
        pl.BlockSpec((tokens, LANES), lambda i: (0, 0)),
    ]
    operands = [queries, keys, values, rows, columns]
    aliases = {}
    if held is not None:
        in_specs.append(pl.BlockSpec(memory_space=pl.ANY))
        operands.append(held)
        aliases = {5: 0}
    return pl.pallas_call(
        functools.partial(attention_kernel, first=first),
        grid=(count,),
        in_specs=in_specs,
        out_specs=[
            pl.BlockSpec((tokens, dv), lambda i: (0, first + i)),
            pl.BlockSpec((tokens, LANES), lambda i: (0, 0)),
        ],
        out_shape=[
            jax.ShapeDtypeStruct((tokens, heads * dv), jnp.bfloat16),
            jax.ShapeDtypeStruct((tokens, LANES), jnp.float32),
        ],
        input_output_aliases=aliases,
        compiler_params=params(32),
        cost_estimate=cost(
            2 * count * tokens * tokens * (dqk + dv) * 0.8, count * 4 * tokens * (dqk + dv)
        ),
        name="attention",
    )(*operands)


def factors_kernel(query_ref, columns_ref, normal_ref, tops_ref, *rest):
    *sums_refs, out_ref, product_ref = rest
    head = pl.program_id(0)
    heads, dqk = normal_ref.shape
    tokens = query_ref.shape[0]

    normal = normal_ref[...]
    high = normal.astype(jnp.bfloat16).astype(jnp.float32)
    middle = (normal - high).astype(jnp.bfloat16).astype(jnp.float32)
    low = normal - high - middle
    filler = jnp.zeros((LANES - 3 * heads, dqk), jnp.float32)
    parts = jnp.concatenate([high, middle, low, filler], axis=0).T
    lanes = lane_iota((dqk, LANES))
    parts = jnp.where((lanes < 3 * heads) & (lax.rem(lanes, heads) == head), parts, 0.0)
    product = jnp.dot(
        query_ref[...], parts.astype(jnp.bfloat16), preferred_element_type=jnp.float32
    )

    @pl.when(head == 0)
    def _():
        product_ref[...] = product

    @pl.when(head > 0)
    def _():
        product_ref[...] += product

    @pl.when(head == heads - 1)
    def _():
        lane = lane_iota((tokens, LANES))
        shift = lambda block, by: pltpu.roll(block, (LANES - by) % LANES, 1)
        product = product_ref[...]
        product = product + shift(product, heads) + shift(product, 2 * heads)
        top = jnp.concatenate(
            [tops_ref[...], jnp.zeros((LANES - heads, LANES), jnp.float32)], axis=0
        ).T[0:1, :]
        running, cumulated = shift(columns_ref[...], heads), shift(columns_ref[...], 2 * heads)
        total = sums_refs[0][...]
        for ref in sums_refs[1:]:
            total = total + ref[...]
        highest = jnp.maximum(running, top)
        scaling = float(dqk) ** -0.5
        local, carried = jnp.exp(running - highest), jnp.exp(top - highest)
        denominator = (local * total + carried * product) * scaling
        divisor = jnp.maximum(jnp.abs(denominator), jnp.exp(-(cumulated + highest)))
        local, carried = local * scaling / divisor, carried * scaling / divisor
        out_ref[...] = jnp.where(lane < heads, local, pltpu.roll(carried, heads, 1))


def factors(queries, columns, normal, tops, sums):
    tokens = queries.shape[0]
    heads, dqk = normal.shape
    whole = lambda shape: pl.BlockSpec(shape, lambda i: (0,) * len(shape))
    return pl.pallas_call(
        factors_kernel,
        grid=(heads,),
        in_specs=[
            pl.BlockSpec((tokens, dqk), lambda i: (0, i)),
            whole((tokens, LANES)),
            whole((heads, dqk)),
            whole((heads, LANES)),
        ]
        + [whole((tokens, LANES))] * len(sums),
        out_specs=whole((tokens, LANES)),
        out_shape=jax.ShapeDtypeStruct((tokens, LANES), jnp.float32),
        scratch_shapes=[pltpu.VMEM((tokens, LANES), jnp.float32)],
        compiler_params=params(24),
        cost_estimate=cost(2 * tokens * heads * dqk * 512, 2 * tokens * heads * dqk),
        name="factors",
    )(queries, columns, normal, tops, *sums)


def finish_kernel(block_ref, query_ref, factors_ref, held_ref, *rest, dv_blocks, heads):
    *memory_refs, out_ref = rest
    turn = pl.program_id(0)
    head = lax.div(block_ref[0] + turn, dv_blocks)
    local = pick_lane(factors_ref[...], head)
    carried = pick_lane(factors_ref[...], heads + head)
    for place, memory_ref in enumerate(memory_refs):

        @pl.when(turn == place)
        def _():
            term = jnp.dot(
                query_ref[...],
                memory_ref[...].astype(jnp.bfloat16),
                preferred_element_type=jnp.float32,
            )
            out_ref[...] = (held_ref[...].astype(jnp.float32) * local + term * carried).astype(
                out_ref.dtype
            )


def finish(first_block, memories, queries, factor, held, heads):
    tokens = queries.shape[0]
    dqk, half = memories[0].shape
    count = len(memories)
    return pl.pallas_call(
        functools.partial(finish_kernel, dv_blocks=2, heads=heads),
        grid_spec=pltpu.PrefetchScalarGridSpec(
            num_scalar_prefetch=1,
            grid=(count,),
            in_specs=[
                pl.BlockSpec((tokens, dqk), lambda i, b: (0, lax.div(b[0] + i, 2))),
                pl.BlockSpec((tokens, LANES), lambda i, b: (0, 0)),
                pl.BlockSpec((tokens, half), lambda i, b: (0, b[0] + i)),
            ]
            + [pl.BlockSpec((dqk, half), lambda i, b: (0, 0))] * count,
            out_specs=pl.BlockSpec((tokens, half), lambda i, b: (0, b[0] + i)),
        ),
        out_shape=jax.ShapeDtypeStruct(held.shape, held.dtype),
        input_output_aliases={3: 0},
        compiler_params=params(24),
        cost_estimate=cost(
            2 * count * tokens * dqk * half, count * (2 * tokens * (dqk + 2 * half) + 4 * dqk * half)
        ),
        name="finish",
    )(first_block, queries, factor, held, *memories)


def down_kernel(level_ref, table_ref, *refs, chunks, first):
    level_refs = refs[:chunks]
    out_ref = refs[-1]
    for c in range(chunks):
        value = level_refs[c][...] * table_ref[ROW_FIN_L, c]
        out_ref[c] = value if first else value + refs[chunks][c]


def down(target, table, level_memories, earlier, rows):
    chunks = len(level_memories)
    half = level_memories[0].shape[1]
    operands = list(level_memories)
    in_specs = [pl.BlockSpec(memory_space=pltpu.SMEM)]
    in_specs += [pl.BlockSpec((rows, half), lambda i, t: (t[0], 0))] * chunks
    if earlier is not None:
        operands.append(earlier)
        in_specs.append(pl.BlockSpec((chunks, rows, half), lambda i, t: (0, 0, 0)))
    return pl.pallas_call(
        functools.partial(down_kernel, chunks=chunks, first=earlier is None),
        grid_spec=pltpu.PrefetchScalarGridSpec(
            num_scalar_prefetch=1,
            grid=(1,),
            in_specs=in_specs,
            out_specs=pl.BlockSpec((chunks, rows, half), lambda i, t: (0, 0, 0)),
        ),
        out_shape=jax.ShapeDtypeStruct((chunks, rows, half), jnp.float32),
        cost_estimate=cost(1e6, 12 * chunks * rows * half),
        name="down",
    )(target, table, *operands)


def final_kernel(level_ref, side_ref, table_ref, *refs, chunks):
    level_refs, own_refs, send_refs = refs[:chunks], refs[chunks : 2 * chunks], refs[2 * chunks : 3 * chunks]
    above_ref, keep_out, send_out = refs[3 * chunks :]
    side = side_ref[0]
    rows = keep_out.shape[1]
    half = level_refs[0].shape[1]
    for c in range(chunks):
        prefix = jnp.where(side == 0, own_refs[c][...], send_refs[c][...])
        value = (
            prefix * table_ref[ROW_FIN_P, c]
            + level_refs[c][...] * table_ref[ROW_FIN_L, c]
            + above_ref[c]
        )
        low, high = value[:rows], value[rows:]
        columns = pl.ds((c % 2) * half, half)
        keep_out[c // 2, :, columns] = jnp.where(side == 0, low, high)
        send_out[c // 2, :, columns] = jnp.where(side == 0, high, low)


def final_rows(level, side, table, level_memories, owns, sends, above):
    chunks = len(level_memories)
    dqk, half = level_memories[0].shape
    rows = above.shape[1]
    out = jax.ShapeDtypeStruct((chunks // 2, rows // 2, 2 * half), jnp.float32)
    return pl.pallas_call(
        functools.partial(final_kernel, chunks=chunks),
        grid_spec=pltpu.PrefetchScalarGridSpec(
            num_scalar_prefetch=2,
            grid=(1,),
            in_specs=[pl.BlockSpec(memory_space=pltpu.SMEM)]
            + [pl.BlockSpec((rows, half), lambda i, t, s: (t[0], 0))] * (3 * chunks)
            + [pl.BlockSpec((chunks, rows, half), lambda i, t, s: (0, 0, 0))],
            out_specs=[pl.BlockSpec(out.shape, lambda i, t, s: (0, 0, 0))] * 2,
        ),
        out_shape=[out, out],
        cost_estimate=cost(1e6, 20 * chunks * rows * half),
        name="final_rows",
    )(level, side, table, *level_memories, *owns, *sends, above)


SKEW = 2


def shards(queries, keys, values, input_gate, forget_gate, *, blocks):
    heads = input_gate.shape[0]
    dqk, dv = queries.shape[1] // heads, values.shape[1] // heads
    lane_heads = heads // 2
    levels = blocks // 2
    chunks = 2 * lane_heads
    place = lax.axis_index("ctx")
    side, level = lax.rem(place, 2), lax.div(place, 2)
    across = [(i, i ^ 1) for i in range(blocks)]
    up = [(i, i + 2) for i in range(blocks - 2)]
    downward = [(i + 2, i) for i in range(blocks - 2)]
    send = lambda value, pairs: lax.ppermute(value, "ctx", pairs)
    scalar = lambda value: jnp.reshape(value, (1,)).astype(jnp.int32)

    own_first, other_first = lane_heads * side, lane_heads * (1 - side)
    rows, columns, stats = gates(input_gate, forget_gate)
    normal_0, away = summaries(scalar(other_first), 1, keys, values, columns, dqk, dv)
    received = [send(a, across) for a in away]
    if lane_heads > 1:
        normal_1, away = summaries(
            scalar(other_first + 1), lane_heads - 1, keys, values, columns, dqk, dv
        )
        received += [send(a, across) for a in away]
        normal_0 = jnp.concatenate([normal_0, normal_1], axis=0)
    normal_own, kept = summaries(scalar(own_first), lane_heads, keys, values, columns, dqk, dv)

    ordered = jnp.where(
        side == 0,
        jnp.concatenate([normal_own, normal_0], axis=0),
        jnp.concatenate([normal_0, normal_own], axis=0),
    ).reshape(heads, dqk)
    gathered = jnp.concatenate([ordered, stats], axis=1)[None]
    while gathered.shape[0] < blocks:
        reach = gathered.shape[0]
        more = send(gathered, [(i, (i - reach) % blocks) for i in range(blocks)])
        gathered = jnp.concatenate([gathered, more], axis=0)[:blocks]
    table, prefix_normal, final_normal, tops = weights(scalar(place), gathered, SKEW)
    entry = lambda row, lane: lax.slice(table, (row, lane), (row + 1, lane + 1))

    held, sums = None, []
    group = 2 if heads % 2 == 0 else 1
    for first in range(0, heads, group):
        held, total = attention(first, group, queries, keys, values, rows, columns, held, dqk, dv)
        sums.append(total)
    factor = factors(queries, columns, prefix_normal, tops, sums)

    pair = [
        kept[c] * entry(ROW_KEEP, c) + received[c] * entry(ROW_RECV, c) for c in range(chunks)
    ]

    def by_level(options):
        result = None
        for z, value in enumerate(options):
            if value is None:
                continue
            result = value if result is None else jnp.where(level == z, value, result)
        return result

    at = lambda items, index: items[index] if 0 <= index < len(items) else None
    steps = chunks + SKEW * (levels - 2)
    arrived = []
    for s in range(steps):
        mine = by_level([at(pair, s - SKEW * z) for z in range(levels - 1)])
        value = mine * entry(ROW_B, s)
        if s >= SKEW:
            value = value + arrived[s - SKEW] * entry(ROW_A, s)
        arrived.append(send(value, up))

    sends, owns, others = [], [], []
    for c in range(chunks):
        prefix = by_level([None] + [arrived[c + SKEW * (z - 1)] for z in range(1, levels)])
        prefix = jnp.where(level == 0, 0.0, prefix)
        sends.append(prefix * entry(ROW_SEND_P, c) + kept[c] * entry(ROW_SEND_S, c))
        owns.append(prefix * entry(ROW_OWN_P, c) + received[c] * entry(ROW_OWN_S, c))
        others.append(send(sends[c], across))

    above = None
    rows_of_level = dqk // levels
    for d in range(1, levels):
        target = jnp.maximum(d - levels + level, 0)
        above = send(down(scalar(target), table, pair, above, rows_of_level), downward)
    keep_rows, send_rows = final_rows(scalar(level), scalar(side), table, pair, owns, sends, above)
    other_rows = send(send_rows, across)
    final_memory = jnp.where(
        side == 0,
        jnp.concatenate([keep_rows, other_rows], axis=0),
        jnp.concatenate([other_rows, keep_rows], axis=0),
    )
    share = dqk // blocks
    final_normalizer = lax.dynamic_slice_in_dim(final_normal, place * share, share, 1)
    final_stabilizer = tops[:, 1]

    hidden = held
    for c in range(0, chunks, 2):
        hidden = finish(scalar(2 * own_first + c), owns[c : c + 2], queries, factor, hidden, heads)
    for c in range(chunks):
        hidden = finish(scalar(2 * other_first + c), others[c : c + 1], queries, factor, hidden, heads)
    return hidden, final_memory, final_normalizer, final_stabilizer


def solution(mesh):
    token_spec = P(("seq", "ctx"), None)
    gate_spec = P(None, ("seq", "ctx"))
    return jax.shard_map(
        functools.partial(shards, blocks=mesh.shape["ctx"]),
        mesh=mesh,
        in_specs=(token_spec, token_spec, token_spec, gate_spec, gate_spec),
        out_specs=(token_spec, P("seq", "ctx", None), P("seq", "ctx"), P("seq")),
        check_vma=False,
    )
```

time: 953 us -> 259 us (0.27)
  waiting for transfers between devices: 558 us -> 0.94 us
  blocking collectives: 177 us -> 0 us
  matrix products: 97.5 us -> 0 us
  Pallas kernels: 0 us -> 76.4 us
  starting transfers between devices: 0.12 us -> 72.5 us
  loops' own time: 26.5 us -> 0 us
  other arithmetic: 46.1 us -> 71.8 us
  between operations: 14.5 us -> 1.33 us
    all_gather x1 -> x0, waiting for transfers between devices: 530 us -> none  [prefix_2(): gathered = jax.tree.map(lambda a: lax.all_gather(a, axis), part)]
    dot_general x32 -> x0, matrix products: 97.5 us -> none  [the longest x8 28.5 us: block_one_head(): lax.dot_general(query_rows, key_rows, (((1,), (1,)), ((), ())), preferred...]
    pallas_call x0 -> x26, Pallas kernels: none -> 76.4 us  [the longest x12 31.7 us: finish(): pl.pallas_call(functools.partial(finish_kernel, dv_blocks=2, heads=heads)...]
    ppermute x0 -> x35, starting transfers between devices: none -> 72.5 us  [shards(): send = lambda value, pairs: lax.ppermute(value, 'ctx', pairs)]
    pmax x1 -> x0, blocking collectives: 67.1 us -> none  [shards(): final_stabilizer = lax.pmax(end_stab, 'ctx')]
    unnamed x1 -> x0, blocking collectives: 65 us -> none
    add x1 -> x18, other arithmetic: 0.01 us -> 64.6 us  [the longest x10 32.4 us: shards(): value = value + arrived[s - SKEW] * entry(ROW_A, s)]
    all_gather x1 -> x0, blocking collectives: 44.6 us -> none  [prefix_2(): gathered = jax.tree.map(lambda a: lax.all_gather(a, axis), part)]
  transfers between devices with their start and end apart: 3 -> 35, of which waited for: 2 -> 1; matrix products, arithmetic and copies ran while one was open for 13% -> 31% of each run, Pallas kernels for 0% -> 25%
where the time goes in v1:
time: 259 us; the launch traced here: 256 us
  Pallas kernels  76.4 us (29%)
  starting transfers between devices  72.5 us (28%)
  other arithmetic  71.8 us (28%)
  local copies, waits for them, and re-layouts  33.3 us (13%)
    ppermute x35, starting transfers between devices, shards(): send = lambda value, pairs: lax.ppermute(value, 'ctx', pairs)  72.5 us
    add x10, other arithmetic, shards(): value = value + arrived[s - SKEW] * entry(ROW_A, s)  32.4 us
    pallas_call x12, Pallas kernels, finish(): pl.pallas_call(functools.partial(finish_kernel, dv_blocks=2, heads=heads)...  31.7 us
    unnamed x118, local copies, waits for them, and re-layouts  23.9 us
    add x6, other arithmetic, shards(): prefix * entry(ROW_OWN_P, c) + received[c] * entry(ROW_OWN_S, c)  20.2 us
    pallas_call x4, Pallas kernels, attention(): pl.pallas_call(functools.partial(attention_kernel, first=first), grid=(co...  17.6 us
    add x2, other arithmetic, shards(): sends.append(prefix * entry(ROW_SEND_P, c) + kept[c] * entry(ROW_SEND_S, c))  12 us
    pallas_call x3, Pallas kernels, summaries(): pl.pallas_call(functools.partial(summary_kernel, count=count), grid_spec=...  8.64 us
  transfers between devices with their start and end apart: 35, of which 1 were waited for; matrix products, arithmetic and copies ran while one was open for 31% of the time, Pallas kernels for 25%

profile of v1, /device:TPU:0, one launch (start us, length us, event | category | flops | bytes accessed | tf_op | source)
XLA Modules:
  0.0 256.4 jit_solution(1462189567282419247)
XLA Ops:
  0.6 2.8 %gates.1 = (f32[8,1024]{1,0:T(8,128)}, f32[1024,128]{1,0:T(8,128)}, f32[8,128]{1,0:T(8,128)}) custom-call(f32[8,1024]{1,0:T(8,128)} %input_ref.1, f32[8,1024]{1,0:T(8,128)} %forget_ref.1), custom_call_target="tpu_custom_call" | custom-call | flops 1000000 | bytes 1000000 | tf_op jit(solution)/shard_map/gates/pallas_call | solution.py:65
  3.5 3.4 %copy-done.3 = bf16[1024,4096]{1,0:T(8,128)(2,1)S(1)} copy-done((bf16[1024,4096]{1,0:T(8,128)(2,1)S(1)}, bf16[1024,4096]{1,0:T(8,128)(2,1)}, u32[]{:S(2)}) %copy-start.3) | copy-done | bytes 8388632
  6.9 2.2 copy-done.6
  10.1 3.6 %summaries.3 = (f32[4,1,256]{2,1,0:T(1,128)S(1)}, f32[256,256]{1,0:T(8,128)S(1)}, f32[256,256]{1,0:T(8,128)S(1)}, f32[256,256]{1,0:T(8,128)S(1)}, f32[256,256]{1...) custom-call(s32[1]{0:T(128)} %bitcast.2.first_ref, ...), custom_call_target="tpu_custom_call" | custom-call | flops 1073741824 | bytes 8388608 | tf_op jit(solution)/shard_map/summaries/pallas_call | solution.py:105
  13.7 3.4 %copy-done.4 = bf16[1024,4096]{1,0:T(8,128)(2,1)S(1)} copy-done((bf16[1024,4096]{1,0:T(8,128)(2,1)S(1)}, bf16[1024,4096]{1,0:T(8,128)(2,1)}, u32[]{:S(2)}) %copy-start.4) | copy-done | bytes 8388632
  17.1 2.2 copy-done.7
  19.3 3.6 %summaries.5 = (f32[3,1,256]{2,1,0:T(1,128)S(1)}, f32[256,256]{1,0:T(8,128)}, f32[256,256]{1,0:T(8,128)}, f32[256,256]{1,0:T(8,128)S(1)}, f32[256,256]{1,0:T(8,1...) custom-call(s32[1]{0:T(128)} %bitcast.5.first_ref, bf16[1024,2048]{1,0:T(8,128)(2,1)S(1)} %copy-done.7, ...), custom_call_target="tpu_custom_call" | custom-call | flops 805306368 | bytes 6291456 | tf_op jit(solution)/shard_map/summaries/pallas_call | solution.py:105
  24.4 6.0 %collective-permute-start = (f32[1,8,384]{2,1,0:T(8,128)S(1)}, f32[1,8,384]{2,1,0:T(8,128)S(1)}, u32[]{:S(2)}, u32[]{:S(2)}) collective-permute-start(f32[1,8,384]{2,1,0:T(8,128)S(1)} %maximum_bitcast_fusion), channel_id=1, source_target_pairs={{0,28},{4,0},{8,4},{12,8},{16,12},{20,16},{24,20},{28,24},{1,29},{... | collective-permute-start | bytes 36872 | tf_op jit(solution)/shard_map/ppermute | solution.py:513
  30.5 2.0 collective-permute-start.10
  34.5 4.4 %attention.4 = (bf16[1024,4096]{1,0:T(8,128)(2,1)}, f32[1024,128]{1,0:T(8,128)S(1)}) custom-call(bf16[1024,2048]{1,0:T(8,128)(2,1)S(1)} %copy-done, bf16[1024,2048]{1,0:T(8,128)(2,1)S(1)} %copy-done.8, bf16[1024,4096]{1,0:T(8,128)(2,1)S(1)} %copy-done.5, f32[8,1024]{1,0:T(8,128)S(1)} %copy-done.19, f32[1024,128]{1,0:T(8,128)S(1)} %copy-done.10), custom_call_target="tpu_custom_call" | custom-call | flops 2576980480 | bytes 6291456 | tf_op jit(solution)/shard_map/attention/pallas_call | solution.py:289
  38.9 4.4 %attention.5 = (bf16[1024,4096]{1,0:T(8,128)(2,1)}, f32[1024,128]{1,0:T(8,128)S(1)}) custom-call(bf16[1024,2048]{1,0:T(8,128)(2,1)S(1)} %copy-done, bf16[1024,2048]{1,0:T(8,128)(2,1)S(1)} %copy-done.8, bf16[1024,4096]{1,0:T(8,128)(2,1)S(1)} %copy-done.5, f32[8,1024]{1,0:T(8,128)S(1)} %copy-done.19, ...), custom_call_target="tpu_custom_call", output_to_operand_aliasing={{0}: (5, {})} | custom-call | flops 2576980480 | bytes 6291456 | tf_op jit(solution)/shard_map/attention/pallas_call | solution.py:289
  43.9 4.4 %attention.6 = (bf16[1024,4096]{1,0:T(8,128)(2,1)}, f32[1024,128]{1,0:T(8,128)S(1)}) custom-call(bf16[1024,2048]{1,0:T(8,128)(2,1)S(1)} %copy-done, bf16[1024,2048]{1,0:T(8,128)(2,1)S(1)} %copy-done.8, bf16[1024,4096]{1,0:T(8,128)(2,1)S(1)} %copy-done.5, f32[8,1024]{1,0:T(8,128)S(1)} %copy-done.19, ...), custom_call_target="tpu_custom_call", output_to_operand_aliasing={{0}: (5, {})} | custom-call | flops 2576980480 | bytes 6291456 | tf_op jit(solution)/shard_map/attention/pallas_call | solution.py:289
  49.1 4.4 %attention.7 = (bf16[1024,4096]{1,0:T(8,128)(2,1)}, f32[1024,128]{1,0:T(8,128)S(1)}) custom-call(bf16[1024,2048]{1,0:T(8,128)(2,1)S(1)} %copy-done, bf16[1024,2048]{1,0:T(8,128)(2,1)S(1)} %copy-done.8, bf16[1024,4096]{1,0:T(8,128)(2,1)S(1)} %copy-done.5, f32[8,1024]{1,0:T(8,128)S(1)} %copy-done.19, ...), custom_call_target="tpu_custom_call", output_to_operand_aliasing={{0}: (5, {})} | custom-call | flops 2576980480 | bytes 6291456 | tf_op jit(solution)/shard_map/attention/pallas_call | solution.py:289
  57.8 2.1 fusion.2
  59.9 2.1 fusion.1
  62.0 2.1 fusion
  65.9 2.2 copy-done.1
  73.6 5.0 %factors.1.factors_ref = f32[1024,128]{1,0:T(8,128)S(1)} custom-call(bf16[1024,2048]{1,0:T(8,128)(2,1)S(1)} %copy-done.1, f32[1024,128]{1,0:T(8,128)S(1)} %copy-done.10, f32[8,256]{1,0:T(8,128)S(1)} %copy-done.31, f32[8,128]{1,0:T(8,128)S(1)} %copy-done.20, f32[1024,128]{1,0:T(8,128)S(1)} %copy-done.22, f32[1024,128]{1,0:T(8,128)S(1)} %copy-done.24, ...), custom_call_target="tpu_custom_call" | custom-call | flops 2147483648 | bytes 4194304 | tf_op jit(solution)/shard_map/factors/pallas_call | solution.py:362
  78.7 2.8 %broadcast_multiply_fusion.1 = (f32[256,256]{1,0:T(8,128)S(1)}, f32[256,256]{1,0:T(8,128)S(1)}) fusion(f32[]{:T(128)} %bitcast.26, f32[256,256]{1,0:T(8,128)} %collective-permute-done.3, f32[]{:T(128)} %bitcast.19, f32[256,256]{1,0:T(8,128)S(1)} %get-tuple-element.56, f32[]{:T(128)} %bitcast.18), kind=kLoop, calls=%fused_computation.44 | loop fusion | flops 262144 | bytes 1048588 | tf_op jit(solution)/shard_map/mul | solution.py:565
  81.5 2.6 %collective-permute-start.6 = (f32[256,256]{1,0:T(8,128)S(1)}, f32[256,256]{1,0:T(8,128)S(1)}, u32[]{:S(2)}, u32[]{:S(2)}) collective-permute-start(f32[256,256]{1,0:T(8,128)S(1)} %get-tuple-element.106), channel_id=1, source_target_pairs={{0,8},{4,12},{8,16},{12,20},{16,24},{20,28},{1,9},{5,13},{9,17},{1... | collective-permute-start | bytes 786440 | tf_op jit(solution)/shard_map/ppermute | solution.py:513
  86.8 2.9 %broadcast_multiply_fusion = (f32[256,256]{1,0:T(8,128)S(1)}, f32[256,256]{1,0:T(8,128)S(1)}) fusion(f32[]{:T(128)} %bitcast.39, f32[256,256]{1,0:T(8,128)} %collective-permute-done.9, f32[]{:T(128)} %bitcast.32, f32[256,256]{1,0:T(8,128)S(1)} %get-tuple-element.63, f32[]{:T(128)} %bitcast.31), kind=kLoop, calls=%fused_computation.43 | loop fusion | flops 262144 | bytes 1048588 | tf_op jit(solution)/shard_map/mul | solution.py:565
  89.8 4.6 %collective-permute-start.12 = (f32[256,256]{1,0:T(8,128)S(1)}, f32[256,256]{1,0:T(8,128)S(1)}, u32[]{:S(2)}, u32[]{:S(2)}) collective-permute-start(f32[256,256]{1,0:T(8,128)S(1)} %get-tuple-element.100), channel_id=1, source_target_pairs={{0,8},{4,12},{8,16},{12,20},{16,24},{20,28},{1,9},{5,13},{9,17},{1... | collective-permute-start | bytes 786440 | tf_op jit(solution)/shard_map/ppermute | solution.py:513
  94.4 3.5 %multiply_add_fusion.30 = (f32[256,256]{1,0:T(8,128)S(1)}, f32[256,256]{1,0:T(8,128)S(1)}) fusion(f32[256,256]{1,0:T(8,128)S(1)} %collective-permute-done.6, f32[256,256]{1,0:T(8,128)S(1)} %get-tuple-element.107.refs_0_, f32[]{:T(128)} %bitcast.27, f32[]{:T(128)} %bitcast.25, pred[]{:T(512)S(6)} %eq.14, f32[256,256]{1,0:T(8,128)} %collective-permute-done.4, ...), kind=kLoop, calls=%fused_computation.39 | loop fusion | flops 458752 | bytes 1572881 | tf_op jit(solution)/shard_map/add | solution.py:567
  99.3 3.5 %collective-permute-start.7 = (f32[256,256]{1,0:T(8,128)S(1)}, f32[256,256]{1,0:T(8,128)S(1)}, u32[]{:S(2)}, u32[]{:S(2)}) collective-permute-start(f32[256,256]{1,0:T(8,128)S(1)} %get-tuple-element.104), channel_id=1, source_target_pairs={{0,8},{4,12},{8,16},{12,20},{16,24},{20,28},{1,9},{5,13},{9,17},{1... | collective-permute-start | bytes 786440 | tf_op jit(solution)/shard_map/ppermute | solution.py:513
  102.8 3.6 %multiply_add_fusion.24 = (f32[256,256]{1,0:T(8,128)S(1)}, f32[256,256]{1,0:T(8,128)S(1)}) fusion(f32[256,256]{1,0:T(8,128)S(1)} %collective-permute-done.12, f32[256,256]{1,0:T(8,128)S(1)} %get-tuple-element.101.refs_1_, f32[]{:T(128)} %bitcast.40, f32[]{:T(128)} %bitcast.38, pred[]{:T(512)S(6)} %eq.14, f32[256,256]{1,0:T(8,128)} %collective-permute-done.10, ...), kind=kLoop, calls=%fused_computation.32 | loop fusion | flops 458752 | bytes 1572881 | tf_op jit(solution)/shard_map/add | solution.py:567
  106.5 2.6 %collective-permute-start.13 = (f32[256,256]{1,0:T(8,128)S(1)}, f32[256,256]{1,0:T(8,128)S(1)}, u32[]{:S(2)}, u32[]{:S(2)}) collective-permute-start(f32[256,256]{1,0:T(8,128)S(1)} %get-tuple-element.98), channel_id=1, source_target_pairs={{0,8},{4,12},{8,16},{12,20},{16,24},{20,28},{1,9},{5,13},{9,17},{1... | collective-permute-start | bytes 786440 | tf_op jit(solution)/shard_map/ppermute | solution.py:513
  109.1 2.6 %multiply_add_fusion.29 = (f32[256,256]{1,0:T(8,128)S(1)}, f32[256,256]{1,0:T(8,128)S(1)}) fusion(f32[256,256]{1,0:T(8,128)S(1)} %collective-permute-done.7, f32[256,256]{1,0:T(8,128)S(1)} %get-tuple-element.107.refs_0_, f32[256,256]{1,0:T(8,128)S(1)} %get-tuple-element.105.refs_2_, f32[]{:T(128)} %bitcast.28, f32[]{:T(128)} %bitcast.24, pred[]{:T(512)S(6)} %eq.14, ...), kind=kLoop, calls=%fused_computation.38 | loop fusion | flops 524288 | bytes 1835026 | tf_op jit(solution)/shard_map/add | solution.py:567
  111.7 3.7 %collective-permute-start.8 = (f32[256,256]{1,0:T(8,128)S(1)}, f32[256,256]{1,0:T(8,128)S(1)}, u32[]{:S(2)}, u32[]{:S(2)}) collective-permute-start(f32[256,256]{1,0:T(8,128)S(1)} %get-tuple-element.102), channel_id=1, source_target_pairs={{0,8},{4,12},{8,16},{12,20},{16,24},{20,28},{1,9},{5,13},{9,17},{1... | collective-permute-start | bytes 786440 | tf_op jit(solution)/shard_map/ppermute | solution.py:513
  115.5 3.5 %multiply_add_fusion.23 = (f32[256,256]{1,0:T(8,128)S(1)}, f32[256,256]{1,0:T(8,128)S(1)}) fusion(f32[256,256]{1,0:T(8,128)S(1)} %collective-permute-done.13, f32[256,256]{1,0:T(8,128)S(1)} %get-tuple-element.101.refs_1_, f32[256,256]{1,0:T(8,128)S(1)} %get-tuple-element.99.refs_3_, f32[]{:T(128)} %bitcast.41, f32[]{:T(128)} %bitcast.37, pred[]{:T(512)S(6)} %eq.14, ...), kind=kLoop, calls=%fused_computation.31 | loop fusion | flops 524288 | bytes 1835026 | tf_op jit(solution)/shard_map/add | solution.py:567
  119.0 4.2 %collective-permute-start.14 = (f32[256,256]{1,0:T(8,128)S(1)}, f32[256,256]{1,0:T(8,128)S(1)}, u32[]{:S(2)}, u32[]{:S(2)}) collective-permute-start(f32[256,256]{1,0:T(8,128)S(1)} %get-tuple-element.96), channel_id=1, source_target_pairs={{0,8},{4,12},{8,16},{12,20},{16,24},{20,28},{1,9},{5,13},{9,17},{1... | collective-permute-start | bytes 786440 | tf_op jit(solution)/shard_map/ppermute | solution.py:513
  123.2 4.9 %multiply_add_fusion.20 = (f32[256,256]{1,0:T(8,128)}, f32[256,256]{1,0:T(8,128)}, f32[256,256]{1,0:T(8,128)}, f32[256,256]{1,0:T(8,128)}) fusion(f32[256,256]{1,0:T(8,128)S(1)} %collective-permute-done.8, f32[256,256]{1,0:T(8,128)S(1)} %get-tuple-element.105.refs_2_, f32[256,256]{1,0:T(8,128)S(1)} %get-tuple-element.103.refs_4_, f32[]{:T(128)} %bitcast.47, ...), kind=kLoop, calls=%fused_computation.27 | loop fusion | flops 917504 | bytes 3145756 | tf_op jit(solution)/shard_map/add | solution.py:567
  128.1 3.3 %collective-permute-start.16 = (f32[256,256]{1,0:T(8,128)}, f32[256,256]{1,0:T(8,128)}, u32[]{:S(2)}, u32[]{:S(2)}) collective-permute-start(f32[256,256]{1,0:T(8,128)} %get-tuple-element.94), channel_id=1, source_target_pairs={{0,8},{4,12},{8,16},{12,20},{16,24},{20,28},{1,9},{5,13},{9,17},{1... | collective-permute-start | bytes 786440 | tf_op jit(solution)/shard_map/ppermute | solution.py:513
  131.4 4.8 %multiply_add_fusion.17 = (f32[256,256]{1,0:T(8,128)}, f32[256,256]{1,0:T(8,128)}, f32[256,256]{1,0:T(8,128)}, f32[256,256]{1,0:T(8,128)}) fusion(f32[256,256]{1,0:T(8,128)S(1)} %collective-permute-done.14, f32[256,256]{1,0:T(8,128)S(1)} %get-tuple-element.99.refs_3_, f32[256,256]{1,0:T(8,128)S(1)} %get-tuple-element.97.refs_5_, f32[]{:T(128)} %bitcast.53, ...), kind=kLoop, calls=%fused_computation.23 | loop fusion | flops 917504 | bytes 3145756 | tf_op jit(solution)/shard_map/add | solution.py:567
  139.5 4.6 %collective-permute-start.18 = (f32[256,256]{1,0:T(8,128)}, f32[256,256]{1,0:T(8,128)S(1)}, u32[]{:S(2)}, u32[]{:S(2)}) collective-permute-start(f32[256,256]{1,0:T(8,128)} %get-tuple-element.92), channel_id=1, source_target_pairs={{0,8},{4,12},{8,16},{12,20},{16,24},{20,28},{1,9},{5,13},{9,17},{1... | collective-permute-start | bytes 786440 | tf_op jit(solution)/shard_map/ppermute | solution.py:513
  146.2 2.3 multiply_add_fusion.15
  148.5 3.0 %collective-permute-start.19 = (f32[256,256]{1,0:T(8,128)S(1)}, f32[256,256]{1,0:T(8,128)S(1)}, u32[]{:S(2)}, u32[]{:S(2)}) collective-permute-start(f32[256,256]{1,0:T(8,128)S(1)} %multiply_add_fusion.15), channel_id=1, source_target_pairs={{0,8},{4,12},{8,16},{12,20},{16,24},{20,28},{1,9},{5,13},{9,17},{1... | collective-permute-start | bytes 786440 | tf_op jit(solution)/shard_map/ppermute | solution.py:513
  151.5 3.0 %multiply_add_fusion.22.rest_1_.refs_9_ = f32[256,256]{1,0:T(8,128)} fusion(f32[256,256]{1,0:T(8,128)} %collective-permute-done.9, f32[256,256]{1,0:T(8,128)} %get-tuple-element.117, f32[]{:T(128)} %bitcast.43, f32[]{:T(128)} %bitcast.42), kind=kLoop, calls=%fused_computation.29 | loop fusion | flops 196608 | bytes 786440 | tf_op jit(solution)/shard_map/add | solution.py:575
  154.5 3.1 %multiply_add_fusion.13 = f32[256,256]{1,0:T(8,128)} fusion(f32[256,256]{1,0:T(8,128)S(1)} %collective-permute-done.18, f32[256,256]{1,0:T(8,128)} %copy-done.35, f32[256,256]{1,0:T(8,128)} %get-tuple-element.93.refs_7_, f32[]{:T(128)} %bitcast.61, f32[]{:T(128)} %bitcast.60, pred[]{:T(512)S(6)} %eq.13), kind=kLoop, calls=%fused_computation.17 | loop fusion | flops 262144 | bytes 1048585 | tf_op jit(solution)/shard_map/add | solution.py:567
  157.6 4.6 %collective-permute-start.20 = (f32[256,256]{1,0:T(8,128)}, f32[256,256]{1,0:T(8,128)}, u32[]{:S(2)}, u32[]{:S(2)}) collective-permute-start(f32[256,256]{1,0:T(8,128)} %multiply_add_fusion.13), channel_id=1, source_target_pairs={{0,8},{4,12},{8,16},{12,20},{16,24},{20,28},{1,9},{5,13},{9,17},{1... | collective-permute-start | bytes 786440 | tf_op jit(solution)/shard_map/ppermute | solution.py:513
  164.1 2.1 collective-permute-start.21
  166.2 3.1 %multiply_add_fusion.28.rest_0_.refs_8_ = f32[256,256]{1,0:T(8,128)} fusion(f32[256,256]{1,0:T(8,128)} %collective-permute-done.3, f32[256,256]{1,0:T(8,128)} %get-tuple-element.119, f32[]{:T(128)} %bitcast.30, f32[]{:T(128)} %bitcast.29), kind=kLoop, calls=%fused_computation.36 | loop fusion | flops 196608 | bytes 786440 | tf_op jit(solution)/shard_map/add | solution.py:575
  169.3 2.2 down.4
  172.9 2.3 multiply_add_fusion.9
  175.2 4.6 %collective-permute-start.22 = (f32[256,256]{1,0:T(8,128)S(1)}, f32[256,256]{1,0:T(8,128)S(1)}, u32[]{:S(2)}, u32[]{:S(2)}) collective-permute-start(f32[256,256]{1,0:T(8,128)S(1)} %multiply_add_fusion.9), channel_id=1, source_target_pairs={{0,8},{4,12},{8,16},{12,20},{16,24},{20,28},{1,9},{5,13},{9,17},{1... | collective-permute-start | bytes 786440 | tf_op jit(solution)/shard_map/ppermute | solution.py:513
  179.8 6.0 %multiply_add_fusion.1 = (f32[256,256]{1,0:T(8,128)}, f32[256,256]{1,0:T(8,128)S(1)}, f32[256,256]{1,0:T(8,128)}, f32[256,256]{1,0:T(8,128)}, f32[256,256]{1,0:T(8,128)}, /*index=5*/f32[256,256]{1,0:T(8,128)}) fusion(f32[256,256]{1,0:T(8,128)S(1)} %get-tuple-element.69, f32[]{:T(128)} %bitcast.85, f32[]{:T(128)} %bitcast.84, ...), kind=kLoop, calls=%fused_computation.2 | loop fusion | flops 1179648 | bytes 3670043 | tf_op jit(solution)/shard_map/add | solution.py:574
  187.7 6.0 %multiply_add_fusion = (f32[256,256]{1,0:T(8,128)}, f32[256,256]{1,0:T(8,128)S(1)}, f32[256,256]{1,0:T(8,128)}, f32[256,256]{1,0:T(8,128)}, f32[256,256]{1,0:T(8,128)}, /*index=5*/f32[256,256]{1,0:T(8,128)}) fusion(f32[256,256]{1,0:T(8,128)S(1)} %get-tuple-element.71, f32[]{:T(128)} %bitcast.87, f32[]{:T(128)} %bitcast.86, ...), kind=kLoop, calls=%fused_computation.1 | loop fusion | flops 1179648 | bytes 3670043 | tf_op jit(solution)/shard_map/add | solution.py:574
  193.8 3.0 %multiply_add_fusion.8.rest_1_.refs_15_ = f32[256,256]{1,0:T(8,128)} fusion(f32[256,256]{1,0:T(8,128)} %copy-done.49, f32[256,256]{1,0:T(8,128)S(1)} %get-tuple-element.77, f32[]{:T(128)} %bitcast.71, f32[]{:T(128)} %bitcast.70), kind=kLoop, calls=%fused_computation.9 | loop fusion | flops 196608 | bytes 786440 | tf_op jit(solution)/shard_map/add | solution.py:575
  198.8 2.2 down.5
  202.2 4.6 %multiply_add_fusion.12 = (f32[256,256]{1,0:T(8,128)}, f32[256,256]{1,0:T(8,128)}) fusion(f32[256,256]{1,0:T(8,128)} %collective-permute-done.11, f32[256,256]{1,0:T(8,128)} %get-tuple-element.109, f32[]{:T(128)} %bitcast.63, f32[]{:T(128)} %bitcast.62, f32[256,256]{1,0:T(8,128)} %collective-permute-done.10, f32[]{:T(128)} %bitcast.55, ...), kind=kLoop, calls=%fused_computation.15 | loop fusion | flops 393216 | bytes 1572880 | tf_op jit(solution)/shard_map/add | solution.py:575
  206.8 4.5 %multiply_add_fusion.14 = (f32[256,256]{1,0:T(8,128)}, f32[256,256]{1,0:T(8,128)}) fusion(f32[256,256]{1,0:T(8,128)} %copy-done.53, f32[256,256]{1,0:T(8,128)} %get-tuple-element.113, f32[]{:T(128)} %bitcast.59, f32[]{:T(128)} %bitcast.58, f32[256,256]{1,0:T(8,128)} %collective-permute-done.4, f32[]{:T(128)} %bitcast.49, f32[256,256]{1,0:T(8,128)} %get-tuple-element.115, ...), kind=kLoop, calls=%fused_computation.18 | loop fusion | flops 393216 | bytes 1572880 | tf_op jit(solution)/shard_map/add | solution.py:575
  214.2 2.6 final_rows.1
  221.6 2.2 copy-done.2
  223.7 3.3 %finish.12.held_ref = bf16[1024,4096]{1,0:T(8,128)(2,1)} custom-call(s32[1]{0:T(128)} %bitcast.17.block_ref, bf16[1024,2048]{1,0:T(8,128)(2,1)S(1)} %copy-done.2, f32[1024,128]{1,0:T(8,128)S(1)} %factors.1.factors_ref, bf16[1024,4096]{1,0:T(8,128)(2,1)} %get-tuple-element.55.held_ref, f32[256,256]{1,0:T(8,128)S(1)} %copy-done.12, ...), custom_call_target="tpu_custom_call", output_to_operand_aliasing={{}: (3, {})} | custom-call | flops 268435456 | bytes 3670016 | tf_op jit(solution)/shard_map/finish/pallas_call | solution.py:405
  227.1 3.3 %finish.13.held_ref = bf16[1024,4096]{1,0:T(8,128)(2,1)} custom-call(s32[1]{0:T(128)} %bitcast.16.block_ref, bf16[1024,2048]{1,0:T(8,128)(2,1)S(1)} %copy-done.2, f32[1024,128]{1,0:T(8,128)S(1)} %factors.1.factors_ref, bf16[1024,4096]{1,0:T(8,128)(2,1)} %finish.12.held_ref, f32[256,256]{1,0:T(8,128)S(1)} %copy-done.18, ...), custom_call_target="tpu_custom_call", output_to_operand_aliasing={{}: (3, {})} | custom-call | flops 268435456 | bytes 3670016 | tf_op jit(solution)/shard_map/finish/pallas_call | solution.py:405
  230.4 3.3 %finish.14.held_ref = bf16[1024,4096]{1,0:T(8,128)(2,1)} custom-call(s32[1]{0:T(128)} %bitcast.15.block_ref, bf16[1024,2048]{1,0:T(8,128)(2,1)S(1)} %copy-done.2, f32[1024,128]{1,0:T(8,128)S(1)} %factors.1.factors_ref, bf16[1024,4096]{1,0:T(8,128)(2,1)} %finish.13.held_ref, f32[256,256]{1,0:T(8,128)S(1)} %copy-done.17, ...), custom_call_target="tpu_custom_call", output_to_operand_aliasing={{}: (3, {})} | custom-call | flops 268435456 | bytes 3670016 | tf_op jit(solution)/shard_map/finish/pallas_call | solution.py:405
  233.7 3.3 %finish.15.held_ref = bf16[1024,4096]{1,0:T(8,128)(2,1)} custom-call(s32[1]{0:T(128)} %bitcast.14.block_ref, bf16[1024,2048]{1,0:T(8,128)(2,1)S(1)} %copy-done.2, f32[1024,128]{1,0:T(8,128)S(1)} %factors.1.factors_ref, bf16[1024,4096]{1,0:T(8,128)(2,1)} %finish.14.held_ref, f32[256,256]{1,0:T(8,128)S(1)} %copy-done.14, ...), custom_call_target="tpu_custom_call", output_to_operand_aliasing={{}: (3, {})} | custom-call | flops 268435456 | bytes 3670016 | tf_op jit(solution)/shard_map/finish/pallas_call | solution.py:405
  237.0 2.3 finish.16.held_ref
  239.3 2.3 finish.17.held_ref
  241.6 2.3 finish.18.held_ref
  243.9 2.3 finish.19.held_ref
  246.2 2.3 finish.20.held_ref
  248.5 2.3 finish.21.held_ref
  250.9 2.3 finish.22.held_ref
  253.2 2.3 finish.23
  (182 shorter events, 44.4 us)
Async XLA Ops:
  22.9 16.1 %copy-start.29 = (f32[256,256]{1,0:T(8,128)}, f32[256,256]{1,0:T(8,128)S(1)}, u32[]{:S(2)}) copy-start(f32[256,256]{1,0:T(8,128)S(1)} %get-tuple-element.70) | copy-start | bytes 786436
  22.9 16.1 %copy-start.30 = (f32[256,256]{1,0:T(8,128)}, f32[256,256]{1,0:T(8,128)S(1)}, u32[]{:S(2)}) copy-start(f32[256,256]{1,0:T(8,128)S(1)} %get-tuple-element.62) | copy-start | bytes 786436
  22.9 11.7 %copy-start = (bf16[1024,2048]{1,0:T(8,128)(2,1)S(1)}, bf16[1024,2048]{1,0:T(8,128)(2,1)}, u32[]{:S(2)}) copy-start(bf16[1024,2048]{1,0:T(8,128)(2,1)} %query_ref.33) | copy-start | bytes 12582916
  22.9 11.7 %copy-start.8 = (bf16[1024,2048]{1,0:T(8,128)(2,1)S(1)}, bf16[1024,2048]{1,0:T(8,128)(2,1)}, u32[]{:S(2)}) copy-start(bf16[1024,2048]{1,0:T(8,128)(2,1)} %key_ref.13) | copy-start | bytes 12582916
  22.9 11.7 %copy-start.19 = (f32[8,1024]{1,0:T(8,128)S(1)}, f32[8,1024]{1,0:T(8,128)}, u32[]{:S(2)}) copy-start(f32[8,1024]{1,0:T(8,128)} %get-tuple-element.47.rows_ref) | copy-start | bytes 98308
  24.4 18.9 %collective-permute-start = (f32[1,8,384]{2,1,0:T(8,128)S(1)}, f32[1,8,384]{2,1,0:T(8,128)S(1)}, u32[]{:S(2)}, u32[]{:S(2)}) collective-permute-start(f32[1,8,384]{2,1,0:T(8,128)S(1)} %maximum_bitcast_fusion), channel_id=1, source_target_pairs={{0,28},{4,0},{8,4},{12,8},{16,12},{20,16},{24,20},{28,24},{1,29},{... | collective-permute-start | bytes 36872 | tf_op jit(solution)/shard_map/ppermute | solution.py:513
  30.5 54.3 %collective-permute-start.9 = (f32[256,256]{1,0:T(8,128)}, f32[256,256]{1,0:T(8,128)}, u32[]{:S(2)}, u32[]{:S(2)}) collective-permute-start(f32[256,256]{1,0:T(8,128)} %get-tuple-element.64), channel_id=1, source_target_pairs={{0,4},{4,0},{8,12},{12,8},{16,20},{20,16},{24,28},{28,24},{1,5},{5... | collective-permute-start | bytes 786440 | tf_op jit(solution)/shard_map/ppermute | solution.py:513
  30.5 67.4 %collective-permute-start.10 = (f32[256,256]{1,0:T(8,128)}, f32[256,256]{1,0:T(8,128)}, u32[]{:S(2)}, u32[]{:S(2)}) collective-permute-start(f32[256,256]{1,0:T(8,128)} %get-tuple-element.66), channel_id=1, source_target_pairs={{0,4},{4,0},{8,12},{12,8},{16,20},{20,16},{24,28},{28,24},{1,5},{5... | collective-permute-start | bytes 786440 | tf_op jit(solution)/shard_map/ppermute | solution.py:513
  32.5 82.9 %collective-permute-start.11 = (f32[256,256]{1,0:T(8,128)}, f32[256,256]{1,0:T(8,128)}, u32[]{:S(2)}, u32[]{:S(2)}) collective-permute-start(f32[256,256]{1,0:T(8,128)} %get-tuple-element.68), channel_id=1, source_target_pairs={{0,4},{4,0},{8,12},{12,8},{16,20},{20,16},{24,28},{28,24},{1,5},{5... | collective-permute-start | bytes 786440 | tf_op jit(solution)/shard_map/ppermute | solution.py:513
  32.6 46.1 %collective-permute-start.3 = (f32[256,256]{1,0:T(8,128)}, f32[256,256]{1,0:T(8,128)}, u32[]{:S(2)}, u32[]{:S(2)}) collective-permute-start(f32[256,256]{1,0:T(8,128)} %get-tuple-element.58), channel_id=1, source_target_pairs={{0,4},{4,0},{8,12},{12,8},{16,20},{20,16},{24,28},{28,24},{1,5},{5... | collective-permute-start | bytes 786440 | tf_op jit(solution)/shard_map/ppermute | solution.py:513
  43.3 4.9 %copy-start.23 = (f32[1024,128]{1,0:T(8,128)}, f32[1024,128]{1,0:T(8,128)S(1)}, u32[]{:S(2)}) copy-start(f32[1024,128]{1,0:T(8,128)S(1)} %get-tuple-element.50.rest_1_) | copy-start | bytes 1572868
  43.3 5.7 %collective-permute-start.1 = (f32[2,8,384]{2,1,0:T(8,128)S(1)}, f32[2,8,384]{2,1,0:T(8,128)S(1)}, u32[]{:S(2)}, u32[]{:S(2)}) collective-permute-start(f32[2,8,384]{2,1,0:T(8,128)S(1)} %pad_maximum_fusion.2), channel_id=1, source_target_pairs={{0,24},{4,28},{8,0},{12,4},{16,8},{20,12},{24,16},{28,20},{1,25},{... | collective-permute-start | bytes 73736 | tf_op jit(solution)/shard_map/ppermute | solution.py:513
  49.0 5.3 %collective-permute-start.2 = (f32[4,8,384]{2,1,0:T(8,128)S(1)}, f32[4,8,384]{2,1,0:T(8,128)S(1)}, u32[]{:S(2)}, u32[]{:S(2)}) collective-permute-start(f32[4,8,384]{2,1,0:T(8,128)S(1)} %pad_maximum_fusion.1), channel_id=1, source_target_pairs={{0,16},{4,20},{8,24},{12,28},{16,0},{20,4},{24,8},{28,12},{1,17},{... | collective-permute-start | bytes 147464 | tf_op jit(solution)/shard_map/ppermute | solution.py:513
  54.3 35.3 %collective-permute-start.4 = (f32[256,256]{1,0:T(8,128)}, f32[256,256]{1,0:T(8,128)}, u32[]{:S(2)}, u32[]{:S(2)}) collective-permute-start(f32[256,256]{1,0:T(8,128)} %get-tuple-element.60), channel_id=1, source_target_pairs={{0,4},{4,0},{8,12},{12,8},{16,20},{20,16},{24,28},{28,24},{1,5},{5... | collective-permute-start | bytes 786440 | tf_op jit(solution)/shard_map/ppermute | solution.py:513
  81.5 33.9 %copy-start.36 = (f32[256,256]{1,0:T(8,128)}, f32[256,256]{1,0:T(8,128)S(1)}, u32[]{:S(2)}) copy-start(f32[256,256]{1,0:T(8,128)S(1)} %get-tuple-element.107.refs_0_) | copy-start | bytes 786436
  81.5 8.3 %collective-permute-start.6 = (f32[256,256]{1,0:T(8,128)S(1)}, f32[256,256]{1,0:T(8,128)S(1)}, u32[]{:S(2)}, u32[]{:S(2)}) collective-permute-start(f32[256,256]{1,0:T(8,128)S(1)} %get-tuple-element.106), channel_id=1, source_target_pairs={{0,8},{4,12},{8,16},{12,20},{16,24},{20,28},{1,9},{5,13},{9,17},{1... | collective-permute-start | bytes 786440 | tf_op jit(solution)/shard_map/ppermute | solution.py:513
  84.8 46.6 %collective-permute-start.17 = (f32[256,256]{1,0:T(8,128)S(1)}, f32[256,256]{1,0:T(8,128)S(1)}, u32[]{:S(2)}, u32[]{:S(2)}) collective-permute-start(f32[256,256]{1,0:T(8,128)S(1)} %get-tuple-element.72), channel_id=1, source_target_pairs={{0,4},{4,0},{8,12},{12,8},{16,20},{20,16},{24,28},{28,24},{1,5},{5... | collective-permute-start | bytes 786440 | tf_op jit(solution)/shard_map/ppermute | solution.py:513
  89.6 25.8 %copy-start.37 = (f32[256,256]{1,0:T(8,128)}, f32[256,256]{1,0:T(8,128)S(1)}, u32[]{:S(2)}) copy-start(f32[256,256]{1,0:T(8,128)S(1)} %get-tuple-element.101.refs_1_) | copy-start | bytes 786436
  89.7 16.8 %collective-permute-start.5 = (f32[256,256]{1,0:T(8,128)}, f32[256,256]{1,0:T(8,128)S(1)}, u32[]{:S(2)}, u32[]{:S(2)}) collective-permute-start(f32[256,256]{1,0:T(8,128)} %copy-done.30), channel_id=1, source_target_pairs={{0,4},{4,0},{8,12},{12,8},{16,20},{20,16},{24,28},{28,24},{1,5},{5... | collective-permute-start | bytes 786440 | tf_op jit(solution)/shard_map/ppermute | solution.py:513
  89.8 9.5 %collective-permute-start.12 = (f32[256,256]{1,0:T(8,128)S(1)}, f32[256,256]{1,0:T(8,128)S(1)}, u32[]{:S(2)}, u32[]{:S(2)}) collective-permute-start(f32[256,256]{1,0:T(8,128)S(1)} %get-tuple-element.100), channel_id=1, source_target_pairs={{0,8},{4,12},{8,16},{12,20},{16,24},{20,28},{1,9},{5,13},{9,17},{1... | collective-permute-start | bytes 786440 | tf_op jit(solution)/shard_map/ppermute | solution.py:513
  97.9 38.3 %copy-start.38 = (f32[256,256]{1,0:T(8,128)}, f32[256,256]{1,0:T(8,128)S(1)}, u32[]{:S(2)}) copy-start(f32[256,256]{1,0:T(8,128)S(1)} %get-tuple-element.105.refs_2_) | copy-start | bytes 786436
  97.9 25.2 %collective-permute-start.15 = (f32[256,256]{1,0:T(8,128)}, f32[256,256]{1,0:T(8,128)S(1)}, u32[]{:S(2)}, u32[]{:S(2)}) collective-permute-start(f32[256,256]{1,0:T(8,128)} %copy-done.29), channel_id=1, source_target_pairs={{0,4},{4,0},{8,12},{12,8},{16,20},{20,16},{24,28},{28,24},{1,5},{5... | collective-permute-start | bytes 786440 | tf_op jit(solution)/shard_map/ppermute | solution.py:513
  99.3 9.7 %collective-permute-start.7 = (f32[256,256]{1,0:T(8,128)S(1)}, f32[256,256]{1,0:T(8,128)S(1)}, u32[]{:S(2)}, u32[]{:S(2)}) collective-permute-start(f32[256,256]{1,0:T(8,128)S(1)} %get-tuple-element.104), channel_id=1, source_target_pairs={{0,8},{4,12},{8,16},{12,20},{16,24},{20,28},{1,9},{5,13},{9,17},{1... | collective-permute-start | bytes 786440 | tf_op jit(solution)/shard_map/ppermute | solution.py:513
  106.4 29.8 %copy-start.39 = (f32[256,256]{1,0:T(8,128)}, f32[256,256]{1,0:T(8,128)S(1)}, u32[]{:S(2)}) copy-start(f32[256,256]{1,0:T(8,128)S(1)} %get-tuple-element.99.refs_3_) | copy-start | bytes 786436
  106.5 9.0 %copy-start.53 = (f32[256,256]{1,0:T(8,128)}, f32[256,256]{1,0:T(8,128)S(1)}, u32[]{:S(2)}) copy-start(f32[256,256]{1,0:T(8,128)S(1)} %collective-permute-done.5) | copy-start | bytes 786436
  106.5 8.9 %collective-permute-start.13 = (f32[256,256]{1,0:T(8,128)S(1)}, f32[256,256]{1,0:T(8,128)S(1)}, u32[]{:S(2)}, u32[]{:S(2)}) collective-permute-start(f32[256,256]{1,0:T(8,128)S(1)} %get-tuple-element.98), channel_id=1, source_target_pairs={{0,8},{4,12},{8,16},{12,20},{16,24},{20,28},{1,9},{5,13},{9,17},{1... | collective-permute-start | bytes 786440 | tf_op jit(solution)/shard_map/ppermute | solution.py:513
  109.1 27.1 %copy-start.42 = (f32[256,256]{1,0:T(8,128)}, f32[256,256]{1,0:T(8,128)S(1)}, u32[]{:S(2)}) copy-start(f32[256,256]{1,0:T(8,128)S(1)} %collective-permute-done.7) | copy-start | bytes 786436
  111.7 24.5 %copy-start.34 = (f32[256,256]{1,0:T(8,128)}, f32[256,256]{1,0:T(8,128)S(1)}, u32[]{:S(2)}) copy-start(f32[256,256]{1,0:T(8,128)S(1)} %get-tuple-element.103.refs_4_) | copy-start | bytes 786436
  111.7 11.4 %collective-permute-start.8 = (f32[256,256]{1,0:T(8,128)S(1)}, f32[256,256]{1,0:T(8,128)S(1)}, u32[]{:S(2)}, u32[]{:S(2)}) collective-permute-start(f32[256,256]{1,0:T(8,128)S(1)} %get-tuple-element.102), channel_id=1, source_target_pairs={{0,8},{4,12},{8,16},{12,20},{16,24},{20,28},{1,9},{5,13},{9,17},{1... | collective-permute-start | bytes 786440 | tf_op jit(solution)/shard_map/ppermute | solution.py:513
  115.4 20.8 %copy-start.40 = (f32[256,256]{1,0:T(8,128)}, f32[256,256]{1,0:T(8,128)S(1)}, u32[]{:S(2)}) copy-start(f32[256,256]{1,0:T(8,128)S(1)} %collective-permute-done.13) | copy-start | bytes 786436
  118.9 17.3 %copy-start.35 = (f32[256,256]{1,0:T(8,128)}, f32[256,256]{1,0:T(8,128)S(1)}, u32[]{:S(2)}) copy-start(f32[256,256]{1,0:T(8,128)S(1)} %get-tuple-element.97.refs_5_) | copy-start | bytes 786436
  119.0 12.5 %collective-permute-start.14 = (f32[256,256]{1,0:T(8,128)S(1)}, f32[256,256]{1,0:T(8,128)S(1)}, u32[]{:S(2)}, u32[]{:S(2)}) collective-permute-start(f32[256,256]{1,0:T(8,128)S(1)} %get-tuple-element.96), channel_id=1, source_target_pairs={{0,8},{4,12},{8,16},{12,20},{16,24},{20,28},{1,9},{5,13},{9,17},{1... | collective-permute-start | bytes 786440 | tf_op jit(solution)/shard_map/ppermute | solution.py:513
  123.1 13.1 %copy-start.50 = (f32[256,256]{1,0:T(8,128)}, f32[256,256]{1,0:T(8,128)S(1)}, u32[]{:S(2)}) copy-start(f32[256,256]{1,0:T(8,128)S(1)} %collective-permute-done.15) | copy-start | bytes 786436
  123.2 13.1 %copy-start.47 = (f32[256,256]{1,0:T(8,128)}, f32[256,256]{1,0:T(8,128)S(1)}, u32[]{:S(2)}) copy-start(f32[256,256]{1,0:T(8,128)S(1)} %collective-permute-done.8) | copy-start | bytes 786436
  128.1 34.1 %copy-start.32 = (f32[256,256]{1,0:T(8,128)S(1)}, f32[256,256]{1,0:T(8,128)}, u32[]{:S(2)}) copy-start(f32[256,256]{1,0:T(8,128)} %get-tuple-element.95.refs_6_) | copy-start | bytes 786436
  128.1 18.1 %collective-permute-start.16 = (f32[256,256]{1,0:T(8,128)}, f32[256,256]{1,0:T(8,128)}, u32[]{:S(2)}, u32[]{:S(2)}) collective-permute-start(f32[256,256]{1,0:T(8,128)} %get-tuple-element.94), channel_id=1, source_target_pairs={{0,8},{4,12},{8,16},{12,20},{16,24},{20,28},{1,9},{5,13},{9,17},{1... | collective-permute-start | bytes 786440 | tf_op jit(solution)/shard_map/ppermute | solution.py:513
  131.4 4.9 %copy-start.46 = (f32[256,256]{1,0:T(8,128)}, f32[256,256]{1,0:T(8,128)S(1)}, u32[]{:S(2)}) copy-start(f32[256,256]{1,0:T(8,128)S(1)} %collective-permute-done.14) | copy-start | bytes 786436
  136.2 36.7 %copy-start.33 = (f32[256,256]{1,0:T(8,128)S(1)}, f32[256,256]{1,0:T(8,128)}, u32[]{:S(2)}) copy-start(f32[256,256]{1,0:T(8,128)} %get-tuple-element.93.refs_7_) | copy-start | bytes 786436
  136.3 43.5 %copy-start.43 = (f32[256,256]{1,0:T(8,128)S(1)}, f32[256,256]{1,0:T(8,128)}, u32[]{:S(2)}) copy-start(f32[256,256]{1,0:T(8,128)} %copy-done.42) | copy-start | bytes 786436
  138.2 31.1 %collective-permute-start.31 = (f32[8,64,256]{2,1,0:T(8,128)}, f32[8,64,256]{2,1,0:T(8,128)}, u32[]{:S(2)}, u32[]{:S(2)}) collective-permute-start(f32[8,64,256]{2,1,0:T(8,128)} %down.3), channel_id=1, source_target_pairs={{8,0},{12,4},{16,8},{20,12},{24,16},{28,20},{9,1},{13,5},{17,9},{2... | collective-permute-start | bytes 1572872 | tf_op jit(solution)/shard_map/ppermute | solution.py:513
  139.5 15.0 %collective-permute-start.18 = (f32[256,256]{1,0:T(8,128)}, f32[256,256]{1,0:T(8,128)S(1)}, u32[]{:S(2)}, u32[]{:S(2)}) collective-permute-start(f32[256,256]{1,0:T(8,128)} %get-tuple-element.92), channel_id=1, source_target_pairs={{0,8},{4,12},{8,16},{12,20},{16,24},{20,28},{1,9},{5,13},{9,17},{1... | collective-permute-start | bytes 786440 | tf_op jit(solution)/shard_map/ppermute | solution.py:513
  144.1 72.6 %collective-permute-start.23 = (f32[256,256]{1,0:T(8,128)}, f32[256,256]{1,0:T(8,128)S(1)}, u32[]{:S(2)}, u32[]{:S(2)}) collective-permute-start(f32[256,256]{1,0:T(8,128)} %get-tuple-element.118.refs_16_), channel_id=1, source_target_pairs={{0,4},{4,0},{8,12},{12,8},{16,20},{20,16},{24,28},{28,24},{1,5},{5... | collective-permute-start | bytes 786440 | tf_op jit(solution)/shard_map/ppermute | solution.py:513
  146.0 71.6 %collective-permute-start.24 = (f32[256,256]{1,0:T(8,128)}, f32[256,256]{1,0:T(8,128)S(1)}, u32[]{:S(2)}, u32[]{:S(2)}) collective-permute-start(f32[256,256]{1,0:T(8,128)} %get-tuple-element.116.refs_17_), channel_id=1, source_target_pairs={{0,4},{4,0},{8,12},{12,8},{16,20},{20,16},{24,28},{28,24},{1,5},{5... | collective-permute-start | bytes 786440 | tf_op jit(solution)/shard_map/ppermute | solution.py:513
  148.5 13.7 %collective-permute-start.19 = (f32[256,256]{1,0:T(8,128)S(1)}, f32[256,256]{1,0:T(8,128)S(1)}, u32[]{:S(2)}, u32[]{:S(2)}) collective-permute-start(f32[256,256]{1,0:T(8,128)S(1)} %multiply_add_fusion.15), channel_id=1, source_target_pairs={{0,8},{4,12},{8,16},{12,20},{16,24},{20,28},{1,9},{5,13},{9,17},{1... | collective-permute-start | bytes 786440 | tf_op jit(solution)/shard_map/ppermute | solution.py:513
  154.5 9.6 %copy-start.48 = (f32[256,256]{1,0:T(8,128)}, f32[256,256]{1,0:T(8,128)S(1)}, u32[]{:S(2)}) copy-start(f32[256,256]{1,0:T(8,128)S(1)} %collective-permute-done.18) | copy-start | bytes 786436
  157.6 15.3 %collective-permute-start.20 = (f32[256,256]{1,0:T(8,128)}, f32[256,256]{1,0:T(8,128)}, u32[]{:S(2)}, u32[]{:S(2)}) collective-permute-start(f32[256,256]{1,0:T(8,128)} %multiply_add_fusion.13), channel_id=1, source_target_pairs={{0,8},{4,12},{8,16},{12,20},{16,24},{20,28},{1,9},{5,13},{9,17},{1... | collective-permute-start | bytes 786440 | tf_op jit(solution)/shard_map/ppermute | solution.py:513
  164.1 23.6 %copy-start.41 = (f32[256,256]{1,0:T(8,128)S(1)}, f32[256,256]{1,0:T(8,128)}, u32[]{:S(2)}) copy-start(f32[256,256]{1,0:T(8,128)} %copy-done.40) | copy-start | bytes 786436
  164.1 15.7 %collective-permute-start.21 = (f32[256,256]{1,0:T(8,128)}, f32[256,256]{1,0:T(8,128)}, u32[]{:S(2)}, u32[]{:S(2)}) collective-permute-start(f32[256,256]{1,0:T(8,128)} %multiply_add_fusion.11), channel_id=1, source_target_pairs={{0,8},{4,12},{8,16},{12,20},{16,24},{20,28},{1,9},{5,13},{9,17},{1... | collective-permute-start | bytes 786440 | tf_op jit(solution)/shard_map/ppermute | solution.py:513
  171.5 25.4 %copy-start.51 = (f32[256,256]{1,0:T(8,128)S(1)}, f32[256,256]{1,0:T(8,128)}, u32[]{:S(2)}) copy-start(f32[256,256]{1,0:T(8,128)} %copy-done.50) | copy-start | bytes 786436
  171.5 27.3 %collective-permute-start.32 = (f32[8,64,256]{2,1,0:T(8,128)}, f32[8,64,256]{2,1,0:T(8,128)}, u32[]{:S(2)}, u32[]{:S(2)}) collective-permute-start(f32[8,64,256]{2,1,0:T(8,128)} %down.4), channel_id=1, source_target_pairs={{8,0},{12,4},{16,8},{20,12},{24,16},{28,20},{9,1},{13,5},{17,9},{2... | collective-permute-start | bytes 1572872 | tf_op jit(solution)/shard_map/ppermute | solution.py:513
  175.2 12.5 %collective-permute-start.22 = (f32[256,256]{1,0:T(8,128)S(1)}, f32[256,256]{1,0:T(8,128)S(1)}, u32[]{:S(2)}, u32[]{:S(2)}) collective-permute-start(f32[256,256]{1,0:T(8,128)S(1)} %multiply_add_fusion.9), channel_id=1, source_target_pairs={{0,8},{4,12},{8,16},{12,20},{16,24},{20,28},{1,9},{5,13},{9,17},{1... | collective-permute-start | bytes 786440 | tf_op jit(solution)/shard_map/ppermute | solution.py:513
  185.7 33.1 %collective-permute-start.25 = (f32[256,256]{1,0:T(8,128)}, f32[256,256]{1,0:T(8,128)S(1)}, u32[]{:S(2)}, u32[]{:S(2)}) collective-permute-start(f32[256,256]{1,0:T(8,128)} %get-tuple-element.114.refs_18_), channel_id=1, source_target_pairs={{0,4},{4,0},{8,12},{12,8},{16,20},{20,16},{24,28},{28,24},{1,5},{5... | collective-permute-start | bytes 786440 | tf_op jit(solution)/shard_map/ppermute | solution.py:513
  187.7 29.9 %copy-start.44 = (f32[256,256]{1,0:T(8,128)S(1)}, f32[256,256]{1,0:T(8,128)}, u32[]{:S(2)}) copy-start(f32[256,256]{1,0:T(8,128)} %get-tuple-element.78.refs_22_) | copy-start | bytes 786436
  187.7 33.2 %copy-start.57 = (f32[8,256]{1,0:T(8,128)S(1)}, f32[8,256]{1,0:T(8,128)}, u32[]{:S(2)}) copy-start(f32[8,256]{1,0:T(8,128)} %get-tuple-element.75) | copy-start | bytes 24580
  187.7 33.8 %copy-start.11 = (f32[256,256]{1,0:T(8,128)S(1)}, f32[256,256]{1,0:T(8,128)}, u32[]{:S(2)}) copy-start(f32[256,256]{1,0:T(8,128)} %multiply_add_fusion.22.rest_1_.refs_9_) | copy-start | bytes 786436
  187.7 33.8 %copy-start.12 = (f32[256,256]{1,0:T(8,128)S(1)}, f32[256,256]{1,0:T(8,128)}, u32[]{:S(2)}) copy-start(f32[256,256]{1,0:T(8,128)} %multiply_add_fusion.28.rest_0_.refs_8_) | copy-start | bytes 786436
  193.7 25.1 %copy-start.45 = (f32[256,256]{1,0:T(8,128)S(1)}, f32[256,256]{1,0:T(8,128)}, u32[]{:S(2)}) copy-start(f32[256,256]{1,0:T(8,128)} %get-tuple-element.76.refs_23_) | copy-start | bytes 786436
  193.7 25.9 %collective-permute-start.26 = (f32[256,256]{1,0:T(8,128)}, f32[256,256]{1,0:T(8,128)S(1)}, u32[]{:S(2)}, u32[]{:S(2)}) collective-permute-start(f32[256,256]{1,0:T(8,128)} %get-tuple-element.110.refs_19_), channel_id=1, source_target_pairs={{0,4},{4,0},{8,12},{12,8},{16,20},{20,16},{24,28},{28,24},{1,5},{5... | collective-permute-start | bytes 786440 | tf_op jit(solution)/shard_map/ppermute | solution.py:513
  201.0 11.3 %collective-permute-start.33 = (f32[8,64,256]{2,1,0:T(8,128)}, f32[8,64,256]{2,1,0:T(8,128)S(1)}, u32[]{:S(2)}, u32[]{:S(2)}) collective-permute-start(f32[8,64,256]{2,1,0:T(8,128)} %down.5), channel_id=1, source_target_pairs={{8,0},{12,4},{16,8},{20,12},{24,16},{28,20},{9,1},{13,5},{17,9},{2... | collective-permute-start | bytes 1572872 | tf_op jit(solution)/shard_map/ppermute | solution.py:513
  212.2 34.0 %collective-permute-start.27 = (f32[256,256]{1,0:T(8,128)}, f32[256,256]{1,0:T(8,128)S(1)}, u32[]{:S(2)}, u32[]{:S(2)}) collective-permute-start(f32[256,256]{1,0:T(8,128)} %get-tuple-element.112.refs_20_), channel_id=1, source_target_pairs={{0,4},{4,0},{8,12},{12,8},{16,20},{20,16},{24,28},{28,24},{1,5},{5... | collective-permute-start | bytes 786440 | tf_op jit(solution)/shard_map/ppermute | solution.py:513
  216.7 31.8 %collective-permute-start.28 = (f32[256,256]{1,0:T(8,128)}, f32[256,256]{1,0:T(8,128)S(1)}, u32[]{:S(2)}, u32[]{:S(2)}) collective-permute-start(f32[256,256]{1,0:T(8,128)} %get-tuple-element.108.refs_21_), channel_id=1, source_target_pairs={{0,4},{4,0},{8,12},{12,8},{16,20},{20,16},{24,28},{28,24},{1,5},{5... | collective-permute-start | bytes 786440 | tf_op jit(solution)/shard_map/ppermute | solution.py:513
  217.6 33.3 %collective-permute-start.29 = (f32[256,256]{1,0:T(8,128)S(1)}, f32[256,256]{1,0:T(8,128)S(1)}, u32[]{:S(2)}, u32[]{:S(2)}) collective-permute-start(f32[256,256]{1,0:T(8,128)S(1)} %copy-done.44), channel_id=1, source_target_pairs={{0,4},{4,0},{8,12},{12,8},{16,20},{20,16},{24,28},{28,24},{1,5},{5... | collective-permute-start | bytes 786440 | tf_op jit(solution)/shard_map/ppermute | solution.py:513
  218.8 34.3 %collective-permute-start.30 = (f32[256,256]{1,0:T(8,128)S(1)}, f32[256,256]{1,0:T(8,128)S(1)}, u32[]{:S(2)}, u32[]{:S(2)}) collective-permute-start(f32[256,256]{1,0:T(8,128)S(1)} %copy-done.45), channel_id=1, source_target_pairs={{0,4},{4,0},{8,12},{12,8},{16,20},{20,16},{24,28},{28,24},{1,5},{5... | collective-permute-start | bytes 786440 | tf_op jit(solution)/shard_map/ppermute | solution.py:513
  219.6 35.9 %collective-permute-start.34 = (f32[4,32,512]{2,1,0:T(8,128)}, f32[4,32,512]{2,1,0:T(8,128)S(1)}, u32[]{:S(2)}, u32[]{:S(2)}) collective-permute-start(f32[4,32,512]{2,1,0:T(8,128)} %get-tuple-element.74), channel_id=1, source_target_pairs={{0,4},{4,0},{8,12},{12,8},{16,20},{20,16},{24,28},{28,24},{1,5},{5... | collective-permute-start | bytes 786440 | tf_op jit(solution)/shard_map/ppermute | solution.py:513
  (29 other events, 70.0 us)

commit v2 on v0

v2 whole, which is shorter than its diff:
```python
import functools

import jax
import jax.numpy as jnp
from jax import lax
from jax.experimental import pallas as pl
from jax.experimental.pallas import tpu as pltpu
from jax.sharding import PartitionSpec as P

VERY_NEGATIVE = -1e30
LANES = 128
MIB = 1 << 20
AXIS = "ctx"

ROW_A, ROW_SEND_P, ROW_SEND_S, ROW_OWN_P, ROW_OWN_S, ROW_FIN_P, ROW_FIN_K, ROW_FIN_R, ROW_CHAIN = range(9)


class Order:
    def __init__(self):
        self.last = None


def call(order, kernel, operands, outs, name, mib=8, scratch=(), aliases=None, flops=1e6, moved=1e6):
    in_specs, arrays = [], []
    count = len(operands)
    if order.last is not None:
        operands = [*operands, order.last]
    body = lambda *refs: kernel(*refs[:count], *refs[len(operands) :])
    for operand in operands:
        if isinstance(operand, tuple):
            in_specs.append(pl.BlockSpec(memory_space=pl.ANY))
            arrays.append(pltpu.with_memory_space_constraint(operand[0], pltpu.HBM))
        else:
            in_specs.append(pl.BlockSpec(memory_space=pltpu.VMEM))
            arrays.append(pltpu.with_memory_space_constraint(operand, pltpu.VMEM))
    out_specs = [
        pl.BlockSpec(memory_space=pl.ANY if out.memory_space == pltpu.HBM else pltpu.VMEM) for out in outs
    ]
    results = pl.pallas_call(
        body,
        in_specs=in_specs,
        out_specs=out_specs,
        out_shape=list(outs),
        scratch_shapes=list(scratch),
        input_output_aliases=aliases or {},
        compiler_params=pltpu.CompilerParams(vmem_limit_bytes=mib * MIB),
        cost_estimate=pl.CostEstimate(flops=int(flops), bytes_accessed=int(moved), transcendentals=0),
        name=name,
    )(*arrays)
    order.last = results[-1]
    return results


class Operands:
    def __init__(self):
        self.arrays = []

    def place(self, array):
        for i, other in enumerate(self.arrays):
            if other is array:
                return i
        self.arrays.append(array)
        return len(self.arrays) - 1

    def view(self, view):
        return self.place(view[0]), view[1]


def position():
    place = lax.axis_index(AXIS)
    return lax.rem(place, 2), lax.div(place, 2)


def lane_iota(shape):
    return lax.broadcasted_iota(jnp.int32, shape, len(shape) - 1)


def row_iota(shape):
    return lax.broadcasted_iota(jnp.int32, shape, 0)


def lane_order(value, side):
    half = value.shape[0] // 2
    return jnp.where(side == 0, value, jnp.concatenate([value[half:], value[:half]], axis=0))


def head_at(index, heads, side):
    return lax.rem(side * (heads // 2) + index, heads)


def columns_of(head, width):
    return pl.ds(pl.multiple_of(head * width, width), width)


def three_parts(value):
    high = value.astype(jnp.bfloat16).astype(jnp.float32)
    middle = (value - high).astype(jnp.bfloat16).astype(jnp.float32)
    return high, middle, value - high - middle


def memory_of(key, value, weight):
    scaled = (key.astype(jnp.float32) * weight).astype(jnp.bfloat16)
    return lax.dot_general(
        scaled, value, (((0,), (0,)), ((), ())), preferred_element_type=jnp.float32
    )


def start_kernel(
    input_hbm, forget_hbm, keys_hbm, values_hbm,
    keys_ref, rows_ref, columns_ref, summary_ref, first_ref, second_ref,
    input_ref, forget_ref, value_ref, sems,
):
    heads, tokens = input_ref.shape
    dqk = keys_ref.shape[1] // heads
    dv = value_ref.shape[1]
    side, _ = position()
    copies = [
        pltpu.make_async_copy(forget_hbm, forget_ref, sems.at[0]),
        pltpu.make_async_copy(input_hbm, input_ref, sems.at[1]),
    ]
    away = head_at(heads // 2, heads, side)
    copies.append(pltpu.make_async_copy(values_hbm.at[:, columns_of(away, dv)], value_ref, sems.at[2]))
    copies.append(pltpu.make_async_copy(keys_hbm, keys_ref, sems.at[3]))
    for copy in copies:
        copy.start()
    copies[0].wait()
    copies[1].wait()

    gate = lane_order(forget_ref[...], side)
    cumulated = jnp.minimum(gate, 0.0) - jnp.log1p(jnp.exp(-jnp.abs(gate)))
    lanes = lane_iota((heads, tokens))
    step = 1
    while step < tokens:
        cumulated = cumulated + jnp.where(lanes >= step, pltpu.roll(cumulated, step, 1), 0.0)
        step *= 2
    level = lane_order(input_ref[...], side) - cumulated
    running = level
    step = 1
    while step < tokens:
        running = jnp.maximum(
            running, jnp.where(lanes >= step, pltpu.roll(running, step, 1), VERY_NEGATIVE)
        )
        step *= 2
    highest = running[:, tokens - 1 : tokens]
    decay = cumulated[:, tokens - 1 : tokens]
    weight = jnp.exp(level - highest)
    rows_ref[...] = level
    filler = jnp.zeros((LANES - 3 * heads, tokens), jnp.float32)
    columns_ref[...] = jnp.concatenate([weight, running, cumulated, filler], axis=0).T

    copies[2].wait()
    copies[3].wait()
    place = heads // 2
    memory = memory_of(
        keys_ref[:, columns_of(away, dqk)], value_ref[...], columns_ref[:, place : place + 1]
    )
    first_ref[...] = memory[:, : dv // 2]
    second_ref[...] = memory[:, dv // 2 :]

    spare = jnp.zeros((-(-3 * heads // 16) * 16 - 3 * heads, tokens), jnp.float32)
    parts = jnp.concatenate([*three_parts(weight), spare], axis=0).astype(jnp.bfloat16)
    sums = []
    for i in range(heads):
        product = jnp.dot(
            parts, keys_ref[:, columns_of(head_at(i, heads, side), dqk)], preferred_element_type=jnp.float32
        )
        sums.append(
            product[i : i + 1] + product[heads + i : heads + i + 1] + product[2 * heads + i : 2 * heads + i + 1]
        )
    lane = lane_iota((heads, LANES))
    stats = jnp.where(lane == 0, decay + highest, jnp.where(lane == 1, decay, 0.0))
    summary = jnp.concatenate([jnp.concatenate(sums, axis=0), stats], axis=1)
    summary_ref[...] = lane_order(summary, side)


def start(order, input_gate, forget_gate, keys, values):
    heads, tokens = input_gate.shape
    dqk, dv = keys.shape[1] // heads, values.shape[1] // heads
    return call(
        order,
        start_kernel,
        [(a, pl.ANY) for a in (input_gate, forget_gate, keys, values)],
        [
            pltpu.VMEM(keys.shape, keys.dtype),
            pltpu.VMEM((heads, tokens), jnp.float32),
            pltpu.VMEM((tokens, LANES), jnp.float32),
            pltpu.VMEM((heads, dqk + LANES), jnp.float32),
            pltpu.VMEM((dqk, dv // 2), jnp.float32),
            pltpu.VMEM((dqk, dv // 2), jnp.float32),
        ],
        "start",
        mib=12,
        scratch=[
            pltpu.VMEM((heads, tokens), jnp.float32),
            pltpu.VMEM((heads, tokens), jnp.float32),
            pltpu.VMEM((tokens, dv), values.dtype),
            pltpu.SemaphoreType.DMA((4,)),
        ],
        flops=4e9,
        moved=8e6,
    )


def load_kernel(keys_ref, columns_ref, big_hbm, big_ref, *refs, heads, indices):
    *memory_refs, sems = refs
    side, _ = position()
    width = big_ref.shape[1] // heads
    dqk = keys_ref.shape[1] // heads
    order = list(indices) + [i for i in range(heads) if i not in indices]
    copies = {}
    for i in order:
        columns = columns_of(head_at(i, heads, side), width)
        copies[i] = pltpu.make_async_copy(big_hbm.at[:, columns], big_ref.at[:, columns], sems.at[i])
        copies[i].start()
    for i, memory_ref in zip(indices, memory_refs):
        head = head_at(i, heads, side)
        copies[i].wait()
        memory_ref[...] = memory_of(
            keys_ref[:, columns_of(head, dqk)], big_ref[:, columns_of(head, width)], columns_ref[:, i : i + 1]
        )
    for i in order[len(indices) :]:
        copies[i].wait()


def load(order, keys, columns, values, indices, heads):
    tokens = keys.shape[0]
    dqk, dv = keys.shape[1] // heads, values.shape[1] // heads
    outs = call(
        order,
        functools.partial(load_kernel, heads=heads, indices=indices),
        [keys, columns, (values, pl.ANY)],
        [pltpu.VMEM(values.shape, values.dtype)] + [pltpu.VMEM((dqk, dv), jnp.float32)] * len(indices),
        "memories_away",
        mib=12,
        scratch=[pltpu.SemaphoreType.DMA((heads,))],
        flops=4 * len(indices) * tokens * dqk * dv,
        moved=8e6,
    )
    return outs[0], outs[1:]


def memories_kernel(keys_ref, columns_ref, values_ref, queries_hbm, queries_ref, *refs, heads, indices):
    *memory_refs, sem = refs
    side, _ = position()
    dqk, dv = keys_ref.shape[1] // heads, values_ref.shape[1] // heads
    copy = pltpu.make_async_copy(queries_hbm, queries_ref, sem)
    copy.start()
    for i, memory_ref in zip(indices, memory_refs):
        head = head_at(i, heads, side)
        memory_ref[...] = memory_of(
            keys_ref[:, columns_of(head, dqk)], values_ref[:, columns_of(head, dv)], columns_ref[:, i : i + 1]
        )
    copy.wait()


def memories(order, keys, columns, values, queries, indices, heads):
    tokens = keys.shape[0]
    dqk, dv = keys.shape[1] // heads, values.shape[1] // heads
    outs = call(
        order,
        functools.partial(memories_kernel, heads=heads, indices=indices),
        [keys, columns, values, (queries, pl.ANY)],
        [pltpu.VMEM(queries.shape, queries.dtype)] + [pltpu.VMEM((dqk, dv), jnp.float32)] * len(indices),
        "memories_more",
        mib=12,
        scratch=[pltpu.SemaphoreType.DMA],
        flops=4 * len(indices) * tokens * dqk * dv,
        moved=4e6,
    )
    return outs[0], outs[1:]


def own_kernel(keys_ref, columns_ref, values_ref, *memory_refs, heads, indices):
    side, _ = position()
    dqk, dv = keys_ref.shape[1] // heads, values_ref.shape[1] // heads
    for i, memory_ref in zip(indices, memory_refs):
        head = head_at(i, heads, side)
        memory_ref[...] = memory_of(
            keys_ref[:, columns_of(head, dqk)], values_ref[:, columns_of(head, dv)], columns_ref[:, i : i + 1]
        )


def own_memories(order, keys, columns, values, indices, heads):
    tokens = keys.shape[0]
    dqk, dv = keys.shape[1] // heads, values.shape[1] // heads
    return call(
        order,
        functools.partial(own_kernel, heads=heads, indices=indices),
        [keys, columns, values],
        [pltpu.VMEM((dqk, dv), jnp.float32)] * len(indices),
        "memories_own",
        mib=12,
        flops=4 * len(indices) * tokens * dqk * dv,
        moved=4e6,
    )


def weights_kernel(gathered_ref, table_ref, parts_ref, top_row_ref):
    blocks, heads, width = gathered_ref.shape
    dqk = width - LANES
    lane_heads = heads // 2
    levels = blocks // 2
    place = lax.axis_index(AXIS)
    side, level = position()

    tops, decays, normals = [], [], []
    for block in range(blocks):
        held = gathered_ref[lax.rem(block - place + blocks, blocks)]
        normals.append(held[:, :dqk])
        tops.append(held[:, dqk : dqk + 1])
        decays.append(held[:, dqk + 1 : dqk + 2])

    pick = lambda at, value, otherwise: jnp.where(level == at, value, otherwise)
    top = jnp.full((heads, 1), VERY_NEGATIVE, jnp.float32)
    normal = jnp.zeros((heads, dqk), jnp.float32)
    zero = jnp.zeros((heads, 1), jnp.float32)
    mine_a = mine_b = mine_first = mine_second = zero
    carry_p = carry_s = zero
    prefix_top, prefix_normal = zero, normal
    scales = []
    for z in range(levels):
        t0, t1, d0, d1 = tops[2 * z], tops[2 * z + 1], decays[2 * z], decays[2 * z + 1]
        pair_top = jnp.maximum(t0 + d1, t1)
        first, second = jnp.exp(t0 + d1 - pair_top), jnp.exp(t1 - pair_top)
        pair_normal = normals[2 * z] * first + normals[2 * z + 1] * second
        middle_top = jnp.maximum(top + d0, t0)
        alpha, beta = jnp.exp(top + d0 - middle_top), jnp.exp(t0 - middle_top)
        middle_normal = normal * alpha + normals[2 * z] * beta
        pair_decay = d0 + d1
        next_top = jnp.maximum(top + pair_decay, pair_top)
        a, b = jnp.exp(top + pair_decay - next_top), jnp.exp(pair_top - next_top)
        mine_a, mine_b = pick(z, a, mine_a), pick(z, b, mine_b)
        mine_first, mine_second = pick(z, first, mine_first), pick(z, second, mine_second)
        carry_p, carry_s = pick(z, alpha, carry_p), pick(z, beta, carry_s)
        prefix_top = pick(z, jnp.where(side == 0, top, middle_top), prefix_top)
        prefix_normal = pick(z, jnp.where(side == 0, normal, middle_normal), prefix_normal)
        normal = normal * a + pair_normal * b
        top = next_top
        scales.append((a, b))
    later = jnp.ones((heads, 1), jnp.float32)
    final_p = final_l = zero
    for z in reversed(range(levels)):
        a, b = scales[z]
        final_l = pick(z, b * later, final_l)
        later = later * a
        final_p = pick(z, later, final_p)

    one = jnp.ones((heads, 1), jnp.float32)
    by_side = lambda zero_value, one_value: jnp.where(side == 0, zero_value, one_value)
    lanes = lane_iota((heads, LANES))
    rows = row_iota((heads, LANES))
    head_of_chunk = lane_heads * side + lax.div(lanes, 2)
    head_of_step = lane_heads * side + lax.div(jnp.clip(lanes - level, 0, 2 * lane_heads - 1), 2)

    def spread(column, heads_wanted):
        return jnp.sum(jnp.where(rows == heads_wanted, column, 0.0), axis=0, keepdims=True)

    mine_own = by_side(mine_first, mine_second)
    mine_partner = by_side(mine_second, mine_first)
    chain_own = spread(mine_b * mine_own, head_of_step)
    chain_partner = spread(mine_b * mine_partner, head_of_step)
    entries = [
        spread(mine_a, head_of_step),
        spread(by_side(carry_p, one), head_of_chunk),
        spread(by_side(carry_s, zero), head_of_chunk),
        spread(by_side(one, carry_p), head_of_chunk),
        spread(by_side(zero, carry_s), head_of_chunk),
        spread(final_p, head_of_chunk),
        spread(final_l * mine_own, head_of_chunk),
        spread(final_l * mine_partner, head_of_chunk),
    ]
    for z in range(levels):
        entries += [pick(z, chain_own, 0.0), pick(z, chain_partner, 0.0)]
    here = jnp.ones((1, LANES), jnp.float32)
    entries += [pick(z, here, 0.0) for z in range(levels)]
    empty = jnp.zeros((1, LANES), jnp.float32)
    entries += [empty] * (table_ref.shape[0] - len(entries))
    table_ref[...] = jnp.concatenate(entries, axis=0)

    filler = jnp.zeros((LANES - 3 * heads, dqk), jnp.float32)
    parts = jnp.concatenate([*three_parts(lane_order(prefix_normal, side)), filler], axis=0)
    parts_ref[...] = parts.T
    prefix_top = lane_order(jnp.broadcast_to(prefix_top, (heads, LANES)), side)
    filler = jnp.zeros((LANES - heads, LANES), jnp.float32)
    top_row_ref[...] = jnp.concatenate([prefix_top, filler], axis=0).T[:8]


def weights(order, gathered):
    blocks, heads, width = gathered.shape
    dqk = width - LANES
    table_rows = -(-(ROW_CHAIN + 3 * (blocks // 2)) // 8) * 8
    return call(
        order,
        weights_kernel,
        [gathered],
        [
            pltpu.VMEM((table_rows, LANES), jnp.float32),
            pltpu.VMEM((dqk, LANES), jnp.float32),
            pltpu.VMEM((8, LANES), jnp.float32),
        ],
        "weights",
    )


def finals_kernel(gathered_ref, normal_ref, tops_ref):
    blocks, heads, width = gathered_ref.shape
    dqk = width - LANES
    place = lax.axis_index(AXIS)
    top = jnp.full((heads, 1), VERY_NEGATIVE, jnp.float32)
    normal = jnp.zeros((heads, dqk), jnp.float32)
    for block in range(blocks):
        held = gathered_ref[lax.rem(block - place + blocks, blocks)]
        block_top, decay = held[:, dqk : dqk + 1], held[:, dqk + 1 : dqk + 2]
        next_top = jnp.maximum(top + decay, block_top)
        normal = normal * jnp.exp(top + decay - next_top) + held[:, :dqk] * jnp.exp(block_top - next_top)
        top = next_top
    normal_ref[...] = normal
    tops_ref[...] = jnp.where(lane_iota((heads, LANES)) == 0, top, 0.0)


def finals(order, gathered):
    _, heads, width = gathered.shape
    return call(
        order,
        finals_kernel,
        [gathered],
        [pltpu.VMEM((heads, width - LANES), jnp.float32), pltpu.VMEM((heads, LANES), jnp.float32)],
        "finals",
    )


def attention_kernel(
    queries_ref, keys_ref, values_ref, rows_ref, columns_ref, parts_ref, *refs, heads, index
):
    out_ref, sums_ref, products_ref = refs[-3:]
    side, _ = position()
    head = head_at(index, heads, side)
    tokens = queries_ref.shape[0]
    dqk, dv = queries_ref.shape[1] // heads, values_ref.shape[1] // heads
    key_columns, value_columns = columns_of(head, dqk), columns_of(head, dv)
    tile = min(256, tokens)
    level = rows_ref[index : index + 1, :]
    causal = row_iota((tile, tile)) >= lane_iota((tile, tile))
    part_lanes = lane_iota(parts_ref.shape)
    mine = (lax.rem(part_lanes, heads) == index) & (part_lanes < 3 * heads)
    parts = jnp.where(mine, parts_ref[...], 0.0).astype(jnp.bfloat16)

    for begin in range(0, tokens, tile):
        end = begin + tile
        here = pl.ds(begin, tile)
        query = queries_ref[here, key_columns]
        running = columns_ref[here, heads + index : heads + index + 1]
        total = jnp.zeros((tile, 1), jnp.float32)
        result = None
        for low in range(0, end, tile):
            there = pl.ds(low, tile)
            scores = lax.dot_general(
                query, keys_ref[there, key_columns], (((1,), (1,)), ((), ())), preferred_element_type=jnp.float32
            )
            attn = jnp.exp(level[:, low : low + tile] - running) * scores
            if low == begin:
                attn = jnp.where(causal, attn, 0.0)
            total = total + jnp.sum(attn, axis=1, keepdims=True)
            term = jnp.dot(
                attn.astype(jnp.bfloat16), values_ref[there, value_columns], preferred_element_type=jnp.float32
            )
            result = term if result is None else result + term
        product = jnp.dot(query, parts, preferred_element_type=jnp.float32)
        lanes = lane_iota((tile, LANES))
        if len(refs) > 3:
            sums_ref[here, :] = jnp.where(lanes == index, total, refs[0][here, :])
            products_ref[here, :] = refs[1][here, :] + product
        else:
            sums_ref[here, :] = jnp.where(lanes == index, total, 0.0)
            products_ref[here, :] = product
        out_ref[here, :] = result.astype(jnp.bfloat16)


def attention(order, index, queries, keys, values, rows, columns, parts, state):
    tokens = queries.shape[0]
    heads = rows.shape[0]
    dqk, dv = queries.shape[1] // heads, values.shape[1] // heads
    return call(
        order,
        functools.partial(attention_kernel, heads=heads, index=index),
        [queries, keys, values, rows, columns, parts, *state],
        [
            pltpu.VMEM((tokens, dv), jnp.bfloat16),
            pltpu.VMEM((tokens, LANES), jnp.float32),
            pltpu.VMEM((tokens, LANES), jnp.float32),
        ],
        "attention",
        mib=12,
        flops=2 * tokens * tokens * (dqk + dv) * 1.5,
    )


def factors_kernel(columns_ref, top_ref, sums_ref, products_ref, out_ref, *, heads, dqk):
    tokens = columns_ref.shape[0]
    tile = min(256, tokens)
    shift = lambda block, by: pltpu.roll(block, (LANES - by) % LANES, 1)
    for begin in range(0, tokens, tile):
        here = pl.ds(begin, tile)
        product = products_ref[here, :]
        product = product + shift(product, heads) + shift(product, 2 * heads)
        column = columns_ref[here, :]
        running, cumulated = shift(column, heads), shift(column, 2 * heads)
        top = top_ref[0:1, :]
        highest = jnp.maximum(running, top)
        scaling = float(dqk) ** -0.5
        local, carried = jnp.exp(running - highest), jnp.exp(top - highest)
        denominator = (local * sums_ref[here, :] + carried * product) * scaling
        divisor = jnp.maximum(jnp.abs(denominator), jnp.exp(-(cumulated + highest)))
        inverse = scaling / divisor
        out_ref[here, :] = jnp.where(
            lane_iota((tile, LANES)) < heads, local * inverse, pltpu.roll(carried * inverse, heads, 1)
        )


def factors(order, columns, top_row, sums, products, heads, dqk):
    return call(
        order,
        functools.partial(factors_kernel, heads=heads, dqk=dqk),
        [columns, top_row, sums, products],
        [pltpu.VMEM(columns.shape, jnp.float32)],
        "factors",
    )[0]


def finish_kernel(queries_ref, factors_ref, *refs, items, heads):
    arrays = refs[: 2 * len(items)]
    *_, out_hbm, token_ref, scratch, sems = refs
    token_ref[...] = jnp.zeros_like(token_ref)
    side, _ = position()
    tokens = queries_ref.shape[0]
    dqk = queries_ref.shape[1] // heads
    tile = min(256, tokens)
    copies = []
    for place, (index, column) in enumerate(items):
        held_ref, memory_ref = arrays[2 * place : 2 * place + 2]
        dv, width = held_ref.shape[1], memory_ref.shape[1]
        head = head_at(index, heads, side)
        memory = memory_ref[...].astype(jnp.bfloat16)
        target = pl.ds(pl.multiple_of(head * dv + column, width), width)
        for begin in range(0, tokens, tile):
            here = pl.ds(begin, tile)
            local = factors_ref[here, index : index + 1]
            carried = factors_ref[here, heads + index : heads + index + 1]
            term = jnp.dot(
                queries_ref[here, columns_of(head, dqk)], memory, preferred_element_type=jnp.float32
            )
            held = held_ref[here, column : column + width].astype(jnp.float32)
            scratch[place, here, :] = (held * local + term * carried).astype(scratch.dtype)
            copy = pltpu.make_async_copy(
                scratch.at[place, here, :], out_hbm.at[here, target], sems.at[len(copies)]
            )
            copy.start()
            copies.append(copy)
    for copy in copies:
        copy.wait()


def finish(order, items, queries, factor, hidden, heads):
    tokens = queries.shape[0]
    dqk = queries.shape[1] // heads
    dv = items[0][2].shape[1]
    width = items[0][3].shape[1]
    operands = [queries, factor]
    for _, _, held, memory in items:
        operands += [held, memory]
    aliases = {}
    if hidden is not None:
        aliases = {len(operands): 0}
        operands.append((hidden, pl.ANY))
    return call(
        order,
        functools.partial(finish_kernel, items=[item[:2] for item in items], heads=heads),
        operands,
        [pltpu.HBM((tokens, heads * dv), jnp.bfloat16), pltpu.VMEM((8, LANES), jnp.float32)],
        "finish",
        mib=12,
        scratch=[
            pltpu.VMEM((len(items), tokens, width), jnp.bfloat16),
            pltpu.SemaphoreType.DMA((len(items) * max(1, tokens // 256),)),
        ],
        aliases=aliases,
        flops=4 * len(items) * tokens * dqk * width,
    )[0]


def entry_of(table_ref):
    return lambda row, lane: table_ref[row : row + 1, lane : lane + 1]


def row_tiles(rows):
    tile = min(32, rows)
    return [pl.ds(begin, tile) for begin in range(0, rows, tile)]


def chain_kernel(table_ref, *refs, step, views, earlier):
    out_ref = refs[-1]
    half = out_ref.shape[1]
    entry = entry_of(table_ref)
    terms = [(0, 0, entry(ROW_A, step))] if earlier else []
    terms += [(place, column, entry(row, step)) for place, column, row in views]
    for here in row_tiles(out_ref.shape[0]):
        total = None
        for place, column, weight in terms:
            term = refs[place][here, column : column + half] * weight
            total = term if total is None else total + term
        out_ref[here, :] = total


def chain_step(order, table, step, kept, received, earlier, levels, half):
    operands = Operands()
    if earlier is not None:
        operands.place(earlier)
    views = []
    for z in range(levels - 1):
        chunk = step - z
        if 0 <= chunk < len(kept):
            views.append((*operands.view(kept[chunk]), ROW_CHAIN + 2 * z))
            views.append((*operands.view(received[chunk]), ROW_CHAIN + 2 * z + 1))
    return call(
        order,
        functools.partial(chain_kernel, step=step, views=views, earlier=earlier is not None),
        [table, *operands.arrays],
        [pltpu.VMEM((kept[0][0].shape[0], half), jnp.float32)],
        "chain",
    )[0]


def prefix_kernel(table_ref, *refs, levels, pieces):
    send_ref, own_ref = refs[-2:]
    half = send_ref.shape[1] // len(pieces)
    entry = entry_of(table_ref)
    here_row = ROW_CHAIN + 2 * levels
    for i, (chunk, arrivals, (keep, keep_column), (take, take_column)) in enumerate(pieces):
        columns = pl.ds(i * half, half)
        picks = [entry(here_row + z, 0) for z in range(1, levels)]
        send_p, send_s = entry(ROW_SEND_P, chunk), entry(ROW_SEND_S, chunk)
        own_p, own_s = entry(ROW_OWN_P, chunk), entry(ROW_OWN_S, chunk)
        for here in row_tiles(send_ref.shape[0]):
            prefix = None
            for place, weight in zip(arrivals, picks):
                term = refs[place][here, :] * weight
                prefix = term if prefix is None else prefix + term
            send_ref[here, columns] = prefix * send_p + refs[keep][here, keep_column : keep_column + half] * send_s
            own_ref[here, columns] = prefix * own_p + refs[take][here, take_column : take_column + half] * own_s


def prefixes(order, table, chunks, arrived, kept, received, levels, half):
    operands = Operands()
    pieces = []
    for chunk in chunks:
        arrivals = [operands.place(arrived[chunk + z - 1]) for z in range(1, levels)]
        pieces.append((chunk, arrivals, operands.view(kept[chunk]), operands.view(received[chunk])))
    out = pltpu.VMEM((kept[0][0].shape[0], len(chunks) * half), jnp.float32)
    return call(
        order,
        functools.partial(prefix_kernel, levels=levels, pieces=pieces),
        [table, *operands.arrays],
        [out, out],
        "prefix",
    )


def down_kernel(table_ref, *refs, step, levels, views, earlier):
    out_ref = refs[-1]
    _, rows, half = out_ref.shape
    _, level = position()
    target = jnp.maximum(step - levels + level, 0)
    here = pl.ds(pl.multiple_of(target * rows, rows), rows)
    entry = entry_of(table_ref)
    for c, ((keep, keep_column), (take, take_column)) in enumerate(views):
        value = refs[keep][here, keep_column : keep_column + half] * entry(ROW_FIN_K, c)
        value = value + refs[take][here, take_column : take_column + half] * entry(ROW_FIN_R, c)
        out_ref[c] = value if earlier is None else value + refs[earlier][c]


def down(order, table, step, levels, kept, received, earlier, rows, half):
    operands = Operands()
    views = [(operands.view(keep), operands.view(take)) for keep, take in zip(kept, received)]
    place = None if earlier is None else operands.place(earlier)
    return call(
        order,
        functools.partial(down_kernel, step=step, levels=levels, views=views, earlier=place),
        [table, *operands.arrays],
        [pltpu.VMEM((len(kept), rows, half), jnp.float32)],
        "down",
    )[0]


def final_kernel(table_ref, *refs, views, own_views):
    above_ref, keep_out, send_out = refs[-3:]
    _, rows, half = above_ref.shape
    side, level = position()
    here = pl.ds(pl.multiple_of(level * rows, rows), rows)
    entry = entry_of(table_ref)
    share = rows // 2
    for c, ((keep, keep_column), (take, take_column)) in enumerate(views):
        own, send, column = own_views[c]
        prefix = jnp.where(
            side == 0, refs[own][here, column : column + half], refs[send][here, column : column + half]
        )
        value = (
            prefix * entry(ROW_FIN_P, c)
            + refs[keep][here, keep_column : keep_column + half] * entry(ROW_FIN_K, c)
            + refs[take][here, take_column : take_column + half] * entry(ROW_FIN_R, c)
            + above_ref[c]
        )
        low, high = value[:share], value[share:]
        columns = pl.ds((c % 2) * half, half)
        keep_out[c // 2, :, columns] = jnp.where(side == 0, low, high)
        send_out[c // 2, :, columns] = jnp.where(side == 0, high, low)


def final_rows(order, table, kept, received, owns, sends, above):
    operands = Operands()
    views = [(operands.view(keep), operands.view(take)) for keep, take in zip(kept, received)]
    own_views = [
        (operands.place(own[0]), operands.place(sent[0]), own[1]) for own, sent in zip(owns, sends)
    ]
    chunks, rows, half = above.shape
    out = pltpu.VMEM((chunks // 2, rows // 2, 2 * half), jnp.float32)
    return call(
        order,
        functools.partial(final_kernel, views=views, own_views=own_views),
        [table, *operands.arrays, above],
        [out, out],
        "final_rows",
    )


def shards(queries, keys, values, input_gate, forget_gate, *, blocks):
    heads = input_gate.shape[0]
    dqk, dv = queries.shape[1] // heads, values.shape[1] // heads
    half = dv // 2
    lane_heads = heads // 2
    levels = blocks // 2
    chunks = 2 * lane_heads
    place = lax.axis_index(AXIS)
    side = lax.rem(place, 2)
    across = [(i, i ^ 1) for i in range(blocks)]
    up = [(i, i + 2) for i in range(blocks - 2)]
    downward = [(i + 2, i) for i in range(blocks - 2)]
    send = lambda value, pairs: lax.ppermute(value, AXIS, pairs)
    order = Order()

    def views_of(arrays):
        return [(array, column) for array in arrays for column in range(0, array.shape[1], half)]

    keys, rows, columns, summary, *away = start(order, input_gate, forget_gate, keys, values)
    gathered = summary[None]
    received = [send(a, across) for a in away]
    values, (first_away, first_kept) = load(order, keys, columns, values, [lane_heads + 1, 0], heads)
    received.append(send(first_away, across))
    queries, away = memories(
        order, keys, columns, values, queries, range(lane_heads + 2, heads), heads
    )
    received = views_of([*received, *[send(a, across) for a in away]])

    while gathered.shape[0] < blocks:
        reach = gathered.shape[0]
        more = send(gathered, [(i, (i - reach) % blocks) for i in range(blocks)])
        gathered = jnp.concatenate([gathered, more], axis=0)[:blocks]
    table, parts, top_row = weights(order, gathered)

    steps = chunks + levels - 2
    arrived, kept = [], views_of([first_kept])
    attended, state = [], []
    sends, owns, others = [], [], []
    hidden = factor = above = None
    final_normal = tops = None

    def attend(count):
        nonlocal state
        for _ in range(count):
            if len(attended) < heads:
                result, *state = attention(
                    order, len(attended), queries, keys, values, rows, columns, parts, state
                )
                attended.append(result)

    def exchange():
        done = sum(a.shape[1] for a in owns) // half
        whole = done < chunks - 2
        group = list(range(done, done + (2 if whole else 1)))
        if done < chunks and group[-1] + levels - 2 < len(arrived):
            to_send, own = prefixes(order, table, group, arrived, kept, received, levels, half)
            sends.append(to_send)
            owns.append(own)
            others.append(send(to_send, across))

    def item(memories, base, c):
        head = base + min(c, lane_heads - 1)
        return head, (c // lane_heads) * half, attended[head], memories[c]

    def put(*items):
        nonlocal hidden
        hidden = finish(order, items, queries, factor, hidden, heads)

    finished = [0, 0]

    def put_next(which):
        memories, base = ((owns, 0), (others, lane_heads))[which]
        if finished[which] < min(len(memories), lane_heads - 1):
            put(item(memories, base, finished[which]))
            finished[which] += 1

    downs = 0
    for step in range(steps):
        earlier = arrived[step - 1] if step else None
        arrived.append(
            send(chain_step(order, table, step, kept, received, earlier, levels, half), up)
        )
        if step == 0 and lane_heads > 1:
            kept += views_of(own_memories(order, keys, columns, values, range(1, lane_heads), heads))
            attend(1)
            continue
        attend(2)
        if step == 2:
            final_normal, tops = finals(order, gathered)
        if len(attended) == heads and factor is None:
            factor = factors(order, columns, top_row, *state, heads, dqk)
        if step >= 4:
            arrived_now = arrived.pop()
            exchange()
            arrived.append(arrived_now)
        if step >= 5 and step % 2 == 1 and downs < levels - 1:
            downs += 1
            above = send(
                down(order, table, downs, levels, kept, received, above, dqk // levels, half), downward
            )
        if factor is not None:
            put_next(0)
            if step >= 7:
                put_next(1)
    attend(heads)
    if final_normal is None:
        final_normal, tops = finals(order, gathered)
    if factor is None:
        factor = factors(order, columns, top_row, *state, heads, dqk)
    while sum(a.shape[1] for a in owns) < chunks * half:
        exchange()
    while downs < levels - 1:
        downs += 1
        above = send(
            down(order, table, downs, levels, kept, received, above, dqk // levels, half), downward
        )
    keep_rows, send_rows = final_rows(
        order, table, kept, received, views_of(owns), views_of(sends), above
    )
    other_rows = send(send_rows, across)
    while finished[0] < lane_heads - 1:
        put_next(0)
    put(*[item(owns, 0, c) for c in range(lane_heads - 1, len(owns))])
    while finished[1] < lane_heads - 1:
        put_next(1)
    for c in range(lane_heads - 1, len(others)):
        put(item(others, lane_heads, c))

    final_memory = jnp.where(
        side == 0,
        jnp.concatenate([keep_rows, other_rows], axis=0),
        jnp.concatenate([other_rows, keep_rows], axis=0),
    )
    share = dqk // blocks
    final_normalizer = lax.dynamic_slice_in_dim(final_normal, place * share, share, 1)
    return hidden, final_memory, final_normalizer, tops[:, 0]


def solution(mesh):
    token_spec = P(("seq", "ctx"), None)
    gate_spec = P(None, ("seq", "ctx"))
    return jax.shard_map(
        functools.partial(shards, blocks=mesh.shape["ctx"]),
        mesh=mesh,
        in_specs=(token_spec, token_spec, token_spec, gate_spec, gate_spec),
        out_specs=(token_spec, P("seq", "ctx", None), P("seq", "ctx"), P("seq")),
        check_vma=False,
    )
```

time: 953 us -> 142 us (0.15)
  waiting for transfers between devices: 558 us -> 13.8 us
  blocking collectives: 177 us -> 0 us
  matrix products: 97.5 us -> 0 us
  starting transfers between devices: 0.12 us -> 64.7 us
  Pallas kernels: 0 us -> 54.4 us
  other arithmetic: 46.1 us -> 0.86 us
  loops' own time: 26.5 us -> 0 us
  local copies, waits for them, and re-layouts: 29.9 us -> 5.79 us
  between operations: 14.5 us -> 1.57 us
    all_gather x1 -> x0, waiting for transfers between devices: 530 us -> none  [prefix_2(): gathered = jax.tree.map(lambda a: lax.all_gather(a, axis), part)]
    dot_general x32 -> x0, matrix products: 97.5 us -> none  [the longest x8 28.5 us: block_one_head(): lax.dot_general(query_rows, key_rows, (((1,), (1,)), ((), ())), preferred...]
    pmax x1 -> x0, blocking collectives: 67.1 us -> none  [shards(): final_stabilizer = lax.pmax(end_stab, 'ctx')]
    unnamed x1 -> x0, blocking collectives: 65 us -> none
    ppermute x0 -> x27, starting transfers between devices: none -> 64.7 us  [shards(): send = lambda value, pairs: lax.ppermute(value, AXIS, pairs)]
    pallas_call x0 -> x43, Pallas kernels: none -> 54.4 us  [call(): pl.pallas_call(body, in_specs=in_specs, out_specs=out_specs, out_shape=li...]
    all_gather x1 -> x0, blocking collectives: 44.6 us -> none  [prefix_2(): gathered = jax.tree.map(lambda a: lax.all_gather(a, axis), part)]
    reduce_scatter x1 -> x0, waiting for transfers between devices: 27.8 us -> none  [shards(): lax.psum_scatter(matrix_memory * rescale[:, None, None], 'ctx', scatter_d...]
  transfers between devices with their start and end apart: 3 -> 27, of which waited for: 2 -> 8; matrix products, arithmetic and copies ran while one was open for 13% -> 1% of each run, Pallas kernels for 0% -> 36%
where the time goes in v2:
time: 142 us; the launch traced here: 141 us
  starting transfers between devices  64.7 us (46%)
  Pallas kernels  54.4 us (38%)
  waiting for transfers between devices  13.8 us (10%)
  local copies, waits for them, and re-layouts  5.79 us (4%)
  between operations  1.57 us (1%)
    ppermute x27, starting transfers between devices, shards(): send = lambda value, pairs: lax.ppermute(value, AXIS, pairs)  64.7 us
    pallas_call x43, Pallas kernels, call(): pl.pallas_call(body, in_specs=in_specs, out_specs=out_specs, out_shape=li...  54.4 us
    ppermute x27, waiting for transfers between devices, shards(): send = lambda value, pairs: lax.ppermute(value, AXIS, pairs)  13.8 us
    unnamed x66, local copies, waits for them, and re-layouts  4.5 us
  transfers between devices with their start and end apart: 27, of which 8 were waited for; matrix products, arithmetic and copies ran while one was open for 1% of the time, Pallas kernels for 36%

profile of v2, /device:TPU:0, one launch (start us, length us, event | category | flops | bytes accessed | tf_op | source)
XLA Modules:
  0.0 141.1 jit_solution(16884772563140610523)
XLA Ops:
  0.6 4.1 %start.1 = (bf16[1024,2048]{1,0:T(8,128)(2,1)S(1)}, f32[8,1024]{1,0:T(8,128)S(1)}, f32[1024,128]{1,0:T(8,128)S(1)}, f32[8,384]{1,0:T(8,128)S(1)}, f32[256,256]{1,0:T(8,128)S(1)}, /*index=5*/f32[256,256]{1,0:T(8,128)S(1)}) custom-call(f32[8,1024]{1,0:T(8,128)} %refs_0_.1, f32[8,1024]{1,0:T(8,128)} %refs_1_.1, bf16[1024,2048]{1,0:T(8,128)(2,1)} %refs_2_.2, ...), custom_call_target="tpu_custom_call" | custom-call | flops 4000000000 | bytes 8000000 | tf_op jit(solution)/shard_map/start/pallas_call | solution.py:39
  4.7 6.1 %collective-permute-start = (f32[1,8,384]{2,1,0:T(8,128)S(1)}, f32[1,8,384]{2,1,0:T(8,128)S(1)}, u32[]{:S(2)}, u32[]{:S(2)}) collective-permute-start(f32[1,8,384]{2,1,0:T(8,128)S(1)} %bitcast.1), channel_id=1, source_target_pairs={{0,28},{4,0},{8,4},{12,8},{16,12},{20,16},{24,20},{28,24},{1,29},{... | collective-permute-start | bytes 36872 | tf_op jit(solution)/shard_map/ppermute | solution.py:747
  10.8 2.0 %collective-permute-start.5 = (f32[256,256]{1,0:T(8,128)S(1)}, f32[256,256]{1,0:T(8,128)S(1)}, u32[]{:S(2)}, u32[]{:S(2)}) collective-permute-start(f32[256,256]{1,0:T(8,128)S(1)} %get-tuple-element.79.refs_3_), channel_id=1, source_target_pairs={{0,4},{4,0},{8,12},{12,8},{16,20},{20,16},{24,28},{28,24},{1,5},{5... | collective-permute-start | bytes 786440 | tf_op jit(solution)/shard_map/ppermute | solution.py:747
  12.8 0.8 collective-permute-start.1
  13.6 3.5 %memories_away.1 = (bf16[1024,4096]{1,0:T(8,128)(2,1)S(1)}, f32[256,512]{1,0:T(8,128)S(1)}, f32[256,512]{1,0:T(8,128)S(1)}) custom-call(bf16[1024,2048]{1,0:T(8,128)(2,1)S(1)} %get-tuple-element.77.refs_0_.refs_1_, f32[1024,128]{1,0:T(8,128)S(1)} %get-tuple-element.78.refs_1_.refs_4_.refs_0_, bf16[1024,4096]{1,0:T(8,128)(2,1)} %refs_2_.3, ...), custom_call_target="tpu_custom_call" | custom-call | flops 1073741824 | bytes 8000000 | tf_op jit(solution)/shard_map/memories_away/pallas_call | solution.py:39
  17.2 4.3 %collective-permute-start.7 = (f32[256,512]{1,0:T(8,128)S(1)}, f32[256,512]{1,0:T(8,128)S(1)}, u32[]{:S(2)}, u32[]{:S(2)}) collective-permute-start(f32[256,512]{1,0:T(8,128)S(1)} %get-tuple-element.98), channel_id=1, source_target_pairs={{0,4},{4,0},{8,12},{12,8},{16,20},{20,16},{24,28},{28,24},{1,5},{5... | collective-permute-start | bytes 1572872 | tf_op jit(solution)/shard_map/ppermute | solution.py:747
  21.5 3.3 %memories_more.1 = (bf16[1024,2048]{1,0:T(8,128)(2,1)S(1)}, f32[256,512]{1,0:T(8,128)S(1)}, f32[256,512]{1,0:T(8,128)S(1)}) custom-call(bf16[1024,2048]{1,0:T(8,128)(2,1)S(1)} %get-tuple-element.77.refs_0_.refs_1_, f32[1024,128]{1,0:T(8,128)S(1)} %get-tuple-element.78.refs_1_.refs_4_.refs_0_, bf16[1024,4096]{1,0:T(8,128)(2,1)S(1)} %get-tuple-element.80.refs_2_, ...), custom_call_target="tpu_custom_call" | custom-call | flops 1073741824 | bytes 4000000 | tf_op jit(solution)/shard_map/memories_more/pallas_call | solution.py:39
  24.9 1.6 %collective-permute-done.2 = f32[4,8,384]{2,1,0:T(8,128)S(1)} collective-permute-done((f32[4,8,384]{2,1,0:T(8,128)S(1)}, f32[4,8,384]{2,1,0:T(8,128)S(1)}, u32[]{:S(2)}, u32[]{:S(2)}) %collective-permute-start.2) | collective-permute-done | bytes 49184 | tf_op jit(solution)/shard_map/ppermute | solution.py:747
  26.5 0.4 collective-permute-start.13
  26.9 0.5 weights.1
  27.5 2.5 %collective-permute-start.4 = (f32[256,256]{1,0:T(8,128)S(1)}, f32[256,256]{1,0:T(8,128)S(1)}, u32[]{:S(2)}, u32[]{:S(2)}) collective-permute-start(f32[256,256]{1,0:T(8,128)S(1)} %chain.10.refs_3_), channel_id=1, source_target_pairs={{0,8},{4,12},{8,16},{12,20},{16,24},{20,28},{1,9},{5,13},{9,17},{1... | collective-permute-start | bytes 786440 | tf_op jit(solution)/shard_map/ppermute | solution.py:747
  30.0 1.7 %memories_own.1 = (f32[256,512]{1,0:T(8,128)S(1)}, f32[256,512]{1,0:T(8,128)S(1)}, f32[256,512]{1,0:T(8,128)S(1)}) custom-call(bf16[1024,2048]{1,0:T(8,128)(2,1)S(1)} %get-tuple-element.77.refs_0_.refs_1_, f32[1024,128]{1,0:T(8,128)S(1)} %get-tuple-element.78.refs_1_.refs_4_.refs_0_, bf16[1024,4096]{1,0:T(8,128)(2,1)S(1)} %get-tuple-element.80.refs_2_, ...), custom_call_target="tpu_custom_call" | custom-call | flops 1610612736 | bytes 4000000 | tf_op jit(solution)/shard_map/memories_own/pallas_call | solution.py:39
  31.7 2.1 %attention.8 = (bf16[1024,512]{1,0:T(8,128)(2,1)S(1)}, f32[1024,128]{1,0:T(8,128)S(1)}, f32[1024,128]{1,0:T(8,128)S(1)}) custom-call(bf16[1024,2048]{1,0:T(8,128)(2,1)S(1)} %get-tuple-element.82.refs_0_, bf16[1024,2048]{1,0:T(8,128)(2,1)S(1)} %get-tuple-element.77.refs_0_.refs_1_, bf16[1024,4096]{1,0:T(8,128)(2,1)S(1)} %get-tuple-element.80.refs_2_, ...), custom_call_target="tpu_custom_call" | custom-call | flops 2415919104 | bytes 1000000 | tf_op jit(solution)/shard_map/attention/pallas_call | solution.py:39
  34.1 4.8 %collective-permute-start.6 = (f32[256,256]{1,0:T(8,128)S(1)}, f32[256,256]{1,0:T(8,128)S(1)}, u32[]{:S(2)}, u32[]{:S(2)}) collective-permute-start(f32[256,256]{1,0:T(8,128)S(1)} %chain.11.refs_8_), channel_id=1, source_target_pairs={{0,8},{4,12},{8,16},{12,20},{16,24},{20,28},{1,9},{5,13},{9,17},{1... | collective-permute-start | bytes 786440 | tf_op jit(solution)/shard_map/ppermute | solution.py:747
  38.9 2.1 %attention.9 = (bf16[1024,512]{1,0:T(8,128)(2,1)S(1)}, f32[1024,128]{1,0:T(8,128)S(1)}, f32[1024,128]{1,0:T(8,128)S(1)}) custom-call(bf16[1024,2048]{1,0:T(8,128)(2,1)S(1)} %get-tuple-element.82.refs_0_, bf16[1024,2048]{1,0:T(8,128)(2,1)S(1)} %get-tuple-element.77.refs_0_.refs_1_, bf16[1024,4096]{1,0:T(8,128)(2,1)S(1)} %get-tuple-element.80.refs_2_, ...), custom_call_target="tpu_custom_call" | custom-call | flops 2415919104 | bytes 1000000 | tf_op jit(solution)/shard_map/attention/pallas_call | solution.py:39
  41.0 2.1 %attention.10 = (bf16[1024,512]{1,0:T(8,128)(2,1)S(1)}, f32[1024,128]{1,0:T(8,128)S(1)}, f32[1024,128]{1,0:T(8,128)S(1)}) custom-call(bf16[1024,2048]{1,0:T(8,128)(2,1)S(1)} %get-tuple-element.82.refs_0_, bf16[1024,2048]{1,0:T(8,128)(2,1)S(1)} %get-tuple-element.77.refs_0_.refs_1_, bf16[1024,4096]{1,0:T(8,128)(2,1)S(1)} %get-tuple-element.80.refs_2_, ...), custom_call_target="tpu_custom_call" | custom-call | flops 2415919104 | bytes 1000000 | tf_op jit(solution)/shard_map/attention/pallas_call | solution.py:39
  43.4 4.6 %collective-permute-start.8 = (f32[256,256]{1,0:T(8,128)S(1)}, f32[256,256]{1,0:T(8,128)S(1)}, u32[]{:S(2)}, u32[]{:S(2)}) collective-permute-start(f32[256,256]{1,0:T(8,128)S(1)} %chain.12.refs_8_), channel_id=1, source_target_pairs={{0,8},{4,12},{8,16},{12,20},{16,24},{20,28},{1,9},{5,13},{9,17},{1... | collective-permute-start | bytes 786440 | tf_op jit(solution)/shard_map/ppermute | solution.py:747
  48.0 2.1 %attention.11 = (bf16[1024,512]{1,0:T(8,128)(2,1)S(1)}, f32[1024,128]{1,0:T(8,128)S(1)}, f32[1024,128]{1,0:T(8,128)S(1)}) custom-call(bf16[1024,2048]{1,0:T(8,128)(2,1)S(1)} %get-tuple-element.82.refs_0_, bf16[1024,2048]{1,0:T(8,128)(2,1)S(1)} %get-tuple-element.77.refs_0_.refs_1_, bf16[1024,4096]{1,0:T(8,128)(2,1)S(1)} %get-tuple-element.80.refs_2_, ...), custom_call_target="tpu_custom_call" | custom-call | flops 2415919104 | bytes 1000000 | tf_op jit(solution)/shard_map/attention/pallas_call | solution.py:39
  50.1 1.0 copy-done.19
  51.1 2.1 %attention.12 = (bf16[1024,512]{1,0:T(8,128)(2,1)S(1)}, f32[1024,128]{1,0:T(8,128)S(1)}, f32[1024,128]{1,0:T(8,128)S(1)}) custom-call(bf16[1024,2048]{1,0:T(8,128)(2,1)S(1)} %get-tuple-element.82.refs_0_, bf16[1024,2048]{1,0:T(8,128)(2,1)S(1)} %get-tuple-element.77.refs_0_.refs_1_, bf16[1024,4096]{1,0:T(8,128)(2,1)S(1)} %get-tuple-element.80.refs_2_, ...), custom_call_target="tpu_custom_call" | custom-call | flops 2415919104 | bytes 1000000 | tf_op jit(solution)/shard_map/attention/pallas_call | solution.py:39
  53.7 4.0 %collective-permute-start.9 = (f32[256,256]{1,0:T(8,128)S(1)}, f32[256,256]{1,0:T(8,128)S(1)}, u32[]{:S(2)}, u32[]{:S(2)}) collective-permute-start(f32[256,256]{1,0:T(8,128)S(1)} %chain.13.refs_8_), channel_id=1, source_target_pairs={{0,8},{4,12},{8,16},{12,20},{16,24},{20,28},{1,9},{5,13},{9,17},{1... | collective-permute-start | bytes 786440 | tf_op jit(solution)/shard_map/ppermute | solution.py:747
  57.7 2.1 %attention.13 = (bf16[1024,512]{1,0:T(8,128)(2,1)S(1)}, f32[1024,128]{1,0:T(8,128)S(1)}, f32[1024,128]{1,0:T(8,128)S(1)}) custom-call(bf16[1024,2048]{1,0:T(8,128)(2,1)S(1)} %get-tuple-element.82.refs_0_, bf16[1024,2048]{1,0:T(8,128)(2,1)S(1)} %get-tuple-element.77.refs_0_.refs_1_, bf16[1024,4096]{1,0:T(8,128)(2,1)S(1)} %get-tuple-element.80.refs_2_, ...), custom_call_target="tpu_custom_call" | custom-call | flops 2415919104 | bytes 1000000 | tf_op jit(solution)/shard_map/attention/pallas_call | solution.py:39
  59.8 2.1 %attention.14 = (bf16[1024,512]{1,0:T(8,128)(2,1)S(1)}, f32[1024,128]{1,0:T(8,128)S(1)}, f32[1024,128]{1,0:T(8,128)S(1)}) custom-call(bf16[1024,2048]{1,0:T(8,128)(2,1)S(1)} %get-tuple-element.82.refs_0_, bf16[1024,2048]{1,0:T(8,128)(2,1)S(1)} %get-tuple-element.77.refs_0_.refs_1_, bf16[1024,4096]{1,0:T(8,128)(2,1)S(1)} %get-tuple-element.80.refs_2_, ...), custom_call_target="tpu_custom_call" | custom-call | flops 2415919104 | bytes 1000000 | tf_op jit(solution)/shard_map/attention/pallas_call | solution.py:39
  62.0 0.7 collective-permute-done.9.refs_1_.refs_6_.refs_2_
  62.9 4.4 %collective-permute-start.11 = (f32[256,256]{1,0:T(8,128)S(1)}, f32[256,256]{1,0:T(8,128)S(1)}, u32[]{:S(2)}, u32[]{:S(2)}) collective-permute-start(f32[256,256]{1,0:T(8,128)S(1)} %chain.14.refs_8_), channel_id=1, source_target_pairs={{0,8},{4,12},{8,16},{12,20},{16,24},{20,28},{1,9},{5,13},{9,17},{1... | collective-permute-start | bytes 786440 | tf_op jit(solution)/shard_map/ppermute | solution.py:747
  67.3 2.1 %attention.15 = (bf16[1024,512]{1,0:T(8,128)(2,1)S(1)}, f32[1024,128]{1,0:T(8,128)S(1)}, f32[1024,128]{1,0:T(8,128)S(1)}) custom-call(bf16[1024,2048]{1,0:T(8,128)(2,1)S(1)} %get-tuple-element.82.refs_0_, bf16[1024,2048]{1,0:T(8,128)(2,1)S(1)} %get-tuple-element.77.refs_0_.refs_1_, bf16[1024,4096]{1,0:T(8,128)(2,1)S(1)} %get-tuple-element.80.refs_2_, ...), custom_call_target="tpu_custom_call" | custom-call | flops 2415919104 | bytes 1000000 | tf_op jit(solution)/shard_map/attention/pallas_call | solution.py:39
  69.4 1.0 factors.1.refs_8_.refs_1_
  70.8 1.4 finish.9
  72.1 1.3 collective-permute-done.11.refs_1_.refs_3_
  73.6 4.4 %collective-permute-start.12 = (f32[256,256]{1,0:T(8,128)S(1)}, f32[256,256]{1,0:T(8,128)S(1)}, u32[]{:S(2)}, u32[]{:S(2)}) collective-permute-start(f32[256,256]{1,0:T(8,128)S(1)} %chain.15.refs_10_), channel_id=1, source_target_pairs={{0,8},{4,12},{8,16},{12,20},{16,24},{20,28},{1,9},{5,13},{9,17},{1... | collective-permute-start | bytes 786440 | tf_op jit(solution)/shard_map/ppermute | solution.py:747
  78.3 1.3 collective-permute-start.17
  79.6 4.5 %collective-permute-done.12.refs_1_.refs_6_.refs_2_ = f32[256,256]{1,0:T(8,128)S(1)} collective-permute-done((f32[256,256]{1,0:T(8,128)S(1)}, f32[256,256]{1,0:T(8,128)S(1)}, u32[]{:S(2)}, u32[]{:S(2)}) %collective-permute-start.12) | collective-permute-done | bytes 262176 | tf_op jit(solution)/shard_map/ppermute | solution.py:747
  84.4 4.6 %collective-permute-start.14 = (f32[256,256]{1,0:T(8,128)S(1)}, f32[256,256]{1,0:T(8,128)S(1)}, u32[]{:S(2)}, u32[]{:S(2)}) collective-permute-start(f32[256,256]{1,0:T(8,128)S(1)} %chain.16.refs_7_), channel_id=1, source_target_pairs={{0,8},{4,12},{8,16},{12,20},{16,24},{20,28},{1,9},{5,13},{9,17},{1... | collective-permute-start | bytes 786440 | tf_op jit(solution)/shard_map/ppermute | solution.py:747
  89.5 1.4 finish.10
  90.9 3.2 %collective-permute-done.14.refs_1_.refs_3_ = f32[256,256]{1,0:T(8,128)S(1)} collective-permute-done((f32[256,256]{1,0:T(8,128)S(1)}, f32[256,256]{1,0:T(8,128)S(1)}, u32[]{:S(2)}, u32[]{:S(2)}) %collective-permute-start.14) | collective-permute-done | bytes 262176 | tf_op jit(solution)/shard_map/ppermute | solution.py:747
  94.3 4.4 %collective-permute-start.15 = (f32[256,256]{1,0:T(8,128)S(1)}, f32[256,256]{1,0:T(8,128)S(1)}, u32[]{:S(2)}, u32[]{:S(2)}) collective-permute-start(f32[256,256]{1,0:T(8,128)S(1)} %chain.17.refs_11_), channel_id=1, source_target_pairs={{0,8},{4,12},{8,16},{12,20},{16,24},{20,28},{1,9},{5,13},{9,17},{1... | collective-permute-start | bytes 786440 | tf_op jit(solution)/shard_map/ppermute | solution.py:747
  98.9 1.3 collective-permute-start.22
  100.2 1.3 finish.11
  101.6 1.4 %collective-permute-done.15.refs_1_.refs_6_.refs_2_ = f32[256,256]{1,0:T(8,128)S(1)} collective-permute-done((f32[256,256]{1,0:T(8,128)S(1)}, f32[256,256]{1,0:T(8,128)S(1)}, u32[]{:S(2)}, u32[]{:S(2)}) %collective-permute-start.15) | collective-permute-done | bytes 262176 | tf_op jit(solution)/shard_map/ppermute | solution.py:747
  103.2 4.4 %collective-permute-start.18 = (f32[256,256]{1,0:T(8,128)S(1)}, f32[256,256]{1,0:T(8,128)S(1)}, u32[]{:S(2)}, u32[]{:S(2)}) collective-permute-start(f32[256,256]{1,0:T(8,128)S(1)} %chain.18.refs_7_), channel_id=1, source_target_pairs={{0,8},{4,12},{8,16},{12,20},{16,24},{20,28},{1,9},{5,13},{9,17},{1... | collective-permute-start | bytes 786440 | tf_op jit(solution)/shard_map/ppermute | solution.py:747
  107.6 1.0 prefix.7
  108.7 0.4 collective-permute-start.21
  109.1 1.3 finish.12
  110.5 1.3 finish.13
  111.8 0.7 collective-permute-done.18.refs_1_.refs_3_.refs_2_
  112.6 0.9 chain.19.refs_6_
  113.4 1.1 prefix.8
  114.6 1.0 down.5.refs_5_
  115.6 1.3 collective-permute-start.25
  116.9 5.7 %collective-permute-start.20 = (f32[256,256]{1,0:T(8,128)}, f32[256,256]{1,0:T(8,128)}, u32[]{:S(2)}, u32[]{:S(2)}) collective-permute-start(f32[256,256]{1,0:T(8,128)} %chain.19.refs_6_), channel_id=1, source_target_pairs={{0,8},{4,12},{8,16},{12,20},{16,24},{20,28},{1,9},{5,13},{9,17},{1... | collective-permute-start | bytes 786440 | tf_op jit(solution)/shard_map/ppermute | solution.py:747
  122.6 0.4 collective-permute-start.24
  123.1 2.2 %copy-done.1 = bf16[1024,2048]{1,0:T(8,128)(2,1)S(1)} copy-done((bf16[1024,2048]{1,0:T(8,128)(2,1)S(1)}, bf16[1024,2048]{1,0:T(8,128)(2,1)}, u32[]{:S(2)}) %copy-start.1) | copy-done | bytes 4194328
  125.3 1.2 copy-done.26
  126.6 2.7 %finish.14 = (bf16[1024,4096]{1,0:T(8,128)(2,1)}, f32[8,128]{1,0:T(8,128)S(1)}) custom-call(bf16[1024,2048]{1,0:T(8,128)(2,1)S(1)} %copy-done.1, f32[1024,128]{1,0:T(8,128)S(1)} %factors.1.refs_8_.refs_1_, bf16[1024,512]{1,0:T(8,128)(2,1)S(1)} %copy-done.26, f32[256,512]{1,0:T(8,128)} %collective-permute-done.21.refs_3_, ...), custom_call_target="tpu_custom_call", output_to_operand_aliasing={{0}: (4, {})} | custom-call | flops 536870912 | bytes 1000000 | tf_op jit(solution)/shard_map/finish/pallas_call | solution.py:39
  129.3 1.3 prefix.9
  130.6 1.7 %collective-permute-start.23 = (f32[256,256]{1,0:T(8,128)S(1)}, f32[256,256]{1,0:T(8,128)S(1)}, u32[]{:S(2)}, u32[]{:S(2)}) collective-permute-start(f32[256,256]{1,0:T(8,128)S(1)} %get-tuple-element.137.refs_19_), channel_id=1, source_target_pairs={{0,4},{4,0},{8,12},{12,8},{16,20},{20,16},{24,28},{28,24},{1,5},{5... | collective-permute-start | bytes 786440 | tf_op jit(solution)/shard_map/ppermute | solution.py:747
  132.4 1.5 %final_rows.1 = (f32[4,32,512]{2,1,0:T(8,128)S(1)}, f32[4,32,512]{2,1,0:T(8,128)S(1)}) custom-call(f32[24,128]{1,0:T(8,128)S(1)} %get-tuple-element.88.refs_0_, f32[256,512]{1,0:T(8,128)S(1)} %get-tuple-element.81.refs_4_.refs_1_.refs_2_, f32[256,256]{1,0:T(8,128)S(1)} %copy-done.8, f32[256,256]{1,0:T(8,128)S(1)} %collective-permute-done.5.refs_3_.refs_5_.refs_7_, ...), custom_call_target="tpu_custom_call" | custom-call | flops 1000000 | bytes 1000000 | tf_op jit(solution)/shard_map/final_rows/pallas_call | solution.py:39
  133.9 0.5 collective-permute-start.26
  134.3 0.7 constant_dynamic-slice_fusion
  135.0 0.6 slice_reduce_fusion
  135.6 1.5 %finish.15 = (bf16[1024,4096]{1,0:T(8,128)(2,1)}, f32[8,128]{1,0:T(8,128)S(1)}) custom-call(bf16[1024,2048]{1,0:T(8,128)(2,1)S(1)} %copy-done.2, f32[1024,128]{1,0:T(8,128)S(1)} %factors.1.refs_8_.refs_1_, bf16[1024,512]{1,0:T(8,128)(2,1)S(1)} %copy-done.20, f32[256,256]{1,0:T(8,128)S(1)} %copy-done.22, ...), custom_call_target="tpu_custom_call", output_to_operand_aliasing={{0}: (6, {})} | custom-call | flops 536870912 | bytes 1000000 | tf_op jit(solution)/shard_map/finish/pallas_call | solution.py:39
  137.1 1.1 finish.16
  138.2 1.7 %finish.17 = (bf16[1024,4096]{1,0:T(8,128)(2,1)}, f32[8,128]{1,0:T(8,128)}) custom-call(bf16[1024,2048]{1,0:T(8,128)(2,1)S(1)} %copy-done.2, f32[1024,128]{1,0:T(8,128)S(1)} %factors.1.refs_8_.refs_1_, bf16[1024,512]{1,0:T(8,128)(2,1)S(1)} %copy-done.18, f32[256,256]{1,0:T(8,128)S(1)} %collective-permute-done.23.refs_3_, ...), custom_call_target="tpu_custom_call", output_to_operand_aliasing={{0}: (4, {})} | custom-call | flops 268435456 | bytes 1000000 | tf_op jit(solution)/shard_map/finish/pallas_call | solution.py:39
  140.3 0.8 maximum_select_fusion
  (105 shorter events, 3.9 us)
Async XLA Ops:
  4.7 8.1 %collective-permute-start = (f32[1,8,384]{2,1,0:T(8,128)S(1)}, f32[1,8,384]{2,1,0:T(8,128)S(1)}, u32[]{:S(2)}, u32[]{:S(2)}) collective-permute-start(f32[1,8,384]{2,1,0:T(8,128)S(1)} %bitcast.1), channel_id=1, source_target_pairs={{0,28},{4,0},{8,4},{12,8},{16,12},{20,16},{24,20},{28,24},{1,29},{... | collective-permute-start | bytes 36872 | tf_op jit(solution)/shard_map/ppermute | solution.py:747
  10.8 16.7 %collective-permute-start.3 = (f32[256,256]{1,0:T(8,128)S(1)}, f32[256,256]{1,0:T(8,128)S(1)}, u32[]{:S(2)}, u32[]{:S(2)}) collective-permute-start(f32[256,256]{1,0:T(8,128)S(1)} %get-tuple-element.89), channel_id=1, source_target_pairs={{0,4},{4,0},{8,12},{12,8},{16,20},{20,16},{24,28},{28,24},{1,5},{5... | collective-permute-start | bytes 786440 | tf_op jit(solution)/shard_map/ppermute | solution.py:747
  10.8 23.1 %collective-permute-start.5 = (f32[256,256]{1,0:T(8,128)S(1)}, f32[256,256]{1,0:T(8,128)S(1)}, u32[]{:S(2)}, u32[]{:S(2)}) collective-permute-start(f32[256,256]{1,0:T(8,128)S(1)} %get-tuple-element.79.refs_3_), channel_id=1, source_target_pairs={{0,4},{4,0},{8,12},{12,8},{16,20},{20,16},{24,28},{28,24},{1,5},{5... | collective-permute-start | bytes 786440 | tf_op jit(solution)/shard_map/ppermute | solution.py:747
  12.8 8.6 %collective-permute-start.1 = (f32[2,8,384]{2,1,0:T(8,128)S(1)}, f32[2,8,384]{2,1,0:T(8,128)S(1)}, u32[]{:S(2)}, u32[]{:S(2)}) collective-permute-start(f32[2,8,384]{2,1,0:T(8,128)S(1)} %pad_maximum_fusion.2), channel_id=1, source_target_pairs={{0,24},{4,28},{8,0},{12,4},{16,8},{20,12},{24,16},{28,20},{1,25},{... | collective-permute-start | bytes 73736 | tf_op jit(solution)/shard_map/ppermute | solution.py:747
  17.2 26.0 %collective-permute-start.7 = (f32[256,512]{1,0:T(8,128)S(1)}, f32[256,512]{1,0:T(8,128)S(1)}, u32[]{:S(2)}, u32[]{:S(2)}) collective-permute-start(f32[256,512]{1,0:T(8,128)S(1)} %get-tuple-element.98), channel_id=1, source_target_pairs={{0,4},{4,0},{8,12},{12,8},{16,20},{20,16},{24,28},{28,24},{1,5},{5... | collective-permute-start | bytes 1572872 | tf_op jit(solution)/shard_map/ppermute | solution.py:747
  21.4 5.0 %collective-permute-start.2 = (f32[4,8,384]{2,1,0:T(8,128)S(1)}, f32[4,8,384]{2,1,0:T(8,128)S(1)}, u32[]{:S(2)}, u32[]{:S(2)}) collective-permute-start(f32[4,8,384]{2,1,0:T(8,128)S(1)} %pad_maximum_fusion.1), channel_id=1, source_target_pairs={{0,16},{4,20},{8,24},{12,28},{16,0},{20,4},{24,8},{28,12},{1,17},{... | collective-permute-start | bytes 147464 | tf_op jit(solution)/shard_map/ppermute | solution.py:747
  24.8 85.7 %copy-start = (bf16[1024,2048]{1,0:T(8,128)(2,1)}, bf16[1024,2048]{1,0:T(8,128)(2,1)S(1)}, u32[]{:S(2)}) copy-start(bf16[1024,2048]{1,0:T(8,128)(2,1)S(1)} %get-tuple-element.82.refs_0_) | copy-start | bytes 12582916
  24.8 37.1 %collective-permute-start.10 = (f32[256,512]{1,0:T(8,128)S(1)}, f32[256,512]{1,0:T(8,128)S(1)}, u32[]{:S(2)}, u32[]{:S(2)}) collective-permute-start(f32[256,512]{1,0:T(8,128)S(1)} %get-tuple-element.109), channel_id=1, source_target_pairs={{0,4},{4,0},{8,12},{12,8},{16,20},{20,16},{24,28},{28,24},{1,5},{5... | collective-permute-start | bytes 1572872 | tf_op jit(solution)/shard_map/ppermute | solution.py:747
  26.5 51.6 %collective-permute-start.13 = (f32[256,512]{1,0:T(8,128)S(1)}, f32[256,512]{1,0:T(8,128)S(1)}, u32[]{:S(2)}, u32[]{:S(2)}) collective-permute-start(f32[256,512]{1,0:T(8,128)S(1)} %get-tuple-element.84.refs_1_), channel_id=1, source_target_pairs={{0,4},{4,0},{8,12},{12,8},{16,20},{20,16},{24,28},{28,24},{1,5},{5... | collective-permute-start | bytes 1572872 | tf_op jit(solution)/shard_map/ppermute | solution.py:747
  27.4 87.2 %copy-start.7 = (f32[256,256]{1,0:T(8,128)}, f32[256,256]{1,0:T(8,128)S(1)}, u32[]{:S(2)}) copy-start(f32[256,256]{1,0:T(8,128)S(1)} %collective-permute-done.3.refs_2_.refs_4_.refs_6_.refs_5_) | copy-start | bytes 786436
  27.5 6.4 %collective-permute-start.4 = (f32[256,256]{1,0:T(8,128)S(1)}, f32[256,256]{1,0:T(8,128)S(1)}, u32[]{:S(2)}, u32[]{:S(2)}) collective-permute-start(f32[256,256]{1,0:T(8,128)S(1)} %chain.10.refs_3_), channel_id=1, source_target_pairs={{0,8},{4,12},{8,16},{12,20},{16,24},{20,28},{1,9},{5,13},{9,17},{1... | collective-permute-start | bytes 786440 | tf_op jit(solution)/shard_map/ppermute | solution.py:747
  31.7 82.9 %copy-start.5 = (f32[256,512]{1,0:T(8,128)}, f32[256,512]{1,0:T(8,128)S(1)}, u32[]{:S(2)}) copy-start(f32[256,512]{1,0:T(8,128)S(1)} %get-tuple-element.97.refs_2_.refs_4_) | copy-start | bytes 1572868
  34.1 9.1 %collective-permute-start.6 = (f32[256,256]{1,0:T(8,128)S(1)}, f32[256,256]{1,0:T(8,128)S(1)}, u32[]{:S(2)}, u32[]{:S(2)}) collective-permute-start(f32[256,256]{1,0:T(8,128)S(1)} %chain.11.refs_8_), channel_id=1, source_target_pairs={{0,8},{4,12},{8,16},{12,20},{16,24},{20,28},{1,9},{5,13},{9,17},{1... | collective-permute-start | bytes 786440 | tf_op jit(solution)/shard_map/ppermute | solution.py:747
  43.1 71.5 %copy-start.3 = (f32[256,512]{1,0:T(8,128)}, f32[256,512]{1,0:T(8,128)S(1)}, u32[]{:S(2)}) copy-start(f32[256,512]{1,0:T(8,128)S(1)} %collective-permute-done.7.refs_3_.refs_5_) | copy-start | bytes 1572868
  43.4 10.0 %collective-permute-start.8 = (f32[256,256]{1,0:T(8,128)S(1)}, f32[256,256]{1,0:T(8,128)S(1)}, u32[]{:S(2)}, u32[]{:S(2)}) collective-permute-start(f32[256,256]{1,0:T(8,128)S(1)} %chain.12.refs_8_), channel_id=1, source_target_pairs={{0,8},{4,12},{8,16},{12,20},{16,24},{20,28},{1,9},{5,13},{9,17},{1... | collective-permute-start | bytes 786440 | tf_op jit(solution)/shard_map/ppermute | solution.py:747
  50.1 1.0 copy-start.19
  53.7 8.9 %collective-permute-start.9 = (f32[256,256]{1,0:T(8,128)S(1)}, f32[256,256]{1,0:T(8,128)S(1)}, u32[]{:S(2)}, u32[]{:S(2)}) collective-permute-start(f32[256,256]{1,0:T(8,128)S(1)} %chain.13.refs_8_), channel_id=1, source_target_pairs={{0,8},{4,12},{8,16},{12,20},{16,24},{20,28},{1,9},{5,13},{9,17},{1... | collective-permute-start | bytes 786440 | tf_op jit(solution)/shard_map/ppermute | solution.py:747
  61.9 5.4 %copy-start.25 = (bf16[1024,512]{1,0:T(8,128)(2,1)}, bf16[1024,512]{1,0:T(8,128)(2,1)S(1)}, u32[]{:S(2)}) copy-start(bf16[1024,512]{1,0:T(8,128)(2,1)S(1)} %get-tuple-element.132.refs_2_) | copy-start | bytes 3145732
  62.9 10.5 %collective-permute-start.11 = (f32[256,256]{1,0:T(8,128)S(1)}, f32[256,256]{1,0:T(8,128)S(1)}, u32[]{:S(2)}, u32[]{:S(2)}) collective-permute-start(f32[256,256]{1,0:T(8,128)S(1)} %chain.14.refs_8_), channel_id=1, source_target_pairs={{0,8},{4,12},{8,16},{12,20},{16,24},{20,28},{1,9},{5,13},{9,17},{1... | collective-permute-start | bytes 786440 | tf_op jit(solution)/shard_map/ppermute | solution.py:747
  69.4 8.8 %copy-start.17 = (bf16[1024,512]{1,0:T(8,128)(2,1)}, bf16[1024,512]{1,0:T(8,128)(2,1)S(1)}, u32[]{:S(2)}) copy-start(bf16[1024,512]{1,0:T(8,128)(2,1)S(1)} %get-tuple-element.112.refs_2_) | copy-start | bytes 3145732
  70.7 13.7 %copy-start.9 = (f32[256,512]{1,0:T(8,128)}, f32[256,512]{1,0:T(8,128)S(1)}, u32[]{:S(2)}) copy-start(f32[256,512]{1,0:T(8,128)S(1)} %get-tuple-element.114.refs_3_.refs_4_.refs_10_) | copy-start | bytes 1572868
  70.7 13.7 %copy-start.27 = (f32[256,512]{1,0:T(8,128)}, f32[256,512]{1,0:T(8,128)S(1)}, u32[]{:S(2)}) copy-start(f32[256,512]{1,0:T(8,128)S(1)} %get-tuple-element.121.refs_11_) | copy-start | bytes 1572868
  73.6 10.5 %collective-permute-start.12 = (f32[256,256]{1,0:T(8,128)S(1)}, f32[256,256]{1,0:T(8,128)S(1)}, u32[]{:S(2)}, u32[]{:S(2)}) collective-permute-start(f32[256,256]{1,0:T(8,128)S(1)} %chain.15.refs_10_), channel_id=1, source_target_pairs={{0,8},{4,12},{8,16},{12,20},{16,24},{20,28},{1,9},{5,13},{9,17},{1... | collective-permute-start | bytes 786440 | tf_op jit(solution)/shard_map/ppermute | solution.py:747
  78.3 20.5 %collective-permute-start.17 = (f32[8,64,256]{2,1,0:T(8,128)S(1)}, f32[8,64,256]{2,1,0:T(8,128)S(1)}, u32[]{:S(2)}, u32[]{:S(2)}) collective-permute-start(f32[8,64,256]{2,1,0:T(8,128)S(1)} %down.3.refs_6_), channel_id=1, source_target_pairs={{8,0},{12,4},{16,8},{20,12},{24,16},{28,20},{9,1},{13,5},{17,9},{2... | collective-permute-start | bytes 1572872 | tf_op jit(solution)/shard_map/ppermute | solution.py:747
  79.6 20.7 %collective-permute-start.16 = (f32[256,512]{1,0:T(8,128)S(1)}, f32[256,512]{1,0:T(8,128)S(1)}, u32[]{:S(2)}, u32[]{:S(2)}) collective-permute-start(f32[256,512]{1,0:T(8,128)S(1)} %get-tuple-element.121.refs_11_), channel_id=1, source_target_pairs={{0,4},{4,0},{8,12},{12,8},{16,20},{20,16},{24,28},{28,24},{1,5},{5... | collective-permute-start | bytes 1572872 | tf_op jit(solution)/shard_map/ppermute | solution.py:747
  84.4 9.7 %collective-permute-start.14 = (f32[256,256]{1,0:T(8,128)S(1)}, f32[256,256]{1,0:T(8,128)S(1)}, u32[]{:S(2)}, u32[]{:S(2)}) collective-permute-start(f32[256,256]{1,0:T(8,128)S(1)} %chain.16.refs_7_), channel_id=1, source_target_pairs={{0,8},{4,12},{8,16},{12,20},{16,24},{20,28},{1,9},{5,13},{9,17},{1... | collective-permute-start | bytes 786440 | tf_op jit(solution)/shard_map/ppermute | solution.py:747
  89.4 5.0 %copy-start.11 = (f32[256,512]{1,0:T(8,128)}, f32[256,512]{1,0:T(8,128)S(1)}, u32[]{:S(2)}) copy-start(f32[256,512]{1,0:T(8,128)S(1)} %get-tuple-element.117.refs_3_.refs_5_.refs_12_) | copy-start | bytes 1572868
  89.4 5.0 %copy-start.29 = (f32[256,512]{1,0:T(8,128)}, f32[256,512]{1,0:T(8,128)S(1)}, u32[]{:S(2)}) copy-start(f32[256,512]{1,0:T(8,128)S(1)} %get-tuple-element.125.refs_13_) | copy-start | bytes 1572868
  89.4 21.1 %collective-permute-start.19 = (f32[256,512]{1,0:T(8,128)S(1)}, f32[256,512]{1,0:T(8,128)S(1)}, u32[]{:S(2)}, u32[]{:S(2)}) collective-permute-start(f32[256,512]{1,0:T(8,128)S(1)} %get-tuple-element.125.refs_13_), channel_id=1, source_target_pairs={{0,4},{4,0},{8,12},{12,8},{16,20},{20,16},{24,28},{28,24},{1,5},{5... | collective-permute-start | bytes 1572872 | tf_op jit(solution)/shard_map/ppermute | solution.py:747
  94.3 8.7 %collective-permute-start.15 = (f32[256,256]{1,0:T(8,128)S(1)}, f32[256,256]{1,0:T(8,128)S(1)}, u32[]{:S(2)}, u32[]{:S(2)}) collective-permute-start(f32[256,256]{1,0:T(8,128)S(1)} %chain.17.refs_11_), channel_id=1, source_target_pairs={{0,8},{4,12},{8,16},{12,20},{16,24},{20,28},{1,9},{5,13},{9,17},{1... | collective-permute-start | bytes 786440 | tf_op jit(solution)/shard_map/ppermute | solution.py:747
  98.9 15.7 %collective-permute-start.22 = (f32[8,64,256]{2,1,0:T(8,128)S(1)}, f32[8,64,256]{2,1,0:T(8,128)S(1)}, u32[]{:S(2)}, u32[]{:S(2)}) collective-permute-start(f32[8,64,256]{2,1,0:T(8,128)S(1)} %down.4.refs_5_), channel_id=1, source_target_pairs={{8,0},{12,4},{16,8},{20,12},{24,16},{28,20},{9,1},{13,5},{17,9},{2... | collective-permute-start | bytes 1572872 | tf_op jit(solution)/shard_map/ppermute | solution.py:747
  103.0 10.4 %copy-start.15 = (f32[256,256]{1,0:T(8,128)}, f32[256,256]{1,0:T(8,128)S(1)}, u32[]{:S(2)}) copy-start(f32[256,256]{1,0:T(8,128)S(1)} %collective-permute-done.15.refs_1_.refs_6_.refs_2_) | copy-start | bytes 786436
  103.2 9.3 %collective-permute-start.18 = (f32[256,256]{1,0:T(8,128)S(1)}, f32[256,256]{1,0:T(8,128)S(1)}, u32[]{:S(2)}, u32[]{:S(2)}) collective-permute-start(f32[256,256]{1,0:T(8,128)S(1)} %chain.18.refs_7_), channel_id=1, source_target_pairs={{0,8},{4,12},{8,16},{12,20},{16,24},{20,28},{1,9},{5,13},{9,17},{1... | collective-permute-start | bytes 786440 | tf_op jit(solution)/shard_map/ppermute | solution.py:747
  108.7 3.1 %copy-start.13 = (f32[256,512]{1,0:T(8,128)}, f32[256,512]{1,0:T(8,128)S(1)}, u32[]{:S(2)}) copy-start(f32[256,512]{1,0:T(8,128)S(1)} %get-tuple-element.127.refs_3_.refs_5_.refs_14_) | copy-start | bytes 1572868
  108.7 14.4 %collective-permute-start.21 = (f32[256,512]{1,0:T(8,128)}, f32[256,512]{1,0:T(8,128)}, u32[]{:S(2)}, u32[]{:S(2)}) collective-permute-start(f32[256,512]{1,0:T(8,128)} %get-tuple-element.133.refs_15_), channel_id=1, source_target_pairs={{0,4},{4,0},{8,12},{12,8},{16,20},{20,16},{24,28},{28,24},{1,5},{5... | collective-permute-start | bytes 1572872 | tf_op jit(solution)/shard_map/ppermute | solution.py:747
  112.6 4.3 %copy-start.23 = (f32[256,256]{1,0:T(8,128)}, f32[256,256]{1,0:T(8,128)S(1)}, u32[]{:S(2)}) copy-start(f32[256,256]{1,0:T(8,128)S(1)} %collective-permute-done.18.refs_1_.refs_3_.refs_2_) | copy-start | bytes 786436
  114.6 1.0 copy-start.21
  114.6 8.1 %copy-start.31 = (f32[256,256]{1,0:T(8,128)}, f32[256,256]{1,0:T(8,128)S(1)}, u32[]{:S(2)}) copy-start(f32[256,256]{1,0:T(8,128)S(1)} %get-tuple-element.138.refs_17_) | copy-start | bytes 786436
  115.6 16.7 %collective-permute-start.25 = (f32[8,64,256]{2,1,0:T(8,128)}, f32[8,64,256]{2,1,0:T(8,128)}, u32[]{:S(2)}, u32[]{:S(2)}) collective-permute-start(f32[8,64,256]{2,1,0:T(8,128)} %down.5.refs_5_), channel_id=1, source_target_pairs={{8,0},{12,4},{16,8},{20,12},{24,16},{28,20},{9,1},{13,5},{17,9},{2... | collective-permute-start | bytes 1572872 | tf_op jit(solution)/shard_map/ppermute | solution.py:747
  116.9 12.4 %collective-permute-start.20 = (f32[256,256]{1,0:T(8,128)}, f32[256,256]{1,0:T(8,128)}, u32[]{:S(2)}, u32[]{:S(2)}) collective-permute-start(f32[256,256]{1,0:T(8,128)} %chain.19.refs_6_), channel_id=1, source_target_pairs={{0,8},{4,12},{8,16},{12,20},{16,24},{20,28},{1,9},{5,13},{9,17},{1... | collective-permute-start | bytes 786440 | tf_op jit(solution)/shard_map/ppermute | solution.py:747
  122.6 14.5 %collective-permute-start.24 = (f32[256,256]{1,0:T(8,128)}, f32[256,256]{1,0:T(8,128)S(1)}, u32[]{:S(2)}, u32[]{:S(2)}) collective-permute-start(f32[256,256]{1,0:T(8,128)} %copy-done.31), channel_id=1, source_target_pairs={{0,4},{4,0},{8,12},{12,8},{16,20},{20,16},{24,28},{28,24},{1,5},{5... | collective-permute-start | bytes 786440 | tf_op jit(solution)/shard_map/ppermute | solution.py:747
  123.1 2.2 %copy-start.1 = (bf16[1024,2048]{1,0:T(8,128)(2,1)S(1)}, bf16[1024,2048]{1,0:T(8,128)(2,1)}, u32[]{:S(2)}) copy-start(bf16[1024,2048]{1,0:T(8,128)(2,1)} %copy-done) | copy-start | bytes 12582916
  125.3 1.2 copy-start.26
  126.5 2.8 %copy-start.16 = (f32[256,256]{1,0:T(8,128)S(1)}, f32[256,256]{1,0:T(8,128)}, u32[]{:S(2)}) copy-start(f32[256,256]{1,0:T(8,128)} %copy-done.15) | copy-start | bytes 786436
  126.5 2.8 %copy-start.24 = (f32[256,256]{1,0:T(8,128)S(1)}, f32[256,256]{1,0:T(8,128)}, u32[]{:S(2)}) copy-start(f32[256,256]{1,0:T(8,128)} %copy-done.23) | copy-start | bytes 786436
  126.5 5.8 %copy-start.4 = (f32[256,512]{1,0:T(8,128)S(1)}, f32[256,512]{1,0:T(8,128)}, u32[]{:S(2)}) copy-start(f32[256,512]{1,0:T(8,128)} %copy-done.3) | copy-start | bytes 1572868
  126.5 5.8 %copy-start.6 = (f32[256,512]{1,0:T(8,128)S(1)}, f32[256,512]{1,0:T(8,128)}, u32[]{:S(2)}) copy-start(f32[256,512]{1,0:T(8,128)} %copy-done.5) | copy-start | bytes 1572868
  126.5 5.8 %copy-start.8 = (f32[256,256]{1,0:T(8,128)S(1)}, f32[256,256]{1,0:T(8,128)}, u32[]{:S(2)}) copy-start(f32[256,256]{1,0:T(8,128)} %copy-done.7) | copy-start | bytes 786436
  126.5 5.8 %copy-start.10 = (f32[256,512]{1,0:T(8,128)S(1)}, f32[256,512]{1,0:T(8,128)}, u32[]{:S(2)}) copy-start(f32[256,512]{1,0:T(8,128)} %copy-done.9) | copy-start | bytes 1572868
  126.5 5.8 %copy-start.12 = (f32[256,512]{1,0:T(8,128)S(1)}, f32[256,512]{1,0:T(8,128)}, u32[]{:S(2)}) copy-start(f32[256,512]{1,0:T(8,128)} %copy-done.11) | copy-start | bytes 1572868
  126.5 5.8 %copy-start.14 = (f32[256,512]{1,0:T(8,128)S(1)}, f32[256,512]{1,0:T(8,128)}, u32[]{:S(2)}) copy-start(f32[256,512]{1,0:T(8,128)} %copy-done.13) | copy-start | bytes 1572868
  126.5 5.8 %copy-start.22 = (f32[256,256]{1,0:T(8,128)S(1)}, f32[256,256]{1,0:T(8,128)}, u32[]{:S(2)}) copy-start(f32[256,256]{1,0:T(8,128)} %copy-done.21) | copy-start | bytes 786436
  126.5 5.8 %copy-start.28 = (f32[256,512]{1,0:T(8,128)S(1)}, f32[256,512]{1,0:T(8,128)}, u32[]{:S(2)}) copy-start(f32[256,512]{1,0:T(8,128)} %copy-done.27) | copy-start | bytes 1572868
  126.6 5.8 %copy-start.30 = (f32[256,512]{1,0:T(8,128)S(1)}, f32[256,512]{1,0:T(8,128)}, u32[]{:S(2)}) copy-start(f32[256,512]{1,0:T(8,128)} %copy-done.29) | copy-start | bytes 1572868
  126.6 5.8 %copy-start.32 = (f32[256,256]{1,0:T(8,128)S(1)}, f32[256,256]{1,0:T(8,128)}, u32[]{:S(2)}) copy-start(f32[256,256]{1,0:T(8,128)} %copy-done.31) | copy-start | bytes 786436
  129.3 6.4 %copy-start.2 = (bf16[1024,2048]{1,0:T(8,128)(2,1)S(1)}, bf16[1024,2048]{1,0:T(8,128)(2,1)}, u32[]{:S(2)}) copy-start(bf16[1024,2048]{1,0:T(8,128)(2,1)} %copy-done) | copy-start | bytes 12582916
  129.3 6.4 %copy-start.20 = (bf16[1024,512]{1,0:T(8,128)(2,1)S(1)}, bf16[1024,512]{1,0:T(8,128)(2,1)}, u32[]{:S(2)}) copy-start(bf16[1024,512]{1,0:T(8,128)(2,1)} %copy-done.19) | copy-start | bytes 3145732
  130.6 7.6 %collective-permute-start.23 = (f32[256,256]{1,0:T(8,128)S(1)}, f32[256,256]{1,0:T(8,128)S(1)}, u32[]{:S(2)}, u32[]{:S(2)}) collective-permute-start(f32[256,256]{1,0:T(8,128)S(1)} %get-tuple-element.137.refs_19_), channel_id=1, source_target_pairs={{0,4},{4,0},{8,12},{12,8},{16,20},{20,16},{24,28},{28,24},{1,5},{5... | collective-permute-start | bytes 786440 | tf_op jit(solution)/shard_map/ppermute | solution.py:747
  133.9 3.3 %copy-start.18 = (bf16[1024,512]{1,0:T(8,128)(2,1)S(1)}, bf16[1024,512]{1,0:T(8,128)(2,1)}, u32[]{:S(2)}) copy-start(bf16[1024,512]{1,0:T(8,128)(2,1)} %copy-done.17) | copy-start | bytes 3145732
  133.9 6.4 %collective-permute-start.26 = (f32[4,32,512]{2,1,0:T(8,128)S(1)}, f32[4,32,512]{2,1,0:T(8,128)S(1)}, u32[]{:S(2)}, u32[]{:S(2)}) collective-permute-start(f32[4,32,512]{2,1,0:T(8,128)S(1)} %get-tuple-element.142.refs_7_), channel_id=1, source_target_pairs={{0,4},{4,0},{8,12},{12,8},{16,20},{20,16},{24,28},{28,24},{1,5},{5... | collective-permute-start | bytes 786440 | tf_op jit(solution)/shard_map/ppermute | solution.py:747

commit v3 on v2

v3 whole, which is shorter than its diff:
```python
import functools

import jax
import jax.numpy as jnp
from jax import lax
from jax.experimental import pallas as pl
from jax.experimental.pallas import tpu as pltpu
from jax.sharding import PartitionSpec as P

VERY_NEGATIVE = -1e30
LANES = 128
MIB = 1 << 20
AXIS = "ctx"

(
    ROW_A, ROW_SEND_P, ROW_SEND_S, ROW_OWN_P, ROW_OWN_S, ROW_FIN_P, ROW_FIN_K, ROW_FIN_R, ROW_FIN_O, ROW_OUT_K, ROW_CHAIN,
) = range(11)


class Order:
    def __init__(self):
        self.last = None
        self.held = []


def call(order, kernel, operands, outs, name, mib=8, scratch=(), aliases=None, flops=1e6, moved=1e6):
    in_specs, arrays = [], []
    count = len(operands)
    for extra in [order.last, *order.held]:
        if extra is not None and not any(extra is operand for operand in operands):
            operands = [*operands, extra]
    body = lambda *refs: kernel(*refs[:count], *refs[len(operands) :])
    for operand in operands:
        if isinstance(operand, tuple):
            in_specs.append(pl.BlockSpec(memory_space=pl.ANY))
            arrays.append(pltpu.with_memory_space_constraint(operand[0], pltpu.HBM))
        else:
            in_specs.append(pl.BlockSpec(memory_space=pltpu.VMEM))
            arrays.append(pltpu.with_memory_space_constraint(operand, pltpu.VMEM))
    out_specs = [
        pl.BlockSpec(memory_space=pl.ANY if out.memory_space == pltpu.HBM else pltpu.VMEM) for out in outs
    ]
    results = pl.pallas_call(
        body,
        in_specs=in_specs,
        out_specs=out_specs,
        out_shape=list(outs),
        scratch_shapes=list(scratch),
        input_output_aliases=aliases or {},
        compiler_params=pltpu.CompilerParams(vmem_limit_bytes=mib * MIB),
        cost_estimate=pl.CostEstimate(flops=int(flops), bytes_accessed=int(moved), transcendentals=0),
        name=name,
    )(*arrays)
    order.last = results[-1]
    return results


class Operands:
    def __init__(self):
        self.arrays = []

    def place(self, array):
        for i, other in enumerate(self.arrays):
            if other is array:
                return i
        self.arrays.append(array)
        return len(self.arrays) - 1

    def view(self, view):
        return self.place(view[0]), view[1]


def position():
    place = lax.axis_index(AXIS)
    return lax.rem(place, 2), lax.div(place, 2)


def lane_iota(shape):
    return lax.broadcasted_iota(jnp.int32, shape, len(shape) - 1)


def row_iota(shape):
    return lax.broadcasted_iota(jnp.int32, shape, 0)


def lane_order(value, side):
    half = value.shape[0] // 2
    return jnp.where(side == 0, value, jnp.concatenate([value[half:], value[:half]], axis=0))


def head_at(index, heads, side):
    return lax.rem(side * (heads // 2) + index, heads)


def columns_of(head, width):
    return pl.ds(pl.multiple_of(head * width, width), width)


def three_parts(value):
    high = value.astype(jnp.bfloat16).astype(jnp.float32)
    middle = (value - high).astype(jnp.bfloat16).astype(jnp.float32)
    return high, middle, value - high - middle


def memory_of(key, value, weight):
    scaled = (key.astype(jnp.float32) * weight).astype(jnp.bfloat16)
    return lax.dot_general(
        scaled, value, (((0,), (0,)), ((), ())), preferred_element_type=jnp.float32
    )


def start_kernel(
    input_hbm, forget_hbm, keys_hbm, values_hbm,
    keys_ref, value_ref, next_ref, rows_ref, columns_ref, summary_ref, input_ref, forget_ref, sems,
):
    heads, tokens = input_ref.shape
    dqk = keys_ref.shape[1] // heads
    dv = value_ref.shape[1]
    side, _ = position()
    away = [head_at(heads // 2 + i, heads, side) for i in range(2)]
    copies = [
        pltpu.make_async_copy(forget_hbm, forget_ref, sems.at[0]),
        pltpu.make_async_copy(input_hbm, input_ref, sems.at[1]),
        pltpu.make_async_copy(keys_hbm, keys_ref, sems.at[2]),
        pltpu.make_async_copy(values_hbm.at[:, columns_of(away[0], dv)], value_ref, sems.at[3]),
        pltpu.make_async_copy(values_hbm.at[:, columns_of(away[1], dv)], next_ref, sems.at[4]),
    ]
    for copy in copies:
        copy.start()
    copies[0].wait()
    copies[1].wait()

    gate = lane_order(forget_ref[...], side)
    cumulated = jnp.minimum(gate, 0.0) - jnp.log1p(jnp.exp(-jnp.abs(gate)))
    lanes = lane_iota((heads, tokens))
    step = 1
    while step < tokens:
        cumulated = cumulated + jnp.where(lanes >= step, pltpu.roll(cumulated, step, 1), 0.0)
        step *= 2
    level = lane_order(input_ref[...], side) - cumulated
    running = level
    step = 1
    while step < tokens:
        running = jnp.maximum(
            running, jnp.where(lanes >= step, pltpu.roll(running, step, 1), VERY_NEGATIVE)
        )
        step *= 2
    highest = running[:, tokens - 1 : tokens]
    decay = cumulated[:, tokens - 1 : tokens]
    weight = jnp.exp(level - highest)
    rows_ref[...] = level
    filler = jnp.zeros((LANES - 3 * heads, tokens), jnp.float32)
    columns_ref[...] = jnp.concatenate([weight, running, cumulated, filler], axis=0).T

    copies[2].wait()
    spare = jnp.zeros((-(-3 * heads // 16) * 16 - 3 * heads, tokens), jnp.float32)
    parts = jnp.concatenate([*three_parts(weight), spare], axis=0).astype(jnp.bfloat16)
    sums = []
    for i in range(heads):
        product = jnp.dot(
            parts, keys_ref[:, columns_of(head_at(i, heads, side), dqk)], preferred_element_type=jnp.float32
        )
        sums.append(
            product[i : i + 1] + product[heads + i : heads + i + 1] + product[2 * heads + i : 2 * heads + i + 1]
        )
    lane = lane_iota((heads, LANES))
    stats = jnp.where(lane == 0, decay + highest, jnp.where(lane == 1, decay, 0.0))
    summary = jnp.concatenate([jnp.concatenate(sums, axis=0), stats], axis=1)
    summary_ref[...] = lane_order(summary, side)
    copies[3].wait()
    copies[4].wait()


def start(order, input_gate, forget_gate, keys, values):
    heads, tokens = input_gate.shape
    dqk, dv = keys.shape[1] // heads, values.shape[1] // heads
    return call(
        order,
        start_kernel,
        [(a, pl.ANY) for a in (input_gate, forget_gate, keys, values)],
        [
            pltpu.VMEM(keys.shape, keys.dtype),
            pltpu.VMEM((tokens, dv), values.dtype),
            pltpu.VMEM((tokens, dv), values.dtype),
            pltpu.VMEM((heads, tokens), jnp.float32),
            pltpu.VMEM((tokens, LANES), jnp.float32),
            pltpu.VMEM((heads, dqk + LANES), jnp.float32),
        ],
        "start",
        mib=12,
        scratch=[
            pltpu.VMEM((heads, tokens), jnp.float32),
            pltpu.VMEM((heads, tokens), jnp.float32),
            pltpu.SemaphoreType.DMA((5,)),
        ],
        flops=2e9,
        moved=5e6,
    )


def away_kernel(keys_ref, columns_ref, value_ref, *refs, heads, place):
    *before, chunk_ref, rest_ref = refs
    side, _ = position()
    index = heads // 2 + place
    dqk, half = rest_ref.shape
    memory = memory_of(
        keys_ref[:, columns_of(head_at(index, heads, side), dqk)], value_ref[...], columns_ref[:, index : index + 1]
    )
    if before:
        chunk_ref[:, :half] = before[0][...]
    chunk_ref[:, chunk_ref.shape[1] - half :] = memory[:, :half]
    rest_ref[...] = memory[:, half:]


def away_memory(order, place, keys, columns, value, before, heads):
    tokens, dv = value.shape
    dqk = keys.shape[1] // heads
    half = dv // 2
    return call(
        order,
        functools.partial(away_kernel, heads=heads, place=place),
        [keys, columns, value, *before],
        [
            pltpu.VMEM((dqk, half * (1 + len(before))), jnp.float32),
            pltpu.VMEM((dqk, half), jnp.float32),
        ],
        "away_memory",
        mib=12,
        flops=0,
        moved=0,
    )


def load_kernel(keys_ref, columns_ref, big_hbm, big_ref, memory_ref, sems, *, heads):
    side, _ = position()
    width = big_ref.shape[1] // heads
    dqk = keys_ref.shape[1] // heads
    copies = []
    for i in range(heads):
        columns = columns_of(head_at(i, heads, side), width)
        copies.append(pltpu.make_async_copy(big_hbm.at[:, columns], big_ref.at[:, columns], sems.at[i]))
        copies[i].start()
    copies[0].wait()
    head = head_at(0, heads, side)
    memory_ref[...] = memory_of(
        keys_ref[:, columns_of(head, dqk)], big_ref[:, columns_of(head, width)], columns_ref[:, 0:1]
    )
    for copy in copies[1:]:
        copy.wait()


def load(order, keys, columns, values, heads):
    tokens = keys.shape[0]
    dqk, dv = keys.shape[1] // heads, values.shape[1] // heads
    return call(
        order,
        functools.partial(load_kernel, heads=heads),
        [keys, columns, (values, pl.ANY)],
        [pltpu.VMEM(values.shape, values.dtype), pltpu.VMEM((dqk, dv), jnp.float32)],
        "load",
        mib=12,
        scratch=[pltpu.SemaphoreType.DMA((heads,))],
        flops=4 * tokens * dqk * dv,
        moved=8e6,
    )


def memories_kernel(keys_ref, columns_ref, values_ref, queries_hbm, rest_ref, queries_ref, *refs, heads):
    *chunk_refs, sem = refs
    side, _ = position()
    dqk, dv = keys_ref.shape[1] // heads, values_ref.shape[1] // heads
    half = dv // 2
    copy = pltpu.make_async_copy(queries_hbm, queries_ref, sem)
    copy.start()
    rest = rest_ref[...]
    for place, chunk_ref in enumerate(chunk_refs[:-1]):
        index = heads // 2 + 2 + place
        head = head_at(index, heads, side)
        memory = memory_of(
            keys_ref[:, columns_of(head, dqk)], values_ref[:, columns_of(head, dv)], columns_ref[:, index : index + 1]
        )
        chunk_ref[:, :half] = rest
        chunk_ref[:, half:] = memory[:, :half]
        rest = memory[:, half:]
    chunk_refs[-1][...] = rest
    copy.wait()


def memories(order, keys, columns, values, queries, rest, heads):
    tokens = keys.shape[0]
    dqk, dv = keys.shape[1] // heads, values.shape[1] // heads
    count = heads // 2 - 2
    outs = call(
        order,
        functools.partial(memories_kernel, heads=heads),
        [keys, columns, values, (queries, pl.ANY), rest],
        [pltpu.VMEM(queries.shape, queries.dtype)]
        + [pltpu.VMEM((dqk, dv), jnp.float32)] * count
        + [pltpu.VMEM((dqk, dv // 2), jnp.float32)],
        "memories_away",
        mib=12,
        scratch=[pltpu.SemaphoreType.DMA],
        flops=4 * count * tokens * dqk * dv,
        moved=4e6,
    )
    return outs[0], outs[1:]


def own_kernel(keys_ref, columns_ref, values_ref, *memory_refs, heads, indices):
    side, _ = position()
    dqk, dv = keys_ref.shape[1] // heads, values_ref.shape[1] // heads
    for i, memory_ref in zip(indices, memory_refs):
        head = head_at(i, heads, side)
        memory_ref[...] = memory_of(
            keys_ref[:, columns_of(head, dqk)], values_ref[:, columns_of(head, dv)], columns_ref[:, i : i + 1]
        )


def own_memories(order, keys, columns, values, indices, heads):
    tokens = keys.shape[0]
    dqk, dv = keys.shape[1] // heads, values.shape[1] // heads
    return call(
        order,
        functools.partial(own_kernel, heads=heads, indices=indices),
        [keys, columns, values],
        [pltpu.VMEM((dqk, dv), jnp.float32)] * len(indices),
        "memories_own",
        mib=12,
        flops=4 * len(indices) * tokens * dqk * dv,
        moved=4e6,
    )


def block_summary(gathered_ref, block, side, level):
    levels = gathered_ref.shape[0]
    turn = lax.rem(block // 2 - level + levels, levels)
    same, other = gathered_ref[turn, 0], gathered_ref[turn, 1]
    return jnp.where(side == block % 2, same, other)


def weights_kernel(gathered_ref, table_ref, parts_ref, top_row_ref):
    levels, _, heads, width = gathered_ref.shape
    blocks = 2 * levels
    dqk = width - LANES
    lane_heads = heads // 2
    side, level = position()

    tops, decays, normals = [], [], []
    for block in range(blocks):
        held = block_summary(gathered_ref, block, side, level)
        normals.append(held[:, :dqk])
        tops.append(held[:, dqk : dqk + 1])
        decays.append(held[:, dqk + 1 : dqk + 2])

    pick = lambda at, value, otherwise: jnp.where(level == at, value, otherwise)
    top = jnp.full((heads, 1), VERY_NEGATIVE, jnp.float32)
    normal = jnp.zeros((heads, dqk), jnp.float32)
    zero = jnp.zeros((heads, 1), jnp.float32)
    mine_a = mine_b = mine_first = mine_second = zero
    carry_p = carry_s = zero
    prefix_top, prefix_normal = zero, normal
    scales = []
    for z in range(levels):
        t0, t1, d0, d1 = tops[2 * z], tops[2 * z + 1], decays[2 * z], decays[2 * z + 1]
        pair_top = jnp.maximum(t0 + d1, t1)
        first, second = jnp.exp(t0 + d1 - pair_top), jnp.exp(t1 - pair_top)
        pair_normal = normals[2 * z] * first + normals[2 * z + 1] * second
        middle_top = jnp.maximum(top + d0, t0)
        alpha, beta = jnp.exp(top + d0 - middle_top), jnp.exp(t0 - middle_top)
        middle_normal = normal * alpha + normals[2 * z] * beta
        pair_decay = d0 + d1
        next_top = jnp.maximum(top + pair_decay, pair_top)
        a, b = jnp.exp(top + pair_decay - next_top), jnp.exp(pair_top - next_top)
        mine_a, mine_b = pick(z, a, mine_a), pick(z, b, mine_b)
        mine_first, mine_second = pick(z, first, mine_first), pick(z, second, mine_second)
        carry_p, carry_s = pick(z, alpha, carry_p), pick(z, beta, carry_s)
        prefix_top = pick(z, jnp.where(side == 0, top, middle_top), prefix_top)
        prefix_normal = pick(z, jnp.where(side == 0, normal, middle_normal), prefix_normal)
        normal = normal * a + pair_normal * b
        top = next_top
        scales.append((a, b, jnp.exp(middle_top + d1 - next_top)))
    later = jnp.ones((heads, 1), jnp.float32)
    final_p = final_l = final_m = zero
    for z in reversed(range(levels)):
        a, b, middle = scales[z]
        final_l = pick(z, b * later, final_l)
        final_m = pick(z, middle * later, final_m)
        later = later * a
        final_p = pick(z, later, final_p)

    one = jnp.ones((heads, 1), jnp.float32)
    by_side = lambda zero_value, one_value: jnp.where(side == 0, zero_value, one_value)
    lanes = lane_iota((heads, LANES))
    rows = row_iota((heads, LANES))
    head_of_unit = lane_heads * side + lax.div(lanes, 2)
    other_of_unit = lane_heads * (1 - side) + lax.div(lanes, 2)
    head_of_step = lane_heads * side + lax.div(jnp.clip(lanes - 2 * level - 1, 0, 2 * lane_heads - 1), 2)

    def spread(column, heads_wanted):
        return jnp.sum(jnp.where(rows == heads_wanted, column, 0.0), axis=0, keepdims=True)

    mine_own = by_side(mine_first, mine_second)
    mine_partner = by_side(mine_second, mine_first)
    chain_own = spread(mine_b * mine_own, head_of_step)
    chain_partner = spread(mine_b * mine_partner, head_of_step)
    entries = [
        spread(mine_a, head_of_step),
        spread(by_side(carry_p, one), head_of_unit),
        spread(by_side(carry_s, zero), head_of_unit),
        spread(by_side(one, carry_p), head_of_unit),
        spread(by_side(zero, carry_s), head_of_unit),
        spread(final_p, head_of_unit),
        spread(final_l * mine_own, head_of_unit),
        spread(final_l * mine_partner, head_of_unit),
        spread(by_side(final_p, final_m), other_of_unit),
        spread(by_side(zero, final_l * mine_own), head_of_unit),
    ]
    for z in range(levels):
        entries += [pick(z, chain_own, 0.0), pick(z, chain_partner, 0.0)]
    here = jnp.ones((1, LANES), jnp.float32)
    entries += [pick(z, here, 0.0) for z in range(levels)]
    empty = jnp.zeros((1, LANES), jnp.float32)
    entries += [empty] * (table_ref.shape[0] - len(entries))
    table_ref[...] = jnp.concatenate(entries, axis=0)

    filler = jnp.zeros((LANES - 3 * heads, dqk), jnp.float32)
    parts = jnp.concatenate([*three_parts(lane_order(prefix_normal, side)), filler], axis=0)
    parts_ref[...] = parts.T
    prefix_top = lane_order(jnp.broadcast_to(prefix_top, (heads, LANES)), side)
    filler = jnp.zeros((LANES - heads, LANES), jnp.float32)
    top_row_ref[...] = jnp.concatenate([prefix_top, filler], axis=0).T[:8]


def weights(order, gathered):
    levels, _, heads, width = gathered.shape
    dqk = width - LANES
    table_rows = -(-(ROW_CHAIN + 3 * levels) // 8) * 8
    return call(
        order,
        weights_kernel,
        [gathered],
        [
            pltpu.VMEM((table_rows, LANES), jnp.float32),
            pltpu.VMEM((dqk, LANES), jnp.float32),
            pltpu.VMEM((8, LANES), jnp.float32),
        ],
        "weights",
    )


def wait_kernel(ref, out_ref):
    out_ref[...] = ref[:8, :LANES]


def wait(order, array):
    return call(order, wait_kernel, [array], [pltpu.VMEM((8, LANES), jnp.float32)], "wait")[0]


def pack_kernel(*refs):
    *in_refs, out_ref = refs
    at = 0
    for ref in in_refs:
        value = ref[...].reshape((-1,) + out_ref.shape[1:])
        count = min(value.shape[0], out_ref.shape[0] - at)
        out_ref[at : at + count] = value[:count]
        at += count


def pack(order, arrays, count):
    shape = arrays[0].shape[-2:] if count == 2 and arrays[0].ndim == 2 else arrays[0].shape[1:]
    return call(order, pack_kernel, arrays, [pltpu.VMEM((count,) + shape, jnp.float32)], "pack")[0]


def finals_kernel(gathered_ref, normal_hbm, tops_hbm, token_ref, normal_ref, tops_ref, sems):
    token_ref[...] = jnp.zeros_like(token_ref)
    levels, _, heads, width = gathered_ref.shape
    dqk = width - LANES
    side, level = position()
    top = jnp.full((heads, 1), VERY_NEGATIVE, jnp.float32)
    normal = jnp.zeros((heads, dqk), jnp.float32)
    for block in range(2 * levels):
        held = block_summary(gathered_ref, block, side, level)
        block_top, decay = held[:, dqk : dqk + 1], held[:, dqk + 1 : dqk + 2]
        next_top = jnp.maximum(top + decay, block_top)
        normal = normal * jnp.exp(top + decay - next_top) + held[:, :dqk] * jnp.exp(block_top - next_top)
        top = next_top
    share = normal_hbm.shape[1]
    place = 2 * level + side
    mine = pltpu.roll(normal, lax.rem(dqk - place * share, dqk), 1)
    normal_ref[...] = mine[:, :share]
    filler = jnp.zeros((LANES - heads, LANES), jnp.float32)
    tops = jnp.concatenate([jnp.broadcast_to(top, (heads, LANES)), filler], axis=0).T
    tops_ref[...] = tops[0:1, :heads]
    copies = [
        pltpu.make_async_copy(normal_ref, normal_hbm, sems.at[0]),
        pltpu.make_async_copy(tops_ref, tops_hbm, sems.at[1]),
    ]
    for copy in copies:
        copy.start()
    for copy in copies:
        copy.wait()


def finals(order, gathered):
    levels, _, heads, width = gathered.shape
    shape = (heads, (width - LANES) // (2 * levels))
    normal, tops, _ = call(
        order,
        finals_kernel,
        [gathered],
        [
            pltpu.HBM(shape, jnp.float32),
            pltpu.HBM((1, heads), jnp.float32),
            pltpu.VMEM((8, LANES), jnp.float32),
        ],
        "finals",
        scratch=[
            pltpu.VMEM(shape, jnp.float32),
            pltpu.VMEM((1, heads), jnp.float32),
            pltpu.SemaphoreType.DMA((2,)),
        ],
    )
    return normal, tops


def attention_kernel(
    queries_ref, keys_ref, values_ref, rows_ref, columns_ref, parts_ref, *refs, heads, index
):
    out_ref, sums_ref, products_ref = refs[-3:]
    side, _ = position()
    head = head_at(index, heads, side)
    tokens = queries_ref.shape[0]
    dqk, dv = queries_ref.shape[1] // heads, values_ref.shape[1] // heads
    key_columns, value_columns = columns_of(head, dqk), columns_of(head, dv)
    tile = min(256, tokens)
    level = rows_ref[index : index + 1, :]
    causal = row_iota((tile, tile)) >= lane_iota((tile, tile))
    part_lanes = lane_iota(parts_ref.shape)
    mine = (lax.rem(part_lanes, heads) == index) & (part_lanes < 3 * heads)
    parts = jnp.where(mine, parts_ref[...], 0.0).astype(jnp.bfloat16)

    for begin in range(0, tokens, tile):
        end = begin + tile
        here = pl.ds(begin, tile)
        query = queries_ref[here, key_columns]
        running = columns_ref[here, heads + index : heads + index + 1]
        total = jnp.zeros((tile, 1), jnp.float32)
        result = None
        for low in range(0, end, tile):
            there = pl.ds(low, tile)
            scores = lax.dot_general(
                query, keys_ref[there, key_columns], (((1,), (1,)), ((), ())), preferred_element_type=jnp.float32
            )
            attn = jnp.exp(level[:, low : low + tile] - running) * scores
            if low == begin:
                attn = jnp.where(causal, attn, 0.0)
            total = total + jnp.sum(attn, axis=1, keepdims=True)
            term = jnp.dot(
                attn.astype(jnp.bfloat16), values_ref[there, value_columns], preferred_element_type=jnp.float32
            )
            result = term if result is None else result + term
        product = jnp.dot(query, parts, preferred_element_type=jnp.float32)
        lanes = lane_iota((tile, LANES))
        if len(refs) > 3:
            sums_ref[here, :] = jnp.where(lanes == index, total, refs[0][here, :])
            products_ref[here, :] = refs[1][here, :] + product
        else:
            sums_ref[here, :] = jnp.where(lanes == index, total, 0.0)
            products_ref[here, :] = product
        out_ref[here, :] = result.astype(jnp.bfloat16)


def attention(order, index, queries, keys, values, rows, columns, parts, state):
    tokens = queries.shape[0]
    heads = rows.shape[0]
    dqk, dv = queries.shape[1] // heads, values.shape[1] // heads
    return call(
        order,
        functools.partial(attention_kernel, heads=heads, index=index),
        [queries, keys, values, rows, columns, parts, *state],
        [
            pltpu.VMEM((tokens, dv), jnp.bfloat16),
            pltpu.VMEM((tokens, LANES), jnp.float32),
            pltpu.VMEM((tokens, LANES), jnp.float32),
        ],
        "attention",
        mib=12,
        flops=2 * tokens * tokens * (dqk + dv) * 1.5,
    )


def factors_kernel(columns_ref, top_ref, sums_ref, products_ref, out_ref, *, heads, dqk):
    tokens = columns_ref.shape[0]
    tile = min(256, tokens)
    shift = lambda block, by: pltpu.roll(block, (LANES - by) % LANES, 1)
    for begin in range(0, tokens, tile):
        here = pl.ds(begin, tile)
        product = products_ref[here, :]
        product = product + shift(product, heads) + shift(product, 2 * heads)
        column = columns_ref[here, :]
        running, cumulated = shift(column, heads), shift(column, 2 * heads)
        top = top_ref[0:1, :]
        highest = jnp.maximum(running, top)
        scaling = float(dqk) ** -0.5
        local, carried = jnp.exp(running - highest), jnp.exp(top - highest)
        denominator = (local * sums_ref[here, :] + carried * product) * scaling
        divisor = jnp.maximum(jnp.abs(denominator), jnp.exp(-(cumulated + highest)))
        inverse = scaling / divisor
        out_ref[here, :] = jnp.where(
            lane_iota((tile, LANES)) < heads, local * inverse, pltpu.roll(carried * inverse, heads, 1)
        )


def factors(order, columns, top_row, sums, products, heads, dqk):
    return call(
        order,
        functools.partial(factors_kernel, heads=heads, dqk=dqk),
        [columns, top_row, sums, products],
        [pltpu.VMEM(columns.shape, jnp.float32)],
        "factors",
    )[0]


def finish_units(queries_ref, factors_ref, refs, items, heads, out_hbm, scratch, sems):
    side, _ = position()
    tokens = queries_ref.shape[0]
    dqk = queries_ref.shape[1] // heads
    half = scratch.shape[2]
    tile = min(256, tokens)
    copies = []
    for at, (index, which, held, place, column) in enumerate(items):
        head = head_at(index, heads, side)
        memory = refs[place][:, column : column + half].astype(jnp.bfloat16)
        target = pl.ds(pl.multiple_of((2 * head + which) * half, half), half)
        for begin in range(0, tokens, tile):
            here = pl.ds(begin, tile)
            local = factors_ref[here, index : index + 1]
            carried = factors_ref[here, heads + index : heads + index + 1]
            term = jnp.dot(
                queries_ref[here, columns_of(head, dqk)], memory, preferred_element_type=jnp.float32
            )
            value = refs[held][here, which * half : (which + 1) * half].astype(jnp.float32)
            scratch[at, here, :] = (value * local + term * carried).astype(scratch.dtype)
            copy = pltpu.make_async_copy(
                scratch.at[at, here, :], out_hbm.at[here, target], sems.at[len(copies)]
            )
            copy.start()
            copies.append(copy)
    return copies


def finish_kernel(queries_ref, factors_ref, *refs, items, heads):
    *_, out_hbm, token_ref, scratch, sems = refs
    token_ref[...] = jnp.zeros_like(token_ref)
    for copy in finish_units(queries_ref, factors_ref, refs, items, heads, out_hbm, scratch, sems):
        copy.wait()


def finish_operands(units):
    operands = Operands()
    items = [
        (index, which, operands.place(held), *operands.view(view)) for index, which, held, view in units
    ]
    return operands, items


def finish_scratch(units, tokens):
    half = units[0][2].shape[1] // 2
    return [
        pltpu.VMEM((len(units), tokens, half), jnp.bfloat16),
        pltpu.SemaphoreType.DMA((len(units) * max(1, tokens // 256),)),
    ]


def finish(order, units, queries, factor, hidden, heads):
    operands, items = finish_operands(units)
    tokens = queries.shape[0]
    dv = units[0][2].shape[1]
    arrays = [queries, factor, *operands.arrays]
    aliases = {}
    if hidden is not None:
        aliases = {len(arrays): 0}
        arrays.append((hidden, pl.ANY))
    return call(
        order,
        functools.partial(finish_kernel, items=items, heads=heads),
        arrays,
        [pltpu.HBM((tokens, heads * dv), jnp.bfloat16), pltpu.VMEM((8, LANES), jnp.float32)],
        "finish",
        mib=12,
        scratch=finish_scratch(units, tokens),
        aliases=aliases,
        flops=8e8 * len(units),
    )[0]


def entry_of(table_ref):
    return lambda row, lane: table_ref[row : row + 1, lane : lane + 1]


def row_tiles(rows):
    tile = min(32, rows)
    return [pl.ds(begin, tile) for begin in range(0, rows, tile)]


def chain_kernel(table_ref, *refs, slots, half):
    out_ref = refs[-1]
    entry = entry_of(table_ref)
    for i, terms in enumerate(slots):
        terms = [(place, column, entry(row, lane)) for place, column, row, lane in terms]
        for here in row_tiles(out_ref.shape[0]):
            total = None
            for place, column, weight in terms:
                term = refs[place][here, column : column + half] * weight
                total = term if total is None else total + term
            out_ref[here, i * half : (i + 1) * half] = total


def first_kernel(pair_ref, keep_ref, take_ref, out_ref):
    side, _ = position()
    heads, width = pair_ref.shape[1:]
    half = out_ref.shape[1]
    top, decay = [], []
    for which in range(2):
        low, high = pair_ref[which, 0:1, width - LANES :], pair_ref[which, heads // 2 : heads // 2 + 1, width - LANES :]
        stats = jnp.where(side == 0, low, high)
        top.append(stats[:, 0:1])
        decay.append(stats[:, 1:2])
    own = top[0] + jnp.where(side == 0, decay[1], 0.0)
    partner = top[1] + jnp.where(side == 0, 0.0, decay[0])
    highest = jnp.maximum(own, partner)
    own, partner = jnp.exp(own - highest), jnp.exp(partner - highest)
    for here in row_tiles(out_ref.shape[0]):
        out_ref[here, :] = keep_ref[here, :half] * own + take_ref[here, :half] * partner


def first_step(order, pair, kept, received, half):
    return call(
        order,
        first_kernel,
        [pair, kept[0][0], received[0][0]],
        [pltpu.VMEM((kept[0][0].shape[0], half), jnp.float32)],
        "chain",
    )[0]


def chain_step(order, table, step, kept, received, earlier, levels, half):
    operands = Operands()
    slots, columns = [], {}
    for slot in range(2):
        terms = []
        lane = 2 * step + slot
        for z in range(levels - 1):
            unit = 2 * (step - z) - 1 + slot
            if 0 <= unit < len(kept):
                terms.append((*operands.view(kept[unit]), ROW_CHAIN + 2 * z, lane))
                terms.append((*operands.view(received[unit]), ROW_CHAIN + 2 * z + 1, lane))
        if terms:
            if slot in earlier[1]:
                terms.append((operands.place(earlier[0]), earlier[1][slot], ROW_A, lane))
            columns[slot] = half * len(slots)
            slots.append(terms)
    value = call(
        order,
        functools.partial(chain_kernel, slots=slots, half=half),
        [table, *operands.arrays],
        [pltpu.VMEM((kept[0][0].shape[0], half * len(slots)), jnp.float32)],
        "chain",
    )[0]
    return value, columns


def prefix_kernel(table_ref, *refs, levels, pieces, half):
    send_ref, own_ref = refs[-2:]
    entry = entry_of(table_ref)
    here_row = ROW_CHAIN + 2 * levels
    picks = [entry(here_row + z, 0) for z in range(1, levels)]
    for i, (unit, arrivals, (keep, keep_column), (take, take_column)) in enumerate(pieces):
        columns = pl.ds(i * half, half)
        send_p, send_s = entry(ROW_SEND_P, unit), entry(ROW_SEND_S, unit)
        own_p, own_s = entry(ROW_OWN_P, unit), entry(ROW_OWN_S, unit)
        for here in row_tiles(send_ref.shape[0]):
            prefix = None
            for (place, column), weight in zip(arrivals, picks):
                term = refs[place][here, column : column + half] * weight
                prefix = term if prefix is None else prefix + term
            send_ref[here, columns] = prefix * send_p + refs[keep][here, keep_column : keep_column + half] * send_s
            own_ref[here, columns] = prefix * own_p + refs[take][here, take_column : take_column + half] * own_s


def prefixes(order, table, chunk, arrived, kept, received, levels, half):
    operands = Operands()
    pieces = []
    for unit in (2 * chunk - 1, 2 * chunk):
        if 0 <= unit < len(kept):
            arrivals = []
            for z in range(1, levels):
                array, columns = arrived[chunk + z - 1]
                arrivals.append(operands.view((array, columns[unit - 2 * chunk + 1])))
            pieces.append((unit, arrivals, operands.view(kept[unit]), operands.view(received[unit])))
    out = pltpu.VMEM((kept[0][0].shape[0], len(pieces) * half), jnp.float32)
    return call(
        order,
        functools.partial(prefix_kernel, levels=levels, pieces=pieces, half=half),
        [table, *operands.arrays],
        [out, out],
        "prefix",
    )


def down_kernel(table_ref, *refs, step, levels, views, earlier):
    out_ref = refs[-1]
    _, rows, half = out_ref.shape
    _, level = position()
    target = jnp.maximum(step - levels + level, 0)
    here = pl.ds(pl.multiple_of(target * rows, rows), rows)
    entry = entry_of(table_ref)
    for c, ((keep, keep_column), (take, take_column)) in enumerate(views):
        value = refs[keep][here, keep_column : keep_column + half] * entry(ROW_FIN_K, c)
        value = value + refs[take][here, take_column : take_column + half] * entry(ROW_FIN_R, c)
        out_ref[c] = value if earlier is None else value + refs[earlier][c]


def down(order, table, step, levels, kept, received, earlier, rows, half):
    operands = Operands()
    views = [(operands.view(keep), operands.view(take)) for keep, take in zip(kept, received)]
    place = None if earlier is None else operands.place(earlier)
    return call(
        order,
        functools.partial(down_kernel, step=step, levels=levels, views=views, earlier=place),
        [table, *operands.arrays],
        [pltpu.VMEM((len(kept), rows, half), jnp.float32)],
        "down",
    )[0]


def outgoing_kernel(table_ref, *refs, views):
    above_ref, out_ref = refs[-2:]
    _, rows, half = above_ref.shape
    side, level = position()
    entry = entry_of(table_ref)
    share = rows // 2
    there = pl.ds(pl.multiple_of((1 - side) * share, share), share)
    here = pl.ds(pl.multiple_of(level * rows + (1 - side) * share, share), share)
    for c, ((keep, keep_column), (take, take_column)) in enumerate(views):
        out_ref[c // 2, :, pl.ds((c % 2) * half, half)] = (
            above_ref[c, there, :]
            + refs[keep][here, keep_column : keep_column + half] * entry(ROW_OUT_K, c)
            + refs[take][here, take_column : take_column + half] * entry(ROW_FIN_R, c)
        )


def outgoing(order, table, kept, received, above):
    operands = Operands()
    views = [(operands.view(keep), operands.view(take)) for keep, take in zip(kept, received)]
    chunks, rows, half = above.shape
    return call(
        order,
        functools.partial(outgoing_kernel, views=views),
        [table, *operands.arrays, above],
        [pltpu.VMEM((chunks // 2, rows // 2, 2 * half), jnp.float32)],
        "outgoing",
    )[0]


def assemble(table_ref, above_ref, partner_ref, refs, out_ref, *, views, prefix_views, other_views):
    _, rows, half = above_ref.shape
    side, level = position()
    entry = entry_of(table_ref)
    share = rows // 2
    lane_heads = len(views) // 2
    there = pl.ds(pl.multiple_of(side * share, share), share)
    here = pl.ds(pl.multiple_of(level * rows + side * share, share), share)
    at = lambda view: refs[view[0]][here, view[1] : view[1] + half]
    for c, (keep, take) in enumerate(views):
        own, sent = prefix_views[c]
        columns = pl.ds((c % 2) * half, half)
        out_ref[lane_heads * side + c // 2, :, columns] = (
            jnp.where(side == 0, at(own), at(sent)) * entry(ROW_FIN_P, c)
            + at(keep) * entry(ROW_FIN_K, c)
            + at(take) * entry(ROW_FIN_R, c)
            + above_ref[c, there, :]
        )
        out_ref[lane_heads * (1 - side) + c // 2, :, columns] = (
            at(other_views[c]) * entry(ROW_FIN_O, c) + partner_ref[c // 2, :, columns]
        )


def last_kernel(queries_ref, factors_ref, table_ref, above_ref, partner_ref, *refs, items, heads, layout):
    out_hbm, final_hbm, token_ref, scratch, sems, final_ref, final_sem = refs[-7:]
    token_ref[...] = jnp.zeros_like(token_ref)
    copies = finish_units(queries_ref, factors_ref, refs, items, heads, out_hbm, scratch, sems)
    assemble(table_ref, above_ref, partner_ref, refs, final_ref, **layout)
    copies.append(pltpu.make_async_copy(final_ref, final_hbm, final_sem))
    copies[-1].start()
    for copy in copies:
        copy.wait()


def last(order, units, queries, factor, hidden, heads, table, above, partner, kept, received, owns, sends, others):
    operands, items = finish_operands(units)
    layout = {
        "views": [(operands.view(keep), operands.view(take)) for keep, take in zip(kept, received)],
        "prefix_views": [(operands.view(own), operands.view(sent)) for own, sent in zip(owns, sends)],
        "other_views": [operands.view(other) for other in others],
    }
    tokens = queries.shape[0]
    dv = units[0][2].shape[1]
    share = above.shape[1] // 2
    arrays = [queries, factor, table, above, partner, *operands.arrays, (hidden, pl.ANY)]
    return call(
        order,
        functools.partial(last_kernel, items=items, heads=heads, layout=layout),
        arrays,
        [
            pltpu.HBM((tokens, heads * dv), jnp.bfloat16),
            pltpu.HBM((heads, share, dv), jnp.float32),
            pltpu.VMEM((8, LANES), jnp.float32),
        ],
        "last",
        mib=12,
        scratch=[
            *finish_scratch(units, tokens),
            pltpu.VMEM((heads, share, dv), jnp.float32),
            pltpu.SemaphoreType.DMA,
        ],
        aliases={len(arrays) - 1: 0},
        flops=1e9,
    )[:2]


def shards(queries, keys, values, input_gate, forget_gate, *, blocks):
    heads = input_gate.shape[0]
    dqk, dv = queries.shape[1] // heads, values.shape[1] // heads
    half = dv // 2
    lane_heads = heads // 2
    levels = blocks // 2
    across = [(i, i ^ 1) for i in range(blocks)]
    up = [(i, i + 2) for i in range(blocks - 2)]
    downward = [(i + 2, i) for i in range(blocks - 2)]
    send = lambda value, pairs: lax.ppermute(value, AXIS, pairs)
    order = Order()

    def views_of(arrays):
        return [(array, column) for array in arrays for column in range(0, array.shape[1], half)]

    keys, value, next_value, rows, columns, summary = start(order, input_gate, forget_gate, keys, values)
    partner_summary = send(summary, across)
    chunk, rest = away_memory(order, 0, keys, columns, value, [], heads)
    taken = [send(chunk, across)]
    pair = pack(order, [summary, partner_summary], 2)
    chunk, rest = away_memory(order, 1, keys, columns, next_value, [rest], heads)
    taken.append(send(chunk, across))

    gathered = pair[None]
    rounds = 0
    while gathered.shape[0] < levels:
        reach = gathered.shape[0]
        more = send(gathered, [(i, (i - 2 * reach) % blocks) for i in range(blocks)])
        if rounds == 0:
            values, first_kept = load(order, keys, columns, values, heads)
            kept = views_of([first_kept])
        if rounds == 1:
            arrived = [(send(first_step(order, pair, kept, views_of(taken), half), up), {1: 0})]
            queries, away = memories(order, keys, columns, values, queries, rest, heads)
            taken += [send(a, across) for a in away]
        gathered = pack(order, [gathered, more], min(2 * reach, levels))
        rounds += 1
    kept += views_of(own_memories(order, keys, columns, values, range(1, 2), heads))
    table, parts, top_row = weights(order, gathered)
    received = views_of(taken)

    units = 2 * lane_heads
    chunks = lane_heads + 1
    steps = chunks + levels - 2
    attended, state = [], ()
    sends, owns, others = [], [], []
    hidden = factor = above = None
    final_normal = tops = None
    falls = 0

    def attend(count):
        nonlocal state
        for _ in range(count):
            if len(attended) < heads:
                result, *state = attention(
                    order, len(attended), queries, keys, values, rows, columns, parts, state
                )
                attended.append(result)

    def exchange():
        to_send, own = prefixes(order, table, len(owns), arrived, kept, received, levels, half)
        sends.append(to_send)
        owns.append(own)
        others.append(send(to_send, across))

    def fall():
        nonlocal falls, above
        falls += 1
        above = send(
            down(order, table, falls, levels, kept, received, above, dqk // levels, half), downward
        )

    def units_of(memories, base, chunk):
        return [
            (base + unit // 2, unit % 2, attended[base + unit // 2], views_of(memories)[unit])
            for unit in (2 * chunk - 1, 2 * chunk)
            if 0 <= unit < units
        ]

    finished = [0, 0]

    def put(*which):
        nonlocal hidden
        wanted = []
        for i in which:
            wanted += units_of((owns, others)[i], (0, lane_heads)[i], finished[i])
            finished[i] += 1
        hidden = finish(order, wanted, queries, factor, hidden, heads)

    plan = {1: "kaaa", 2: "aa3aa4", 3: "apFd", 4: "wpod", 5: "pwod", 6: "pwo"}
    for step in range(1, steps):
        value, slots = chain_step(order, table, step, kept, received, arrived[-1], levels, half)
        arrived.append((send(value, up), slots))
        for what in plan.get(step, ""):
            if what == "a":
                attend(1)
            elif what == "k":
                kept += views_of(own_memories(order, keys, columns, values, range(2, lane_heads), heads))
            elif what in "234":
                wait(order, taken[int(what)])
            elif what == "f":
                final_normal, tops = finals(order, gathered)
            elif what == "F" and len(attended) == heads:
                factor = factors(order, columns, top_row, *state, heads, dqk)
            elif what == "p" and len(owns) + levels - 2 < step:
                exchange()
            elif what == "d" and falls < levels - 1:
                fall()
            elif what in "wo" and factor is not None and finished["wo".index(what)] < len(owns):
                put("wo".index(what))
            elif what == "b" and min(finished) < len(owns):
                put(0, 1)
    attend(heads)
    if factor is None:
        factor = factors(order, columns, top_row, *state, heads, dqk)
    while len(owns) < chunks:
        exchange()
    while falls < levels - 1:
        fall()
    partner = send(outgoing(order, table, kept, received, above), across)
    if final_normal is None:
        final_normal, tops = finals(order, gathered)
    while finished[0] < chunks:
        put(0)
    while finished[1] < chunks - 1:
        put(1)
    hidden, final_memory = last(
        order, units_of(others, lane_heads, chunks - 1), queries, factor, hidden, heads, table, above, partner,
        kept, received, views_of(owns), views_of(sends), views_of(others),
    )
    return hidden, final_memory, final_normal, tops.reshape(heads)


def solution(mesh):
    token_spec = P(("seq", "ctx"), None)
    gate_spec = P(None, ("seq", "ctx"))
    return jax.shard_map(
        functools.partial(shards, blocks=mesh.shape["ctx"]),
        mesh=mesh,
        in_specs=(token_spec, token_spec, token_spec, gate_spec, gate_spec),
        out_specs=(token_spec, P("seq", "ctx", None), P("seq", "ctx"), P("seq")),
        check_vma=False,
    )
```

time: 142 us -> 122 us (0.86)
  starting transfers between devices: 64.7 us -> 47.8 us
  waiting for transfers between devices: 13.8 us -> 21.6 us
  local copies, waits for them, and re-layouts: 5.79 us -> 0 us
  Pallas kernels: 54.4 us -> 50.6 us
    ppermute x27 -> x24, starting transfers between devices: 64.7 us -> 47.8 us  [shards(): send = lambda value, pairs: lax.ppermute(value, AXIS, pairs)]
    ppermute x27 -> x24, waiting for transfers between devices: 13.8 us -> 21.6 us  [shards(): send = lambda value, pairs: lax.ppermute(value, AXIS, pairs)]
    unnamed x66 -> x0, local copies, waits for them, and re-layouts: 4.5 us -> none
    pallas_call x43 -> x49, Pallas kernels: 54.4 us -> 50.6 us  [call(): pl.pallas_call(body, in_specs=in_specs, out_specs=out_specs, out_shape=li...]
  transfers between devices with their start and end apart: 27 -> 24, of which waited for: 8 -> 10; matrix products, arithmetic and copies ran while one was open for 1% -> 0% of each run, Pallas kernels for 36% -> 37%
where the time goes in v3:
time: 122 us; the launch traced here: 121 us
  Pallas kernels  50.6 us (41%)
  starting transfers between devices  47.8 us (39%)
  waiting for transfers between devices  21.6 us (18%)
  between operations  1.3 us (1%)
    pallas_call x49, Pallas kernels, call(): pl.pallas_call(body, in_specs=in_specs, out_specs=out_specs, out_shape=li...  50.6 us
    ppermute x24, starting transfers between devices, shards(): send = lambda value, pairs: lax.ppermute(value, AXIS, pairs)  47.8 us
    ppermute x24, waiting for transfers between devices, shards(): send = lambda value, pairs: lax.ppermute(value, AXIS, pairs)  21.6 us
  transfers between devices with their start and end apart: 24, of which 10 were waited for; matrix products, arithmetic and copies ran while one was open for 0% of the time, Pallas kernels for 37%

profile of v3, /device:TPU:0, one launch (start us, length us, event | category | flops | bytes accessed | tf_op | source)
XLA Modules:
  0.0 121.2 jit_solution(13672032099010197076)
XLA Ops:
  0.6 3.1 %start.1 = (bf16[1024,2048]{1,0:T(8,128)(2,1)S(1)}, bf16[1024,512]{1,0:T(8,128)(2,1)S(1)}, bf16[1024,512]{1,0:T(8,128)(2,1)S(1)}, f32[8,1024]{1,0:T(8,128)S(1)},...) custom-call(f32[8,1024]{1,0:T(8,128)} %refs_0_.1, f32[8,1024]{1,0:T(8,128)} %refs_1_.1, bf16[1024,2048]{1,0:T(8,128)(2,1)} %refs_2_.2, ...), custom_call_target="tpu_custom_call" | custom-call | flops 2000000000 | bytes 5000000 | tf_op jit(solution)/shard_map/start/pallas_call | solution.py:43
  3.7 3.0 %collective-permute-start = (f32[8,384]{1,0:T(8,128)S(1)}, f32[8,384]{1,0:T(8,128)S(1)}, u32[]{:S(2)}, u32[]{:S(2)}) collective-permute-start(f32[8,384]{1,0:T(8,128)S(1)} %get-tuple-element.86.refs_3_.refs_0_), channel_id=1, source_target_pairs={{0,4},{4,0},{8,12},{12,8},{16,20},{20,16},{24,28},{28,24},{1,5},{5... | collective-permute-start | bytes 36872 | tf_op jit(solution)/shard_map/ppermute | solution.py:941
  6.8 0.8 away_memory.2
  7.6 0.8 collective-permute-done.refs_1_
  8.4 0.8 away_memory.3
  9.2 2.2 %collective-permute-start.4 = (f32[256,512]{1,0:T(8,128)S(1)}, f32[256,512]{1,0:T(8,128)S(1)}, u32[]{:S(2)}, u32[]{:S(2)}) collective-permute-start(f32[256,512]{1,0:T(8,128)S(1)} %get-tuple-element.98), channel_id=1, source_target_pairs={{0,4},{4,0},{8,12},{12,8},{16,20},{20,16},{24,28},{28,24},{1,5},{5... | collective-permute-start | bytes 1572872 | tf_op jit(solution)/shard_map/ppermute | solution.py:941
  11.4 3.6 %collective-permute-start.2 = (f32[1,2,8,384]{3,2,1,0:T(8,128)S(1)}, f32[1,2,8,384]{3,2,1,0:T(8,128)S(1)}, u32[]{:S(2)}, u32[]{:S(2)}) collective-permute-start(f32[1,2,8,384]{3,2,1,0:T(8,128)S(1)} %bitcast.2), channel_id=1, source_target_pairs={{0,24},{4,28},{8,0},{12,4},{16,8},{20,12},{24,16},{28,20},{1,25},{... | collective-permute-start | bytes 73736 | tf_op jit(solution)/shard_map/ppermute | solution.py:941
  15.0 3.5 %load.1 = (bf16[1024,4096]{1,0:T(8,128)(2,1)S(1)}, f32[256,512]{1,0:T(8,128)S(1)}) custom-call(bf16[1024,2048]{1,0:T(8,128)(2,1)S(1)} %get-tuple-element.82.refs_0_.refs_1_, f32[1024,128]{1,0:T(8,128)S(1)} %get-tuple-element.83.refs_1_.refs_4_.refs_0_, bf16[1024,4096]{1,0:T(8,128)(2,1)} %refs_2_.3, f32[256,256]{1,0:T(8,128)S(1)} %get-tuple-element.88.refs_3_.refs_4_), custom_call_target="tpu_custom_call" | custom-call | flops 536870912 | bytes 8000000 | tf_op jit(solution)/shard_map/load/pallas_call | solution.py:43
  18.8 1.7 %collective-permute-start.5 = (f32[256,256]{1,0:T(8,128)S(1)}, f32[256,256]{1,0:T(8,128)S(1)}, u32[]{:S(2)}, u32[]{:S(2)}) collective-permute-start(f32[256,256]{1,0:T(8,128)S(1)} %chain.7.refs_5_), channel_id=1, source_target_pairs={{0,8},{4,12},{8,16},{12,20},{16,24},{20,28},{1,9},{5,13},{9,17},{1... | collective-permute-start | bytes 786440 | tf_op jit(solution)/shard_map/ppermute | solution.py:941
  20.5 2.9 %collective-permute-start.3 = (f32[2,2,8,384]{3,2,1,0:T(8,128)S(1)}, f32[2,2,8,384]{3,2,1,0:T(8,128)S(1)}, u32[]{:S(2)}, u32[]{:S(2)}) collective-permute-start(f32[2,2,8,384]{3,2,1,0:T(8,128)S(1)} %pack.4.refs_3_.refs_0_), channel_id=1, source_target_pairs={{0,16},{4,20},{8,24},{12,28},{16,0},{20,4},{24,8},{28,12},{1,17},{... | collective-permute-start | bytes 147464 | tf_op jit(solution)/shard_map/ppermute | solution.py:941
  23.4 3.3 %memories_away.1 = (bf16[1024,2048]{1,0:T(8,128)(2,1)S(1)}, f32[256,512]{1,0:T(8,128)S(1)}, f32[256,512]{1,0:T(8,128)S(1)}, f32[256,256]{1,0:T(8,128)S(1)}) custom-call(bf16[1024,2048]{1,0:T(8,128)(2,1)S(1)} %get-tuple-element.82.refs_0_.refs_1_, f32[1024,128]{1,0:T(8,128)S(1)} %get-tuple-element.83.refs_1_.refs_4_.refs_0_, ...), custom_call_target="tpu_custom_call" | custom-call | flops 1073741824 | bytes 4000000 | tf_op jit(solution)/shard_map/memories_away/pallas_call | solution.py:43
  26.7 0.4 collective-permute-start.6
  27.1 1.6 %collective-permute-start.8 = (f32[256,512]{1,0:T(8,128)S(1)}, f32[256,512]{1,0:T(8,128)S(1)}, u32[]{:S(2)}, u32[]{:S(2)}) collective-permute-start(f32[256,512]{1,0:T(8,128)S(1)} %get-tuple-element.112), channel_id=1, source_target_pairs={{0,4},{4,0},{8,12},{12,8},{16,20},{20,16},{24,28},{28,24},{1,5},{5... | collective-permute-start | bytes 1572872 | tf_op jit(solution)/shard_map/ppermute | solution.py:941
  28.8 0.4 collective-permute-start.10
  29.2 0.8 memories_own.2.refs_1_.refs_3_.refs_4_.refs_5_.refs_6_.refs_10_
  29.9 0.5 weights.1
  30.7 1.4 %memories_own.3 = (f32[256,512]{1,0:T(8,128)S(1)}, f32[256,512]{1,0:T(8,128)S(1)}) custom-call(bf16[1024,2048]{1,0:T(8,128)(2,1)S(1)} %get-tuple-element.82.refs_0_.refs_1_, f32[1024,128]{1,0:T(8,128)S(1)} %get-tuple-element.83.refs_1_.refs_4_.refs_0_, bf16[1024,4096]{1,0:T(8,128)(2,1)S(1)} %get-tuple-element.89.refs_2_, f32[256,512]{1,0:T(8,128)S(1)} %chain.8.refs_3_), custom_call_target="tpu_custom_call" | custom-call | flops 1073741824 | bytes 4000000 | tf_op jit(solution)/shard_map/memories_own/pallas_call | solution.py:43
  32.0 1.3 %collective-permute-start.7 = (f32[256,512]{1,0:T(8,128)S(1)}, f32[256,512]{1,0:T(8,128)S(1)}, u32[]{:S(2)}, u32[]{:S(2)}) collective-permute-start(f32[256,512]{1,0:T(8,128)S(1)} %chain.8.refs_3_), channel_id=1, source_target_pairs={{0,8},{4,12},{8,16},{12,20},{16,24},{20,28},{1,9},{5,13},{9,17},{1... | collective-permute-start | bytes 1572872 | tf_op jit(solution)/shard_map/ppermute | solution.py:941
  33.4 2.1 %attention.8 = (bf16[1024,512]{1,0:T(8,128)(2,1)S(1)}, f32[1024,128]{1,0:T(8,128)S(1)}, f32[1024,128]{1,0:T(8,128)S(1)}) custom-call(bf16[1024,2048]{1,0:T(8,128)(2,1)S(1)} %get-tuple-element.92.refs_0_, bf16[1024,2048]{1,0:T(8,128)(2,1)S(1)} %get-tuple-element.82.refs_0_.refs_1_, bf16[1024,4096]{1,0:T(8,128)(2,1)S(1)} %get-tuple-element.89.refs_2_, ...), custom_call_target="tpu_custom_call" | custom-call | flops 2415919104 | bytes 1000000 | tf_op jit(solution)/shard_map/attention/pallas_call | solution.py:43
  35.5 2.1 %attention.9 = (bf16[1024,512]{1,0:T(8,128)(2,1)S(1)}, f32[1024,128]{1,0:T(8,128)S(1)}, f32[1024,128]{1,0:T(8,128)S(1)}) custom-call(bf16[1024,2048]{1,0:T(8,128)(2,1)S(1)} %get-tuple-element.92.refs_0_, bf16[1024,2048]{1,0:T(8,128)(2,1)S(1)} %get-tuple-element.82.refs_0_.refs_1_, bf16[1024,4096]{1,0:T(8,128)(2,1)S(1)} %get-tuple-element.89.refs_2_, ...), custom_call_target="tpu_custom_call" | custom-call | flops 2415919104 | bytes 1000000 | tf_op jit(solution)/shard_map/attention/pallas_call | solution.py:43
  37.6 2.1 %attention.10 = (bf16[1024,512]{1,0:T(8,128)(2,1)S(1)}, f32[1024,128]{1,0:T(8,128)S(1)}, f32[1024,128]{1,0:T(8,128)S(1)}) custom-call(bf16[1024,2048]{1,0:T(8,128)(2,1)S(1)} %get-tuple-element.92.refs_0_, bf16[1024,2048]{1,0:T(8,128)(2,1)S(1)} %get-tuple-element.82.refs_0_.refs_1_, bf16[1024,4096]{1,0:T(8,128)(2,1)S(1)} %get-tuple-element.89.refs_2_, ...), custom_call_target="tpu_custom_call" | custom-call | flops 2415919104 | bytes 1000000 | tf_op jit(solution)/shard_map/attention/pallas_call | solution.py:43
  39.7 1.9 %collective-permute-done.6.refs_2_.refs_4_.refs_5_.refs_6_.refs_11_ = f32[256,512]{1,0:T(8,128)S(1)} collective-permute-done((f32[256,512]{1,0:T(8,128)S(1)}, f32[256,512]{1,0:T(8,128)S(1)}, u32[]{:S(2)}, u32[]{:S(2)}) %collective-permute-start.6) | collective-permute-done | bytes 524320 | tf_op jit(solution)/shard_map/ppermute | solution.py:941
  41.7 0.3 chain.9.refs_8_
  42.0 4.6 %collective-permute-start.9 = (f32[256,512]{1,0:T(8,128)S(1)}, f32[256,512]{1,0:T(8,128)S(1)}, u32[]{:S(2)}, u32[]{:S(2)}) collective-permute-start(f32[256,512]{1,0:T(8,128)S(1)} %chain.9.refs_8_), channel_id=1, source_target_pairs={{0,8},{4,12},{8,16},{12,20},{16,24},{20,28},{1,9},{5,13},{9,17},{1... | collective-permute-start | bytes 1572872 | tf_op jit(solution)/shard_map/ppermute | solution.py:941
  46.6 2.1 %attention.11 = (bf16[1024,512]{1,0:T(8,128)(2,1)S(1)}, f32[1024,128]{1,0:T(8,128)S(1)}, f32[1024,128]{1,0:T(8,128)S(1)}) custom-call(bf16[1024,2048]{1,0:T(8,128)(2,1)S(1)} %get-tuple-element.92.refs_0_, bf16[1024,2048]{1,0:T(8,128)(2,1)S(1)} %get-tuple-element.82.refs_0_.refs_1_, bf16[1024,4096]{1,0:T(8,128)(2,1)S(1)} %get-tuple-element.89.refs_2_, ...), custom_call_target="tpu_custom_call" | custom-call | flops 2415919104 | bytes 1000000 | tf_op jit(solution)/shard_map/attention/pallas_call | solution.py:43
  48.7 2.1 %attention.12 = (bf16[1024,512]{1,0:T(8,128)(2,1)S(1)}, f32[1024,128]{1,0:T(8,128)S(1)}, f32[1024,128]{1,0:T(8,128)S(1)}) custom-call(bf16[1024,2048]{1,0:T(8,128)(2,1)S(1)} %get-tuple-element.92.refs_0_, bf16[1024,2048]{1,0:T(8,128)(2,1)S(1)} %get-tuple-element.82.refs_0_.refs_1_, bf16[1024,4096]{1,0:T(8,128)(2,1)S(1)} %get-tuple-element.89.refs_2_, ...), custom_call_target="tpu_custom_call" | custom-call | flops 2415919104 | bytes 1000000 | tf_op jit(solution)/shard_map/attention/pallas_call | solution.py:43
  50.8 1.0 collective-permute-done.8.refs_0_.refs_2_.refs_7_.refs_4_.refs_5_.refs_13_
  51.9 2.1 %attention.13 = (bf16[1024,512]{1,0:T(8,128)(2,1)S(1)}, f32[1024,128]{1,0:T(8,128)S(1)}, f32[1024,128]{1,0:T(8,128)S(1)}) custom-call(bf16[1024,2048]{1,0:T(8,128)(2,1)S(1)} %get-tuple-element.92.refs_0_, bf16[1024,2048]{1,0:T(8,128)(2,1)S(1)} %get-tuple-element.82.refs_0_.refs_1_, bf16[1024,4096]{1,0:T(8,128)(2,1)S(1)} %get-tuple-element.89.refs_2_, ...), custom_call_target="tpu_custom_call" | custom-call | flops 2415919104 | bytes 1000000 | tf_op jit(solution)/shard_map/attention/pallas_call | solution.py:43
  54.0 2.1 %attention.14 = (bf16[1024,512]{1,0:T(8,128)(2,1)S(1)}, f32[1024,128]{1,0:T(8,128)S(1)}, f32[1024,128]{1,0:T(8,128)S(1)}) custom-call(bf16[1024,2048]{1,0:T(8,128)(2,1)S(1)} %get-tuple-element.92.refs_0_, bf16[1024,2048]{1,0:T(8,128)(2,1)S(1)} %get-tuple-element.82.refs_0_.refs_1_, bf16[1024,4096]{1,0:T(8,128)(2,1)S(1)} %get-tuple-element.89.refs_2_, ...), custom_call_target="tpu_custom_call" | custom-call | flops 2415919104 | bytes 1000000 | tf_op jit(solution)/shard_map/attention/pallas_call | solution.py:43
  56.1 0.4 chain.10.refs_8_
  56.5 2.5 %collective-permute-start.13 = (f32[256,512]{1,0:T(8,128)S(1)}, f32[256,512]{1,0:T(8,128)S(1)}, u32[]{:S(2)}, u32[]{:S(2)}) collective-permute-start(f32[256,512]{1,0:T(8,128)S(1)} %chain.10.refs_8_), channel_id=1, source_target_pairs={{0,8},{4,12},{8,16},{12,20},{16,24},{20,28},{1,9},{5,13},{9,17},{1... | collective-permute-start | bytes 1572872 | tf_op jit(solution)/shard_map/ppermute | solution.py:941
  59.0 2.1 %attention.15 = (bf16[1024,512]{1,0:T(8,128)(2,1)S(1)}, f32[1024,128]{1,0:T(8,128)S(1)}, f32[1024,128]{1,0:T(8,128)S(1)}) custom-call(bf16[1024,2048]{1,0:T(8,128)(2,1)S(1)} %get-tuple-element.92.refs_0_, bf16[1024,2048]{1,0:T(8,128)(2,1)S(1)} %get-tuple-element.82.refs_0_.refs_1_, bf16[1024,4096]{1,0:T(8,128)(2,1)S(1)} %get-tuple-element.89.refs_2_, ...), custom_call_target="tpu_custom_call" | custom-call | flops 2415919104 | bytes 1000000 | tf_op jit(solution)/shard_map/attention/pallas_call | solution.py:43
  61.3 1.0 factors.1.refs_10_.refs_1_
  62.4 1.3 %collective-permute-start.11 = (f32[8,64,256]{2,1,0:T(8,128)S(1)}, f32[8,64,256]{2,1,0:T(8,128)S(1)}, u32[]{:S(2)}, u32[]{:S(2)}) collective-permute-start(f32[8,64,256]{2,1,0:T(8,128)S(1)} %down.3.refs_8_), channel_id=1, source_target_pairs={{8,0},{12,4},{16,8},{20,12},{24,16},{28,20},{9,1},{13,5},{17,9},{2... | collective-permute-start | bytes 1572872 | tf_op jit(solution)/shard_map/ppermute | solution.py:941
  63.7 0.9 collective-permute-start.12
  64.6 3.8 %collective-permute-done.13.refs_7_.refs_3_.refs_2_.refs_1_ = f32[256,512]{1,0:T(8,128)S(1)} collective-permute-done((f32[256,512]{1,0:T(8,128)S(1)}, f32[256,512]{1,0:T(8,128)S(1)}, u32[]{:S(2)}, u32[]{:S(2)}) %collective-permute-start.13) | collective-permute-done | bytes 524320 | tf_op jit(solution)/shard_map/ppermute | solution.py:941
  68.4 0.3 chain.11.refs_4_
  68.8 4.4 %collective-permute-start.16 = (f32[256,512]{1,0:T(8,128)S(1)}, f32[256,512]{1,0:T(8,128)S(1)}, u32[]{:S(2)}, u32[]{:S(2)}) collective-permute-start(f32[256,512]{1,0:T(8,128)S(1)} %chain.11.refs_4_), channel_id=1, source_target_pairs={{0,8},{4,12},{8,16},{12,20},{16,24},{20,28},{1,9},{5,13},{9,17},{1... | collective-permute-start | bytes 1572872 | tf_op jit(solution)/shard_map/ppermute | solution.py:941
  73.2 1.1 finish.9
  74.3 0.3 prefix.6
  74.6 1.0 collective-permute-start.15
  75.5 1.1 finish.10
  76.8 1.5 %collective-permute-start.14 = (f32[8,64,256]{2,1,0:T(8,128)S(1)}, f32[8,64,256]{2,1,0:T(8,128)S(1)}, u32[]{:S(2)}, u32[]{:S(2)}) collective-permute-start(f32[8,64,256]{2,1,0:T(8,128)S(1)} %down.4.refs_6_), channel_id=1, source_target_pairs={{8,0},{12,4},{16,8},{20,12},{24,16},{28,20},{9,1},{13,5},{17,9},{2... | collective-permute-start | bytes 1572872 | tf_op jit(solution)/shard_map/ppermute | solution.py:941
  78.4 3.3 %collective-permute-done.16.refs_5_.refs_3_.refs_2_.refs_1_ = f32[256,512]{1,0:T(8,128)S(1)} collective-permute-done((f32[256,512]{1,0:T(8,128)S(1)}, f32[256,512]{1,0:T(8,128)S(1)}, u32[]{:S(2)}, u32[]{:S(2)}) %collective-permute-start.16) | collective-permute-done | bytes 524320 | tf_op jit(solution)/shard_map/ppermute | solution.py:941
  81.9 4.4 %collective-permute-start.18 = (f32[256,512]{1,0:T(8,128)S(1)}, f32[256,512]{1,0:T(8,128)S(1)}, u32[]{:S(2)}, u32[]{:S(2)}) collective-permute-start(f32[256,512]{1,0:T(8,128)S(1)} %chain.12.refs_7_), channel_id=1, source_target_pairs={{0,8},{4,12},{8,16},{12,20},{16,24},{20,28},{1,9},{5,13},{9,17},{1... | collective-permute-start | bytes 1572872 | tf_op jit(solution)/shard_map/ppermute | solution.py:941
  86.7 1.0 collective-permute-start.20
  87.7 1.5 %finish.11 = (bf16[1024,4096]{1,0:T(8,128)(2,1)}, f32[8,128]{1,0:T(8,128)S(1)}) custom-call(bf16[1024,2048]{1,0:T(8,128)(2,1)S(1)} %get-tuple-element.92.refs_0_, f32[1024,128]{1,0:T(8,128)S(1)} %factors.1.refs_10_.refs_1_, bf16[1024,512]{1,0:T(8,128)(2,1)S(1)} %get-tuple-element.122.refs_2_, ...), custom_call_target="tpu_custom_call", output_to_operand_aliasing={{0}: (5, {})} | custom-call | flops 1600000000 | bytes 1000000 | tf_op jit(solution)/shard_map/finish/pallas_call | solution.py:43
  89.2 1.5 %finish.12 = (bf16[1024,4096]{1,0:T(8,128)(2,1)}, f32[8,128]{1,0:T(8,128)S(1)}) custom-call(bf16[1024,2048]{1,0:T(8,128)(2,1)S(1)} %get-tuple-element.92.refs_0_, f32[1024,128]{1,0:T(8,128)S(1)} %factors.1.refs_10_.refs_1_, bf16[1024,512]{1,0:T(8,128)(2,1)S(1)} %get-tuple-element.120.refs_2_, ...), custom_call_target="tpu_custom_call", output_to_operand_aliasing={{0}: (5, {})} | custom-call | flops 1600000000 | bytes 1000000 | tf_op jit(solution)/shard_map/finish/pallas_call | solution.py:43
  90.8 1.3 %collective-permute-start.17 = (f32[8,64,256]{2,1,0:T(8,128)S(1)}, f32[8,64,256]{2,1,0:T(8,128)S(1)}, u32[]{:S(2)}, u32[]{:S(2)}) collective-permute-start(f32[8,64,256]{2,1,0:T(8,128)S(1)} %down.5.refs_4_), channel_id=1, source_target_pairs={{8,0},{12,4},{16,8},{20,12},{24,16},{28,20},{9,1},{13,5},{17,9},{2... | collective-permute-start | bytes 1572872 | tf_op jit(solution)/shard_map/ppermute | solution.py:941
  92.1 1.8 %collective-permute-done.18.refs_3_.refs_2_ = f32[256,512]{1,0:T(8,128)S(1)} collective-permute-done((f32[256,512]{1,0:T(8,128)S(1)}, f32[256,512]{1,0:T(8,128)S(1)}, u32[]{:S(2)}, u32[]{:S(2)}) %collective-permute-start.18) | collective-permute-done | bytes 524320 | tf_op jit(solution)/shard_map/ppermute | solution.py:941
  94.1 4.4 %collective-permute-start.19 = (f32[256,256]{1,0:T(8,128)S(1)}, f32[256,256]{1,0:T(8,128)S(1)}, u32[]{:S(2)}, u32[]{:S(2)}) collective-permute-start(f32[256,256]{1,0:T(8,128)S(1)} %chain.13.refs_7_), channel_id=1, source_target_pairs={{0,8},{4,12},{8,16},{12,20},{16,24},{20,28},{1,9},{5,13},{9,17},{1... | collective-permute-start | bytes 786440 | tf_op jit(solution)/shard_map/ppermute | solution.py:941
  98.8 1.1 collective-permute-start.23
  99.9 1.5 %finish.13 = (bf16[1024,4096]{1,0:T(8,128)(2,1)}, f32[8,128]{1,0:T(8,128)S(1)}) custom-call(bf16[1024,2048]{1,0:T(8,128)(2,1)S(1)} %get-tuple-element.92.refs_0_, f32[1024,128]{1,0:T(8,128)S(1)} %factors.1.refs_10_.refs_1_, bf16[1024,512]{1,0:T(8,128)(2,1)S(1)} %get-tuple-element.129.refs_4_.refs_2_, ...), custom_call_target="tpu_custom_call", output_to_operand_aliasing={{0}: (5, {})} | custom-call | flops 1600000000 | bytes 1000000 | tf_op jit(solution)/shard_map/finish/pallas_call | solution.py:43
  101.4 1.5 %finish.14 = (bf16[1024,4096]{1,0:T(8,128)(2,1)}, f32[8,128]{1,0:T(8,128)S(1)}) custom-call(bf16[1024,2048]{1,0:T(8,128)(2,1)S(1)} %get-tuple-element.92.refs_0_, f32[1024,128]{1,0:T(8,128)S(1)} %factors.1.refs_10_.refs_1_, bf16[1024,512]{1,0:T(8,128)(2,1)S(1)} %get-tuple-element.128.refs_4_.refs_2_, ...), custom_call_target="tpu_custom_call", output_to_operand_aliasing={{0}: (5, {})} | custom-call | flops 1600000000 | bytes 1000000 | tf_op jit(solution)/shard_map/finish/pallas_call | solution.py:43
  103.2 1.1 collective-permute-start.21
  104.3 1.0 collective-permute-start.22
  105.3 0.9 finals.1
  106.2 1.5 %finish.15 = (bf16[1024,4096]{1,0:T(8,128)(2,1)}, f32[8,128]{1,0:T(8,128)S(1)}) custom-call(bf16[1024,2048]{1,0:T(8,128)(2,1)S(1)} %get-tuple-element.92.refs_0_, f32[1024,128]{1,0:T(8,128)S(1)} %factors.1.refs_10_.refs_1_, bf16[1024,512]{1,0:T(8,128)(2,1)S(1)} %get-tuple-element.137.refs_4_.refs_2_, ...), custom_call_target="tpu_custom_call", output_to_operand_aliasing={{0}: (5, {})} | custom-call | flops 1600000000 | bytes 1000000 | tf_op jit(solution)/shard_map/finish/pallas_call | solution.py:43
  107.7 1.1 finish.16
  108.8 4.7 %collective-permute-done.23.refs_3_.refs_29_ = f32[256,512]{1,0:T(8,128)S(1)} collective-permute-done((f32[256,512]{1,0:T(8,128)S(1)}, f32[256,512]{1,0:T(8,128)S(1)}, u32[]{:S(2)}, u32[]{:S(2)}) %collective-permute-start.23) | collective-permute-done | bytes 524320 | tf_op jit(solution)/shard_map/ppermute | solution.py:941
  113.5 1.4 %finish.17 = (bf16[1024,4096]{1,0:T(8,128)(2,1)}, f32[8,128]{1,0:T(8,128)S(1)}) custom-call(bf16[1024,2048]{1,0:T(8,128)(2,1)S(1)} %get-tuple-element.92.refs_0_, f32[1024,128]{1,0:T(8,128)S(1)} %factors.1.refs_10_.refs_1_, bf16[1024,512]{1,0:T(8,128)(2,1)S(1)} %get-tuple-element.136.refs_4_.refs_2_, ...), custom_call_target="tpu_custom_call", output_to_operand_aliasing={{0}: (5, {})} | custom-call | flops 1600000000 | bytes 1000000 | tf_op jit(solution)/shard_map/finish/pallas_call | solution.py:43
  114.9 1.4 %collective-permute-done.21.refs_4_ = f32[4,32,512]{2,1,0:T(8,128)S(1)} collective-permute-done((f32[4,32,512]{2,1,0:T(8,128)S(1)}, f32[4,32,512]{2,1,0:T(8,128)S(1)}, u32[]{:S(2)}, u32[]{:S(2)}) %collective-permute-start.21) | collective-permute-done | bytes 262176 | tf_op jit(solution)/shard_map/ppermute | solution.py:941
  116.3 2.8 %collective-permute-done.22.refs_6_ = f32[256,256]{1,0:T(8,128)S(1)} collective-permute-done((f32[256,256]{1,0:T(8,128)S(1)}, f32[256,256]{1,0:T(8,128)S(1)}, u32[]{:S(2)}, u32[]{:S(2)}) %collective-permute-start.22) | collective-permute-done | bytes 262176 | tf_op jit(solution)/shard_map/ppermute | solution.py:941
  119.1 2.0 %last.1 = (bf16[1024,4096]{1,0:T(8,128)(2,1)}, f32[8,32,512]{2,1,0:T(8,128)}, f32[8,128]{1,0:T(8,128)}) custom-call(bf16[1024,2048]{1,0:T(8,128)(2,1)S(1)} %get-tuple-element.92.refs_0_, f32[1024,128]{1,0:T(8,128)S(1)} %factors.1.refs_10_.refs_1_, f32[24,128]{1,0:T(8,128)S(1)} %get-tuple-element.97.refs_0_.refs_2_, ...), custom_call_target="tpu_custom_call", output_to_operand_aliasing={{0}: (30, {})} | custom-call | flops 1000000000 | bytes 1000000 | tf_op jit(solution)/shard_map/last/pallas_call | solution.py:43
  (33 shorter events, 2.6 us)
Async XLA Ops:
  3.7 4.7 %collective-permute-start = (f32[8,384]{1,0:T(8,128)S(1)}, f32[8,384]{1,0:T(8,128)S(1)}, u32[]{:S(2)}, u32[]{:S(2)}) collective-permute-start(f32[8,384]{1,0:T(8,128)S(1)} %get-tuple-element.86.refs_3_.refs_0_), channel_id=1, source_target_pairs={{0,4},{4,0},{8,12},{12,8},{16,20},{20,16},{24,28},{28,24},{1,5},{5... | collective-permute-start | bytes 36872 | tf_op jit(solution)/shard_map/ppermute | solution.py:941
  7.5 11.1 %collective-permute-start.1 = (f32[256,256]{1,0:T(8,128)S(1)}, f32[256,256]{1,0:T(8,128)S(1)}, u32[]{:S(2)}, u32[]{:S(2)}) collective-permute-start(f32[256,256]{1,0:T(8,128)S(1)} %get-tuple-element.91), channel_id=1, source_target_pairs={{0,4},{4,0},{8,12},{12,8},{16,20},{20,16},{24,28},{28,24},{1,5},{5... | collective-permute-start | bytes 786440 | tf_op jit(solution)/shard_map/ppermute | solution.py:941
  9.2 21.2 %collective-permute-start.4 = (f32[256,512]{1,0:T(8,128)S(1)}, f32[256,512]{1,0:T(8,128)S(1)}, u32[]{:S(2)}, u32[]{:S(2)}) collective-permute-start(f32[256,512]{1,0:T(8,128)S(1)} %get-tuple-element.98), channel_id=1, source_target_pairs={{0,4},{4,0},{8,12},{12,8},{16,20},{20,16},{24,28},{28,24},{1,5},{5... | collective-permute-start | bytes 1572872 | tf_op jit(solution)/shard_map/ppermute | solution.py:941
  11.4 7.1 %collective-permute-start.2 = (f32[1,2,8,384]{3,2,1,0:T(8,128)S(1)}, f32[1,2,8,384]{3,2,1,0:T(8,128)S(1)}, u32[]{:S(2)}, u32[]{:S(2)}) collective-permute-start(f32[1,2,8,384]{3,2,1,0:T(8,128)S(1)} %bitcast.2), channel_id=1, source_target_pairs={{0,24},{4,28},{8,0},{12,4},{16,8},{20,12},{24,16},{28,20},{1,25},{... | collective-permute-start | bytes 73736 | tf_op jit(solution)/shard_map/ppermute | solution.py:941
  18.8 11.6 %collective-permute-start.5 = (f32[256,256]{1,0:T(8,128)S(1)}, f32[256,256]{1,0:T(8,128)S(1)}, u32[]{:S(2)}, u32[]{:S(2)}) collective-permute-start(f32[256,256]{1,0:T(8,128)S(1)} %chain.7.refs_5_), channel_id=1, source_target_pairs={{0,8},{4,12},{8,16},{12,20},{16,24},{20,28},{1,9},{5,13},{9,17},{1... | collective-permute-start | bytes 786440 | tf_op jit(solution)/shard_map/ppermute | solution.py:941
  20.5 8.3 %collective-permute-start.3 = (f32[2,2,8,384]{3,2,1,0:T(8,128)S(1)}, f32[2,2,8,384]{3,2,1,0:T(8,128)S(1)}, u32[]{:S(2)}, u32[]{:S(2)}) collective-permute-start(f32[2,2,8,384]{3,2,1,0:T(8,128)S(1)} %pack.4.refs_3_.refs_0_), channel_id=1, source_target_pairs={{0,16},{4,20},{8,24},{12,28},{16,0},{20,4},{24,8},{28,12},{1,17},{... | collective-permute-start | bytes 147464 | tf_op jit(solution)/shard_map/ppermute | solution.py:941
  26.7 14.9 %collective-permute-start.6 = (f32[256,512]{1,0:T(8,128)S(1)}, f32[256,512]{1,0:T(8,128)S(1)}, u32[]{:S(2)}, u32[]{:S(2)}) collective-permute-start(f32[256,512]{1,0:T(8,128)S(1)} %get-tuple-element.106), channel_id=1, source_target_pairs={{0,4},{4,0},{8,12},{12,8},{16,20},{20,16},{24,28},{28,24},{1,5},{5... | collective-permute-start | bytes 1572872 | tf_op jit(solution)/shard_map/ppermute | solution.py:941
  27.1 24.7 %collective-permute-start.8 = (f32[256,512]{1,0:T(8,128)S(1)}, f32[256,512]{1,0:T(8,128)S(1)}, u32[]{:S(2)}, u32[]{:S(2)}) collective-permute-start(f32[256,512]{1,0:T(8,128)S(1)} %get-tuple-element.112), channel_id=1, source_target_pairs={{0,4},{4,0},{8,12},{12,8},{16,20},{20,16},{24,28},{28,24},{1,5},{5... | collective-permute-start | bytes 1572872 | tf_op jit(solution)/shard_map/ppermute | solution.py:941
  28.8 27.3 %collective-permute-start.10 = (f32[256,256]{1,0:T(8,128)S(1)}, f32[256,256]{1,0:T(8,128)S(1)}, u32[]{:S(2)}, u32[]{:S(2)}) collective-permute-start(f32[256,256]{1,0:T(8,128)S(1)} %get-tuple-element.93.refs_2_), channel_id=1, source_target_pairs={{0,4},{4,0},{8,12},{12,8},{16,20},{20,16},{24,28},{28,24},{1,5},{5... | collective-permute-start | bytes 786440 | tf_op jit(solution)/shard_map/ppermute | solution.py:941
  32.0 9.6 %collective-permute-start.7 = (f32[256,512]{1,0:T(8,128)S(1)}, f32[256,512]{1,0:T(8,128)S(1)}, u32[]{:S(2)}, u32[]{:S(2)}) collective-permute-start(f32[256,512]{1,0:T(8,128)S(1)} %chain.8.refs_3_), channel_id=1, source_target_pairs={{0,8},{4,12},{8,16},{12,20},{16,24},{20,28},{1,9},{5,13},{9,17},{1... | collective-permute-start | bytes 1572872 | tf_op jit(solution)/shard_map/ppermute | solution.py:941
  42.0 14.1 %collective-permute-start.9 = (f32[256,512]{1,0:T(8,128)S(1)}, f32[256,512]{1,0:T(8,128)S(1)}, u32[]{:S(2)}, u32[]{:S(2)}) collective-permute-start(f32[256,512]{1,0:T(8,128)S(1)} %chain.9.refs_8_), channel_id=1, source_target_pairs={{0,8},{4,12},{8,16},{12,20},{16,24},{20,28},{1,9},{5,13},{9,17},{1... | collective-permute-start | bytes 1572872 | tf_op jit(solution)/shard_map/ppermute | solution.py:941
  56.5 11.9 %collective-permute-start.13 = (f32[256,512]{1,0:T(8,128)S(1)}, f32[256,512]{1,0:T(8,128)S(1)}, u32[]{:S(2)}, u32[]{:S(2)}) collective-permute-start(f32[256,512]{1,0:T(8,128)S(1)} %chain.10.refs_8_), channel_id=1, source_target_pairs={{0,8},{4,12},{8,16},{12,20},{16,24},{20,28},{1,9},{5,13},{9,17},{1... | collective-permute-start | bytes 1572872 | tf_op jit(solution)/shard_map/ppermute | solution.py:941
  62.4 14.2 %collective-permute-start.11 = (f32[8,64,256]{2,1,0:T(8,128)S(1)}, f32[8,64,256]{2,1,0:T(8,128)S(1)}, u32[]{:S(2)}, u32[]{:S(2)}) collective-permute-start(f32[8,64,256]{2,1,0:T(8,128)S(1)} %down.3.refs_8_), channel_id=1, source_target_pairs={{8,0},{12,4},{16,8},{20,12},{24,16},{28,20},{9,1},{13,5},{17,9},{2... | collective-permute-start | bytes 1572872 | tf_op jit(solution)/shard_map/ppermute | solution.py:941
  63.7 11.8 %collective-permute-start.12 = (f32[256,256]{1,0:T(8,128)S(1)}, f32[256,256]{1,0:T(8,128)S(1)}, u32[]{:S(2)}, u32[]{:S(2)}) collective-permute-start(f32[256,256]{1,0:T(8,128)S(1)} %get-tuple-element.121.refs_17_), channel_id=1, source_target_pairs={{0,4},{4,0},{8,12},{12,8},{16,20},{20,16},{24,28},{28,24},{1,5},{5... | collective-permute-start | bytes 786440 | tf_op jit(solution)/shard_map/ppermute | solution.py:941
  68.8 12.9 %collective-permute-start.16 = (f32[256,512]{1,0:T(8,128)S(1)}, f32[256,512]{1,0:T(8,128)S(1)}, u32[]{:S(2)}, u32[]{:S(2)}) collective-permute-start(f32[256,512]{1,0:T(8,128)S(1)} %chain.11.refs_4_), channel_id=1, source_target_pairs={{0,8},{4,12},{8,16},{12,20},{16,24},{20,28},{1,9},{5,13},{9,17},{1... | collective-permute-start | bytes 1572872 | tf_op jit(solution)/shard_map/ppermute | solution.py:941
  74.6 14.6 %collective-permute-start.15 = (f32[256,512]{1,0:T(8,128)S(1)}, f32[256,512]{1,0:T(8,128)S(1)}, u32[]{:S(2)}, u32[]{:S(2)}) collective-permute-start(f32[256,512]{1,0:T(8,128)S(1)} %get-tuple-element.127.refs_19_), channel_id=1, source_target_pairs={{0,4},{4,0},{8,12},{12,8},{16,20},{20,16},{24,28},{28,24},{1,5},{5... | collective-permute-start | bytes 1572872 | tf_op jit(solution)/shard_map/ppermute | solution.py:941
  76.8 13.8 %collective-permute-start.14 = (f32[8,64,256]{2,1,0:T(8,128)S(1)}, f32[8,64,256]{2,1,0:T(8,128)S(1)}, u32[]{:S(2)}, u32[]{:S(2)}) collective-permute-start(f32[8,64,256]{2,1,0:T(8,128)S(1)} %down.4.refs_6_), channel_id=1, source_target_pairs={{8,0},{12,4},{16,8},{20,12},{24,16},{28,20},{9,1},{13,5},{17,9},{2... | collective-permute-start | bytes 1572872 | tf_op jit(solution)/shard_map/ppermute | solution.py:941
  81.9 12.0 %collective-permute-start.18 = (f32[256,512]{1,0:T(8,128)S(1)}, f32[256,512]{1,0:T(8,128)S(1)}, u32[]{:S(2)}, u32[]{:S(2)}) collective-permute-start(f32[256,512]{1,0:T(8,128)S(1)} %chain.12.refs_7_), channel_id=1, source_target_pairs={{0,8},{4,12},{8,16},{12,20},{16,24},{20,28},{1,9},{5,13},{9,17},{1... | collective-permute-start | bytes 1572872 | tf_op jit(solution)/shard_map/ppermute | solution.py:941
  86.7 14.7 %collective-permute-start.20 = (f32[256,512]{1,0:T(8,128)S(1)}, f32[256,512]{1,0:T(8,128)S(1)}, u32[]{:S(2)}, u32[]{:S(2)}) collective-permute-start(f32[256,512]{1,0:T(8,128)S(1)} %get-tuple-element.135.refs_21_), channel_id=1, source_target_pairs={{0,4},{4,0},{8,12},{12,8},{16,20},{20,16},{24,28},{28,24},{1,5},{5... | collective-permute-start | bytes 1572872 | tf_op jit(solution)/shard_map/ppermute | solution.py:941
  90.8 12.2 %collective-permute-start.17 = (f32[8,64,256]{2,1,0:T(8,128)S(1)}, f32[8,64,256]{2,1,0:T(8,128)S(1)}, u32[]{:S(2)}, u32[]{:S(2)}) collective-permute-start(f32[8,64,256]{2,1,0:T(8,128)S(1)} %down.5.refs_4_), channel_id=1, source_target_pairs={{8,0},{12,4},{16,8},{20,12},{24,16},{28,20},{9,1},{13,5},{17,9},{2... | collective-permute-start | bytes 1572872 | tf_op jit(solution)/shard_map/ppermute | solution.py:941
  94.1 8.7 %collective-permute-start.19 = (f32[256,256]{1,0:T(8,128)S(1)}, f32[256,256]{1,0:T(8,128)S(1)}, u32[]{:S(2)}, u32[]{:S(2)}) collective-permute-start(f32[256,256]{1,0:T(8,128)S(1)} %chain.13.refs_7_), channel_id=1, source_target_pairs={{0,8},{4,12},{8,16},{12,20},{16,24},{20,28},{1,9},{5,13},{9,17},{1... | collective-permute-start | bytes 786440 | tf_op jit(solution)/shard_map/ppermute | solution.py:941
  98.8 14.7 %collective-permute-start.23 = (f32[256,512]{1,0:T(8,128)S(1)}, f32[256,512]{1,0:T(8,128)S(1)}, u32[]{:S(2)}, u32[]{:S(2)}) collective-permute-start(f32[256,512]{1,0:T(8,128)S(1)} %get-tuple-element.146.refs_23_), channel_id=1, source_target_pairs={{0,4},{4,0},{8,12},{12,8},{16,20},{20,16},{24,28},{28,24},{1,5},{5... | collective-permute-start | bytes 1572872 | tf_op jit(solution)/shard_map/ppermute | solution.py:941
  103.2 13.1 %collective-permute-start.21 = (f32[4,32,512]{2,1,0:T(8,128)S(1)}, f32[4,32,512]{2,1,0:T(8,128)S(1)}, u32[]{:S(2)}, u32[]{:S(2)}) collective-permute-start(f32[4,32,512]{2,1,0:T(8,128)S(1)} %outgoing.1.refs_1_), channel_id=1, source_target_pairs={{0,4},{4,0},{8,12},{12,8},{16,20},{20,16},{24,28},{28,24},{1,5},{5... | collective-permute-start | bytes 786440 | tf_op jit(solution)/shard_map/ppermute | solution.py:941
  104.3 14.8 %collective-permute-start.22 = (f32[256,256]{1,0:T(8,128)S(1)}, f32[256,256]{1,0:T(8,128)S(1)}, u32[]{:S(2)}, u32[]{:S(2)}) collective-permute-start(f32[256,256]{1,0:T(8,128)S(1)} %get-tuple-element.145.refs_25_), channel_id=1, source_target_pairs={{0,4},{4,0},{8,12},{12,8},{16,20},{20,16},{24,28},{28,24},{1,5},{5... | collective-permute-start | bytes 786440 | tf_op jit(solution)/shard_map/ppermute | solution.py:941

commit v4 on v3

v4 whole, which is shorter than its diff:
```python
import functools

import jax
import jax.numpy as jnp
from jax import lax
from jax.experimental import pallas as pl
from jax.experimental.pallas import tpu as pltpu
from jax.sharding import PartitionSpec as P

VERY_NEGATIVE = -1e30
LANES = 128
MIB = 1 << 20
AXIS = "ctx"

(
    ROW_A, ROW_SEND_P, ROW_SEND_S, ROW_OWN_P, ROW_OWN_S, ROW_FIN_P, ROW_FIN_K, ROW_FIN_R, ROW_CHAIN,
) = range(9)


def chunks_of(heads):
    sizes = (1,1,2,2,2)
    result, head = [], 0
    while head < heads:
        size = min(sizes[min(len(result), len(sizes) - 1)], heads - head)
        result.append(list(range(head, head + size)))
        head += size
    return result


class Order:
    def __init__(self):
        self.last = None
        self.held = []


def call(order, kernel, operands, outs, name, mib=8, scratch=(), aliases=None, flops=0):
    in_specs, arrays = [], []
    count = len(operands)
    for extra in [order.last, *order.held]:
        if extra is not None and not any(extra is operand for operand in operands):
            operands = [*operands, extra]
    body = lambda *refs: kernel(*refs[:count], *refs[len(operands) :])
    for operand in operands:
        if isinstance(operand, tuple):
            in_specs.append(pl.BlockSpec(memory_space=pl.ANY))
            arrays.append(pltpu.with_memory_space_constraint(operand[0], pltpu.HBM))
        else:
            in_specs.append(pl.BlockSpec(memory_space=pltpu.VMEM))
            arrays.append(pltpu.with_memory_space_constraint(operand, pltpu.VMEM))
    out_specs = [
        pl.BlockSpec(memory_space=pl.ANY if out.memory_space == pltpu.HBM else pltpu.VMEM) for out in outs
    ]
    results = pl.pallas_call(
        body,
        in_specs=in_specs,
        out_specs=out_specs,
        out_shape=list(outs),
        scratch_shapes=list(scratch),
        input_output_aliases=aliases or {},
        compiler_params=pltpu.CompilerParams(vmem_limit_bytes=mib * MIB),
        cost_estimate=pl.CostEstimate(flops=int(flops), bytes_accessed=0, transcendentals=0),
        name=name,
    )(*arrays)
    order.last = results[-1]
    return results


class Operands:
    def __init__(self):
        self.arrays = []

    def place(self, array):
        for i, other in enumerate(self.arrays):
            if other is array:
                return i
        self.arrays.append(array)
        return len(self.arrays) - 1

    def view(self, view):
        return self.place(view[0]), view[1]


def position():
    place = lax.axis_index(AXIS)
    return lax.rem(place, 2), lax.div(place, 2)


def lane_iota(shape):
    return lax.broadcasted_iota(jnp.int32, shape, len(shape) - 1)


def row_iota(shape):
    return lax.broadcasted_iota(jnp.int32, shape, 0)


def columns_of(head, width):
    return pl.ds(pl.multiple_of(head * width, width), width)


def three_parts(value):
    high = value.astype(jnp.bfloat16).astype(jnp.float32)
    middle = (value - high).astype(jnp.bfloat16).astype(jnp.float32)
    return high, middle, value - high - middle


def memory_of(key, value, weight):
    scaled = (key.astype(jnp.float32) * weight).astype(jnp.bfloat16)
    return lax.dot_general(
        scaled, value, (((0,), (0,)), ((), ())), preferred_element_type=jnp.float32
    )


def start_kernel(
    input_hbm, forget_hbm, keys_hbm, values_hbm,
    keys_ref, value_ref, rows_ref, columns_ref, summary_ref, input_ref, forget_ref, sems,
):
    heads, tokens = input_ref.shape
    dqk = keys_ref.shape[1] // heads
    dv = value_ref.shape[1]
    copies = [
        pltpu.make_async_copy(forget_hbm, forget_ref, sems.at[0]),
        pltpu.make_async_copy(input_hbm, input_ref, sems.at[1]),
        pltpu.make_async_copy(keys_hbm, keys_ref, sems.at[2]),
        pltpu.make_async_copy(values_hbm.at[:, 0:dv], value_ref, sems.at[3]),
    ]
    for copy in copies:
        copy.start()
    copies[0].wait()
    copies[1].wait()

    gate = forget_ref[...]
    cumulated = jnp.minimum(gate, 0.0) - jnp.log1p(jnp.exp(-jnp.abs(gate)))
    lanes = lane_iota((heads, tokens))
    step = 1
    while step < tokens:
        cumulated = cumulated + jnp.where(lanes >= step, pltpu.roll(cumulated, step, 1), 0.0)
        step *= 2
    level = input_ref[...] - cumulated
    running = level
    step = 1
    while step < tokens:
        running = jnp.maximum(
            running, jnp.where(lanes >= step, pltpu.roll(running, step, 1), VERY_NEGATIVE)
        )
        step *= 2
    highest = running[:, tokens - 1 : tokens]
    decay = cumulated[:, tokens - 1 : tokens]
    weight = jnp.exp(level - highest)
    rows_ref[...] = level
    filler = jnp.zeros((LANES - 3 * heads, tokens), jnp.float32)
    columns_ref[...] = jnp.concatenate([weight, running, cumulated, filler], axis=0).T

    copies[2].wait()
    spare = jnp.zeros((-(-3 * heads // 16) * 16 - 3 * heads, tokens), jnp.float32)
    parts = jnp.concatenate([*three_parts(weight), spare], axis=0).astype(jnp.bfloat16)
    sums = []
    for i in range(heads):
        product = jnp.dot(
            parts, keys_ref[:, i * dqk : (i + 1) * dqk], preferred_element_type=jnp.float32
        )
        sums.append(
            product[i : i + 1] + product[heads + i : heads + i + 1] + product[2 * heads + i : 2 * heads + i + 1]
        )
    lane = lane_iota((heads, LANES))
    stats = jnp.where(lane == 0, decay + highest, jnp.where(lane == 1, decay, 0.0))
    summary_ref[...] = jnp.concatenate([jnp.concatenate(sums, axis=0), stats], axis=1)
    copies[3].wait()


def start(order, input_gate, forget_gate, keys, values):
    heads, tokens = input_gate.shape
    dqk, dv = keys.shape[1] // heads, values.shape[1] // heads
    return call(
        order,
        start_kernel,
        [(a, pl.ANY) for a in (input_gate, forget_gate, keys, values)],
        [
            pltpu.VMEM(keys.shape, keys.dtype),
            pltpu.VMEM((tokens, dv), values.dtype),
            pltpu.VMEM((heads, tokens), jnp.float32),
            pltpu.VMEM((tokens, LANES), jnp.float32),
            pltpu.VMEM((heads, dqk + LANES), jnp.float32),
        ],
        "start",
        mib=12,
        scratch=[
            pltpu.VMEM((heads, tokens), jnp.float32),
            pltpu.VMEM((heads, tokens), jnp.float32),
            pltpu.SemaphoreType.DMA((4,)),
        ],
    )


def load_kernel(in_hbm, out_ref, sem):
    copy = pltpu.make_async_copy(in_hbm, out_ref, sem)
    copy.start()
    copy.wait()


def load(order, array):
    return call(
        order,
        load_kernel,
        [(array, pl.ANY)],
        [pltpu.VMEM(array.shape, array.dtype)],
        "load",
        scratch=[pltpu.SemaphoreType.DMA],
    )[0]


def memories_kernel(keys_ref, columns_ref, values_ref, *refs, heads, first, count, with_summary, with_queries):
    if with_summary:
        summary_ref, away_ref, kept_ref = refs
        rest = away_ref.shape[0] - kept_ref.shape[0], away_ref.shape[1] - summary_ref.shape[1]
        away_ref[kept_ref.shape[0] :, :] = jnp.concatenate(
            [summary_ref[...], jnp.zeros(rest, jnp.float32)], axis=1
        )
    elif with_queries:
        queries_hbm, away_ref, kept_ref, queries_ref, sem = refs
        copy = pltpu.make_async_copy(queries_hbm, queries_ref, sem)
        copy.start()
    else:
        away_ref, kept_ref = refs
    side, _ = position()
    dqk = keys_ref.shape[1] // heads
    rows, dv = kept_ref.shape[0] // count, kept_ref.shape[1]
    stripe = dqk // lax.axis_size(AXIS)
    for i in range(count):
        head = first + i
        value = values_ref[...] if with_summary else values_ref[:, head * dv : (head + 1) * dv]
        memory = memory_of(keys_ref[:, head * dqk : (head + 1) * dqk], value, columns_ref[:, head : head + 1])
        memory = memory.reshape(rows // stripe, 2, stripe, dv)
        low, high = memory[:, 0].reshape(rows, dv), memory[:, 1].reshape(rows, dv)
        here = pl.ds(i * rows, rows)
        away_ref[here, :] = jnp.where(side == 0, high, low)
        kept_ref[here, :] = jnp.where(side == 0, low, high)
    if with_queries:
        copy.wait()


def memories(order, keys, columns, values, chunk, heads, summary=None, queries=None):
    tokens = keys.shape[0]
    dqk = keys.shape[1] // heads
    dv = values.shape[1] // (heads if summary is None else 1)
    more = [] if queries is None else [(queries, pl.ANY)]
    rows = len(chunk) * dqk // 2
    behind = 0 if summary is None else summary.shape[0]
    return call(
        order,
        functools.partial(
            memories_kernel, heads=heads, first=chunk[0], count=len(chunk), with_summary=behind > 0,
            with_queries=bool(more),
        ),
        [keys, columns, values, *([] if summary is None else [summary]), *more],
        [pltpu.VMEM((rows + behind, dv), jnp.float32), pltpu.VMEM((rows, dv), jnp.float32)]
        + [pltpu.VMEM(a.shape, a.dtype) for a, _ in more],
        "memories",
        mib=12,
        scratch=[pltpu.SemaphoreType.DMA] * len(more),
    )


def block_summary(gathered_ref, block, side, level):
    levels = gathered_ref.shape[0]
    turn = lax.rem(block // 2 - level + levels, levels)
    same, other = gathered_ref[turn, 0], gathered_ref[turn, 1]
    return jnp.where(side == block % 2, same, other)


def weights_kernel(gathered_ref, table_ref, parts_ref, top_row_ref):
    levels, _, heads, width = gathered_ref.shape
    blocks = 2 * levels
    dqk = width - LANES
    side, level = position()

    tops, decays, normals = [], [], []
    for block in range(blocks):
        held = block_summary(gathered_ref, block, side, level)
        normals.append(held[:, :dqk])
        tops.append(held[:, dqk : dqk + 1])
        decays.append(held[:, dqk + 1 : dqk + 2])

    pick = lambda at, value, otherwise: jnp.where(level == at, value, otherwise)
    top = jnp.full((heads, 1), VERY_NEGATIVE, jnp.float32)
    normal = jnp.zeros((heads, dqk), jnp.float32)
    zero = jnp.zeros((heads, 1), jnp.float32)
    mine_a = mine_b = mine_first = mine_second = zero
    carry_p = carry_s = zero
    prefix_top, prefix_normal = zero, normal
    scales = []
    for z in range(levels):
        t0, t1, d0, d1 = tops[2 * z], tops[2 * z + 1], decays[2 * z], decays[2 * z + 1]
        pair_top = jnp.maximum(t0 + d1, t1)
        first, second = jnp.exp(t0 + d1 - pair_top), jnp.exp(t1 - pair_top)
        pair_normal = normals[2 * z] * first + normals[2 * z + 1] * second
        middle_top = jnp.maximum(top + d0, t0)
        alpha, beta = jnp.exp(top + d0 - middle_top), jnp.exp(t0 - middle_top)
        middle_normal = normal * alpha + normals[2 * z] * beta
        pair_decay = d0 + d1
        next_top = jnp.maximum(top + pair_decay, pair_top)
        a, b = jnp.exp(top + pair_decay - next_top), jnp.exp(pair_top - next_top)
        mine_a, mine_b = pick(z, a, mine_a), pick(z, b, mine_b)
        mine_first, mine_second = pick(z, first, mine_first), pick(z, second, mine_second)
        carry_p, carry_s = pick(z, alpha, carry_p), pick(z, beta, carry_s)
        prefix_top = pick(z, jnp.where(side == 0, top, middle_top), prefix_top)
        prefix_normal = pick(z, jnp.where(side == 0, normal, middle_normal), prefix_normal)
        normal = normal * a + pair_normal * b
        top = next_top
        scales.append((a, b))
    later = jnp.ones((heads, 1), jnp.float32)
    final_p = final_l = zero
    for z in reversed(range(levels)):
        a, b = scales[z]
        final_l = pick(z, b * later, final_l)
        later = later * a
        final_p = pick(z, later, final_p)

    one = jnp.ones((heads, 1), jnp.float32)
    by_side = lambda zero_value, one_value: jnp.where(side == 0, zero_value, one_value)
    lanes = lane_iota((heads, LANES))
    rows = row_iota((heads, LANES))
    chunks = chunks_of(heads)
    head_of_step = jnp.zeros((heads, LANES), jnp.int32)
    for z in range(levels):
        for c, chunk in enumerate(chunks):
            for slot, head in enumerate(chunk):
                wanted = (lanes == 2 * (c + z) + slot) & (level == z)
                head_of_step = jnp.where(wanted, head, head_of_step)

    def spread(column, heads_wanted):
        return jnp.sum(jnp.where(rows == heads_wanted, column, 0.0), axis=0, keepdims=True)

    mine_own = by_side(mine_first, mine_second)
    mine_partner = by_side(mine_second, mine_first)
    chain_own = spread(mine_b * mine_own, head_of_step)
    chain_partner = spread(mine_b * mine_partner, head_of_step)
    entries = [
        spread(mine_a, head_of_step),
        spread(by_side(carry_p, one), lanes),
        spread(by_side(carry_s, zero), lanes),
        spread(by_side(one, carry_p), lanes),
        spread(by_side(zero, carry_s), lanes),
        spread(final_p, lanes),
        spread(final_l * mine_own, lanes),
        spread(final_l * mine_partner, lanes),
    ]
    for z in range(levels):
        entries += [pick(z, chain_own, 0.0), pick(z, chain_partner, 0.0)]
    here = jnp.ones((1, LANES), jnp.float32)
    entries += [pick(z, here, 0.0) for z in range(levels)]
    empty = jnp.zeros((1, LANES), jnp.float32)
    entries += [empty] * (table_ref.shape[0] - len(entries))
    table_ref[...] = jnp.concatenate(entries, axis=0)

    filler = jnp.zeros((LANES - 3 * heads, dqk), jnp.float32)
    parts = jnp.concatenate([*three_parts(prefix_normal), filler], axis=0)
    parts_ref[...] = parts.T
    prefix_top = jnp.broadcast_to(prefix_top, (heads, LANES))
    filler = jnp.zeros((LANES - heads, LANES), jnp.float32)
    top_row_ref[...] = jnp.concatenate([prefix_top, filler], axis=0).T[:8]


def weights(order, gathered):
    levels, _, heads, width = gathered.shape
    dqk = width - LANES
    table_rows = -(-(ROW_CHAIN + 3 * levels) // 8) * 8
    return call(
        order,
        weights_kernel,
        [gathered],
        [
            pltpu.VMEM((table_rows, LANES), jnp.float32),
            pltpu.VMEM((dqk, LANES), jnp.float32),
            pltpu.VMEM((8, LANES), jnp.float32),
        ],
        "weights",
    )


def wait_kernel(ref, out_ref):
    out_ref[...] = ref[:8, :LANES] if len(ref.shape) == 2 else ref[0, :8, :LANES]


def wait(order, array, flops=0):
    return call(order, wait_kernel, [array], [pltpu.VMEM((8, LANES), jnp.float32)], "wait", flops=flops)[0]


def pair_kernel(summary_ref, taken_ref, out_ref):
    heads, width = summary_ref.shape
    out_ref[0] = summary_ref[...]
    out_ref[1] = taken_ref[taken_ref.shape[0] - heads :, :width]


def pair_of(order, summary, taken):
    return call(order, pair_kernel, [summary, taken], [pltpu.VMEM((2,) + summary.shape, jnp.float32)], "pair")[0]


def pack_kernel(*refs):
    *in_refs, out_ref = refs
    at = 0
    for ref in in_refs:
        value = ref[...].reshape((-1,) + out_ref.shape[1:])
        count = min(value.shape[0], out_ref.shape[0] - at)
        out_ref[at : at + count] = value[:count]
        at += count


def pack(order, arrays, count):
    return call(order, pack_kernel, arrays, [pltpu.VMEM((count,) + arrays[0].shape[1:], jnp.float32)], "pack")[0]


def finals_kernel(gathered_ref, normal_hbm, tops_hbm, token_ref, normal_ref, tops_ref, sems):
    token_ref[...] = jnp.zeros_like(token_ref)
    levels, _, heads, width = gathered_ref.shape
    dqk = width - LANES
    side, level = position()
    top = jnp.full((heads, 1), VERY_NEGATIVE, jnp.float32)
    normal = jnp.zeros((heads, dqk), jnp.float32)
    for block in range(2 * levels):
        held = block_summary(gathered_ref, block, side, level)
        block_top, decay = held[:, dqk : dqk + 1], held[:, dqk + 1 : dqk + 2]
        next_top = jnp.maximum(top + decay, block_top)
        normal = normal * jnp.exp(top + decay - next_top) + held[:, :dqk] * jnp.exp(block_top - next_top)
        top = next_top
    share = normal_hbm.shape[1]
    place = 2 * level + side
    mine = pltpu.roll(normal, lax.rem(dqk - place * share, dqk), 1)
    normal_ref[...] = mine[:, :share]
    filler = jnp.zeros((LANES - heads, LANES), jnp.float32)
    tops = jnp.concatenate([jnp.broadcast_to(top, (heads, LANES)), filler], axis=0).T
    tops_ref[...] = tops[0:1, :heads]
    copies = [
        pltpu.make_async_copy(normal_ref, normal_hbm, sems.at[0]),
        pltpu.make_async_copy(tops_ref, tops_hbm, sems.at[1]),
    ]
    for copy in copies:
        copy.start()
    for copy in copies:
        copy.wait()


def finals(order, gathered):
    levels, _, heads, width = gathered.shape
    shape = (heads, (width - LANES) // (2 * levels))
    normal, tops, _ = call(
        order,
        finals_kernel,
        [gathered],
        [
            pltpu.HBM(shape, jnp.float32),
            pltpu.HBM((1, heads), jnp.float32),
            pltpu.VMEM((8, LANES), jnp.float32),
        ],
        "finals",
        scratch=[
            pltpu.VMEM(shape, jnp.float32),
            pltpu.VMEM((1, heads), jnp.float32),
            pltpu.SemaphoreType.DMA((2,)),
        ],
    )
    return normal, tops


def attention_kernel(
    queries_ref, keys_ref, values_ref, rows_ref, columns_ref, parts_ref, *refs, heads, index
):
    out_ref, sums_ref, products_ref = refs[-3:]
    tokens = queries_ref.shape[0]
    dqk, dv = queries_ref.shape[1] // heads, values_ref.shape[1] // heads
    key_columns, value_columns = pl.ds(index * dqk, dqk), pl.ds(index * dv, dv)
    tile = min(256, tokens)
    level = rows_ref[index : index + 1, :]
    causal = row_iota((tile, tile)) >= lane_iota((tile, tile))
    part_lanes = lane_iota(parts_ref.shape)
    mine = (lax.rem(part_lanes, heads) == index) & (part_lanes < 3 * heads)
    parts = jnp.where(mine, parts_ref[...], 0.0).astype(jnp.bfloat16)

    for begin in range(0, tokens, tile):
        end = begin + tile
        here = pl.ds(begin, tile)
        query = queries_ref[here, key_columns]
        running = columns_ref[here, heads + index : heads + index + 1]
        total = jnp.zeros((tile, 1), jnp.float32)
        result = None
        for low in range(0, end, tile):
            there = pl.ds(low, tile)
            scores = lax.dot_general(
                query, keys_ref[there, key_columns], (((1,), (1,)), ((), ())), preferred_element_type=jnp.float32
            )
            attn = jnp.exp(level[:, low : low + tile] - running) * scores
            if low == begin:
                attn = jnp.where(causal, attn, 0.0)
            total = total + jnp.sum(attn, axis=1, keepdims=True)
            term = jnp.dot(
                attn.astype(jnp.bfloat16), values_ref[there, value_columns], preferred_element_type=jnp.float32
            )
            result = term if result is None else result + term
        product = jnp.dot(query, parts, preferred_element_type=jnp.float32)
        lanes = lane_iota((tile, LANES))
        if len(refs) > 3:
            sums_ref[here, :] = jnp.where(lanes == index, total, refs[0][here, :])
            products_ref[here, :] = refs[1][here, :] + product
        else:
            sums_ref[here, :] = jnp.where(lanes == index, total, 0.0)
            products_ref[here, :] = product
        out_ref[here, :] = result.astype(jnp.bfloat16)


def attention(order, index, queries, keys, values, rows, columns, parts, state):
    tokens = queries.shape[0]
    heads = rows.shape[0]
    dqk, dv = queries.shape[1] // heads, values.shape[1] // heads
    return call(
        order,
        functools.partial(attention_kernel, heads=heads, index=index),
        [queries, keys, values, rows, columns, parts, *state],
        [
            pltpu.VMEM((tokens, dv), jnp.bfloat16),
            pltpu.VMEM((tokens, LANES), jnp.float32),
            pltpu.VMEM((tokens, LANES), jnp.float32),
        ],
        "attention",
        mib=12,
    )


def factors_kernel(columns_ref, top_ref, sums_ref, products_ref, out_ref, *, heads, dqk):
    tokens = columns_ref.shape[0]
    tile = min(256, tokens)
    shift = lambda block, by: pltpu.roll(block, (LANES - by) % LANES, 1)
    for begin in range(0, tokens, tile):
        here = pl.ds(begin, tile)
        product = products_ref[here, :]
        product = product + shift(product, heads) + shift(product, 2 * heads)
        column = columns_ref[here, :]
        running, cumulated = shift(column, heads), shift(column, 2 * heads)
        top = top_ref[0:1, :]
        highest = jnp.maximum(running, top)
        scaling = float(dqk) ** -0.5
        local, carried = jnp.exp(running - highest), jnp.exp(top - highest)
        denominator = (local * sums_ref[here, :] + carried * product) * scaling
        divisor = jnp.maximum(jnp.abs(denominator), jnp.exp(-(cumulated + highest)))
        inverse = scaling / divisor
        out_ref[here, :] = jnp.where(
            lane_iota((tile, LANES)) < heads, local * inverse, pltpu.roll(carried * inverse, heads, 1)
        )


def factors(order, columns, top_row, sums, products, heads, dqk):
    return call(
        order,
        functools.partial(factors_kernel, heads=heads, dqk=dqk),
        [columns, top_row, sums, products],
        [pltpu.VMEM(columns.shape, jnp.float32)],
        "factors",
    )[0]


def finish_heads(queries_ref, factors_ref, refs, items, heads, out_hbm, memory, scratch, sems):
    side, _ = position()
    tokens = queries_ref.shape[0]
    dqk = queries_ref.shape[1] // heads
    dv = scratch.shape[2]
    rows = dqk // 2
    stripe = dqk // lax.axis_size(AXIS)
    tile = min(256, tokens)
    copies = []
    for at, (head, held, own, other) in enumerate(items):
        own = refs[own[0]][own[1] : own[1] + rows, :].astype(jnp.bfloat16)
        other = refs[other[0]][other[1] : other[1] + rows, :].astype(jnp.bfloat16)
        low, high = jnp.where(side == 0, own, other), jnp.where(side == 0, other, own)
        for i in range(rows // stripe):
            memory[2 * i * stripe : (2 * i + 1) * stripe, :] = low[i * stripe : (i + 1) * stripe]
            memory[(2 * i + 1) * stripe : (2 * i + 2) * stripe, :] = high[i * stripe : (i + 1) * stripe]
        prefix = memory[...]
        for begin in range(0, tokens, tile):
            here = pl.ds(begin, tile)
            local = factors_ref[here, head : head + 1]
            carried = factors_ref[here, heads + head : heads + head + 1]
            term = jnp.dot(
                queries_ref[here, head * dqk : (head + 1) * dqk], prefix, preferred_element_type=jnp.float32
            )
            value = refs[held][here, :].astype(jnp.float32)
            scratch[at, here, :] = (value * local + term * carried).astype(scratch.dtype)
            copy = pltpu.make_async_copy(
                scratch.at[at, here, :], out_hbm.at[here, pl.ds(head * dv, dv)], sems.at[len(copies)]
            )
            copy.start()
            copies.append(copy)
    return copies


def finish_kernel(queries_ref, factors_ref, *refs, items, heads):
    *_, out_hbm, token_ref, memory, scratch, sems = refs
    token_ref[...] = jnp.zeros_like(token_ref)
    for copy in finish_heads(queries_ref, factors_ref, refs, items, heads, out_hbm, memory, scratch, sems):
        copy.wait()


def finish_operands(wanted):
    operands = Operands()
    items = [
        (head, operands.place(held), operands.view(own), operands.view(other)) for head, held, own, other in wanted
    ]
    return operands, items


def finish_scratch(wanted, tokens):
    dv = wanted[0][1].shape[1]
    rows = wanted[0][2][0].shape[0] // wanted[0][2][2]
    return [
        pltpu.VMEM((2 * rows, dv), jnp.bfloat16),
        pltpu.VMEM((len(wanted), tokens, dv), jnp.bfloat16),
        pltpu.SemaphoreType.DMA((len(wanted) * max(1, tokens // 256),)),
    ]


def finish(order, wanted, queries, factor, hidden, heads):
    operands, items = finish_operands(wanted)
    tokens = queries.shape[0]
    dv = wanted[0][1].shape[1]
    arrays = [queries, factor, *operands.arrays]
    aliases = {}
    if hidden is not None:
        aliases = {len(arrays): 0}
        arrays.append((hidden, pl.ANY))
    return call(
        order,
        functools.partial(finish_kernel, items=items, heads=heads),
        arrays,
        [pltpu.HBM((tokens, heads * dv), jnp.bfloat16), pltpu.VMEM((8, LANES), jnp.float32)],
        "finish",
        mib=12,
        scratch=finish_scratch(wanted, tokens),
        aliases=aliases,
    )[0]


def entry_of(table_ref):
    return lambda row, lane: table_ref[row : row + 1, lane : lane + 1]


def row_tiles(rows):
    tile = min(16, rows)
    return [(begin, tile) for begin in range(0, rows, tile)]


def chain_kernel(table_ref, *refs, slots):
    out_ref = refs[-1]
    entry = entry_of(table_ref)
    rows = out_ref.shape[0] // len(slots)
    for i, terms in enumerate(slots):
        terms = [(place, row, entry(which, lane)) for (place, row), which, lane in terms]
        for begin, size in row_tiles(rows):
            total = None
            for place, row, weight in terms:
                term = refs[place][row + begin : row + begin + size, :] * weight
                total = term if total is None else total + term
            out_ref[i * rows + begin : i * rows + begin + size, :] = total


def first_kernel(pair_ref, keep_ref, take_ref, out_ref):
    side, _ = position()
    width = pair_ref.shape[2]
    top, decay = [], []
    for which in range(2):
        top.append(pair_ref[which, 0:1, width - LANES : width - LANES + 1])
        decay.append(pair_ref[which, 0:1, width - LANES + 1 : width - LANES + 2])
    own = top[0] + jnp.where(side == 0, decay[1], 0.0)
    partner = top[1] + jnp.where(side == 0, 0.0, decay[0])
    highest = jnp.maximum(own, partner)
    own, partner = jnp.exp(own - highest), jnp.exp(partner - highest)
    for begin, size in row_tiles(out_ref.shape[0]):
        here = pl.ds(begin, size)
        out_ref[here, :] = keep_ref[here, :] * own + take_ref[here, :] * partner


def first_step(order, pair, keep, take):
    return call(
        order, first_kernel, [pair, keep, take], [pltpu.VMEM(keep.shape, jnp.float32)], "chain"
    )[0]


def chain_step(order, table, step, chunks, kept, received, earlier, levels):
    operands = Operands()
    slots = []
    for slot in range(2):
        terms = []
        lane = 2 * step + slot
        for z in range(levels - 1):
            if 0 <= step - z < len(chunks) and slot < len(chunks[step - z]):
                head = chunks[step - z][slot]
                terms.append((operands.view(kept[head]), ROW_CHAIN + 2 * z, lane))
                terms.append((operands.view(received[head]), ROW_CHAIN + 2 * z + 1, lane))
        if terms:
            if slot < earlier[2]:
                terms.append((operands.view((earlier[0], slot * earlier[1], earlier[2])), ROW_A, lane))
            slots.append(terms)
    rows, dv = earlier[1], earlier[0].shape[1]
    value = call(
        order,
        functools.partial(chain_kernel, slots=slots),
        [table, *operands.arrays],
        [pltpu.VMEM((rows * len(slots), dv), jnp.float32)],
        "chain",
    )[0]
    return value, rows, len(slots)


def prefix_kernel(table_ref, *refs, levels, pieces):
    send_ref, own_ref = refs[-2:]
    rows = send_ref.shape[0] // len(pieces)
    entry = entry_of(table_ref)
    here_row = ROW_CHAIN + 2 * levels
    picks = [entry(here_row + z, 0) for z in range(1, levels)]
    for i, (head, arrivals, (keep, keep_row), (take, take_row)) in enumerate(pieces):
        send_p, send_s = entry(ROW_SEND_P, head), entry(ROW_SEND_S, head)
        own_p, own_s = entry(ROW_OWN_P, head), entry(ROW_OWN_S, head)
        for begin, size in row_tiles(rows):
            prefix = None
            for (place, row), weight in zip(arrivals, picks):
                term = refs[place][row + begin : row + begin + size, :] * weight
                prefix = term if prefix is None else prefix + term
            here = pl.ds(i * rows + begin, size)
            send_ref[here, :] = prefix * send_p + refs[keep][keep_row + begin : keep_row + begin + size, :] * send_s
            own_ref[here, :] = prefix * own_p + refs[take][take_row + begin : take_row + begin + size, :] * own_s


def prefixes(order, table, index, chunks, arrived, kept, received, levels):
    operands = Operands()
    pieces = []
    for slot, head in enumerate(chunks[index]):
        arrivals = []
        for z in range(1, levels):
            array, rows, count = arrived[index + z - 1]
            arrivals.append(operands.view((array, slot * rows, count)))
        pieces.append((head, arrivals, operands.view(kept[head]), operands.view(received[head])))
    out = pltpu.VMEM((len(pieces) * arrived[0][1], kept[0][0].shape[1]), jnp.float32)
    return call(
        order,
        functools.partial(prefix_kernel, levels=levels, pieces=pieces),
        [table, *operands.arrays],
        [out, out],
        "prefix",
    )


def level_rows(table_ref, refs, views, level, stripe):
    entry = entry_of(table_ref)
    for head, ((keep, keep_row), (take, take_row)) in enumerate(views):
        here = lambda row: pl.ds(pl.multiple_of(row + level * stripe, stripe), stripe)
        yield (
            head,
            refs[keep][here(keep_row), :] * entry(ROW_FIN_K, head)
            + refs[take][here(take_row), :] * entry(ROW_FIN_R, head),
        )


def down_kernel(table_ref, *refs, step, levels, views, earlier):
    out_ref = refs[-1]
    stripe = out_ref.shape[1]
    _, level = position()
    target = jnp.maximum(step - levels + level, 0)
    for head, value in level_rows(table_ref, refs, views, target, stripe):
        out_ref[head] = value if earlier is None else value + refs[earlier][head]


def down(order, table, step, levels, kept, received, earlier, stripe):
    operands = Operands()
    views = [(operands.view(keep), operands.view(take)) for keep, take in zip(kept, received)]
    place = None if earlier is None else operands.place(earlier)
    return call(
        order,
        functools.partial(down_kernel, step=step, levels=levels, views=views, earlier=place),
        [table, *operands.arrays],
        [pltpu.VMEM((len(kept), stripe, kept[0][0].shape[1]), jnp.float32)],
        "down",
    )[0]


def last_kernel(queries_ref, factors_ref, table_ref, above_ref, *refs, items, heads, views, prefix_views):
    out_hbm, final_hbm, token_ref, memory, scratch, sems, final_ref, final_sem = refs[-8:]
    token_ref[...] = jnp.zeros_like(token_ref)
    copies = finish_heads(queries_ref, factors_ref, refs, items, heads, out_hbm, memory, scratch, sems)
    side, level = position()
    stripe = above_ref.shape[1]
    entry = entry_of(table_ref)
    for head, value in level_rows(table_ref, refs, views, level, stripe):
        (own, own_row), (sent, sent_row) = prefix_views[head]
        here = lambda row: pl.ds(pl.multiple_of(row + level * stripe, stripe), stripe)
        prefix = jnp.where(side == 0, refs[own][here(own_row), :], refs[sent][here(sent_row), :])
        final_ref[head] = value + prefix * entry(ROW_FIN_P, head) + above_ref[head]
    copies.append(pltpu.make_async_copy(final_ref, final_hbm, final_sem))
    copies[-1].start()
    for copy in copies:
        copy.wait()


def last(order, wanted, queries, factor, hidden, heads, table, above, kept, received, owns, sends):
    operands, items = finish_operands(wanted)
    views = [(operands.view(keep), operands.view(take)) for keep, take in zip(kept, received)]
    prefix_views = [(operands.view(own), operands.view(sent)) for own, sent in zip(owns, sends)]
    tokens = queries.shape[0]
    dv = wanted[0][1].shape[1]
    arrays = [queries, factor, table, above, *operands.arrays, (hidden, pl.ANY)]
    return call(
        order,
        functools.partial(last_kernel, items=items, heads=heads, views=views, prefix_views=prefix_views),
        arrays,
        [
            pltpu.HBM((tokens, heads * dv), jnp.bfloat16),
            pltpu.HBM(above.shape, jnp.float32),
            pltpu.VMEM((8, LANES), jnp.float32),
        ],
        "last",
        mib=12,
        scratch=[
            *finish_scratch(wanted, tokens),
            pltpu.VMEM(above.shape, jnp.float32),
            pltpu.SemaphoreType.DMA,
        ],
        aliases={len(arrays) - 1: 0},
    )[:2]


def shards(queries, keys, values, input_gate, forget_gate, *, blocks):
    heads = input_gate.shape[0]
    dqk, dv = queries.shape[1] // heads, values.shape[1] // heads
    rows_of_unit = dqk // 2
    levels = blocks // 2
    across = [(i, i ^ 1) for i in range(blocks)]
    up = [(i, i + 2) for i in range(blocks - 2)]
    downward = [(i + 2, i) for i in range(blocks - 2)]
    send = lambda value, pairs: lax.ppermute(value, AXIS, pairs)
    order = Order()
    chunks = chunks_of(heads)
    steps = len(chunks) + levels - 2

    def views_of(arrays):
        return [
            (array, slot * rows_of_unit, len(chunk))
            for array, chunk in zip(arrays, chunks)
            for slot in range(len(chunk))
        ]

    keys, first_value, rows, columns, summary = start(order, input_gate, forget_gate, keys, values)
    taken, kept = [], []

    def remember(held_values, chunk, **more):
        away, keep, *rest = memories(order, keys, columns, held_values, chunk, heads, **more)
        taken.append(send(away, across))
        kept.append(keep)
        return rest

    remember(first_value, chunks[0], summary=summary)
    values = load(order, values)
    remember(values, chunks[1])

    pair = pair_of(order, summary, taken[0])
    arrived = [(send(first_step(order, pair, kept[0], taken[0]), up), rows_of_unit, 1)]
    gathered = pair[None]
    while gathered.shape[0] < levels:
        reach = gathered.shape[0]
        more = send(gathered, [(i, (i - 2 * reach) % blocks) for i in range(blocks)])
        if reach > 1 and len(taken) < len(chunks) - 1:
            remember(values, chunks[len(taken)])
        gathered = pack(order, [gathered, more], min(2 * reach, levels))
    while len(taken) < len(chunks) - 1:
        remember(values, chunks[len(taken)])
    table, parts, top_row = weights(order, gathered)

    attended, state = [], ()
    sends, owns, others = [], [], []
    hidden = factor = above = final_normal = tops = None
    falls = finished = 0

    def attend(count):
        nonlocal state
        for _ in range(count):
            if len(attended) < heads:
                result, *state = attention(
                    order, len(attended), queries, keys, values, rows, columns, parts, state
                )
                attended.append(result)

    def exchange():
        to_send, own = prefixes(
            order, table, len(owns), chunks, arrived, views_of(kept), views_of(taken), levels
        )
        sends.append(to_send)
        owns.append(own)
        others.append(send(to_send, across))

    def fall():
        nonlocal falls, above
        falls += 1
        above = send(
            down(order, table, falls, levels, views_of(kept), views_of(taken), above, dqk // blocks), downward
        )

    def wanted(chunk):
        return [(head, attended[head], views_of(owns)[head], views_of(others)[head]) for head in chunks[chunk]]

    def put():
        nonlocal hidden, finished
        hidden = finish(order, wanted(finished), queries, factor, hidden, heads)
        finished += 1

    plan = {1: "ma", 2: "aaaa", 3: "paadx", 4: "paFodx", 5: "pod", 6: "fXpoY"}
    for step in range(1, steps):
        value, unit_rows, count = chain_step(
            order, table, step, chunks, views_of(kept), views_of(taken), arrived[-1], levels
        )
        arrived.append((send(value, up), unit_rows, count))
        for what in plan.get(step, ""):
            if what == "m":
                (queries,) = remember(values, chunks[-1], queries=queries)
            elif what == "a":
                attend(1)
            elif what == "f":
                final_normal, tops = finals(order, gathered)
            elif what == "F" and len(attended) == heads:
                factor = factors(order, columns, top_row, *state, heads, dqk)
            elif what == "p" and len(owns) + levels - 2 < step:
                exchange()
            elif what == "d" and falls < levels - 1:
                fall()
            elif what == "o" and factor is not None and finished < len(owns):
                put()
            elif what == "x" and others:
                wait(order, others[-1])
            elif what == "X" and others:
                wait(order, others[-1], 3e9)
            elif what == "Y" and above is not None:
                wait(order, above, 3e9)
    attend(heads)
    if factor is None:
        factor = factors(order, columns, top_row, *state, heads, dqk)
    while len(owns) < len(chunks):
        exchange()
    while falls < levels - 1:
        fall()
    if final_normal is None:
        final_normal, tops = finals(order, gathered)
    while finished < len(chunks) - 1:
        put()
    hidden, final_memory = last(
        order, wanted(len(chunks) - 1), queries, factor, hidden, heads, table, above,
        views_of(kept), views_of(taken), views_of(owns), views_of(sends),
    )
    return hidden, final_memory, final_normal, tops.reshape(heads)


def solution(mesh):
    token_spec = P(("seq", "ctx"), None)
    gate_spec = P(None, ("seq", "ctx"))
    return jax.shard_map(
        functools.partial(shards, blocks=mesh.shape["ctx"]),
        mesh=mesh,
        in_specs=(token_spec, token_spec, token_spec, gate_spec, gate_spec),
        out_specs=(token_spec, P("seq", "ctx", None), P("seq", "ctx"), P("seq")),
        check_vma=False,
    )
```

time: 122 us -> 116 us (0.951)
  Pallas kernels: 50.6 us -> 44.7 us
    pallas_call x49 -> x45, Pallas kernels: 50.6 us -> 44.7 us  [call(): pl.pallas_call(body, in_specs=in_specs, out_specs=out_specs, out_shape=li...]
    ppermute x24 -> x22, starting transfers between devices: 47.8 us -> 48.2 us  [shards(): send = lambda value, pairs: lax.ppermute(value, AXIS, pairs)]
    ppermute x24 -> x22, waiting for transfers between devices: 21.6 us -> 21.8 us  [shards(): send = lambda value, pairs: lax.ppermute(value, AXIS, pairs)]
  transfers between devices with their start and end apart: 24 -> 22, of which waited for: 10 -> 8; matrix products, arithmetic and copies ran while one was open for 0% -> 0% of each run, Pallas kernels for 37% -> 33%
where the time goes in v4:
time: 116 us
  starting transfers between devices  48.2 us (42%)
  Pallas kernels  44.7 us (39%)
  waiting for transfers between devices  21.8 us (19%)
  between operations  1.27 us (1%)
    ppermute x22, starting transfers between devices, shards(): send = lambda value, pairs: lax.ppermute(value, AXIS, pairs)  48.2 us
    pallas_call x45, Pallas kernels, call(): pl.pallas_call(body, in_specs=in_specs, out_specs=out_specs, out_shape=li...  44.7 us
    ppermute x22, waiting for transfers between devices, shards(): send = lambda value, pairs: lax.ppermute(value, AXIS, pairs)  21.8 us
  transfers between devices with their start and end apart: 22, of which 8 were waited for; matrix products, arithmetic and copies ran while one was open for 0% of the time, Pallas kernels for 33%

profile of v4, /device:TPU:0, one launch (start us, length us, event | category | flops | bytes accessed | tf_op | source)
XLA Modules:
  0.0 115.9 jit_solution(9221576316802184213)
XLA Ops:
  0.6 3.1 %start.1 = (bf16[1024,2048]{1,0:T(8,128)(2,1)S(1)}, bf16[1024,512]{1,0:T(8,128)(2,1)S(1)}, f32[8,1024]{1,0:T(8,128)S(1)}, f32[1024,128]{1,0:T(8,128)S(1)}, f32[8,384]{1,0:T(8,128)S(1)}) custom-call(f32[8,1024]{1,0:T(8,128)} %refs_0_.2, f32[8,1024]{1,0:T(8,128)} %refs_1_.1, bf16[1024,2048]{1,0:T(8,128)(2,1)} %refs_2_.1, bf16[1024,4096]{1,0:T(8,128)(2,1)} %refs_0_.3), custom_call_target="tpu_custom_call" | custom-call | tf_op jit(solution)/shard_map/start/pallas_call | solution.py:53
  3.7 0.8 memories.5
  4.5 3.0 %collective-permute-start = (f32[136,512]{1,0:T(8,128)S(1)}, f32[136,512]{1,0:T(8,128)S(1)}, u32[]{:S(2)}, u32[]{:S(2)}) collective-permute-start(f32[136,512]{1,0:T(8,128)S(1)} %get-tuple-element.75), channel_id=1, source_target_pairs={{0,4},{4,0},{8,12},{12,8},{16,20},{20,16},{24,28},{28,24},{1,5},{5... | collective-permute-start | bytes 835592 | tf_op jit(solution)/shard_map/ppermute | solution.py:834
  7.6 3.4 %load.1.refs_2_ = bf16[1024,4096]{1,0:T(8,128)(2,1)S(1)} custom-call(bf16[1024,4096]{1,0:T(8,128)(2,1)} %refs_0_.3, f32[128,512]{1,0:T(8,128)S(1)} %get-tuple-element.74.refs_1_.refs_3_.refs_5_.refs_4_.refs_8_), custom_call_target="tpu_custom_call" | custom-call | tf_op jit(solution)/shard_map/load/pallas_call | solution.py:53
  11.0 0.8 memories.6
  11.8 2.5 %collective-permute-done.refs_1_.refs_2_.refs_4_.refs_6_.refs_5_.refs_9_ = f32[136,512]{1,0:T(8,128)S(1)} collective-permute-done((f32[136,512]{1,0:T(8,128)S(1)}, f32[136,512]{1,0:T(8,128)S(1)}, u32[]{:S(2)}, u32[]{:S(2)}) %collective-permute-start) | collective-permute-done | bytes 278560 | tf_op jit(solution)/shard_map/ppermute | solution.py:834
  14.2 3.8 %collective-permute-start.1 = (f32[1,2,8,384]{3,2,1,0:T(8,128)S(1)}, f32[1,2,8,384]{3,2,1,0:T(8,128)S(1)}, u32[]{:S(2)}, u32[]{:S(2)}) collective-permute-start(f32[1,2,8,384]{3,2,1,0:T(8,128)S(1)} %bitcast.2), channel_id=1, source_target_pairs={{0,24},{4,28},{8,0},{12,4},{16,8},{20,12},{24,16},{28,20},{1,25},{... | collective-permute-start | bytes 73736 | tf_op jit(solution)/shard_map/ppermute | solution.py:834
  18.0 1.5 %collective-permute-start.3 = (f32[128,512]{1,0:T(8,128)S(1)}, f32[128,512]{1,0:T(8,128)S(1)}, u32[]{:S(2)}, u32[]{:S(2)}) collective-permute-start(f32[128,512]{1,0:T(8,128)S(1)} %get-tuple-element.80), channel_id=1, source_target_pairs={{0,4},{4,0},{8,12},{12,8},{16,20},{20,16},{24,28},{28,24},{1,5},{5... | collective-permute-start | bytes 786440 | tf_op jit(solution)/shard_map/ppermute | solution.py:834
  19.7 1.3 %collective-permute-start.4 = (f32[128,512]{1,0:T(8,128)S(1)}, f32[128,512]{1,0:T(8,128)S(1)}, u32[]{:S(2)}, u32[]{:S(2)}) collective-permute-start(f32[128,512]{1,0:T(8,128)S(1)} %chain.7.refs_2_), channel_id=1, source_target_pairs={{0,8},{4,12},{8,16},{12,20},{16,24},{20,28},{1,9},{5,13},{9,17},{1... | collective-permute-start | bytes 786440 | tf_op jit(solution)/shard_map/ppermute | solution.py:834
  21.1 1.3 %memories.7 = (f32[256,512]{1,0:T(8,128)S(1)}, f32[256,512]{1,0:T(8,128)S(1)}) custom-call(bf16[1024,2048]{1,0:T(8,128)(2,1)S(1)} %get-tuple-element.70.refs_0_.refs_1_, f32[1024,128]{1,0:T(8,128)S(1)} %get-tuple-element.71.refs_1_.refs_4_.refs_0_, bf16[1024,4096]{1,0:T(8,128)(2,1)S(1)} %load.1.refs_2_, f32[2,2,8,384]{3,2,1,0:T(8,128)S(1)} %pack.2.refs_3_.refs_0_), custom_call_target="tpu_custom_call" | custom-call | tf_op jit(solution)/shard_map/memories/pallas_call | solution.py:53
  22.4 0.6 collective-permute-start.5
  23.0 1.6 %collective-permute-start.2 = (f32[2,2,8,384]{3,2,1,0:T(8,128)S(1)}, f32[2,2,8,384]{3,2,1,0:T(8,128)S(1)}, u32[]{:S(2)}, u32[]{:S(2)}) collective-permute-start(f32[2,2,8,384]{3,2,1,0:T(8,128)S(1)} %pack.2.refs_3_.refs_0_), channel_id=1, source_target_pairs={{0,16},{4,20},{8,24},{12,28},{16,0},{20,4},{24,8},{28,12},{1,17},{... | collective-permute-start | bytes 147464 | tf_op jit(solution)/shard_map/ppermute | solution.py:834
  24.6 3.4 %collective-permute-done.2.refs_1_ = f32[2,2,8,384]{3,2,1,0:T(8,128)S(1)} collective-permute-done((f32[2,2,8,384]{3,2,1,0:T(8,128)S(1)}, f32[2,2,8,384]{3,2,1,0:T(8,128)S(1)}, u32[]{:S(2)}, u32[]{:S(2)}) %collective-permute-start.2) | collective-permute-done | bytes 49184 | tf_op jit(solution)/shard_map/ppermute | solution.py:834
  28.0 1.3 %memories.8 = (f32[256,512]{1,0:T(8,128)S(1)}, f32[256,512]{1,0:T(8,128)S(1)}) custom-call(bf16[1024,2048]{1,0:T(8,128)(2,1)S(1)} %get-tuple-element.70.refs_0_.refs_1_, f32[1024,128]{1,0:T(8,128)S(1)} %get-tuple-element.71.refs_1_.refs_4_.refs_0_, bf16[1024,4096]{1,0:T(8,128)(2,1)S(1)} %load.1.refs_2_, f32[4,2,8,384]{3,2,1,0:T(8,128)S(1)} %pack.3.refs_3_.refs_0_), custom_call_target="tpu_custom_call" | custom-call | tf_op jit(solution)/shard_map/memories/pallas_call | solution.py:53
  29.3 0.5 weights.1
  29.8 0.2 chain.8.refs_4_
  30.0 3.4 %collective-permute-start.6 = (f32[128,512]{1,0:T(8,128)S(1)}, f32[128,512]{1,0:T(8,128)S(1)}, u32[]{:S(2)}, u32[]{:S(2)}) collective-permute-start(f32[128,512]{1,0:T(8,128)S(1)} %chain.8.refs_4_), channel_id=1, source_target_pairs={{0,8},{4,12},{8,16},{12,20},{16,24},{20,28},{1,9},{5,13},{9,17},{1... | collective-permute-start | bytes 786440 | tf_op jit(solution)/shard_map/ppermute | solution.py:834
  33.5 0.8 collective-permute-start.8
  34.2 2.2 %memories.9 = (f32[256,512]{1,0:T(8,128)S(1)}, f32[256,512]{1,0:T(8,128)S(1)}, bf16[1024,2048]{1,0:T(8,128)(2,1)S(1)}) custom-call(bf16[1024,2048]{1,0:T(8,128)(2,1)S(1)} %get-tuple-element.70.refs_0_.refs_1_, f32[1024,128]{1,0:T(8,128)S(1)} %get-tuple-element.71.refs_1_.refs_4_.refs_0_, bf16[1024,4096]{1,0:T(8,128)(2,1)S(1)} %load.1.refs_2_, ...), custom_call_target="tpu_custom_call" | custom-call | tf_op jit(solution)/shard_map/memories/pallas_call | solution.py:53
  36.4 2.1 %attention.8 = (bf16[1024,512]{1,0:T(8,128)(2,1)S(1)}, f32[1024,128]{1,0:T(8,128)S(1)}, f32[1024,128]{1,0:T(8,128)S(1)}) custom-call(bf16[1024,2048]{1,0:T(8,128)(2,1)S(1)} %get-tuple-element.82.refs_0_, bf16[1024,2048]{1,0:T(8,128)(2,1)S(1)} %get-tuple-element.70.refs_0_.refs_1_, bf16[1024,4096]{1,0:T(8,128)(2,1)S(1)} %load.1.refs_2_, ...), custom_call_target="tpu_custom_call" | custom-call | tf_op jit(solution)/shard_map/attention/pallas_call | solution.py:53
  38.6 0.3 chain.9.refs_8_
  38.8 3.6 %collective-permute-start.7 = (f32[256,512]{1,0:T(8,128)S(1)}, f32[256,512]{1,0:T(8,128)S(1)}, u32[]{:S(2)}, u32[]{:S(2)}) collective-permute-start(f32[256,512]{1,0:T(8,128)S(1)} %chain.9.refs_8_), channel_id=1, source_target_pairs={{0,8},{4,12},{8,16},{12,20},{16,24},{20,28},{1,9},{5,13},{9,17},{1... | collective-permute-start | bytes 1572872 | tf_op jit(solution)/shard_map/ppermute | solution.py:834
  42.5 0.8 collective-permute-start.10
  43.3 2.1 %attention.9 = (bf16[1024,512]{1,0:T(8,128)(2,1)S(1)}, f32[1024,128]{1,0:T(8,128)S(1)}, f32[1024,128]{1,0:T(8,128)S(1)}) custom-call(bf16[1024,2048]{1,0:T(8,128)(2,1)S(1)} %get-tuple-element.82.refs_0_, bf16[1024,2048]{1,0:T(8,128)(2,1)S(1)} %get-tuple-element.70.refs_0_.refs_1_, bf16[1024,4096]{1,0:T(8,128)(2,1)S(1)} %load.1.refs_2_, ...), custom_call_target="tpu_custom_call" | custom-call | tf_op jit(solution)/shard_map/attention/pallas_call | solution.py:53
  45.4 2.1 %attention.10 = (bf16[1024,512]{1,0:T(8,128)(2,1)S(1)}, f32[1024,128]{1,0:T(8,128)S(1)}, f32[1024,128]{1,0:T(8,128)S(1)}) custom-call(bf16[1024,2048]{1,0:T(8,128)(2,1)S(1)} %get-tuple-element.82.refs_0_, bf16[1024,2048]{1,0:T(8,128)(2,1)S(1)} %get-tuple-element.70.refs_0_.refs_1_, bf16[1024,4096]{1,0:T(8,128)(2,1)S(1)} %load.1.refs_2_, ...), custom_call_target="tpu_custom_call" | custom-call | tf_op jit(solution)/shard_map/attention/pallas_call | solution.py:53
  47.5 2.1 %attention.11 = (bf16[1024,512]{1,0:T(8,128)(2,1)S(1)}, f32[1024,128]{1,0:T(8,128)S(1)}, f32[1024,128]{1,0:T(8,128)S(1)}) custom-call(bf16[1024,2048]{1,0:T(8,128)(2,1)S(1)} %get-tuple-element.82.refs_0_, bf16[1024,2048]{1,0:T(8,128)(2,1)S(1)} %get-tuple-element.70.refs_0_.refs_1_, bf16[1024,4096]{1,0:T(8,128)(2,1)S(1)} %load.1.refs_2_, ...), custom_call_target="tpu_custom_call" | custom-call | tf_op jit(solution)/shard_map/attention/pallas_call | solution.py:53
  49.6 2.1 %attention.12 = (bf16[1024,512]{1,0:T(8,128)(2,1)S(1)}, f32[1024,128]{1,0:T(8,128)S(1)}, f32[1024,128]{1,0:T(8,128)S(1)}) custom-call(bf16[1024,2048]{1,0:T(8,128)(2,1)S(1)} %get-tuple-element.82.refs_0_, bf16[1024,2048]{1,0:T(8,128)(2,1)S(1)} %get-tuple-element.70.refs_0_.refs_1_, bf16[1024,4096]{1,0:T(8,128)(2,1)S(1)} %load.1.refs_2_, ...), custom_call_target="tpu_custom_call" | custom-call | tf_op jit(solution)/shard_map/attention/pallas_call | solution.py:53
  51.7 0.3 chain.10.refs_6_
  52.1 4.5 %collective-permute-start.9 = (f32[256,512]{1,0:T(8,128)S(1)}, f32[256,512]{1,0:T(8,128)S(1)}, u32[]{:S(2)}, u32[]{:S(2)}) collective-permute-start(f32[256,512]{1,0:T(8,128)S(1)} %chain.10.refs_6_), channel_id=1, source_target_pairs={{0,8},{4,12},{8,16},{12,20},{16,24},{20,28},{1,9},{5,13},{9,17},{1... | collective-permute-start | bytes 1572872 | tf_op jit(solution)/shard_map/ppermute | solution.py:834
  56.7 0.7 collective-permute-start.11
  57.4 2.1 %attention.13 = (bf16[1024,512]{1,0:T(8,128)(2,1)S(1)}, f32[1024,128]{1,0:T(8,128)S(1)}, f32[1024,128]{1,0:T(8,128)S(1)}) custom-call(bf16[1024,2048]{1,0:T(8,128)(2,1)S(1)} %get-tuple-element.82.refs_0_, bf16[1024,2048]{1,0:T(8,128)(2,1)S(1)} %get-tuple-element.70.refs_0_.refs_1_, bf16[1024,4096]{1,0:T(8,128)(2,1)S(1)} %load.1.refs_2_, ...), custom_call_target="tpu_custom_call" | custom-call | tf_op jit(solution)/shard_map/attention/pallas_call | solution.py:53
  59.5 2.1 %attention.14 = (bf16[1024,512]{1,0:T(8,128)(2,1)S(1)}, f32[1024,128]{1,0:T(8,128)S(1)}, f32[1024,128]{1,0:T(8,128)S(1)}) custom-call(bf16[1024,2048]{1,0:T(8,128)(2,1)S(1)} %get-tuple-element.82.refs_0_, bf16[1024,2048]{1,0:T(8,128)(2,1)S(1)} %get-tuple-element.70.refs_0_.refs_1_, bf16[1024,4096]{1,0:T(8,128)(2,1)S(1)} %load.1.refs_2_, ...), custom_call_target="tpu_custom_call" | custom-call | tf_op jit(solution)/shard_map/attention/pallas_call | solution.py:53
  61.8 1.3 %collective-permute-start.12 = (f32[8,32,512]{2,1,0:T(8,128)S(1)}, f32[8,32,512]{2,1,0:T(8,128)S(1)}, u32[]{:S(2)}, u32[]{:S(2)}) collective-permute-start(f32[8,32,512]{2,1,0:T(8,128)S(1)} %down.3.refs_1_), channel_id=1, source_target_pairs={{8,0},{12,4},{16,8},{20,12},{24,16},{28,20},{9,1},{13,5},{17,9},{2... | collective-permute-start | bytes 1572872 | tf_op jit(solution)/shard_map/ppermute | solution.py:834
  63.1 1.1 collective-permute-done.11.refs_0_.refs_4_
  64.3 0.4 chain.11.refs_6_
  64.7 4.2 %collective-permute-start.15 = (f32[256,512]{1,0:T(8,128)S(1)}, f32[256,512]{1,0:T(8,128)S(1)}, u32[]{:S(2)}, u32[]{:S(2)}) collective-permute-start(f32[256,512]{1,0:T(8,128)S(1)} %chain.11.refs_6_), channel_id=1, source_target_pairs={{0,8},{4,12},{8,16},{12,20},{16,24},{20,28},{1,9},{5,13},{9,17},{1... | collective-permute-start | bytes 1572872 | tf_op jit(solution)/shard_map/ppermute | solution.py:834
  68.9 0.2 prefix.6
  69.1 0.9 collective-permute-start.14
  70.0 2.1 %attention.15 = (bf16[1024,512]{1,0:T(8,128)(2,1)S(1)}, f32[1024,128]{1,0:T(8,128)S(1)}, f32[1024,128]{1,0:T(8,128)S(1)}) custom-call(bf16[1024,2048]{1,0:T(8,128)(2,1)S(1)} %get-tuple-element.82.refs_0_, bf16[1024,2048]{1,0:T(8,128)(2,1)S(1)} %get-tuple-element.70.refs_0_.refs_1_, bf16[1024,4096]{1,0:T(8,128)(2,1)S(1)} %load.1.refs_2_, ...), custom_call_target="tpu_custom_call" | custom-call | tf_op jit(solution)/shard_map/attention/pallas_call | solution.py:53
  72.1 1.0 factors.1.refs_1_
  73.1 1.3 %finish.4 = (bf16[1024,4096]{1,0:T(8,128)(2,1)}, f32[8,128]{1,0:T(8,128)S(1)}) custom-call(bf16[1024,2048]{1,0:T(8,128)(2,1)S(1)} %get-tuple-element.82.refs_0_, f32[1024,128]{1,0:T(8,128)S(1)} %factors.1.refs_1_, bf16[1024,512]{1,0:T(8,128)(2,1)S(1)} %get-tuple-element.108.refs_2_, f32[128,512]{1,0:T(8,128)S(1)} %get-tuple-element.97.refs_8_.refs_3_.refs_18_, ...), custom_call_target="tpu_custom_call" | custom-call | tf_op jit(solution)/shard_map/finish/pallas_call | solution.py:53
  74.4 0.2 down.4.refs_1_
  74.6 1.3 %collective-permute-start.13 = (f32[8,32,512]{2,1,0:T(8,128)S(1)}, f32[8,32,512]{2,1,0:T(8,128)S(1)}, u32[]{:S(2)}, u32[]{:S(2)}) collective-permute-start(f32[8,32,512]{2,1,0:T(8,128)S(1)} %down.4.refs_1_), channel_id=1, source_target_pairs={{8,0},{12,4},{16,8},{20,12},{24,16},{28,20},{9,1},{13,5},{17,9},{2... | collective-permute-start | bytes 1572872 | tf_op jit(solution)/shard_map/ppermute | solution.py:834
  76.0 0.3 chain.12.refs_6_
  76.3 4.6 %collective-permute-start.17 = (f32[256,512]{1,0:T(8,128)S(1)}, f32[256,512]{1,0:T(8,128)S(1)}, u32[]{:S(2)}, u32[]{:S(2)}) collective-permute-start(f32[256,512]{1,0:T(8,128)S(1)} %chain.12.refs_6_), channel_id=1, source_target_pairs={{0,8},{4,12},{8,16},{12,20},{16,24},{20,28},{1,9},{5,13},{9,17},{1... | collective-permute-start | bytes 1572872 | tf_op jit(solution)/shard_map/ppermute | solution.py:834
  80.9 0.3 prefix.7
  81.1 1.2 %collective-permute-start.19 = (f32[256,512]{1,0:T(8,128)S(1)}, f32[256,512]{1,0:T(8,128)S(1)}, u32[]{:S(2)}, u32[]{:S(2)}) collective-permute-start(f32[256,512]{1,0:T(8,128)S(1)} %get-tuple-element.117.refs_23_), channel_id=1, source_target_pairs={{0,4},{4,0},{8,12},{12,8},{16,20},{20,16},{24,28},{28,24},{1,5},{5... | collective-permute-start | bytes 1572872 | tf_op jit(solution)/shard_map/ppermute | solution.py:834
  82.4 1.3 %finish.5 = (bf16[1024,4096]{1,0:T(8,128)(2,1)}, f32[8,128]{1,0:T(8,128)S(1)}) custom-call(bf16[1024,2048]{1,0:T(8,128)(2,1)S(1)} %get-tuple-element.82.refs_0_, f32[1024,128]{1,0:T(8,128)S(1)} %factors.1.refs_1_, bf16[1024,512]{1,0:T(8,128)(2,1)S(1)} %get-tuple-element.110.refs_2_, ...), custom_call_target="tpu_custom_call", output_to_operand_aliasing={{0}: (5, {})} | custom-call | tf_op jit(solution)/shard_map/finish/pallas_call | solution.py:53
  83.7 2.8 %collective-permute-done.13.refs_11_ = f32[8,32,512]{2,1,0:T(8,128)S(1)} collective-permute-done((f32[8,32,512]{2,1,0:T(8,128)S(1)}, f32[8,32,512]{2,1,0:T(8,128)S(1)}, u32[]{:S(2)}, u32[]{:S(2)}) %collective-permute-start.13) | collective-permute-done | bytes 524320 | tf_op jit(solution)/shard_map/ppermute | solution.py:834
  86.7 1.3 %collective-permute-start.16 = (f32[8,32,512]{2,1,0:T(8,128)S(1)}, f32[8,32,512]{2,1,0:T(8,128)S(1)}, u32[]{:S(2)}, u32[]{:S(2)}) collective-permute-start(f32[8,32,512]{2,1,0:T(8,128)S(1)} %down.5.refs_4_), channel_id=1, source_target_pairs={{8,0},{12,4},{16,8},{20,12},{24,16},{28,20},{9,1},{13,5},{17,9},{2... | collective-permute-start | bytes 1572872 | tf_op jit(solution)/shard_map/ppermute | solution.py:834
  88.0 0.2 chain.13.refs_1_
  88.2 0.9 finals.1
  89.2 4.6 %collective-permute-start.18 = (f32[256,512]{1,0:T(8,128)S(1)}, f32[256,512]{1,0:T(8,128)S(1)}, u32[]{:S(2)}, u32[]{:S(2)}) collective-permute-start(f32[256,512]{1,0:T(8,128)S(1)} %chain.13.refs_1_), channel_id=1, source_target_pairs={{0,8},{4,12},{8,16},{12,20},{16,24},{20,28},{1,9},{5,13},{9,17},{1... | collective-permute-start | bytes 1572872 | tf_op jit(solution)/shard_map/ppermute | solution.py:834
  93.8 0.3 prefix.8
  94.1 1.5 %collective-permute-start.21 = (f32[256,512]{1,0:T(8,128)S(1)}, f32[256,512]{1,0:T(8,128)S(1)}, u32[]{:S(2)}, u32[]{:S(2)}) collective-permute-start(f32[256,512]{1,0:T(8,128)S(1)} %get-tuple-element.126.refs_25_), channel_id=1, source_target_pairs={{0,4},{4,0},{8,12},{12,8},{16,20},{20,16},{24,28},{28,24},{1,5},{5... | collective-permute-start | bytes 1572872 | tf_op jit(solution)/shard_map/ppermute | solution.py:834
  95.6 1.8 %finish.6 = (bf16[1024,4096]{1,0:T(8,128)(2,1)}, f32[8,128]{1,0:T(8,128)S(1)}) custom-call(bf16[1024,2048]{1,0:T(8,128)(2,1)S(1)} %get-tuple-element.82.refs_0_, f32[1024,128]{1,0:T(8,128)S(1)} %factors.1.refs_1_, bf16[1024,512]{1,0:T(8,128)(2,1)S(1)} %get-tuple-element.116.refs_2_, ...), custom_call_target="tpu_custom_call", output_to_operand_aliasing={{0}: (6, {})} | custom-call | tf_op jit(solution)/shard_map/finish/pallas_call | solution.py:53
  97.4 0.4 collective-permute-done.16.refs_0_.refs_3_
  97.8 2.6 %collective-permute-done.18.refs_3_ = f32[256,512]{1,0:T(8,128)S(1)} collective-permute-done((f32[256,512]{1,0:T(8,128)S(1)}, f32[256,512]{1,0:T(8,128)S(1)}, u32[]{:S(2)}, u32[]{:S(2)}) %collective-permute-start.18) | collective-permute-done | bytes 524320 | tf_op jit(solution)/shard_map/ppermute | solution.py:834
  100.4 0.3 prefix.9
  100.7 1.5 %collective-permute-start.20 = (f32[256,512]{1,0:T(8,128)S(1)}, f32[256,512]{1,0:T(8,128)S(1)}, u32[]{:S(2)}, u32[]{:S(2)}) collective-permute-start(f32[256,512]{1,0:T(8,128)S(1)} %get-tuple-element.124.refs_26_), channel_id=1, source_target_pairs={{0,4},{4,0},{8,12},{12,8},{16,20},{20,16},{24,28},{28,24},{1,5},{5... | collective-permute-start | bytes 1572872 | tf_op jit(solution)/shard_map/ppermute | solution.py:834
  102.2 5.2 %collective-permute-done.21.refs_4_ = f32[256,512]{1,0:T(8,128)S(1)} collective-permute-done((f32[256,512]{1,0:T(8,128)S(1)}, f32[256,512]{1,0:T(8,128)S(1)}, u32[]{:S(2)}, u32[]{:S(2)}) %collective-permute-start.21) | collective-permute-done | bytes 524320 | tf_op jit(solution)/shard_map/ppermute | solution.py:834
  107.4 1.8 %finish.7 = (bf16[1024,4096]{1,0:T(8,128)(2,1)}, f32[8,128]{1,0:T(8,128)S(1)}) custom-call(bf16[1024,2048]{1,0:T(8,128)(2,1)S(1)} %get-tuple-element.82.refs_0_, f32[1024,128]{1,0:T(8,128)S(1)} %factors.1.refs_1_, bf16[1024,512]{1,0:T(8,128)(2,1)S(1)} %get-tuple-element.127.refs_2_, ...), custom_call_target="tpu_custom_call", output_to_operand_aliasing={{0}: (6, {})} | custom-call | tf_op jit(solution)/shard_map/finish/pallas_call | solution.py:53
  109.2 3.8 %collective-permute-done.20.refs_6_ = f32[256,512]{1,0:T(8,128)S(1)} collective-permute-done((f32[256,512]{1,0:T(8,128)S(1)}, f32[256,512]{1,0:T(8,128)S(1)}, u32[]{:S(2)}, u32[]{:S(2)}) %collective-permute-start.20) | collective-permute-done | bytes 524320 | tf_op jit(solution)/shard_map/ppermute | solution.py:834
  113.0 2.7 %last.1 = (bf16[1024,4096]{1,0:T(8,128)(2,1)}, f32[8,32,512]{2,1,0:T(8,128)}, f32[8,128]{1,0:T(8,128)}) custom-call(bf16[1024,2048]{1,0:T(8,128)(2,1)S(1)} %get-tuple-element.82.refs_0_, f32[1024,128]{1,0:T(8,128)S(1)} %factors.1.refs_1_, f32[24,128]{1,0:T(8,128)S(1)} %get-tuple-element.79.refs_0_.refs_2_, ...), custom_call_target="tpu_custom_call", output_to_operand_aliasing={{0}: (27, {})} | custom-call | tf_op jit(solution)/shard_map/last/pallas_call | solution.py:53
  (25 shorter events, 0.7 us)
Async XLA Ops:
  4.5 9.7 %collective-permute-start = (f32[136,512]{1,0:T(8,128)S(1)}, f32[136,512]{1,0:T(8,128)S(1)}, u32[]{:S(2)}, u32[]{:S(2)}) collective-permute-start(f32[136,512]{1,0:T(8,128)S(1)} %get-tuple-element.75), channel_id=1, source_target_pairs={{0,4},{4,0},{8,12},{12,8},{16,20},{20,16},{24,28},{28,24},{1,5},{5... | collective-permute-start | bytes 835592 | tf_op jit(solution)/shard_map/ppermute | solution.py:834
  14.2 6.8 %collective-permute-start.1 = (f32[1,2,8,384]{3,2,1,0:T(8,128)S(1)}, f32[1,2,8,384]{3,2,1,0:T(8,128)S(1)}, u32[]{:S(2)}, u32[]{:S(2)}) collective-permute-start(f32[1,2,8,384]{3,2,1,0:T(8,128)S(1)} %bitcast.2), channel_id=1, source_target_pairs={{0,24},{4,28},{8,0},{12,4},{16,8},{20,12},{24,16},{28,20},{1,25},{... | collective-permute-start | bytes 73736 | tf_op jit(solution)/shard_map/ppermute | solution.py:834
  18.0 11.8 %collective-permute-start.3 = (f32[128,512]{1,0:T(8,128)S(1)}, f32[128,512]{1,0:T(8,128)S(1)}, u32[]{:S(2)}, u32[]{:S(2)}) collective-permute-start(f32[128,512]{1,0:T(8,128)S(1)} %get-tuple-element.80), channel_id=1, source_target_pairs={{0,4},{4,0},{8,12},{12,8},{16,20},{20,16},{24,28},{28,24},{1,5},{5... | collective-permute-start | bytes 786440 | tf_op jit(solution)/shard_map/ppermute | solution.py:834
  19.7 10.1 %collective-permute-start.4 = (f32[128,512]{1,0:T(8,128)S(1)}, f32[128,512]{1,0:T(8,128)S(1)}, u32[]{:S(2)}, u32[]{:S(2)}) collective-permute-start(f32[128,512]{1,0:T(8,128)S(1)} %chain.7.refs_2_), channel_id=1, source_target_pairs={{0,8},{4,12},{8,16},{12,20},{16,24},{20,28},{1,9},{5,13},{9,17},{1... | collective-permute-start | bytes 786440 | tf_op jit(solution)/shard_map/ppermute | solution.py:834
  22.4 16.1 %collective-permute-start.5 = (f32[256,512]{1,0:T(8,128)S(1)}, f32[256,512]{1,0:T(8,128)S(1)}, u32[]{:S(2)}, u32[]{:S(2)}) collective-permute-start(f32[256,512]{1,0:T(8,128)S(1)} %get-tuple-element.87), channel_id=1, source_target_pairs={{0,4},{4,0},{8,12},{12,8},{16,20},{20,16},{24,28},{28,24},{1,5},{5... | collective-permute-start | bytes 1572872 | tf_op jit(solution)/shard_map/ppermute | solution.py:834
  23.0 5.0 %collective-permute-start.2 = (f32[2,2,8,384]{3,2,1,0:T(8,128)S(1)}, f32[2,2,8,384]{3,2,1,0:T(8,128)S(1)}, u32[]{:S(2)}, u32[]{:S(2)}) collective-permute-start(f32[2,2,8,384]{3,2,1,0:T(8,128)S(1)} %pack.2.refs_3_.refs_0_), channel_id=1, source_target_pairs={{0,16},{4,20},{8,24},{12,28},{16,0},{20,4},{24,8},{28,12},{1,17},{... | collective-permute-start | bytes 147464 | tf_op jit(solution)/shard_map/ppermute | solution.py:834
  30.0 8.5 %collective-permute-start.6 = (f32[128,512]{1,0:T(8,128)S(1)}, f32[128,512]{1,0:T(8,128)S(1)}, u32[]{:S(2)}, u32[]{:S(2)}) collective-permute-start(f32[128,512]{1,0:T(8,128)S(1)} %chain.8.refs_4_), channel_id=1, source_target_pairs={{0,8},{4,12},{8,16},{12,20},{16,24},{20,28},{1,9},{5,13},{9,17},{1... | collective-permute-start | bytes 786440 | tf_op jit(solution)/shard_map/ppermute | solution.py:834
  33.5 18.2 %collective-permute-start.8 = (f32[256,512]{1,0:T(8,128)S(1)}, f32[256,512]{1,0:T(8,128)S(1)}, u32[]{:S(2)}, u32[]{:S(2)}) collective-permute-start(f32[256,512]{1,0:T(8,128)S(1)} %get-tuple-element.96), channel_id=1, source_target_pairs={{0,4},{4,0},{8,12},{12,8},{16,20},{20,16},{24,28},{28,24},{1,5},{5... | collective-permute-start | bytes 1572872 | tf_op jit(solution)/shard_map/ppermute | solution.py:834
  38.8 12.9 %collective-permute-start.7 = (f32[256,512]{1,0:T(8,128)S(1)}, f32[256,512]{1,0:T(8,128)S(1)}, u32[]{:S(2)}, u32[]{:S(2)}) collective-permute-start(f32[256,512]{1,0:T(8,128)S(1)} %chain.9.refs_8_), channel_id=1, source_target_pairs={{0,8},{4,12},{8,16},{12,20},{16,24},{20,28},{1,9},{5,13},{9,17},{1... | collective-permute-start | bytes 1572872 | tf_op jit(solution)/shard_map/ppermute | solution.py:834
  42.5 19.2 %collective-permute-start.10 = (f32[256,512]{1,0:T(8,128)S(1)}, f32[256,512]{1,0:T(8,128)S(1)}, u32[]{:S(2)}, u32[]{:S(2)}) collective-permute-start(f32[256,512]{1,0:T(8,128)S(1)} %get-tuple-element.103), channel_id=1, source_target_pairs={{0,4},{4,0},{8,12},{12,8},{16,20},{20,16},{24,28},{28,24},{1,5},{5... | collective-permute-start | bytes 1572872 | tf_op jit(solution)/shard_map/ppermute | solution.py:834
  52.1 12.2 %collective-permute-start.9 = (f32[256,512]{1,0:T(8,128)S(1)}, f32[256,512]{1,0:T(8,128)S(1)}, u32[]{:S(2)}, u32[]{:S(2)}) collective-permute-start(f32[256,512]{1,0:T(8,128)S(1)} %chain.10.refs_6_), channel_id=1, source_target_pairs={{0,8},{4,12},{8,16},{12,20},{16,24},{20,28},{1,9},{5,13},{9,17},{1... | collective-permute-start | bytes 1572872 | tf_op jit(solution)/shard_map/ppermute | solution.py:834
  56.7 7.6 %collective-permute-start.11 = (f32[128,512]{1,0:T(8,128)S(1)}, f32[128,512]{1,0:T(8,128)S(1)}, u32[]{:S(2)}, u32[]{:S(2)}) collective-permute-start(f32[128,512]{1,0:T(8,128)S(1)} %get-tuple-element.104.refs_19_), channel_id=1, source_target_pairs={{0,4},{4,0},{8,12},{12,8},{16,20},{20,16},{24,28},{28,24},{1,5},{5... | collective-permute-start | bytes 786440 | tf_op jit(solution)/shard_map/ppermute | solution.py:834
  61.8 12.6 %collective-permute-start.12 = (f32[8,32,512]{2,1,0:T(8,128)S(1)}, f32[8,32,512]{2,1,0:T(8,128)S(1)}, u32[]{:S(2)}, u32[]{:S(2)}) collective-permute-start(f32[8,32,512]{2,1,0:T(8,128)S(1)} %down.3.refs_1_), channel_id=1, source_target_pairs={{8,0},{12,4},{16,8},{20,12},{24,16},{28,20},{9,1},{13,5},{17,9},{2... | collective-permute-start | bytes 1572872 | tf_op jit(solution)/shard_map/ppermute | solution.py:834
  64.7 11.3 %collective-permute-start.15 = (f32[256,512]{1,0:T(8,128)S(1)}, f32[256,512]{1,0:T(8,128)S(1)}, u32[]{:S(2)}, u32[]{:S(2)}) collective-permute-start(f32[256,512]{1,0:T(8,128)S(1)} %chain.11.refs_6_), channel_id=1, source_target_pairs={{0,8},{4,12},{8,16},{12,20},{16,24},{20,28},{1,9},{5,13},{9,17},{1... | collective-permute-start | bytes 1572872 | tf_op jit(solution)/shard_map/ppermute | solution.py:834
  69.1 6.9 %collective-permute-start.14 = (f32[128,512]{1,0:T(8,128)S(1)}, f32[128,512]{1,0:T(8,128)S(1)}, u32[]{:S(2)}, u32[]{:S(2)}) collective-permute-start(f32[128,512]{1,0:T(8,128)S(1)} %get-tuple-element.111.refs_21_), channel_id=1, source_target_pairs={{0,4},{4,0},{8,12},{12,8},{16,20},{20,16},{24,28},{28,24},{1,5},{5... | collective-permute-start | bytes 786440 | tf_op jit(solution)/shard_map/ppermute | solution.py:834
  74.6 11.9 %collective-permute-start.13 = (f32[8,32,512]{2,1,0:T(8,128)S(1)}, f32[8,32,512]{2,1,0:T(8,128)S(1)}, u32[]{:S(2)}, u32[]{:S(2)}) collective-permute-start(f32[8,32,512]{2,1,0:T(8,128)S(1)} %down.4.refs_1_), channel_id=1, source_target_pairs={{8,0},{12,4},{16,8},{20,12},{24,16},{28,20},{9,1},{13,5},{17,9},{2... | collective-permute-start | bytes 1572872 | tf_op jit(solution)/shard_map/ppermute | solution.py:834
  76.3 11.7 %collective-permute-start.17 = (f32[256,512]{1,0:T(8,128)S(1)}, f32[256,512]{1,0:T(8,128)S(1)}, u32[]{:S(2)}, u32[]{:S(2)}) collective-permute-start(f32[256,512]{1,0:T(8,128)S(1)} %chain.12.refs_6_), channel_id=1, source_target_pairs={{0,8},{4,12},{8,16},{12,20},{16,24},{20,28},{1,9},{5,13},{9,17},{1... | collective-permute-start | bytes 1572872 | tf_op jit(solution)/shard_map/ppermute | solution.py:834
  81.1 12.6 %collective-permute-start.19 = (f32[256,512]{1,0:T(8,128)S(1)}, f32[256,512]{1,0:T(8,128)S(1)}, u32[]{:S(2)}, u32[]{:S(2)}) collective-permute-start(f32[256,512]{1,0:T(8,128)S(1)} %get-tuple-element.117.refs_23_), channel_id=1, source_target_pairs={{0,4},{4,0},{8,12},{12,8},{16,20},{20,16},{24,28},{28,24},{1,5},{5... | collective-permute-start | bytes 1572872 | tf_op jit(solution)/shard_map/ppermute | solution.py:834
  86.7 11.1 %collective-permute-start.16 = (f32[8,32,512]{2,1,0:T(8,128)S(1)}, f32[8,32,512]{2,1,0:T(8,128)S(1)}, u32[]{:S(2)}, u32[]{:S(2)}) collective-permute-start(f32[8,32,512]{2,1,0:T(8,128)S(1)} %down.5.refs_4_), channel_id=1, source_target_pairs={{8,0},{12,4},{16,8},{20,12},{24,16},{28,20},{9,1},{13,5},{17,9},{2... | collective-permute-start | bytes 1572872 | tf_op jit(solution)/shard_map/ppermute | solution.py:834
  89.2 11.2 %collective-permute-start.18 = (f32[256,512]{1,0:T(8,128)S(1)}, f32[256,512]{1,0:T(8,128)S(1)}, u32[]{:S(2)}, u32[]{:S(2)}) collective-permute-start(f32[256,512]{1,0:T(8,128)S(1)} %chain.13.refs_1_), channel_id=1, source_target_pairs={{0,8},{4,12},{8,16},{12,20},{16,24},{20,28},{1,9},{5,13},{9,17},{1... | collective-permute-start | bytes 1572872 | tf_op jit(solution)/shard_map/ppermute | solution.py:834
  94.1 13.3 %collective-permute-start.21 = (f32[256,512]{1,0:T(8,128)S(1)}, f32[256,512]{1,0:T(8,128)S(1)}, u32[]{:S(2)}, u32[]{:S(2)}) collective-permute-start(f32[256,512]{1,0:T(8,128)S(1)} %get-tuple-element.126.refs_25_), channel_id=1, source_target_pairs={{0,4},{4,0},{8,12},{12,8},{16,20},{20,16},{24,28},{28,24},{1,5},{5... | collective-permute-start | bytes 1572872 | tf_op jit(solution)/shard_map/ppermute | solution.py:834
  100.7 12.3 %collective-permute-start.20 = (f32[256,512]{1,0:T(8,128)S(1)}, f32[256,512]{1,0:T(8,128)S(1)}, u32[]{:S(2)}, u32[]{:S(2)}) collective-permute-start(f32[256,512]{1,0:T(8,128)S(1)} %get-tuple-element.124.refs_26_), channel_id=1, source_target_pairs={{0,4},{4,0},{8,12},{12,8},{16,20},{20,16},{24,28},{28,24},{1,5},{5... | collective-permute-start | bytes 1572872 | tf_op jit(solution)/shard_map/ppermute | solution.py:834

commit v5 on v4

--- a/solution.py
+++ b/solution.py
@@ -116,12 +116,12 @@
 ):
     heads, tokens = input_ref.shape
     dqk = keys_ref.shape[1] // heads
-    dv = value_ref.shape[1]
+    dv = values_hbm.shape[1] // heads
     copies = [
         pltpu.make_async_copy(forget_hbm, forget_ref, sems.at[0]),
         pltpu.make_async_copy(input_hbm, input_ref, sems.at[1]),
         pltpu.make_async_copy(keys_hbm, keys_ref, sems.at[2]),
-        pltpu.make_async_copy(values_hbm.at[:, 0:dv], value_ref, sems.at[3]),
+        pltpu.make_async_copy(values_hbm.at[:, 0 : value_ref.shape[1]], value_ref, sems.at[3]),
     ]
     for copy in copies:
         copy.start()
@@ -176,7 +176,7 @@
         [(a, pl.ANY) for a in (input_gate, forget_gate, keys, values)],
         [
             pltpu.VMEM(keys.shape, keys.dtype),
-            pltpu.VMEM((tokens, dv), values.dtype),
+            pltpu.VMEM((tokens, len(chunks_of(heads)[0]) * dv), values.dtype),
             pltpu.VMEM((heads, tokens), jnp.float32),
             pltpu.VMEM((tokens, LANES), jnp.float32),
             pltpu.VMEM((heads, dqk + LANES), jnp.float32),
@@ -191,72 +191,65 @@
     )
 
 
-def load_kernel(in_hbm, out_ref, sem):
-    copy = pltpu.make_async_copy(in_hbm, out_ref, sem)
-    copy.start()
-    copy.wait()
-
-
-def load(order, array):
+def load_kernel(*refs):
+    *refs, sems = refs
+    count = len(refs) // 2
+    copies = [pltpu.make_async_copy(refs[i], refs[count + i], sems.at[i]) for i in range(count)]
+    for copy in copies:
+        copy.start()
+    for copy in copies:
+        copy.wait()
+
+
+def load(order, arrays):
     return call(
         order,
         load_kernel,
-        [(array, pl.ANY)],
-        [pltpu.VMEM(array.shape, array.dtype)],
+        [(array, pl.ANY) for array in arrays],
+        [pltpu.VMEM(array.shape, array.dtype) for array in arrays],
         "load",
-        scratch=[pltpu.SemaphoreType.DMA],
-    )[0]
-
-
-def memories_kernel(keys_ref, columns_ref, values_ref, *refs, heads, first, count, with_summary, with_queries):
+        scratch=[pltpu.SemaphoreType.DMA((len(arrays),))],
+    )
+
+
+def memories_kernel(keys_ref, columns_ref, values_ref, *refs, heads, first, count, with_summary):
+    *summary_ref, away_ref, kept_ref = refs
     if with_summary:
-        summary_ref, away_ref, kept_ref = refs
-        rest = away_ref.shape[0] - kept_ref.shape[0], away_ref.shape[1] - summary_ref.shape[1]
+        rest = away_ref.shape[0] - kept_ref.shape[0], away_ref.shape[1] - summary_ref[0].shape[1]
         away_ref[kept_ref.shape[0] :, :] = jnp.concatenate(
-            [summary_ref[...], jnp.zeros(rest, jnp.float32)], axis=1
+            [summary_ref[0][...], jnp.zeros(rest, jnp.float32)], axis=1
         )
-    elif with_queries:
-        queries_hbm, away_ref, kept_ref, queries_ref, sem = refs
-        copy = pltpu.make_async_copy(queries_hbm, queries_ref, sem)
-        copy.start()
-    else:
-        away_ref, kept_ref = refs
     side, _ = position()
     dqk = keys_ref.shape[1] // heads
     rows, dv = kept_ref.shape[0] // count, kept_ref.shape[1]
     stripe = dqk // lax.axis_size(AXIS)
     for i in range(count):
         head = first + i
-        value = values_ref[...] if with_summary else values_ref[:, head * dv : (head + 1) * dv]
+        place = i if with_summary else head
+        value = values_ref[:, place * dv : (place + 1) * dv]
         memory = memory_of(keys_ref[:, head * dqk : (head + 1) * dqk], value, columns_ref[:, head : head + 1])
         memory = memory.reshape(rows // stripe, 2, stripe, dv)
         low, high = memory[:, 0].reshape(rows, dv), memory[:, 1].reshape(rows, dv)
         here = pl.ds(i * rows, rows)
         away_ref[here, :] = jnp.where(side == 0, high, low)
         kept_ref[here, :] = jnp.where(side == 0, low, high)
-    if with_queries:
-        copy.wait()
-
-
-def memories(order, keys, columns, values, chunk, heads, summary=None, queries=None):
-    tokens = keys.shape[0]
+
+
+def memories(order, keys, columns, values, chunk, heads, summary=None):
     dqk = keys.shape[1] // heads
-    dv = values.shape[1] // (heads if summary is None else 1)
-    more = [] if queries is None else [(queries, pl.ANY)]
+    dv = values.shape[1] // (heads if summary is None else len(chunk))
+    more = [] if summary is None else [summary]
     rows = len(chunk) * dqk // 2
-    behind = 0 if summary is None else summary.shape[0]
+    behind = sum(a.shape[0] for a in more)
     return call(
         order,
         functools.partial(
-            memories_kernel, heads=heads, first=chunk[0], count=len(chunk), with_summary=behind > 0,
-            with_queries=bool(more),
+            memories_kernel, heads=heads, first=chunk[0], count=len(chunk), with_summary=bool(more)
         ),
-        [keys, columns, values, *([] if summary is None else [summary]), *more],
-        [pltpu.VMEM((rows + behind, dv), jnp.float32), pltpu.VMEM((rows, dv), jnp.float32)]
-        + [pltpu.VMEM(a.shape, a.dtype) for a, _ in more],
+        [keys, columns, values, *more],
+        [pltpu.VMEM((rows + behind, dv), jnp.float32), pltpu.VMEM((rows, dv), jnp.float32)],
         "memories",
         mib=12,
-        scratch=[pltpu.SemaphoreType.DMA] * len(more),
     )
 
 
@@ -480,21 +473,20 @@
         here = pl.ds(begin, tile)
         query = queries_ref[here, key_columns]
         running = columns_ref[here, heads + index : heads + index + 1]
-        total = jnp.zeros((tile, 1), jnp.float32)
-        result = None
+        total, pieces = jnp.zeros((tile, 1), jnp.float32), []
         for low in range(0, end, tile):
-            there = pl.ds(low, tile)
             scores = lax.dot_general(
-                query, keys_ref[there, key_columns], (((1,), (1,)), ((), ())), preferred_element_type=jnp.float32
+                query, keys_ref[pl.ds(low, tile), key_columns], (((1,), (1,)), ((), ())),
+                preferred_element_type=jnp.float32,
             )
             attn = jnp.exp(level[:, low : low + tile] - running) * scores
             if low == begin:
                 attn = jnp.where(causal, attn, 0.0)
             total = total + jnp.sum(attn, axis=1, keepdims=True)
-            term = jnp.dot(
-                attn.astype(jnp.bfloat16), values_ref[there, value_columns], preferred_element_type=jnp.float32
-            )
-            result = term if result is None else result + term
+            pieces.append(attn.astype(jnp.bfloat16))
+        result = jnp.dot(
+            jnp.concatenate(pieces, axis=1), values_ref[:end, value_columns], preferred_element_type=jnp.float32
+        )
         product = jnp.dot(query, parts, preferred_element_type=jnp.float32)
         lanes = lane_iota((tile, LANES))
         if len(refs) > 3:
@@ -659,25 +651,31 @@
             out_ref[i * rows + begin : i * rows + begin + size, :] = total
 
 
-def first_kernel(pair_ref, keep_ref, take_ref, out_ref):
+def first_kernel(pair_ref, keep_ref, take_ref, out_ref, *, count):
     side, _ = position()
     width = pair_ref.shape[2]
-    top, decay = [], []
-    for which in range(2):
-        top.append(pair_ref[which, 0:1, width - LANES : width - LANES + 1])
-        decay.append(pair_ref[which, 0:1, width - LANES + 1 : width - LANES + 2])
-    own = top[0] + jnp.where(side == 0, decay[1], 0.0)
-    partner = top[1] + jnp.where(side == 0, 0.0, decay[0])
-    highest = jnp.maximum(own, partner)
-    own, partner = jnp.exp(own - highest), jnp.exp(partner - highest)
-    for begin, size in row_tiles(out_ref.shape[0]):
-        here = pl.ds(begin, size)
-        out_ref[here, :] = keep_ref[here, :] * own + take_ref[here, :] * partner
-
-
-def first_step(order, pair, keep, take):
-    return call(
-        order, first_kernel, [pair, keep, take], [pltpu.VMEM(keep.shape, jnp.float32)], "chain"
+    rows = out_ref.shape[0] // count
+    for i in range(count):
+        top, decay = [], []
+        for which in range(2):
+            top.append(pair_ref[which, i : i + 1, width - LANES : width - LANES + 1])
+            decay.append(pair_ref[which, i : i + 1, width - LANES + 1 : width - LANES + 2])
+        own = top[0] + jnp.where(side == 0, decay[1], 0.0)
+        partner = top[1] + jnp.where(side == 0, 0.0, decay[0])
+        highest = jnp.maximum(own, partner)
+        own, partner = jnp.exp(own - highest), jnp.exp(partner - highest)
+        for begin, size in row_tiles(rows):
+            here = pl.ds(i * rows + begin, size)
+            out_ref[here, :] = keep_ref[here, :] * own + take_ref[here, :] * partner
+
+
+def first_step(order, pair, keep, take, count):
+    return call(
+        order,
+        functools.partial(first_kernel, count=count),
+        [pair, keep, take],
+        [pltpu.VMEM(keep.shape, jnp.float32)],
+        "chain",
     )[0]
 
 
@@ -778,10 +776,9 @@
     )[0]
 
 
-def last_kernel(queries_ref, factors_ref, table_ref, above_ref, *refs, items, heads, views, prefix_views):
-    out_hbm, final_hbm, token_ref, memory, scratch, sems, final_ref, final_sem = refs[-8:]
+def final_kernel(table_ref, above_ref, *refs, views, prefix_views):
+    *_, final_hbm, token_ref, final_ref, sem = refs
     token_ref[...] = jnp.zeros_like(token_ref)
-    copies = finish_heads(queries_ref, factors_ref, refs, items, heads, out_hbm, memory, scratch, sems)
     side, level = position()
     stripe = above_ref.shape[1]
     entry = entry_of(table_ref)
@@ -790,37 +787,23 @@
         here = lambda row: pl.ds(pl.multiple_of(row + level * stripe, stripe), stripe)
         prefix = jnp.where(side == 0, refs[own][here(own_row), :], refs[sent][here(sent_row), :])
         final_ref[head] = value + prefix * entry(ROW_FIN_P, head) + above_ref[head]
-    copies.append(pltpu.make_async_copy(final_ref, final_hbm, final_sem))
-    copies[-1].start()
-    for copy in copies:
-        copy.wait()
-
-
-def last(order, wanted, queries, factor, hidden, heads, table, above, kept, received, owns, sends):
-    operands, items = finish_operands(wanted)
+    copy = pltpu.make_async_copy(final_ref, final_hbm, sem)
+    copy.start()
+    copy.wait()
+
+
+def final_rows(order, table, above, kept, received, owns, sends):
+    operands = Operands()
     views = [(operands.view(keep), operands.view(take)) for keep, take in zip(kept, received)]
     prefix_views = [(operands.view(own), operands.view(sent)) for own, sent in zip(owns, sends)]
-    tokens = queries.shape[0]
-    dv = wanted[0][1].shape[1]
-    arrays = [queries, factor, table, above, *operands.arrays, (hidden, pl.ANY)]
-    return call(
-        order,
-        functools.partial(last_kernel, items=items, heads=heads, views=views, prefix_views=prefix_views),
-        arrays,
-        [
-            pltpu.HBM((tokens, heads * dv), jnp.bfloat16),
-            pltpu.HBM(above.shape, jnp.float32),
-            pltpu.VMEM((8, LANES), jnp.float32),
-        ],
-        "last",
-        mib=12,
-        scratch=[
-            *finish_scratch(wanted, tokens),
-            pltpu.VMEM(above.shape, jnp.float32),
-            pltpu.SemaphoreType.DMA,
-        ],
-        aliases={len(arrays) - 1: 0},
-    )[:2]
+    return call(
+        order,
+        functools.partial(final_kernel, views=views, prefix_views=prefix_views),
+        [table, above, *operands.arrays],
+        [pltpu.HBM(above.shape, jnp.float32), pltpu.VMEM((8, LANES), jnp.float32)],
+        "final_rows",
+        scratch=[pltpu.VMEM(above.shape, jnp.float32), pltpu.SemaphoreType.DMA],
+    )[0]
 
 
 def shards(queries, keys, values, input_gate, forget_gate, *, blocks):
@@ -829,8 +812,10 @@
     rows_of_unit = dqk // 2
     levels = blocks // 2
     across = [(i, i ^ 1) for i in range(blocks)]
-    up = [(i, i + 2) for i in range(blocks - 2)]
-    downward = [(i + 2, i) for i in range(blocks - 2)]
+    hops = lambda levels_sending, by: [(2 * z + i, 2 * (z + by) + i) for z in levels_sending for i in range(2)]
+    up = lambda step: hops([z for z in range(levels - 1) if 0 <= step - z < len(chunks)], 1)
+    downward = lambda step: hops([z for z in range(1, levels) if step - levels + z >= 0], -1)
+    back = [(i, i ^ 1) for i in range(blocks) if i != 1]
     send = lambda value, pairs: lax.ppermute(value, AXIS, pairs)
     order = Order()
     chunks = chunks_of(heads)
@@ -847,22 +832,22 @@
     taken, kept = [], []
 
     def remember(held_values, chunk, **more):
-        away, keep, *rest = memories(order, keys, columns, held_values, chunk, heads, **more)
+        away, keep = memories(order, keys, columns, held_values, chunk, heads, **more)
         taken.append(send(away, across))
         kept.append(keep)
-        return rest
 
     remember(first_value, chunks[0], summary=summary)
-    values = load(order, values)
+    values, queries = load(order, [values, queries])
     remember(values, chunks[1])
 
     pair = pair_of(order, summary, taken[0])
-    arrived = [(send(first_step(order, pair, kept[0], taken[0]), up), rows_of_unit, 1)]
+    alone = len(chunks[0])
+    arrived = [(send(first_step(order, pair, kept[0], taken[0], alone), up(0)), rows_of_unit, alone)]
     gathered = pair[None]
     while gathered.shape[0] < levels:
         reach = gathered.shape[0]
         more = send(gathered, [(i, (i - 2 * reach) % blocks) for i in range(blocks)])
-        if reach > 1 and len(taken) < len(chunks) - 1:
+        if len(taken) < len(chunks) - 1:
             remember(values, chunks[len(taken)])
         gathered = pack(order, [gathered, more], min(2 * reach, levels))
     while len(taken) < len(chunks) - 1:
@@ -889,13 +874,13 @@
         )
         sends.append(to_send)
         owns.append(own)
-        others.append(send(to_send, across))
+        others.append(send(to_send, back))
 
     def fall():
         nonlocal falls, above
         falls += 1
         above = send(
-            down(order, table, falls, levels, views_of(kept), views_of(taken), above, dqk // blocks), downward
+            down(order, table, falls, levels, views_of(kept), views_of(taken), above, dqk // blocks), downward(falls)
         )
 
     def wanted(chunk):
@@ -906,15 +891,15 @@
         hidden = finish(order, wanted(finished), queries, factor, hidden, heads)
         finished += 1
 
-    plan = {1: "ma", 2: "aaaa", 3: "paadx", 4: "paFodx", 5: "pod", 6: "fXpoY"}
+    plan = {1: "ma", 2: "aaaa", 3: "paadx", 4: "paFodx", 5: "pofd", 6: "XpoY"}
     for step in range(1, steps):
         value, unit_rows, count = chain_step(
             order, table, step, chunks, views_of(kept), views_of(taken), arrived[-1], levels
         )
-        arrived.append((send(value, up), unit_rows, count))
+        arrived.append((send(value, up(step)), unit_rows, count))
         for what in plan.get(step, ""):
             if what == "m":
-                (queries,) = remember(values, chunks[-1], queries=queries)
+                remember(values, chunks[-1])
             elif what == "a":
                 attend(1)
             elif what == "f":
@@ -929,6 +914,8 @@
                 put()
             elif what == "x" and others:
                 wait(order, others[-1])
+            elif what == "W":
+                wait(order, taken[-1], 3e9)
             elif what == "X" and others:
                 wait(order, others[-1], 3e9)
             elif what == "Y" and above is not None:
@@ -942,12 +929,11 @@
         fall()
     if final_normal is None:
         final_normal, tops = finals(order, gathered)
-    while finished < len(chunks) - 1:
+    final_memory = final_rows(
+        order, table, above, views_of(kept), views_of(taken), views_of(owns), views_of(sends)
+    )
+    while finished < len(chunks):
         put()
-    hidden, final_memory = last(
-        order, wanted(len(chunks) - 1), queries, factor, hidden, heads, table, above,
-        views_of(kept), views_of(taken), views_of(owns), views_of(sends),
-    )
     return hidden, final_memory, final_normal, tops.reshape(heads)
 
 

time: 116 us -> 114 us (0.983)
  Pallas kernels: 44.7 us -> 41.9 us
  waiting for transfers between devices: 21.8 us -> 23 us
    pallas_call x45 -> x46, Pallas kernels: 44.7 us -> 41.9 us  [call(): pl.pallas_call(body, in_specs=in_specs, out_specs=out_specs, out_shape=li...]
    ppermute x22, waiting for transfers between devices: 21.8 us -> 23 us  [shards(): send = lambda value, pairs: lax.ppermute(value, AXIS, pairs)]
  transfers between devices with their start and end apart: 22 -> 22, of which waited for: 8 -> 6; matrix products, arithmetic and copies ran while one was open for 0% -> 0% of each run, Pallas kernels for 33% -> 31%
where the time goes in v5:
time: 114 us
  starting transfers between devices  47.8 us (42%)
  Pallas kernels  41.9 us (37%)
  waiting for transfers between devices  23 us (20%)
  between operations  1.34 us (1%)
    ppermute x22, starting transfers between devices, shards(): send = lambda value, pairs: lax.ppermute(value, AXIS, pairs)  47.8 us
    pallas_call x46, Pallas kernels, call(): pl.pallas_call(body, in_specs=in_specs, out_specs=out_specs, out_shape=li...  41.9 us
    ppermute x22, waiting for transfers between devices, shards(): send = lambda value, pairs: lax.ppermute(value, AXIS, pairs)  23 us
  transfers between devices with their start and end apart: 22, of which 6 were waited for; matrix products, arithmetic and copies ran while one was open for 0% of the time, Pallas kernels for 31%

profile of v5, /device:TPU:0, one launch (start us, length us, event | category | flops | bytes accessed | tf_op | source)
XLA Modules:
  0.0 114.0 jit_solution(12562162535590861300)
XLA Ops:
  0.6 3.1 %start.1 = (bf16[1024,2048]{1,0:T(8,128)(2,1)S(1)}, bf16[1024,512]{1,0:T(8,128)(2,1)S(1)}, f32[8,1024]{1,0:T(8,128)S(1)}, f32[1024,128]{1,0:T(8,128)S(1)}, f32[8,384]{1,0:T(8,128)S(1)}) custom-call(f32[8,1024]{1,0:T(8,128)} %refs_0_.2, f32[8,1024]{1,0:T(8,128)} %refs_1_.2, bf16[1024,2048]{1,0:T(8,128)(2,1)} %refs_2_.1, bf16[1024,4096]{1,0:T(8,128)(2,1)} %refs_0_.3), custom_call_target="tpu_custom_call" | custom-call | tf_op jit(solution)/shard_map/start/pallas_call | solution.py:53
  3.7 0.8 memories.5
  4.5 3.0 %collective-permute-start = (f32[136,512]{1,0:T(8,128)S(1)}, f32[136,512]{1,0:T(8,128)S(1)}, u32[]{:S(2)}, u32[]{:S(2)}) collective-permute-start(f32[136,512]{1,0:T(8,128)S(1)} %get-tuple-element.78), channel_id=1, source_target_pairs={{0,4},{4,0},{8,12},{12,8},{16,20},{20,16},{24,28},{28,24},{1,5},{5... | collective-permute-start | bytes 835592 | tf_op jit(solution)/shard_map/ppermute | solution.py:819
  7.6 4.6 %load.1 = (bf16[1024,4096]{1,0:T(8,128)(2,1)S(1)}, bf16[1024,2048]{1,0:T(8,128)(2,1)S(1)}) custom-call(bf16[1024,4096]{1,0:T(8,128)(2,1)} %refs_0_.3, bf16[1024,2048]{1,0:T(8,128)(2,1)} %refs_1_.3, f32[128,512]{1,0:T(8,128)S(1)} %get-tuple-element.76.refs_2_.refs_1_.refs_3_.refs_5_.refs_4_), custom_call_target="tpu_custom_call" | custom-call | tf_op jit(solution)/shard_map/load/pallas_call | solution.py:53
  12.2 0.8 memories.6
  13.0 1.2 %collective-permute-done.refs_1_.refs_2_.refs_4_.refs_6_.refs_5_.refs_3_ = f32[136,512]{1,0:T(8,128)S(1)} collective-permute-done((f32[136,512]{1,0:T(8,128)S(1)}, f32[136,512]{1,0:T(8,128)S(1)}, u32[]{:S(2)}, u32[]{:S(2)}) %collective-permute-start) | collective-permute-done | bytes 278560 | tf_op jit(solution)/shard_map/ppermute | solution.py:819
  14.2 0.2 chain.7.refs_3_
  14.4 3.7 %collective-permute-start.4 = (f32[128,512]{1,0:T(8,128)S(1)}, f32[128,512]{1,0:T(8,128)S(1)}, u32[]{:S(2)}, u32[]{:S(2)}) collective-permute-start(f32[128,512]{1,0:T(8,128)S(1)} %chain.7.refs_3_), channel_id=1, source_target_pairs={{0,8},{4,12},{1,9},{5,13},{2,10},{6,14},{3,11},{7,15}} | collective-permute-start | bytes 786440 | tf_op jit(solution)/shard_map/ppermute | solution.py:819
  18.1 1.3 %memories.7 = (f32[256,512]{1,0:T(8,128)S(1)}, f32[256,512]{1,0:T(8,128)S(1)}) custom-call(bf16[1024,2048]{1,0:T(8,128)(2,1)S(1)} %get-tuple-element.72.refs_0_.refs_1_, f32[1024,128]{1,0:T(8,128)S(1)} %get-tuple-element.73.refs_1_.refs_4_.refs_0_, bf16[1024,4096]{1,0:T(8,128)(2,1)S(1)} %get-tuple-element.79.refs_2_, f32[128,512]{1,0:T(8,128)S(1)} %chain.7.refs_3_), custom_call_target="tpu_custom_call" | custom-call | tf_op jit(solution)/shard_map/memories/pallas_call | solution.py:53
  19.5 1.8 %collective-permute-start.5 = (f32[256,512]{1,0:T(8,128)S(1)}, f32[256,512]{1,0:T(8,128)S(1)}, u32[]{:S(2)}, u32[]{:S(2)}) collective-permute-start(f32[256,512]{1,0:T(8,128)S(1)} %get-tuple-element.91), channel_id=1, source_target_pairs={{0,4},{4,0},{8,12},{12,8},{16,20},{20,16},{24,28},{28,24},{1,5},{5... | collective-permute-start | bytes 1572872 | tf_op jit(solution)/shard_map/ppermute | solution.py:819
  21.2 0.8 collective-permute-start.1
  22.0 3.0 %collective-permute-done.1.refs_1_ = f32[1,2,8,384]{3,2,1,0:T(8,128)S(1)} collective-permute-done((f32[1,2,8,384]{3,2,1,0:T(8,128)S(1)}, f32[1,2,8,384]{3,2,1,0:T(8,128)S(1)}, u32[]{:S(2)}, u32[]{:S(2)}) %collective-permute-start.1) | collective-permute-done | bytes 24608 | tf_op jit(solution)/shard_map/ppermute | solution.py:819
  25.1 1.3 %memories.8 = (f32[256,512]{1,0:T(8,128)S(1)}, f32[256,512]{1,0:T(8,128)S(1)}) custom-call(bf16[1024,2048]{1,0:T(8,128)(2,1)S(1)} %get-tuple-element.72.refs_0_.refs_1_, f32[1024,128]{1,0:T(8,128)S(1)} %get-tuple-element.73.refs_1_.refs_4_.refs_0_, bf16[1024,4096]{1,0:T(8,128)(2,1)S(1)} %get-tuple-element.79.refs_2_, f32[2,2,8,384]{3,2,1,0:T(8,128)S(1)} %pack.2.refs_3_.refs_0_), custom_call_target="tpu_custom_call" | custom-call | tf_op jit(solution)/shard_map/memories/pallas_call | solution.py:53
  26.4 4.2 %collective-permute-done.2.refs_1_ = f32[2,2,8,384]{3,2,1,0:T(8,128)S(1)} collective-permute-done((f32[2,2,8,384]{3,2,1,0:T(8,128)S(1)}, f32[2,2,8,384]{3,2,1,0:T(8,128)S(1)}, u32[]{:S(2)}, u32[]{:S(2)}) %collective-permute-start.2) | collective-permute-done | bytes 49184 | tf_op jit(solution)/shard_map/ppermute | solution.py:819
  30.6 0.5 weights.1
  31.1 0.2 chain.8.refs_3_
  31.3 2.2 %collective-permute-start.6 = (f32[128,512]{1,0:T(8,128)S(1)}, f32[128,512]{1,0:T(8,128)S(1)}, u32[]{:S(2)}, u32[]{:S(2)}) collective-permute-start(f32[128,512]{1,0:T(8,128)S(1)} %chain.8.refs_3_), channel_id=1, source_target_pairs={{0,8},{4,12},{8,16},{12,20},{1,9},{5,13},{9,17},{13,21},{2,10},{6,... | collective-permute-start | bytes 786440 | tf_op jit(solution)/shard_map/ppermute | solution.py:819
  33.5 1.5 %collective-permute-start.8 = (f32[256,512]{1,0:T(8,128)S(1)}, f32[256,512]{1,0:T(8,128)S(1)}, u32[]{:S(2)}, u32[]{:S(2)}) collective-permute-start(f32[256,512]{1,0:T(8,128)S(1)} %get-tuple-element.100), channel_id=1, source_target_pairs={{0,4},{4,0},{8,12},{12,8},{16,20},{20,16},{24,28},{28,24},{1,5},{5... | collective-permute-start | bytes 1572872 | tf_op jit(solution)/shard_map/ppermute | solution.py:819
  34.9 1.3 %memories.9 = (f32[256,512]{1,0:T(8,128)S(1)}, f32[256,512]{1,0:T(8,128)S(1)}) custom-call(bf16[1024,2048]{1,0:T(8,128)(2,1)S(1)} %get-tuple-element.72.refs_0_.refs_1_, f32[1024,128]{1,0:T(8,128)S(1)} %get-tuple-element.73.refs_1_.refs_4_.refs_0_, bf16[1024,4096]{1,0:T(8,128)(2,1)S(1)} %get-tuple-element.79.refs_2_, f32[128,512]{1,0:T(8,128)S(1)} %chain.8.refs_3_), custom_call_target="tpu_custom_call" | custom-call | tf_op jit(solution)/shard_map/memories/pallas_call | solution.py:53
  36.3 1.6 %attention.8 = (bf16[1024,512]{1,0:T(8,128)(2,1)S(1)}, f32[1024,128]{1,0:T(8,128)S(1)}, f32[1024,128]{1,0:T(8,128)S(1)}) custom-call(bf16[1024,2048]{1,0:T(8,128)(2,1)S(1)} %get-tuple-element.77.refs_3_.refs_0_, bf16[1024,2048]{1,0:T(8,128)(2,1)S(1)} %get-tuple-element.72.refs_0_.refs_1_, bf16[1024,4096]{1,0:T(8,128)(2,1)S(1)} %get-tuple-element.79.refs_2_, ...), custom_call_target="tpu_custom_call" | custom-call | tf_op jit(solution)/shard_map/attention/pallas_call | solution.py:53
  37.9 0.3 chain.9.refs_8_
  38.2 4.1 %collective-permute-start.7 = (f32[256,512]{1,0:T(8,128)S(1)}, f32[256,512]{1,0:T(8,128)S(1)}, u32[]{:S(2)}, u32[]{:S(2)}) collective-permute-start(f32[256,512]{1,0:T(8,128)S(1)} %chain.9.refs_8_), channel_id=1, source_target_pairs={{0,8},{4,12},{8,16},{12,20},{16,24},{20,28},{1,9},{5,13},{9,17},{1... | collective-permute-start | bytes 1572872 | tf_op jit(solution)/shard_map/ppermute | solution.py:819
  42.3 1.6 %collective-permute-start.10 = (f32[256,512]{1,0:T(8,128)S(1)}, f32[256,512]{1,0:T(8,128)S(1)}, u32[]{:S(2)}, u32[]{:S(2)}) collective-permute-start(f32[256,512]{1,0:T(8,128)S(1)} %get-tuple-element.106), channel_id=1, source_target_pairs={{0,4},{4,0},{8,12},{12,8},{16,20},{20,16},{24,28},{28,24},{1,5},{5... | collective-permute-start | bytes 1572872 | tf_op jit(solution)/shard_map/ppermute | solution.py:819
  43.9 1.6 %attention.9 = (bf16[1024,512]{1,0:T(8,128)(2,1)S(1)}, f32[1024,128]{1,0:T(8,128)S(1)}, f32[1024,128]{1,0:T(8,128)S(1)}) custom-call(bf16[1024,2048]{1,0:T(8,128)(2,1)S(1)} %get-tuple-element.77.refs_3_.refs_0_, bf16[1024,2048]{1,0:T(8,128)(2,1)S(1)} %get-tuple-element.72.refs_0_.refs_1_, bf16[1024,4096]{1,0:T(8,128)(2,1)S(1)} %get-tuple-element.79.refs_2_, ...), custom_call_target="tpu_custom_call" | custom-call | tf_op jit(solution)/shard_map/attention/pallas_call | solution.py:53
  45.5 1.6 %attention.10 = (bf16[1024,512]{1,0:T(8,128)(2,1)S(1)}, f32[1024,128]{1,0:T(8,128)S(1)}, f32[1024,128]{1,0:T(8,128)S(1)}) custom-call(bf16[1024,2048]{1,0:T(8,128)(2,1)S(1)} %get-tuple-element.77.refs_3_.refs_0_, bf16[1024,2048]{1,0:T(8,128)(2,1)S(1)} %get-tuple-element.72.refs_0_.refs_1_, bf16[1024,4096]{1,0:T(8,128)(2,1)S(1)} %get-tuple-element.79.refs_2_, ...), custom_call_target="tpu_custom_call" | custom-call | tf_op jit(solution)/shard_map/attention/pallas_call | solution.py:53
  47.1 1.6 %attention.11 = (bf16[1024,512]{1,0:T(8,128)(2,1)S(1)}, f32[1024,128]{1,0:T(8,128)S(1)}, f32[1024,128]{1,0:T(8,128)S(1)}) custom-call(bf16[1024,2048]{1,0:T(8,128)(2,1)S(1)} %get-tuple-element.77.refs_3_.refs_0_, bf16[1024,2048]{1,0:T(8,128)(2,1)S(1)} %get-tuple-element.72.refs_0_.refs_1_, bf16[1024,4096]{1,0:T(8,128)(2,1)S(1)} %get-tuple-element.79.refs_2_, ...), custom_call_target="tpu_custom_call" | custom-call | tf_op jit(solution)/shard_map/attention/pallas_call | solution.py:53
  48.7 1.6 %attention.12 = (bf16[1024,512]{1,0:T(8,128)(2,1)S(1)}, f32[1024,128]{1,0:T(8,128)S(1)}, f32[1024,128]{1,0:T(8,128)S(1)}) custom-call(bf16[1024,2048]{1,0:T(8,128)(2,1)S(1)} %get-tuple-element.77.refs_3_.refs_0_, bf16[1024,2048]{1,0:T(8,128)(2,1)S(1)} %get-tuple-element.72.refs_0_.refs_1_, bf16[1024,4096]{1,0:T(8,128)(2,1)S(1)} %get-tuple-element.79.refs_2_, ...), custom_call_target="tpu_custom_call" | custom-call | tf_op jit(solution)/shard_map/attention/pallas_call | solution.py:53
  50.4 0.3 chain.10.refs_6_
  50.7 3.5 %collective-permute-start.9 = (f32[256,512]{1,0:T(8,128)S(1)}, f32[256,512]{1,0:T(8,128)S(1)}, u32[]{:S(2)}, u32[]{:S(2)}) collective-permute-start(f32[256,512]{1,0:T(8,128)S(1)} %chain.10.refs_6_), channel_id=1, source_target_pairs={{0,8},{4,12},{8,16},{12,20},{16,24},{20,28},{1,9},{5,13},{9,17},{1... | collective-permute-start | bytes 1572872 | tf_op jit(solution)/shard_map/ppermute | solution.py:819
  54.4 3.6 %collective-permute-start.11 = (f32[128,512]{1,0:T(8,128)S(1)}, f32[128,512]{1,0:T(8,128)S(1)}, u32[]{:S(2)}, u32[]{:S(2)}) collective-permute-start(f32[128,512]{1,0:T(8,128)S(1)} %get-tuple-element.107.refs_13_), channel_id=1, source_target_pairs={{0,4},{8,12},{12,8},{16,20},{20,16},{24,28},{28,24},{1,5},{9,13},{... | collective-permute-start | bytes 786440 | tf_op jit(solution)/shard_map/ppermute | solution.py:819
  58.0 1.6 %attention.13 = (bf16[1024,512]{1,0:T(8,128)(2,1)S(1)}, f32[1024,128]{1,0:T(8,128)S(1)}, f32[1024,128]{1,0:T(8,128)S(1)}) custom-call(bf16[1024,2048]{1,0:T(8,128)(2,1)S(1)} %get-tuple-element.77.refs_3_.refs_0_, bf16[1024,2048]{1,0:T(8,128)(2,1)S(1)} %get-tuple-element.72.refs_0_.refs_1_, bf16[1024,4096]{1,0:T(8,128)(2,1)S(1)} %get-tuple-element.79.refs_2_, ...), custom_call_target="tpu_custom_call" | custom-call | tf_op jit(solution)/shard_map/attention/pallas_call | solution.py:53
  59.6 1.6 %attention.14 = (bf16[1024,512]{1,0:T(8,128)(2,1)S(1)}, f32[1024,128]{1,0:T(8,128)S(1)}, f32[1024,128]{1,0:T(8,128)S(1)}) custom-call(bf16[1024,2048]{1,0:T(8,128)(2,1)S(1)} %get-tuple-element.77.refs_3_.refs_0_, bf16[1024,2048]{1,0:T(8,128)(2,1)S(1)} %get-tuple-element.72.refs_0_.refs_1_, bf16[1024,4096]{1,0:T(8,128)(2,1)S(1)} %get-tuple-element.79.refs_2_, ...), custom_call_target="tpu_custom_call" | custom-call | tf_op jit(solution)/shard_map/attention/pallas_call | solution.py:53
  61.3 0.2 down.3.refs_1_
  61.4 0.7 collective-permute-start.14
  62.2 0.4 chain.11.refs_6_
  62.6 3.1 %collective-permute-start.12 = (f32[256,512]{1,0:T(8,128)S(1)}, f32[256,512]{1,0:T(8,128)S(1)}, u32[]{:S(2)}, u32[]{:S(2)}) collective-permute-start(f32[256,512]{1,0:T(8,128)S(1)} %chain.11.refs_6_), channel_id=1, source_target_pairs={{0,8},{4,12},{8,16},{12,20},{16,24},{20,28},{1,9},{5,13},{9,17},{1... | collective-permute-start | bytes 1572872 | tf_op jit(solution)/shard_map/ppermute | solution.py:819
  65.7 0.2 prefix.6
  65.9 4.2 %collective-permute-start.13 = (f32[128,512]{1,0:T(8,128)S(1)}, f32[128,512]{1,0:T(8,128)S(1)}, u32[]{:S(2)}, u32[]{:S(2)}) collective-permute-start(f32[128,512]{1,0:T(8,128)S(1)} %get-tuple-element.112.refs_15_), channel_id=1, source_target_pairs={{0,4},{8,12},{12,8},{16,20},{20,16},{24,28},{28,24},{1,5},{9,13},{... | collective-permute-start | bytes 786440 | tf_op jit(solution)/shard_map/ppermute | solution.py:819
  70.1 1.6 %attention.15 = (bf16[1024,512]{1,0:T(8,128)(2,1)S(1)}, f32[1024,128]{1,0:T(8,128)S(1)}, f32[1024,128]{1,0:T(8,128)S(1)}) custom-call(bf16[1024,2048]{1,0:T(8,128)(2,1)S(1)} %get-tuple-element.77.refs_3_.refs_0_, bf16[1024,2048]{1,0:T(8,128)(2,1)S(1)} %get-tuple-element.72.refs_0_.refs_1_, bf16[1024,4096]{1,0:T(8,128)(2,1)S(1)} %get-tuple-element.79.refs_2_, ...), custom_call_target="tpu_custom_call" | custom-call | tf_op jit(solution)/shard_map/attention/pallas_call | solution.py:53
  71.7 1.0 factors.1.refs_1_
  72.7 1.3 %finish.5 = (bf16[1024,4096]{1,0:T(8,128)(2,1)}, f32[8,128]{1,0:T(8,128)S(1)}) custom-call(bf16[1024,2048]{1,0:T(8,128)(2,1)S(1)} %get-tuple-element.77.refs_3_.refs_0_, f32[1024,128]{1,0:T(8,128)S(1)} %factors.1.refs_1_, bf16[1024,512]{1,0:T(8,128)(2,1)S(1)} %get-tuple-element.113.refs_2_, f32[128,512]{1,0:T(8,128)S(1)} %get-tuple-element.101.refs_8_.refs_3_.refs_12_, ...), custom_call_target="tpu_custom_call" | custom-call | tf_op jit(solution)/shard_map/finish/pallas_call | solution.py:53
  74.1 0.2 down.4.refs_1_
  74.3 0.7 collective-permute-start.16
  75.0 0.3 chain.12.refs_6_
  75.3 0.7 collective-permute-start.15
  76.0 0.3 prefix.7
  76.3 4.4 %collective-permute-start.19 = (f32[256,512]{1,0:T(8,128)S(1)}, f32[256,512]{1,0:T(8,128)S(1)}, u32[]{:S(2)}, u32[]{:S(2)}) collective-permute-start(f32[256,512]{1,0:T(8,128)S(1)} %get-tuple-element.121.refs_17_), channel_id=1, source_target_pairs={{0,4},{8,12},{12,8},{16,20},{20,16},{24,28},{28,24},{1,5},{9,13},{... | collective-permute-start | bytes 1572872 | tf_op jit(solution)/shard_map/ppermute | solution.py:819
  80.7 1.3 %finish.6 = (bf16[1024,4096]{1,0:T(8,128)(2,1)}, f32[8,128]{1,0:T(8,128)S(1)}) custom-call(bf16[1024,2048]{1,0:T(8,128)(2,1)S(1)} %get-tuple-element.77.refs_3_.refs_0_, f32[1024,128]{1,0:T(8,128)S(1)} %factors.1.refs_1_, bf16[1024,512]{1,0:T(8,128)(2,1)S(1)} %get-tuple-element.115.refs_2_, ...), custom_call_target="tpu_custom_call", output_to_operand_aliasing={{0}: (5, {})} | custom-call | tf_op jit(solution)/shard_map/finish/pallas_call | solution.py:53
  82.0 0.9 finals.1
  83.0 0.2 down.5.refs_4_
  83.1 1.3 %collective-permute-start.18 = (f32[8,32,512]{2,1,0:T(8,128)S(1)}, f32[8,32,512]{2,1,0:T(8,128)S(1)}, u32[]{:S(2)}, u32[]{:S(2)}) collective-permute-start(f32[8,32,512]{2,1,0:T(8,128)S(1)} %down.5.refs_4_), channel_id=1, source_target_pairs={{8,0},{12,4},{16,8},{20,12},{24,16},{28,20},{9,1},{13,5},{17,9},{2... | collective-permute-start | bytes 1572872 | tf_op jit(solution)/shard_map/ppermute | solution.py:819
  84.5 0.2 chain.13.refs_1_
  84.7 0.7 collective-permute-start.17
  85.4 5.3 %collective-permute-done.19.refs_0_.refs_4_ = f32[256,512]{1,0:T(8,128)S(1)} collective-permute-done((f32[256,512]{1,0:T(8,128)S(1)}, f32[256,512]{1,0:T(8,128)S(1)}, u32[]{:S(2)}, u32[]{:S(2)}) %collective-permute-start.19) | collective-permute-done | bytes 524320 | tf_op jit(solution)/shard_map/ppermute | solution.py:819
  90.6 0.3 prefix.8
  90.9 4.4 %collective-permute-start.21 = (f32[256,512]{1,0:T(8,128)S(1)}, f32[256,512]{1,0:T(8,128)S(1)}, u32[]{:S(2)}, u32[]{:S(2)}) collective-permute-start(f32[256,512]{1,0:T(8,128)S(1)} %get-tuple-element.130.refs_19_), channel_id=1, source_target_pairs={{0,4},{8,12},{12,8},{16,20},{20,16},{24,28},{28,24},{1,5},{9,13},{... | collective-permute-start | bytes 1572872 | tf_op jit(solution)/shard_map/ppermute | solution.py:819
  95.3 1.8 %finish.7 = (bf16[1024,4096]{1,0:T(8,128)(2,1)}, f32[8,128]{1,0:T(8,128)S(1)}) custom-call(bf16[1024,2048]{1,0:T(8,128)(2,1)S(1)} %get-tuple-element.77.refs_3_.refs_0_, f32[1024,128]{1,0:T(8,128)S(1)} %factors.1.refs_1_, bf16[1024,512]{1,0:T(8,128)(2,1)S(1)} %get-tuple-element.120.refs_2_, ...), custom_call_target="tpu_custom_call", output_to_operand_aliasing={{0}: (6, {})} | custom-call | tf_op jit(solution)/shard_map/finish/pallas_call | solution.py:53
  97.2 0.3 prefix.9
  97.5 1.8 %collective-permute-start.20 = (f32[256,512]{1,0:T(8,128)S(1)}, f32[256,512]{1,0:T(8,128)S(1)}, u32[]{:S(2)}, u32[]{:S(2)}) collective-permute-start(f32[256,512]{1,0:T(8,128)S(1)} %get-tuple-element.127.refs_21_), channel_id=1, source_target_pairs={{0,4},{8,12},{12,8},{16,20},{20,16},{24,28},{28,24},{1,5},{9,13},{... | collective-permute-start | bytes 1572872 | tf_op jit(solution)/shard_map/ppermute | solution.py:819
  99.3 1.0 final_rows.1
  100.3 5.5 %collective-permute-done.21.refs_4_ = f32[256,512]{1,0:T(8,128)S(1)} collective-permute-done((f32[256,512]{1,0:T(8,128)S(1)}, f32[256,512]{1,0:T(8,128)S(1)}, u32[]{:S(2)}, u32[]{:S(2)}) %collective-permute-start.21) | collective-permute-done | bytes 524320 | tf_op jit(solution)/shard_map/ppermute | solution.py:819
  105.8 1.8 %finish.8 = (bf16[1024,4096]{1,0:T(8,128)(2,1)}, f32[8,128]{1,0:T(8,128)S(1)}) custom-call(bf16[1024,2048]{1,0:T(8,128)(2,1)S(1)} %get-tuple-element.77.refs_3_.refs_0_, f32[1024,128]{1,0:T(8,128)S(1)} %factors.1.refs_1_, bf16[1024,512]{1,0:T(8,128)(2,1)S(1)} %get-tuple-element.129.refs_2_, ...), custom_call_target="tpu_custom_call", output_to_operand_aliasing={{0}: (6, {})} | custom-call | tf_op jit(solution)/shard_map/finish/pallas_call | solution.py:53
  107.6 3.8 %collective-permute-done.20.refs_4_ = f32[256,512]{1,0:T(8,128)S(1)} collective-permute-done((f32[256,512]{1,0:T(8,128)S(1)}, f32[256,512]{1,0:T(8,128)S(1)}, u32[]{:S(2)}, u32[]{:S(2)}) %collective-permute-start.20) | collective-permute-done | bytes 524320 | tf_op jit(solution)/shard_map/ppermute | solution.py:819
  111.4 2.4 %finish.9 = (bf16[1024,4096]{1,0:T(8,128)(2,1)}, f32[8,128]{1,0:T(8,128)}) custom-call(bf16[1024,2048]{1,0:T(8,128)(2,1)S(1)} %get-tuple-element.77.refs_3_.refs_0_, f32[1024,128]{1,0:T(8,128)S(1)} %factors.1.refs_1_, bf16[1024,512]{1,0:T(8,128)(2,1)S(1)} %get-tuple-element.111.refs_2_, ...), custom_call_target="tpu_custom_call", output_to_operand_aliasing={{0}: (6, {})} | custom-call | tf_op jit(solution)/shard_map/finish/pallas_call | solution.py:53
  (26 shorter events, 0.3 us)
Async XLA Ops:
  4.5 9.7 %collective-permute-start = (f32[136,512]{1,0:T(8,128)S(1)}, f32[136,512]{1,0:T(8,128)S(1)}, u32[]{:S(2)}, u32[]{:S(2)}) collective-permute-start(f32[136,512]{1,0:T(8,128)S(1)} %get-tuple-element.78), channel_id=1, source_target_pairs={{0,4},{4,0},{8,12},{12,8},{16,20},{20,16},{24,28},{28,24},{1,5},{5... | collective-permute-start | bytes 835592 | tf_op jit(solution)/shard_map/ppermute | solution.py:819
  13.0 18.1 %collective-permute-start.3 = (f32[128,512]{1,0:T(8,128)S(1)}, f32[128,512]{1,0:T(8,128)S(1)}, u32[]{:S(2)}, u32[]{:S(2)}) collective-permute-start(f32[128,512]{1,0:T(8,128)S(1)} %get-tuple-element.87), channel_id=1, source_target_pairs={{0,4},{4,0},{8,12},{12,8},{16,20},{20,16},{24,28},{28,24},{1,5},{5... | collective-permute-start | bytes 786440 | tf_op jit(solution)/shard_map/ppermute | solution.py:819
  14.4 16.7 %collective-permute-start.4 = (f32[128,512]{1,0:T(8,128)S(1)}, f32[128,512]{1,0:T(8,128)S(1)}, u32[]{:S(2)}, u32[]{:S(2)}) collective-permute-start(f32[128,512]{1,0:T(8,128)S(1)} %chain.7.refs_3_), channel_id=1, source_target_pairs={{0,8},{4,12},{1,9},{5,13},{2,10},{6,14},{3,11},{7,15}} | collective-permute-start | bytes 786440 | tf_op jit(solution)/shard_map/ppermute | solution.py:819
  19.5 18.4 %collective-permute-start.5 = (f32[256,512]{1,0:T(8,128)S(1)}, f32[256,512]{1,0:T(8,128)S(1)}, u32[]{:S(2)}, u32[]{:S(2)}) collective-permute-start(f32[256,512]{1,0:T(8,128)S(1)} %get-tuple-element.91), channel_id=1, source_target_pairs={{0,4},{4,0},{8,12},{12,8},{16,20},{20,16},{24,28},{28,24},{1,5},{5... | collective-permute-start | bytes 1572872 | tf_op jit(solution)/shard_map/ppermute | solution.py:819
  21.2 3.8 %collective-permute-start.1 = (f32[1,2,8,384]{3,2,1,0:T(8,128)S(1)}, f32[1,2,8,384]{3,2,1,0:T(8,128)S(1)}, u32[]{:S(2)}, u32[]{:S(2)}) collective-permute-start(f32[1,2,8,384]{3,2,1,0:T(8,128)S(1)} %bitcast.2), channel_id=1, source_target_pairs={{0,24},{4,28},{8,0},{12,4},{16,8},{20,12},{24,16},{28,20},{1,25},{... | collective-permute-start | bytes 73736 | tf_op jit(solution)/shard_map/ppermute | solution.py:819
  25.1 5.5 %collective-permute-start.2 = (f32[2,2,8,384]{3,2,1,0:T(8,128)S(1)}, f32[2,2,8,384]{3,2,1,0:T(8,128)S(1)}, u32[]{:S(2)}, u32[]{:S(2)}) collective-permute-start(f32[2,2,8,384]{3,2,1,0:T(8,128)S(1)} %pack.2.refs_3_.refs_0_), channel_id=1, source_target_pairs={{0,16},{4,20},{8,24},{12,28},{16,0},{20,4},{24,8},{28,12},{1,17},{... | collective-permute-start | bytes 147464 | tf_op jit(solution)/shard_map/ppermute | solution.py:819
  31.3 6.6 %collective-permute-start.6 = (f32[128,512]{1,0:T(8,128)S(1)}, f32[128,512]{1,0:T(8,128)S(1)}, u32[]{:S(2)}, u32[]{:S(2)}) collective-permute-start(f32[128,512]{1,0:T(8,128)S(1)} %chain.8.refs_3_), channel_id=1, source_target_pairs={{0,8},{4,12},{8,16},{12,20},{1,9},{5,13},{9,17},{13,21},{2,10},{6,... | collective-permute-start | bytes 786440 | tf_op jit(solution)/shard_map/ppermute | solution.py:819
  33.5 16.9 %collective-permute-start.8 = (f32[256,512]{1,0:T(8,128)S(1)}, f32[256,512]{1,0:T(8,128)S(1)}, u32[]{:S(2)}, u32[]{:S(2)}) collective-permute-start(f32[256,512]{1,0:T(8,128)S(1)} %get-tuple-element.100), channel_id=1, source_target_pairs={{0,4},{4,0},{8,12},{12,8},{16,20},{20,16},{24,28},{28,24},{1,5},{5... | collective-permute-start | bytes 1572872 | tf_op jit(solution)/shard_map/ppermute | solution.py:819
  38.2 12.2 %collective-permute-start.7 = (f32[256,512]{1,0:T(8,128)S(1)}, f32[256,512]{1,0:T(8,128)S(1)}, u32[]{:S(2)}, u32[]{:S(2)}) collective-permute-start(f32[256,512]{1,0:T(8,128)S(1)} %chain.9.refs_8_), channel_id=1, source_target_pairs={{0,8},{4,12},{8,16},{12,20},{16,24},{20,28},{1,9},{5,13},{9,17},{1... | collective-permute-start | bytes 1572872 | tf_op jit(solution)/shard_map/ppermute | solution.py:819
  42.3 19.0 %collective-permute-start.10 = (f32[256,512]{1,0:T(8,128)S(1)}, f32[256,512]{1,0:T(8,128)S(1)}, u32[]{:S(2)}, u32[]{:S(2)}) collective-permute-start(f32[256,512]{1,0:T(8,128)S(1)} %get-tuple-element.106), channel_id=1, source_target_pairs={{0,4},{4,0},{8,12},{12,8},{16,20},{20,16},{24,28},{28,24},{1,5},{5... | collective-permute-start | bytes 1572872 | tf_op jit(solution)/shard_map/ppermute | solution.py:819
  50.7 11.5 %collective-permute-start.9 = (f32[256,512]{1,0:T(8,128)S(1)}, f32[256,512]{1,0:T(8,128)S(1)}, u32[]{:S(2)}, u32[]{:S(2)}) collective-permute-start(f32[256,512]{1,0:T(8,128)S(1)} %chain.10.refs_6_), channel_id=1, source_target_pairs={{0,8},{4,12},{8,16},{12,20},{16,24},{20,28},{1,9},{5,13},{9,17},{1... | collective-permute-start | bytes 1572872 | tf_op jit(solution)/shard_map/ppermute | solution.py:819
  54.4 7.8 %collective-permute-start.11 = (f32[128,512]{1,0:T(8,128)S(1)}, f32[128,512]{1,0:T(8,128)S(1)}, u32[]{:S(2)}, u32[]{:S(2)}) collective-permute-start(f32[128,512]{1,0:T(8,128)S(1)} %get-tuple-element.107.refs_13_), channel_id=1, source_target_pairs={{0,4},{8,12},{12,8},{16,20},{20,16},{24,28},{28,24},{1,5},{9,13},{... | collective-permute-start | bytes 786440 | tf_op jit(solution)/shard_map/ppermute | solution.py:819
  61.4 12.6 %collective-permute-start.14 = (f32[8,32,512]{2,1,0:T(8,128)S(1)}, f32[8,32,512]{2,1,0:T(8,128)S(1)}, u32[]{:S(2)}, u32[]{:S(2)}) collective-permute-start(f32[8,32,512]{2,1,0:T(8,128)S(1)} %down.3.refs_1_), channel_id=1, source_target_pairs={{24,16},{28,20},{25,17},{29,21},{26,18},{30,22},{27,19},{31,23}} | collective-permute-start | bytes 1572872 | tf_op jit(solution)/shard_map/ppermute | solution.py:819
  62.6 12.4 %collective-permute-start.12 = (f32[256,512]{1,0:T(8,128)S(1)}, f32[256,512]{1,0:T(8,128)S(1)}, u32[]{:S(2)}, u32[]{:S(2)}) collective-permute-start(f32[256,512]{1,0:T(8,128)S(1)} %chain.11.refs_6_), channel_id=1, source_target_pairs={{0,8},{4,12},{8,16},{12,20},{16,24},{20,28},{1,9},{5,13},{9,17},{1... | collective-permute-start | bytes 1572872 | tf_op jit(solution)/shard_map/ppermute | solution.py:819
  65.9 9.1 %collective-permute-start.13 = (f32[128,512]{1,0:T(8,128)S(1)}, f32[128,512]{1,0:T(8,128)S(1)}, u32[]{:S(2)}, u32[]{:S(2)}) collective-permute-start(f32[128,512]{1,0:T(8,128)S(1)} %get-tuple-element.112.refs_15_), channel_id=1, source_target_pairs={{0,4},{8,12},{12,8},{16,20},{20,16},{24,28},{28,24},{1,5},{9,13},{... | collective-permute-start | bytes 786440 | tf_op jit(solution)/shard_map/ppermute | solution.py:819
  74.3 8.7 %collective-permute-start.16 = (f32[8,32,512]{2,1,0:T(8,128)S(1)}, f32[8,32,512]{2,1,0:T(8,128)S(1)}, u32[]{:S(2)}, u32[]{:S(2)}) collective-permute-start(f32[8,32,512]{2,1,0:T(8,128)S(1)} %down.4.refs_1_), channel_id=1, source_target_pairs={{16,8},{20,12},{24,16},{28,20},{17,9},{21,13},{25,17},{29,21},{18,... | collective-permute-start | bytes 1572872 | tf_op jit(solution)/shard_map/ppermute | solution.py:819
  75.3 9.2 %collective-permute-start.15 = (f32[256,512]{1,0:T(8,128)S(1)}, f32[256,512]{1,0:T(8,128)S(1)}, u32[]{:S(2)}, u32[]{:S(2)}) collective-permute-start(f32[256,512]{1,0:T(8,128)S(1)} %chain.12.refs_6_), channel_id=1, source_target_pairs={{8,16},{12,20},{16,24},{20,28},{9,17},{13,21},{17,25},{21,29},{10,... | collective-permute-start | bytes 1572872 | tf_op jit(solution)/shard_map/ppermute | solution.py:819
  76.3 14.4 %collective-permute-start.19 = (f32[256,512]{1,0:T(8,128)S(1)}, f32[256,512]{1,0:T(8,128)S(1)}, u32[]{:S(2)}, u32[]{:S(2)}) collective-permute-start(f32[256,512]{1,0:T(8,128)S(1)} %get-tuple-element.121.refs_17_), channel_id=1, source_target_pairs={{0,4},{8,12},{12,8},{16,20},{20,16},{24,28},{28,24},{1,5},{9,13},{... | collective-permute-start | bytes 1572872 | tf_op jit(solution)/shard_map/ppermute | solution.py:819
  83.1 14.0 %collective-permute-start.18 = (f32[8,32,512]{2,1,0:T(8,128)S(1)}, f32[8,32,512]{2,1,0:T(8,128)S(1)}, u32[]{:S(2)}, u32[]{:S(2)}) collective-permute-start(f32[8,32,512]{2,1,0:T(8,128)S(1)} %down.5.refs_4_), channel_id=1, source_target_pairs={{8,0},{12,4},{16,8},{20,12},{24,16},{28,20},{9,1},{13,5},{17,9},{2... | collective-permute-start | bytes 1572872 | tf_op jit(solution)/shard_map/ppermute | solution.py:819
  84.7 12.5 %collective-permute-start.17 = (f32[256,512]{1,0:T(8,128)S(1)}, f32[256,512]{1,0:T(8,128)S(1)}, u32[]{:S(2)}, u32[]{:S(2)}) collective-permute-start(f32[256,512]{1,0:T(8,128)S(1)} %chain.13.refs_1_), channel_id=1, source_target_pairs={{16,24},{20,28},{17,25},{21,29},{18,26},{22,30},{19,27},{23,31}} | collective-permute-start | bytes 1572872 | tf_op jit(solution)/shard_map/ppermute | solution.py:819
  90.9 14.9 %collective-permute-start.21 = (f32[256,512]{1,0:T(8,128)S(1)}, f32[256,512]{1,0:T(8,128)S(1)}, u32[]{:S(2)}, u32[]{:S(2)}) collective-permute-start(f32[256,512]{1,0:T(8,128)S(1)} %get-tuple-element.130.refs_19_), channel_id=1, source_target_pairs={{0,4},{8,12},{12,8},{16,20},{20,16},{24,28},{28,24},{1,5},{9,13},{... | collective-permute-start | bytes 1572872 | tf_op jit(solution)/shard_map/ppermute | solution.py:819
  97.5 13.9 %collective-permute-start.20 = (f32[256,512]{1,0:T(8,128)S(1)}, f32[256,512]{1,0:T(8,128)S(1)}, u32[]{:S(2)}, u32[]{:S(2)}) collective-permute-start(f32[256,512]{1,0:T(8,128)S(1)} %get-tuple-element.127.refs_21_), channel_id=1, source_target_pairs={{0,4},{8,12},{12,8},{16,20},{20,16},{24,28},{28,24},{1,5},{9,13},{... | collective-permute-start | bytes 1572872 | tf_op jit(solution)/shard_map/ppermute | solution.py:819
